TPU v7x, 32 devices: a whole 2x2x4 slice. The times are simulated.
32 devices in a mesh: group: 8 (over y, x, core), member: 4 (over z).
Axes of the slice: x: 2, y: 2, z: 4, core: 2. Of those that a mesh axis runs over, the one named last changes fastest.
Arguments:
- state: bfloat16 [8, 4, 128, 9, 256], P('group', 'member'), may hold values from -6 to 6
- coef: bfloat16 [8, 4, 128, 256], P('group', 'member'), may hold values from 0.5 to 2
- new_group: int32 [8, 4, 128], P('group', 'member'), may hold values from -1 to 7, as said below
- face_lists: int32 [8, 4, 6, 128], P('group', 'member'), may hold values from -1 to 127
- lewis: float32 [9], replicated, may hold values from 0.3 to 3
Outputs:
- smoothed: float32 [8, 4, 128, 9, 256], P('group', 'member')
Inputs may be any that keep to these rules, and one draw needn't show every extreme that they name: -1 marks an old slot that holds no patch. A patch keeps its member index. At most 16 patches go from one device to one device, and at most 128 arrive at one device. Counts, offsets and slot numbers derived from new_group may cross devices in any integer encoding.
All inputs are finite; a program needn't handle non-finite values.
Results may differ from a plain program's by a relative error of at most 0.0003.
Values may be sent and summed in bfloat16 or wider, within the bound.
No kernel may reach another device: no remote copies, remote signals or barrier semaphores. Data moves between devices by JAX's collectives and lax.ppermute only.
A program may use at most 128 MiB of HBM per device.

v0:
```python
import jax
import jax.numpy as jnp
from jax import lax
from jax.sharding import PartitionSpec as P

PX = 16
PY = 16
SWEEPS = 2


def with_halo(block, sides, width):
    for axis, dim in sides:
        count = lax.axis_size(axis)
        forward = [(i, i + 1) for i in range(count - 1)]
        backward = [(target, source) for source, target in forward]
        low = lax.ppermute(
            lax.slice_in_dim(block, block.shape[dim] - width, None, axis=dim), axis, forward
        )
        high = lax.ppermute(lax.slice_in_dim(block, 0, width, axis=dim), axis, backward)
        block = jnp.concatenate([low, block, high], axis=dim)
    return block


def prefix(part, axis, combine, identity):
    place = lax.axis_index(axis)
    gathered = lax.all_gather(part, axis)
    state = jnp.zeros_like(part) + jnp.asarray(identity, part.dtype)

    def one(lap, state):
        return combine(state, lax.dynamic_index_in_dim(gathered, lap, 0, False))

    return lax.fori_loop(0, place, one, state)


def pick_rows(field, index):
    taken = jnp.take(field, jnp.clip(index, 0, field.shape[0] - 1), axis=0)
    return jnp.where((index >= 0)[:, None, None], taken, 0.0)


def beside_all(field, lists, lower, upper):
    slots, kinds, count = field.shape
    span = PX * PY
    depth = count // span
    cell = jnp.arange(count, dtype=jnp.int32)
    xpos = cell % PX
    ypos = cell // PX % PY
    x_low_edge = jnp.repeat(pick_rows(field[..., PX - 1 :: PX], lists[0]), PX, axis=-1)
    x_high_edge = jnp.repeat(pick_rows(field[..., 0::PX], lists[1]), PX, axis=-1)
    x_low = jnp.where(xpos == 0, x_low_edge, jnp.roll(field, 1, -1))
    x_high = jnp.where(xpos == PX - 1, x_high_edge, jnp.roll(field, -1, -1))
    layered = field.reshape(slots, kinds, depth, span)
    top_rows = layered[..., (PY - 1) * PX :].reshape(slots, kinds, depth * PX)
    bottom_rows = layered[..., :PX].reshape(slots, kinds, depth * PX)

    def spread(rows):
        shaped = rows.reshape(slots, kinds, depth, 1, PX)
        return jnp.broadcast_to(shaped, (slots, kinds, depth, PY, PX)).reshape(slots, kinds, count)

    y_low = jnp.where(ypos == 0, spread(pick_rows(top_rows, lists[2])), jnp.roll(field, PX, -1))
    y_high = jnp.where(
        ypos == PY - 1, spread(pick_rows(bottom_rows, lists[3])), jnp.roll(field, -PX, -1)
    )
    z_low = jnp.concatenate([pick_rows(lower, lists[4]), field[..., : count - span]], -1)
    z_high = jnp.concatenate([field[..., span:], pick_rows(upper, lists[5])], -1)
    return (x_low, x_high, y_low, y_high, z_low, z_high)


def sweep(phi, rhs, weights, lists, lower, upper, lewis):
    near = beside_all(phi, lists, lower, upper)
    flow = weights[0] * near[0]
    total = weights[0]
    for face in range(1, 6):
        flow = flow + weights[face] * near[face]
        total = total + weights[face]
    factor = lewis[:, None]
    return (rhs + factor * flow) / (1.0 + factor * total)


def faces_of(field):
    return jnp.stack([field, field], 0)


def face_fill(stacked):
    return with_halo(stacked, (("member", 0),), 1)


def make_weights(cell_coef, lists, lower, upper):
    near = beside_all(cell_coef, lists, lower, upper)
    return tuple((0.5 * (cell_coef + item) for item in near))


def per_device(state, coef, new_group, face_lists, lewis):
    groups = lax.axis_size("group")
    old_state = state[0, 0]
    old_coef = coef[0, 0]
    dest = new_group[0, 0]
    lists = face_lists[0, 0]
    slots = old_state.shape[0]
    capacity = slots // groups
    valid = dest >= 0
    onehot = (dest[:, None] == jnp.arange(groups, dtype=jnp.int32)[None, :]).astype(jnp.int32)
    running = jnp.sum(jnp.cumsum(onehot, 0) * onehot, axis=1) - 1
    position = jnp.where(valid, dest * capacity + running, groups * capacity)
    counts = jnp.sum(onehot, axis=0)
    offsets = prefix(
        counts, "group", lambda earlier, later: earlier + later, jnp.zeros_like(counts)
    )
    chosen = jnp.sum(onehot * offsets[None, :], axis=1) + running
    labels = (
        jnp.full((groups * capacity,), slots, jnp.int32)
        .at[position]
        .set(chosen.astype(jnp.int32), mode="drop")
    )
    send_state = (
        jnp.zeros((groups * capacity,) + old_state.shape[1:], jnp.bfloat16)
        .at[position]
        .set(old_state, mode="drop")
    )
    send_coef = (
        jnp.zeros((groups * capacity,) + old_coef.shape[1:], jnp.bfloat16)
        .at[position]
        .set(old_coef, mode="drop")
    )
    got_state, got_coef, got_labels = (
        lax.all_to_all(send_state, "group", split_axis=0, concat_axis=0, tiled=True),
        lax.all_to_all(send_coef, "group", split_axis=0, concat_axis=0, tiled=True),
        lax.all_to_all(labels, "group", split_axis=0, concat_axis=0, tiled=True),
    )
    rhs = (
        jnp.zeros(old_state.shape, jnp.float32)
        .at[got_labels]
        .set(got_state.astype(jnp.float32), mode="drop")
    )
    cell_coef = (
        jnp.zeros(old_coef.shape, jnp.float32)
        .at[got_labels]
        .set(got_coef.astype(jnp.float32), mode="drop")[:, None, :]
    )
    weights = None
    coef_ghosts = with_halo(faces_of(cell_coef).astype(jnp.bfloat16), (("member", 0),), 1).astype(
        jnp.float32
    )
    weights = make_weights(cell_coef, lists, coef_ghosts[0], coef_ghosts[3])
    phi = rhs
    for step in range(SWEEPS):
        ghosts = face_fill(faces_of(phi))
        lower = ghosts[0]
        upper = ghosts[3]
        phi = sweep(phi, rhs, weights, lists, lower, upper, lewis)
    return phi[None, None]


def solution(mesh):
    return jax.shard_map(
        per_device,
        mesh=mesh,
        in_specs=(
            P("group", "member", None, None, None),
            P("group", "member", None, None),
            P("group", "member", None),
            P("group", "member", None, None),
            P(),
        ),
        out_specs=P("group", "member", None, None, None),
        check_vma=False,
    )
```

profile of v0, /device:TPU:0, one launch (start us, length us, event | category | flops | bytes accessed | tf_op | source)
XLA Modules:
  0.0 264.5 jit_solution(9964619632945682898)
XLA Ops:
  3.6 9.5 %all-reduce = s32[64]{0:T(128)S(1)} all-reduce(s32[64]{0:T(128)S(1)} %dynamic-update-slice), channel_id=2, replica_groups=mesh['group'=8,'member'=4] {'group'}, use_global_device_ids=true, to_apply=%add | all-reduce | flops 64 | bytes 512
  16.5 3.3 %all-to-all-start = ((s32[8,16,1]{1,2,0:T(1,128)}), s32[8,16,1]{1,2,0:T(1,128)S(1)}, u32[]{:S(2)}, u32[]{:S(2)}) async-start(s32[8,16,1]{1,2,0:T(1,128)} %bitcast.7), calls=%async_computation | async-start | bytes 8192 | tf_op jit(solution)/shard_map/all_to_all | solution.py:127
  23.0 1.6 scatter_custom_fusion.3
  25.7 14.2 %scatter_fusion = bf16[128,9,256]{2,1,0:T(8,128)(2,1)} fusion(bf16[128,9,256]{2,1,0:T(8,128)(2,1)} %broadcast_in_dim.306, s32[128]{0:T(128)S(1)} %fusion.64, bf16[128,9,256]{2,1,0:T(8,128)(2,1)S(1)} %copy.37), kind=kCustom, calls=%fused_computation.19 | custom fusion | bytes 1769984 | tf_op jit(solution)/shard_map/scatter | solution.py:117
  39.8 4.9 %all-to-all-start.2 = ((bf16[8,16,256]{2,1,0:T(8,128)(2,1)}), bf16[8,16,256]{2,1,0:T(8,128)(2,1)S(1)}, u32[]{:S(2)}, u32[]{:S(2)}) async-start(bf16[8,16,256]{2,1,0:T(8,128)(2,1)} %bitcast.11), calls=%async_computation.2 | async-start | bytes 131072 | tf_op jit(solution)/shard_map/all_to_all | solution.py:126
  45.9 3.8 %all-to-all-done.2 = bf16[8,16,256]{2,1,0:T(8,128)(2,1)S(1)} async-done(((bf16[8,16,256]{2,1,0:T(8,128)(2,1)}), bf16[8,16,256]{2,1,0:T(8,128)(2,1)S(1)}, u32[]{:S(2)}, u32[]{:S(2)}) %all-to-all-start.2) | async-done | bytes 65568 | tf_op jit(solution)/shard_map/all_to_all | solution.py:126
  49.7 3.6 %all-to-all-start.1 = ((bf16[128,9,256]{2,1,0:T(8,128)(2,1)}), bf16[128,9,256]{2,1,0:T(8,128)(2,1)S(1)}, u32[]{:S(2)}, u32[]{:S(2)}) async-start(bf16[128,9,256]{2,1,0:T(8,128)(2,1)} %scatter_fusion), calls=%async_computation.1 | async-start | bytes 2097152 | tf_op jit(solution)/shard_map/all_to_all | solution.py:125
  55.7 4.7 %collective-permute-start = (bf16[1,128,1,256]{3,1,0,2:T(8,128)(2,1)S(1)}, bf16[1,128,1,256]{3,1,0,2:T(8,128)(2,1)S(1)}, u32[]{:S(2)}, u32[]{:S(2)}) collective-permute-start(bf16[1,128,1,256]{3,1,0,2:T(8,128)(2,1)S(1)} %get-tuple-element.95), channel_id=1, source_target_pairs={{0,1},{1,2},{2,3},{4,5},{5,6},{6,7},{8,9},{9,10},{10,11},{12,13},{... | collective-permute-start | bytes 196616 | tf_op jit(solution)/shard_map/ppermute | solution.py:16
  68.8 1.6 convert_element_type.40
  70.7 11.9 %scatter_fusion.1 = f32[128,9,256]{2,1,0:T(8,128)S(1)} fusion(f32[128,9,256]{2,1,0:T(8,128)S(1)} %broadcast_in_dim.305, s32[128]{0:T(128)S(1)} %fusion.63, f32[128,9,256]{2,1,0:T(8,128)} %convert_element_type.40), kind=kCustom, calls=%fused_computation.20 | custom fusion | bytes 3539456 | tf_op jit(solution)/shard_map/scatter | solution.py:132
  82.7 7.0 %slice.174 = f32[128,9,16]{2,1,0:T(8,128)S(1)} slice(f32[128,9,256]{2,1,0:T(8,128)S(1)} %scatter_fusion.1), slice={[0:128:1], [0:9:1], [15:256:16]} | slice | bytes 147456 | tf_op jit(solution)/shard_map/slice | solution.py:47
  89.7 1.6 fusion.80
  91.3 7.4 %slice.181 = f32[128,9,16]{2,1,0:T(8,128)} slice(f32[128,9,256]{2,1,0:T(8,128)S(1)} %scatter_fusion.1), slice={[0:128:1], [0:9:1], [0:256:16]} | slice | bytes 147456 | tf_op jit(solution)/shard_map/slice | solution.py:48
  98.7 1.7 copy.56
  101.7 5.6 %collective-permute-start.2 = (f32[1,128,9,256]{3,1,2,0:T(8,128)}, f32[1,128,9,256]{3,1,2,0:T(8,128)}, u32[]{:S(2)}, u32[]{:S(2)}) collective-permute-start(f32[1,128,9,256]{3,1,2,0:T(8,128)} %copy.56), channel_id=1, source_target_pairs={{0,1},{1,2},{2,3},{4,5},{5,6},{6,7},{8,9},{9,10},{10,11},{12,13},{... | collective-permute-start | bytes 3538952 | tf_op jit(solution)/shard_map/ppermute | solution.py:16
  107.3 1.7 gather_fusion.1
  109.1 2.6 select_select_fusion.11
  111.7 1.8 gather_fusion.3
  113.5 2.6 select_select_fusion.10
  116.1 1.7 slice_bitcast_fusion.2
  117.8 1.9 gather_fusion.5
  121.0 1.9 gather_fusion.7
  124.3 1.4 copy.41
  125.8 2.0 copy.42
  129.3 2.0 copy.47
  131.3 1.4 copy.50
  132.8 1.9 copy.51
  134.8 1.4 copy.54
  136.3 1.9 copy.55
  138.2 1.7 fusion.78
  139.9 2.7 %fusion.79 = (f32[128,9,255]{2,1,0:T(8,128)}, f32[128,9,255]{2,1,0:T(8,128)}) fusion(f32[128,9,256]{2,1,0:T(8,128)S(1)} %scatter_fusion.1), kind=kLoop, calls=%fused_computation.200 | loop fusion | bytes 4700160 | tf_op jit(solution)/shard_map/jit(_roll_static)/slice | solution.py:50
  142.6 2.7 %fusion.77 = (f32[128,9,240]{2,1,0:T(8,128)}, f32[128,9,240]{2,1,0:T(8,128)}) fusion(f32[128,9,256]{2,1,0:T(8,128)S(1)} %scatter_fusion.1), kind=kLoop, calls=%fused_computation.198 | loop fusion | bytes 4423680 | tf_op jit(solution)/shard_map/jit(_roll_static)/slice | solution.py:61
  145.3 3.4 %copy.79 = f32[1,128,9,256]{3,2,1,0:T(8,128)} copy(f32[1,128,9,256]{3,1,2,0:T(8,128)} %collective-permute-done.3) | data formatting | bytes 2359296 | tf_op jit(solution)/shard_map/ppermute | solution.py:19
  148.6 3.8 %gather_fusion.11 = f32[128,9,256]{2,1,0:T(8,128)} fusion(f32[128,9,256]{2,1,0:T(8,128)} %bitcast.236, s32[1024]{0:T(1024)} %copy-done.35), kind=kCustom, calls=%fused_computation.15.clone | custom fusion | bytes 2359808 | tf_op jit(solution)/shard_map/jit(_take)/gather | solution.py:36
  152.4 3.4 %copy.80 = f32[1,128,9,256]{3,2,1,0:T(8,128)} copy(f32[1,128,9,256]{3,1,2,0:T(8,128)} %collective-permute-done.2) | data formatting | bytes 2359296 | tf_op jit(solution)/shard_map/ppermute | solution.py:16
  155.8 3.8 %gather_fusion.9 = f32[128,9,256]{2,1,0:T(8,128)} fusion(f32[128,9,256]{2,1,0:T(8,128)} %bitcast.237, s32[1024]{0:T(1024)} %copy-done.34), kind=kCustom, calls=%fused_computation.3.clone | custom fusion | bytes 2359808 | tf_op jit(solution)/shard_map/jit(_take)/gather | solution.py:36
  159.7 10.2 %fusion.8 = f32[128,9,256]{2,1,0:T(8,128)S(1)} fusion(f32[128,9,256]{2,1,0:T(8,128)S(1)} %scatter_fusion.1, f32[128,9,256]{2,1,0:T(8,128)} %copy.42, f32[128,9,255]{2,1,0:T(8,128)} %get-tuple-element.77, f32[128,9,1]{2,1,0:T(8,128)} %get-tuple-element.79, f32[128,9,256]{2,1,0:T(8,128)} %copy.47, f32[128,9,1]{2,1,0:T(8,128)S(1)} %copy-done.6, ...), kind=kLoop, calls=%fused_computation.33 | loop fusion | flops 8257536 | bytes 15074852 | tf_op jit(solution)/shard_map/div | solution.py:76
  171.2 1.7 copy.68
  174.2 5.6 %collective-permute-start.4 = (f32[1,128,9,256]{3,1,2,0:T(8,128)}, f32[1,128,9,256]{3,1,2,0:T(8,128)}, u32[]{:S(2)}, u32[]{:S(2)}) collective-permute-start(f32[1,128,9,256]{3,1,2,0:T(8,128)} %copy.68), channel_id=1, source_target_pairs={{0,1},{1,2},{2,3},{4,5},{5,6},{6,7},{8,9},{9,10},{10,11},{12,13},{... | collective-permute-start | bytes 3538952 | tf_op jit(solution)/shard_map/ppermute | solution.py:16
  179.8 7.6 %slice.206 = f32[128,9,16]{2,1,0:T(8,128)} slice(f32[128,9,256]{2,1,0:T(8,128)} %copy-done.2), slice={[0:128:1], [0:9:1], [0:256:16]} | slice | bytes 147456 | tf_op jit(solution)/shard_map/slice | solution.py:48
  187.4 6.9 %slice.203 = f32[128,9,16]{2,1,0:T(8,128)S(1)} slice(f32[128,9,256]{2,1,0:T(8,128)} %copy-done.2), slice={[0:128:1], [0:9:1], [15:256:16]} | slice | bytes 147456 | tf_op jit(solution)/shard_map/slice | solution.py:47
  194.4 3.2 %slice_bitcast_fusion.1 = (f32[128,9,16]{2,1,0:T(8,128)}, f32[128,9,16]{2,1,0:T(8,128)}) fusion(f32[128,9,1,256]{3,1,0,2:T(8,128)} %bitcast.226), kind=kLoop, calls=%fused_computation.71 | loop fusion | bytes 294912 | tf_op jit(solution)/shard_map/reshape | solution.py:52
  197.6 3.0 %gather_fusion.15 = f32[128,9,16]{2,1,0:T(8,128)} fusion(f32[128,9,16]{2,1,0:T(8,128)} %get-tuple-element.69, s32[1024]{0:T(1024)} %copy-done.39), kind=kCustom, calls=%fused_computation.13.clone | custom fusion | bytes 147968 | tf_op jit(solution)/shard_map/jit(_take)/gather | solution.py:36
  200.6 3.0 %gather_fusion.14 = f32[128,9,16]{2,1,0:T(8,128)} fusion(f32[128,9,16]{2,1,0:T(8,128)} %get-tuple-element.68, s32[1024]{0:T(1024)} %copy-done.38), kind=kCustom, calls=%fused_computation.12.clone | custom fusion | bytes 147968 | tf_op jit(solution)/shard_map/jit(_take)/gather | solution.py:36
  203.6 3.0 %gather_fusion.13 = f32[128,9,16]{2,1,0:T(8,128)} fusion(f32[128,9,16]{2,1,0:T(8,128)} %slice.206, s32[1024]{0:T(1024)} %copy-done.37), kind=kCustom, calls=%fused_computation.11.clone | custom fusion | bytes 147968 | tf_op jit(solution)/shard_map/jit(_take)/gather | solution.py:36
  206.6 1.9 gather_fusion.12
  208.6 3.8 %select_select_fusion.4 = (f32[128,9,16]{2,1,0:T(8,128)S(1)}, f32[128,9,16]{2,1,0:T(8,128)}) fusion(f32[128,9,16]{2,1,0:T(8,128)} %gather_fusion.15, pred[128]{0:T(512)(128)(4,1)S(1)} %copy-done.29, pred[128]{0:T(512)(128)(4,1)S(1)} %copy-done.31, f32[128,9,16]{2,1,0:T(8,128)} %gather_fusion.14, pred[128]{0:T(512)(128)(4,1)S(1)} %copy-done.27, ...), kind=kLoop, calls=%fused_computation.74 | loop fusion | flops 73728 | bytes 295424 | tf_op jit(solution)/shard_map/jit(_where)/select_n | solution.py:37
  212.5 2.3 select_select_fusion.6
  214.8 1.7 fusion.75
  216.9 2.0 copy.67
  218.9 1.4 copy.64
  220.4 1.9 copy.65
  222.4 1.4 copy.62
  223.9 2.0 copy.63
  227.5 2.0 copy.61
  229.4 3.3 %fusion.73 = (f32[128,9,1]{2,1,0:T(8,128)}, f32[128,9,1]{2,1,0:T(8,128)}) fusion(f32[128,9,256]{2,1,0:T(8,128)} %copy-done.2), kind=kLoop, calls=%fused_computation.194 | loop fusion | bytes 18432 | tf_op jit(solution)/shard_map/jit(_roll_static)/slice | solution.py:49
  232.7 2.7 %fusion.76 = (f32[128,9,240]{2,1,0:T(8,128)}, f32[128,9,240]{2,1,0:T(8,128)}) fusion(f32[128,9,256]{2,1,0:T(8,128)S(1)} %copy-done.4), kind=kLoop, calls=%fused_computation.197 | loop fusion | bytes 4423680 | tf_op jit(solution)/shard_map/jit(_roll_static)/slice | solution.py:59
  235.5 2.8 %fusion.74 = (f32[128,9,255]{2,1,0:T(8,128)}, f32[128,9,255]{2,1,0:T(8,128)}) fusion(f32[128,9,256]{2,1,0:T(8,128)S(1)} %copy-done.4), kind=kLoop, calls=%fused_computation.195 | loop fusion | bytes 4700160 | tf_op jit(solution)/shard_map/jit(_roll_static)/slice | solution.py:49
  238.3 3.4 %copy.77 = f32[1,128,9,256]{3,2,1,0:T(8,128)} copy(f32[1,128,9,256]{3,1,2,0:T(8,128)} %collective-permute-done.5) | data formatting | bytes 2359296 | tf_op jit(solution)/shard_map/ppermute | solution.py:19
  241.6 3.8 %gather_fusion.17 = f32[128,9,256]{2,1,0:T(8,128)} fusion(f32[128,9,256]{2,1,0:T(8,128)} %bitcast.234, s32[1024]{0:T(1024)} %copy-done.35), kind=kCustom, calls=%fused_computation.17.clone | custom fusion | bytes 2359808 | tf_op jit(solution)/shard_map/jit(_take)/gather | solution.py:36
  245.4 3.4 %copy.78 = f32[1,128,9,256]{3,2,1,0:T(8,128)} copy(f32[1,128,9,256]{3,1,2,0:T(8,128)} %collective-permute-done.4) | data formatting | bytes 2359296 | tf_op jit(solution)/shard_map/ppermute | solution.py:16
  248.8 3.8 %gather_fusion.16 = f32[128,9,256]{2,1,0:T(8,128)} fusion(f32[128,9,256]{2,1,0:T(8,128)} %bitcast.235, s32[1024]{0:T(1024)} %copy-done.34), kind=kCustom, calls=%fused_computation.16.clone | custom fusion | bytes 2359808 | tf_op jit(solution)/shard_map/jit(_take)/gather | solution.py:36
  252.7 10.1 %fusion.28 = f32[1,1,128,9,256]{4,3,2,1,0:T(8,128)S(1)} fusion(f32[128,9,256]{2,1,0:T(8,128)S(1)} %scatter_fusion.1, f32[128,9,256]{2,1,0:T(8,128)} %gather_fusion.17, f32[128,9,256]{2,1,0:T(8,128)} %gather_fusion.16, f32[128,9,256]{2,1,0:T(8,128)} %copy.67, f32[128,9,16]{2,1,0:T(8,128)} %get-tuple-element.65, f32[128,9,240]{2,1,0:T(8,128)} %get-tuple-element.67, ...), kind=kLoop, calls=%fused_computation.69 | loop fusion | flops 8257536 | bytes 15074852 | tf_op jit(solution)/shard_map/broadcast_in_dim | solution.py:150
  262.8 1.7 copy.72
  (200 shorter events, 33.1 us)
Async XLA Ops:
  0.0 23.0 %copy-start = (bf16[1,1,128,256]{3,2,1,0:T(8,128)(2,1)S(1)}, bf16[1,1,128,256]{3,2,1,0:T(8,128)(2,1)}, u32[]{:S(2)}) copy-start(bf16[1,1,128,256]{3,2,1,0:T(8,128)(2,1)} %param.16) | copy-start | bytes 196612
  16.5 23.4 %all-to-all-start = ((s32[8,16,1]{1,2,0:T(1,128)}), s32[8,16,1]{1,2,0:T(1,128)S(1)}, u32[]{:S(2)}, u32[]{:S(2)}) async-start(s32[8,16,1]{1,2,0:T(1,128)} %bitcast.7), calls=%async_computation | async-start | bytes 8192 | tf_op jit(solution)/shard_map/all_to_all | solution.py:127
  20.5 88.5 %copy-start.18 = (pred[128]{0:T(512)(128)(4,1)}, pred[128]{0:T(512)(128)(4,1)S(1)}, u32[]{:S(2)}) copy-start(pred[128]{0:T(512)(128)(4,1)S(1)} %get-tuple-element.102) | copy-start | bytes 388
  20.5 93.0 %copy-start.20 = (pred[128]{0:T(512)(128)(4,1)}, pred[128]{0:T(512)(128)(4,1)S(1)}, u32[]{:S(2)}) copy-start(pred[128]{0:T(512)(128)(4,1)S(1)} %get-tuple-element.104) | copy-start | bytes 388
  20.5 99.2 %copy-start.26 = (pred[128]{0:T(512)(128)(4,1)}, pred[128]{0:T(512)(128)(4,1)S(1)}, u32[]{:S(2)}) copy-start(pred[128]{0:T(512)(128)(4,1)S(1)} %get-tuple-element.106) | copy-start | bytes 388
  20.5 102.4 %copy-start.28 = (pred[128]{0:T(512)(128)(4,1)}, pred[128]{0:T(512)(128)(4,1)S(1)}, u32[]{:S(2)}) copy-start(pred[128]{0:T(512)(128)(4,1)S(1)} %get-tuple-element.108) | copy-start | bytes 388
  21.3 46.4 %copy-start.12 = (pred[128]{0:T(512)(128)(4,1)}, pred[128]{0:T(512)(128)(4,1)S(1)}, u32[]{:S(2)}) copy-start(pred[128]{0:T(512)(128)(4,1)S(1)} %get-tuple-element.96) | copy-start | bytes 388
  21.3 46.4 %copy-start.15 = (pred[128]{0:T(512)(128)(4,1)}, pred[128]{0:T(512)(128)(4,1)S(1)}, u32[]{:S(2)}) copy-start(pred[128]{0:T(512)(128)(4,1)S(1)} %get-tuple-element.101) | copy-start | bytes 388
  21.3 87.7 %copy-start.24 = (pred[128]{0:T(512)(128)(4,1)}, pred[128]{0:T(512)(128)(4,1)S(1)}, u32[]{:S(2)}) copy-start(pred[128]{0:T(512)(128)(4,1)S(1)} %get-tuple-element.100) | copy-start | bytes 388
  21.3 92.2 %copy-start.22 = (pred[128]{0:T(512)(128)(4,1)}, pred[128]{0:T(512)(128)(4,1)S(1)}, u32[]{:S(2)}) copy-start(pred[128]{0:T(512)(128)(4,1)S(1)} %get-tuple-element.99) | copy-start | bytes 388
  21.3 98.4 %copy-start.32 = (pred[128]{0:T(512)(128)(4,1)}, pred[128]{0:T(512)(128)(4,1)S(1)}, u32[]{:S(2)}) copy-start(pred[128]{0:T(512)(128)(4,1)S(1)} %get-tuple-element.98) | copy-start | bytes 388
  21.3 101.6 %copy-start.30 = (pred[128]{0:T(512)(128)(4,1)}, pred[128]{0:T(512)(128)(4,1)S(1)}, u32[]{:S(2)}) copy-start(pred[128]{0:T(512)(128)(4,1)S(1)} %get-tuple-element.97) | copy-start | bytes 388
  21.4 46.3 %copy-start.40 = (pred[256]{0:T(512)(128)(4,1)}, pred[256]{0:T(512)(128)(4,1)S(1)}, u32[]{:S(2)}) copy-start(pred[256]{0:T(512)(128)(4,1)S(1)} %broadcast_compare_fusion.3) | copy-start | bytes 772
  21.4 46.3 %copy-start.43 = (pred[256]{0:T(512)(128)(4,1)}, pred[256]{0:T(512)(128)(4,1)S(1)}, u32[]{:S(2)}) copy-start(pred[256]{0:T(512)(128)(4,1)S(1)} %broadcast_compare_fusion.1) | copy-start | bytes 772
  21.4 46.3 %copy-start.46 = (pred[256]{0:T(512)(128)(4,1)}, pred[256]{0:T(512)(128)(4,1)S(1)}, u32[]{:S(2)}) copy-start(pred[256]{0:T(512)(128)(4,1)S(1)} %broadcast_compare_fusion) | copy-start | bytes 772
  21.4 85.9 %copy-start.36 = (s32[1024]{0:T(1024)}, s32[1024]{0:T(1024)S(1)}, u32[]{:S(2)}) copy-start(s32[1024]{0:T(1024)S(1)} %pad_clamp_fusion.5) | copy-start | bytes 12292
  21.5 90.2 %copy-start.37 = (s32[1024]{0:T(1024)}, s32[1024]{0:T(1024)S(1)}, u32[]{:S(2)}) copy-start(s32[1024]{0:T(1024)S(1)} %pad_clamp_fusion.4) | copy-start | bytes 12292
  21.5 96.4 %copy-start.38 = (s32[1024]{0:T(1024)}, s32[1024]{0:T(1024)S(1)}, u32[]{:S(2)}) copy-start(s32[1024]{0:T(1024)S(1)} %pad_clamp_fusion.3) | copy-start | bytes 12292
  21.5 99.5 %copy-start.39 = (s32[1024]{0:T(1024)}, s32[1024]{0:T(1024)S(1)}, u32[]{:S(2)}) copy-start(s32[1024]{0:T(1024)S(1)} %pad_clamp_fusion.2) | copy-start | bytes 12292
  21.5 44.6 %copy-start.35 = (s32[1024]{0:T(1024)}, s32[1024]{0:T(1024)S(1)}, u32[]{:S(2)}) copy-start(s32[1024]{0:T(1024)S(1)} %pad_clamp_fusion) | copy-start | bytes 12292
  21.6 43.8 %copy-start.34 = (s32[1024]{0:T(1024)}, s32[1024]{0:T(1024)S(1)}, u32[]{:S(2)}) copy-start(s32[1024]{0:T(1024)S(1)} %pad_clamp_fusion.1) | copy-start | bytes 12292
  21.6 46.1 %copy-start.49 = (pred[256]{0:T(512)(128)(4,1)}, pred[256]{0:T(512)(128)(4,1)S(1)}, u32[]{:S(2)}) copy-start(pred[256]{0:T(512)(128)(4,1)S(1)} %broadcast_compare_fusion.2) | copy-start | bytes 772
  39.8 9.9 %all-to-all-start.2 = ((bf16[8,16,256]{2,1,0:T(8,128)(2,1)}), bf16[8,16,256]{2,1,0:T(8,128)(2,1)S(1)}, u32[]{:S(2)}, u32[]{:S(2)}) async-start(bf16[8,16,256]{2,1,0:T(8,128)(2,1)} %bitcast.11), calls=%async_computation.2 | async-start | bytes 131072 | tf_op jit(solution)/shard_map/all_to_all | solution.py:126
  49.7 19.1 %all-to-all-start.1 = ((bf16[128,9,256]{2,1,0:T(8,128)(2,1)}), bf16[128,9,256]{2,1,0:T(8,128)(2,1)S(1)}, u32[]{:S(2)}, u32[]{:S(2)}) async-start(bf16[128,9,256]{2,1,0:T(8,128)(2,1)} %scatter_fusion), calls=%async_computation.1 | async-start | bytes 2097152 | tf_op jit(solution)/shard_map/all_to_all | solution.py:125
  54.4 11.0 %collective-permute-start.1 = (bf16[1,128,1,256]{3,1,0,2:T(8,128)(2,1)S(1)}, bf16[1,128,1,256]{3,1,0,2:T(8,128)(2,1)S(1)}, u32[]{:S(2)}, u32[]{:S(2)}) collective-permute-start(bf16[1,128,1,256]{3,1,0,2:T(8,128)(2,1)S(1)} %get-tuple-element.95), channel_id=1, source_target_pairs={{1,0},{2,1},{3,2},{5,4},{6,5},{7,6},{9,8},{10,9},{11,10},{13,12},{... | collective-permute-start | bytes 196616 | tf_op jit(solution)/shard_map/ppermute | solution.py:19
  55.7 9.7 %collective-permute-start = (bf16[1,128,1,256]{3,1,0,2:T(8,128)(2,1)S(1)}, bf16[1,128,1,256]{3,1,0,2:T(8,128)(2,1)S(1)}, u32[]{:S(2)}, u32[]{:S(2)}) collective-permute-start(bf16[1,128,1,256]{3,1,0,2:T(8,128)(2,1)S(1)} %get-tuple-element.95), channel_id=1, source_target_pairs={{0,1},{1,2},{2,3},{4,5},{5,6},{6,7},{8,9},{9,10},{10,11},{12,13},{... | collective-permute-start | bytes 196616 | tf_op jit(solution)/shard_map/ppermute | solution.py:16
  100.4 44.8 %collective-permute-start.3 = (f32[1,128,9,256]{3,1,2,0:T(8,128)}, f32[1,128,9,256]{3,1,2,0:T(8,128)}, u32[]{:S(2)}, u32[]{:S(2)}) collective-permute-start(f32[1,128,9,256]{3,1,2,0:T(8,128)} %copy.56), channel_id=1, source_target_pairs={{1,0},{2,1},{3,2},{5,4},{6,5},{7,6},{9,8},{10,9},{11,10},{13,12},{... | collective-permute-start | bytes 3538952 | tf_op jit(solution)/shard_map/ppermute | solution.py:19
  101.7 50.7 %collective-permute-start.2 = (f32[1,128,9,256]{3,1,2,0:T(8,128)}, f32[1,128,9,256]{3,1,2,0:T(8,128)}, u32[]{:S(2)}, u32[]{:S(2)}) collective-permute-start(f32[1,128,9,256]{3,1,2,0:T(8,128)} %copy.56), channel_id=1, source_target_pairs={{0,1},{1,2},{2,3},{4,5},{5,6},{6,7},{8,9},{9,10},{10,11},{12,13},{... | collective-permute-start | bytes 3538952 | tf_op jit(solution)/shard_map/ppermute | solution.py:16
  109.1 2.6 copy-start.5
  155.8 3.9 %copy-start.6 = (f32[128,9,1]{2,1,0:T(8,128)S(1)}, f32[128,9,1]{2,1,0:T(8,128)}, u32[]{:S(2)}) copy-start(f32[128,9,1]{2,1,0:T(8,128)} %get-tuple-element.78) | copy-start | bytes 13828
  155.8 3.9 %copy-start.10 = (f32[128,256]{1,0:T(8,128)S(1)}, f32[128,256]{1,0:T(8,128)}, u32[]{:S(2)}) copy-start(f32[128,256]{1,0:T(8,128)} %get-tuple-element.83) | copy-start | bytes 393220
  155.8 3.9 %copy-start.13 = (pred[128]{0:T(512)(128)(4,1)S(1)}, pred[128]{0:T(512)(128)(4,1)}, u32[]{:S(2)}) copy-start(pred[128]{0:T(512)(128)(4,1)} %copy-done.12) | copy-start | bytes 388
  155.8 3.9 %copy-start.16 = (pred[128]{0:T(512)(128)(4,1)S(1)}, pred[128]{0:T(512)(128)(4,1)}, u32[]{:S(2)}) copy-start(pred[128]{0:T(512)(128)(4,1)} %copy-done.15) | copy-start | bytes 388
  155.8 3.9 %copy-start.41 = (pred[256]{0:T(512)(128)(4,1)S(1)}, pred[256]{0:T(512)(128)(4,1)}, u32[]{:S(2)}) copy-start(pred[256]{0:T(512)(128)(4,1)} %copy-done.40) | copy-start | bytes 772
  155.8 3.9 %copy-start.44 = (pred[256]{0:T(512)(128)(4,1)S(1)}, pred[256]{0:T(512)(128)(4,1)}, u32[]{:S(2)}) copy-start(pred[256]{0:T(512)(128)(4,1)} %copy-done.43) | copy-start | bytes 772
  155.8 3.9 %copy-start.47 = (pred[256]{0:T(512)(128)(4,1)S(1)}, pred[256]{0:T(512)(128)(4,1)}, u32[]{:S(2)}) copy-start(pred[256]{0:T(512)(128)(4,1)} %copy-done.46) | copy-start | bytes 772
  155.8 3.9 %copy-start.50 = (pred[256]{0:T(512)(128)(4,1)S(1)}, pred[256]{0:T(512)(128)(4,1)}, u32[]{:S(2)}) copy-start(pred[256]{0:T(512)(128)(4,1)} %copy-done.49) | copy-start | bytes 772
  155.8 3.9 %copy-start.52 = (f32[9]{0:T(128)S(1)}, f32[9]{0:T(128)}, u32[]{:S(2)}) copy-start(f32[9]{0:T(128)} %param.19) | copy-start | bytes 112
  169.9 1.4 copy-start.2
  172.9 65.3 %collective-permute-start.5 = (f32[1,128,9,256]{3,1,2,0:T(8,128)}, f32[1,128,9,256]{3,1,2,0:T(8,128)}, u32[]{:S(2)}, u32[]{:S(2)}) collective-permute-start(f32[1,128,9,256]{3,1,2,0:T(8,128)} %copy.68), channel_id=1, source_target_pairs={{1,0},{2,1},{3,2},{5,4},{6,5},{7,6},{9,8},{10,9},{11,10},{13,12},{... | collective-permute-start | bytes 3538952 | tf_op jit(solution)/shard_map/ppermute | solution.py:19
  174.2 71.2 %collective-permute-start.4 = (f32[1,128,9,256]{3,1,2,0:T(8,128)}, f32[1,128,9,256]{3,1,2,0:T(8,128)}, u32[]{:S(2)}, u32[]{:S(2)}) collective-permute-start(f32[1,128,9,256]{3,1,2,0:T(8,128)} %copy.68), channel_id=1, source_target_pairs={{0,1},{1,2},{2,3},{4,5},{5,6},{6,7},{8,9},{9,10},{10,11},{12,13},{... | collective-permute-start | bytes 3538952 | tf_op jit(solution)/shard_map/ppermute | solution.py:16
  203.5 5.0 %copy-start.27 = (pred[128]{0:T(512)(128)(4,1)S(1)}, pred[128]{0:T(512)(128)(4,1)}, u32[]{:S(2)}) copy-start(pred[128]{0:T(512)(128)(4,1)} %copy-done.26) | copy-start | bytes 388
  203.6 5.0 %copy-start.29 = (pred[128]{0:T(512)(128)(4,1)S(1)}, pred[128]{0:T(512)(128)(4,1)}, u32[]{:S(2)}) copy-start(pred[128]{0:T(512)(128)(4,1)} %copy-done.28) | copy-start | bytes 388
  203.6 5.0 %copy-start.31 = (pred[128]{0:T(512)(128)(4,1)S(1)}, pred[128]{0:T(512)(128)(4,1)}, u32[]{:S(2)}) copy-start(pred[128]{0:T(512)(128)(4,1)} %copy-done.30) | copy-start | bytes 388
  203.6 5.0 %copy-start.33 = (pred[128]{0:T(512)(128)(4,1)S(1)}, pred[128]{0:T(512)(128)(4,1)}, u32[]{:S(2)}) copy-start(pred[128]{0:T(512)(128)(4,1)} %copy-done.32) | copy-start | bytes 388
  208.6 3.9 %copy-start.8 = (f32[128,9,16]{2,1,0:T(8,128)S(1)}, f32[128,9,16]{2,1,0:T(8,128)}, u32[]{:S(2)}) copy-start(f32[128,9,16]{2,1,0:T(8,128)} %gather_fusion.13) | copy-start | bytes 221188
  208.6 3.9 %copy-start.9 = (f32[128,9,16]{2,1,0:T(8,128)S(1)}, f32[128,9,16]{2,1,0:T(8,128)}, u32[]{:S(2)}) copy-start(f32[128,9,16]{2,1,0:T(8,128)} %gather_fusion.12) | copy-start | bytes 221188
  208.6 3.9 %copy-start.19 = (pred[128]{0:T(512)(128)(4,1)S(1)}, pred[128]{0:T(512)(128)(4,1)}, u32[]{:S(2)}) copy-start(pred[128]{0:T(512)(128)(4,1)} %copy-done.18) | copy-start | bytes 388
  208.6 3.9 %copy-start.21 = (pred[128]{0:T(512)(128)(4,1)S(1)}, pred[128]{0:T(512)(128)(4,1)}, u32[]{:S(2)}) copy-start(pred[128]{0:T(512)(128)(4,1)} %copy-done.20) | copy-start | bytes 388
  208.6 3.9 %copy-start.23 = (pred[128]{0:T(512)(128)(4,1)S(1)}, pred[128]{0:T(512)(128)(4,1)}, u32[]{:S(2)}) copy-start(pred[128]{0:T(512)(128)(4,1)} %copy-done.22) | copy-start | bytes 388
  208.6 3.9 %copy-start.25 = (pred[128]{0:T(512)(128)(4,1)S(1)}, pred[128]{0:T(512)(128)(4,1)}, u32[]{:S(2)}) copy-start(pred[128]{0:T(512)(128)(4,1)} %copy-done.24) | copy-start | bytes 388
  212.5 2.4 copy-start.3
  229.4 3.3 %copy-start.4 = (f32[128,9,256]{2,1,0:T(8,128)S(1)}, f32[128,9,256]{2,1,0:T(8,128)}, u32[]{:S(2)}) copy-start(f32[128,9,256]{2,1,0:T(8,128)} %copy-done.2) | copy-start | bytes 3538948
  248.8 3.8 %copy-start.7 = (f32[128,9,16]{2,1,0:T(8,128)S(1)}, f32[128,9,16]{2,1,0:T(8,128)}, u32[]{:S(2)}) copy-start(f32[128,9,16]{2,1,0:T(8,128)} %get-tuple-element.64) | copy-start | bytes 221188
  248.8 3.8 %copy-start.11 = (f32[128,256]{1,0:T(8,128)S(1)}, f32[128,256]{1,0:T(8,128)}, u32[]{:S(2)}) copy-start(f32[128,256]{1,0:T(8,128)} %get-tuple-element.83) | copy-start | bytes 393220
  248.8 3.9 %copy-start.14 = (pred[128]{0:T(512)(128)(4,1)S(1)}, pred[128]{0:T(512)(128)(4,1)}, u32[]{:S(2)}) copy-start(pred[128]{0:T(512)(128)(4,1)} %copy-done.12) | copy-start | bytes 388
  248.8 3.9 %copy-start.17 = (pred[128]{0:T(512)(128)(4,1)S(1)}, pred[128]{0:T(512)(128)(4,1)}, u32[]{:S(2)}) copy-start(pred[128]{0:T(512)(128)(4,1)} %copy-done.15) | copy-start | bytes 388
  248.8 3.9 %copy-start.42 = (pred[256]{0:T(512)(128)(4,1)S(1)}, pred[256]{0:T(512)(128)(4,1)}, u32[]{:S(2)}) copy-start(pred[256]{0:T(512)(128)(4,1)} %copy-done.40) | copy-start | bytes 772
  248.8 3.9 %copy-start.45 = (pred[256]{0:T(512)(128)(4,1)S(1)}, pred[256]{0:T(512)(128)(4,1)}, u32[]{:S(2)}) copy-start(pred[256]{0:T(512)(128)(4,1)} %copy-done.43) | copy-start | bytes 772
  248.8 3.9 %copy-start.48 = (pred[256]{0:T(512)(128)(4,1)S(1)}, pred[256]{0:T(512)(128)(4,1)}, u32[]{:S(2)}) copy-start(pred[256]{0:T(512)(128)(4,1)} %copy-done.46) | copy-start | bytes 772
  248.8 3.9 %copy-start.51 = (pred[256]{0:T(512)(128)(4,1)S(1)}, pred[256]{0:T(512)(128)(4,1)}, u32[]{:S(2)}) copy-start(pred[256]{0:T(512)(128)(4,1)} %copy-done.49) | copy-start | bytes 772
  248.8 3.9 %copy-start.53 = (f32[9]{0:T(128)S(1)}, f32[9]{0:T(128)}, u32[]{:S(2)}) copy-start(f32[9]{0:T(128)} %param.19) | copy-start | bytes 112
  252.7 11.9 %copy-start.1 = (bf16[1,1,128,256]{3,2,1,0:T(8,128)(2,1)S(1)}, bf16[1,1,128,256]{3,2,1,0:T(8,128)(2,1)}, u32[]{:S(2)}) copy-start(bf16[1,1,128,256]{3,2,1,0:T(8,128)(2,1)} %param.16) | copy-start | bytes 196612
where the time goes:
time: 267 us; the launch traced here: 265 us
  local copies, waits for them, and re-layouts  173 us (65%)
  other arithmetic  44.8 us (17%)
  starting transfers between devices  31.4 us (12%)
  blocking collectives  9.46 us (4%)
  waiting for transfers between devices  3.85 us (1%)
    gather x18, local copies, waits for them, and re-layouts, pick_rows(): taken = jnp.take(field, jnp.clip(index, 0, field.shape[0] - 1), axis=0)  37.4 us
    ppermute x3, starting transfers between devices, with_halo(): lax.ppermute(lax.slice_in_dim(block, block.shape[dim] - width, None, axis...  15.9 us
    slice x3, local copies, waits for them, and re-layouts, beside_all(): field[..., 0::PX]  15.4 us
    select_n x8, other arithmetic, pick_rows(): return jnp.where((index >= 0)[:, None, None], taken, 0.0)  14.3 us
    slice x3, local copies, waits for them, and re-layouts, beside_all(): field[..., PX - 1::PX]  14.3 us
    scatter x1, local copies, waits for them, and re-layouts, per_device(): send_state = jnp.zeros((groups * capacity,) + old_state.shape[1:], jnp.bf...  14.2 us
    scatter x1, local copies, waits for them, and re-layouts, per_device(): rhs = jnp.zeros(old_state.shape, jnp.float32).at[got_labels].set(got_stat...  11.9 us
    select_n x10, local copies, waits for them, and re-layouts, pick_rows(): return jnp.where((index >= 0)[:, None, None], taken, 0.0)  10.5 us
  transfers between devices with their start and end apart: 9, of which 1 were waited for; matrix products, arithmetic and copies ran while one was open for 53% of the time, Pallas kernels for 0%

commit v1 on v0

v1 whole, which is shorter than its diff:
```python
import functools

import jax
import jax.numpy as jnp
from jax import lax
from jax.experimental import pallas as pl
from jax.experimental.pallas import tpu as pltpu
from jax.sharding import PartitionSpec as P

PX = 16
PY = 16
FACES = 6
LANES = 128
BLOCK = 32
F32 = jnp.float32
BF16 = jnp.bfloat16
VMEM_LIMIT = 28 * 1024 * 1024


def dot(a, b):
    return jnp.dot(a, b, preferred_element_type=F32)


def dot_t(a, b):
    return lax.dot_general(a, b, (((1,), (1,)), ((), ())), preferred_element_type=F32)


def iota(shape, dim):
    return lax.broadcasted_iota(jnp.int32, shape, dim)


def ones_where(mask):
    return jnp.where(mask, 1.0, 0.0).astype(BF16)


def before(n):
    return ones_where(iota((n, n), 0) < iota((n, n), 1))


def list_columns(groups):
    return -(-FACES * groups // LANES) * LANES


def pack_kernel(groups, capacity, dest_ref, lists_ref, state_ref, coef_ref, send_ref):
    species, slots, cells = state_ref.shape
    extra = list_columns(groups)
    dest = dest_ref[...]
    onehot = iota((groups, slots), 0) == dest
    earlier = dot(ones_where(onehot), before(slots))
    running = jnp.sum(jnp.where(onehot, earlier, 0.0), axis=0, keepdims=True).astype(jnp.int32)
    position = jnp.where(dest >= 0, dest * capacity + running, -1)
    place = ones_where(iota((slots, slots), 0) == position)
    send_ref[:, :cells] = dot(place, coef_ref[...]).astype(BF16)
    first = (iota((slots, slots), 0) - lax.axis_index("group") * capacity) * groups
    ahead = iota((slots, slots), 1) - first
    rows = (ahead >= 0) & (ahead < groups)
    slot = lax.rem(iota((slots, extra), 0), groups)
    column = iota((slots, extra), 1)
    packed = jnp.zeros((slots, extra), F32)
    for face in range(FACES):
        entry = (lists_ref[face] + 1).astype(F32)
        packed = packed + dot(
            jnp.where(rows, entry, 0.0).astype(BF16), ones_where(column == slot + face * groups)
        )
    send_ref[:, cells : cells + extra] = packed.astype(BF16)
    start = cells + extra
    for k in range(species):
        at = slice(start + k * cells, start + (k + 1) * cells)
        send_ref[:, at] = dot(place, state_ref[k]).astype(BF16)


def unpack_lists(groups, extra_rows):
    slots, extra = extra_rows.shape
    capacity = slots // groups
    row = lax.rem(iota((slots, slots), 1), capacity)
    ahead = iota((slots, slots), 0) - row * groups
    own = dot(ones_where((ahead >= 0) & (ahead < groups)), extra_rows)
    same = lax.rem(iota((slots, extra), 1), groups) == lax.rem(iota((slots, extra), 0), groups)
    own = jnp.where(same, own, 0.0).astype(BF16)
    ahead = iota((extra, LANES), 0) - iota((extra, LANES), 1) * groups
    return dot(own, ones_where((ahead >= 0) & (ahead < groups))).astype(jnp.int32) - 1


def sorting(coef_rows):
    slots, cells = coef_rows.shape
    lead = dot_t(ones_where(iota((8, cells), 1) == 0), coef_rows)
    valid = lead > 0.0
    slot = dot(ones_where(valid), before(slots)).astype(jnp.int32)
    slot = jnp.where(valid, slot, -1)[:1]
    return ones_where(iota((slots, slots), 0) == slot)


def picking(lists, face):
    slots = lists.shape[0]
    return ones_where(iota((slots, slots), 1) == lists[:, face : face + 1])


def edge_sources(field):
    rows = field.shape[0]
    lane = iota((rows, LANES), 1)
    x = lax.rem(lane, PX)
    sides = (field[:, :LANES], field[:, LANES:])
    turn = LANES - (PX - 1)
    x_low = [jnp.where(x == 0, pltpu.roll(s, turn, 1), 0.0) for s in sides]
    x_high = [jnp.where(x == PX - 1, pltpu.roll(s, PX - 1, 1), 0.0) for s in sides]
    y_low = jnp.where(lane < PX, pltpu.roll(sides[1], PX, 1), 0.0)
    y_high = jnp.where(lane >= LANES - PX, pltpu.roll(sides[0], LANES - PX, 1), 0.0)
    none = jnp.zeros_like(y_low)
    x_faces = jnp.concatenate([jnp.concatenate(x_low, 1), jnp.concatenate(x_high, 1)], 0)
    y_faces = jnp.concatenate(
        [jnp.concatenate([y_low, none], 1), jnp.concatenate([none, y_high], 1)], 0
    )
    return x_faces.astype(BF16), y_faces.astype(BF16)


def beside_xy(field, x_edge, y_edge):
    rows = field.shape[0]
    lane = iota((rows, LANES), 1)
    x = lax.rem(lane, PX)
    low, top = lane < PX, lane >= LANES - PX
    a, b = field[:, :LANES], field[:, LANES:]
    xa, xb = x_edge[:, :LANES], x_edge[:, LANES:]
    ya, yb = y_edge[:, :LANES], y_edge[:, LANES:]
    near0 = [jnp.where(x == 0, e, pltpu.roll(f, 1, 1)) for f, e in ((a, xa), (b, xb))]
    near1 = [jnp.where(x == PX - 1, e, pltpu.roll(f, LANES - 1, 1)) for f, e in ((a, xa), (b, xb))]
    ra, rb = pltpu.roll(a, PX, 1), pltpu.roll(b, PX, 1)
    near2 = [jnp.where(low, ya, ra), jnp.where(low, ra, rb)]
    ra, rb = pltpu.roll(a, LANES - PX, 1), pltpu.roll(b, LANES - PX, 1)
    near3 = [jnp.where(top, rb, ra), jnp.where(top, yb, rb)]
    return [jnp.concatenate(n, 1) for n in (near0, near1, near2, near3)]


def split(field):
    high = field.astype(BF16)
    return high, (field - high.astype(F32)).astype(BF16)


def blocks(slots):
    return [slice(r, r + BLOCK) for r in range(0, slots, BLOCK)]


def prepare_kernel(
    groups, head0, head_lo, head_hi,
    sort_ref, x_pick, y_pick, z_pick, weights_ref, total_ref, coef_lo, coef_hi,
):
    slots = head0.shape[0]
    cells = coef_lo.shape[1]
    heads = (head0, head_lo, head_hi)
    coefs, flat, lists = [], [], []
    for d in range(3):
        rows = heads[d][:, :cells]
        sort_ref[d] = sorting(rows)
        coef = dot(sort_ref[d], rows)
        coefs.append(coef)
        flat.append(coef.astype(BF16))
        lists.append(unpack_lists(groups, heads[d][:, cells : cells + list_columns(groups)]))
        for face, target in ((0, x_pick), (2, y_pick)):
            target[d] = jnp.concatenate(
                [picking(lists[d], face), picking(lists[d], face + 1)], 1
            )
    for i, (d, face) in enumerate(((0, 4), (0, 5), (1, 5), (2, 4), (1, 4), (2, 5))):
        z_pick[i] = picking(lists[d], face)
    coef_lo[...] = coefs[1]
    coef_hi[...] = coefs[2]
    for d in range(3):
        x_faces, y_faces = edge_sources(coefs[d])
        near = beside_xy(coefs[d], dot(x_pick[d], x_faces), dot(y_pick[d], y_faces))
        for i, source in (((0, 1), (1, 2)), ((2, 0),), ((3, 0),))[d]:
            near.append(dot(z_pick[i], flat[source]))
        total = None
        for i, n in enumerate(near):
            w = 0.5 * (coefs[d] + n)
            weights_ref[d, i] = w
            total = w if total is None else total + w
        total_ref[d] = total


def inner_kernel(
    first, start, lewis_ref, sort_ref, x_pick, y_pick, z_pick, weights_ref, total_ref,
    got0, got_lo, got_hi, num0, num_lo, num_hi, field_ref, x_ref, y_ref, z_ref, phi_ref,
):
    species, slots, cells = num0.shape
    gots = (got0, got_lo, got_hi)
    numbers = (num0, num_lo, num_hi)
    depth = field_ref.shape[0]
    for k in range(species):
        b = k % depth
        at = slice(start + k * cells, start + (k + 1) * cells)
        factor = lewis_ref[first + k]
        flat = []
        for d in range(3):
            field = dot(sort_ref[d], gots[d][:, at])
            field_ref[b, d] = field
            flat.append(field.astype(BF16))
            x_faces, y_faces = edge_sources(field)
            x_ref[b, d] = dot(x_pick[d], x_faces)
            y_ref[b, d] = dot(y_pick[d], y_faces)
        for i, source in enumerate((1, 2, 0, 0)):
            z_ref[b, i] = dot(z_pick[i], flat[source])
        for d in range(3):
            for rows in blocks(slots):
                field = field_ref[b, d, rows]
                near = beside_xy(field, x_ref[b, d, rows], y_ref[b, d, rows])
                flow = weights_ref[d, 0, rows] * near[0]
                for f in range(1, 4):
                    flow = flow + weights_ref[d, f, rows] * near[f]
                if d == 0:
                    flow = flow + weights_ref[0, 4, rows] * z_ref[b, 0, rows]
                    flow = flow + weights_ref[0, 5, rows] * z_ref[b, 1, rows]
                    number = field + factor * flow
                    phi_ref[b, rows] = number / (1.0 + factor * total_ref[0, rows])
                else:
                    flow = flow + weights_ref[d, 4, rows] * z_ref[b, 1 + d, rows]
                    numbers[d][k, rows] = field + factor * flow
        high, low = split(phi_ref[b])
        x_high, y_high = edge_sources(high.astype(F32))
        x_low, y_low = edge_sources(low.astype(F32))
        x_two = jnp.concatenate([x_pick[0], x_pick[0]], 1)
        y_two = jnp.concatenate([y_pick[0], y_pick[0]], 1)
        x_ref[b, 3] = dot(x_two, jnp.concatenate([x_high, x_low], 0))
        y_ref[b, 3] = dot(y_two, jnp.concatenate([y_high, y_low], 0))
        for rows in blocks(slots):
            near = beside_xy(phi_ref[b, rows], x_ref[b, 3, rows], y_ref[b, 3, rows])
            flow = weights_ref[0, 0, rows] * near[0]
            for f in range(1, 4):
                flow = flow + weights_ref[0, f, rows] * near[f]
            num0[k, rows] = field_ref[b, 0, rows] + factor * flow


def outer_kernel(
    first, start, head, lewis_ref, z_pick, weights_ref, total_ref, coef_lo, coef_hi,
    num0, num_lo, num_hi, got_lo2, got_hi2, head_lo2, head_hi2,
    out_ref, far_ref, w_ref, t_ref, two_ref, flow_ref,
):
    species, slots, cells = num0.shape
    gots, numbers = (got_lo2, got_hi2), (num_lo, num_hi)
    for i, (rows, coef) in enumerate(((head_lo2, coef_lo), (head_hi2, coef_hi))):
        far = dot(z_pick[4 + i], sorting(rows[:, :cells])).astype(BF16)
        far_ref[i] = far
        w = 0.5 * (coef[...] + dot(far, rows[:, :cells]))
        w_ref[i] = w
        t_ref[i] = total_ref[1 + i] + w
        two_ref[i] = jnp.concatenate([z_pick[i], z_pick[i]], 1)
    for k in range(species):
        at = slice(start + k * cells, start + (k + 1) * cells)
        factor = lewis_ref[first + k]
        for i in range(2):
            ghost = dot(far_ref[i], gots[i][:, at])
            phi = (numbers[i][k] + factor * (w_ref[i] * ghost)) / (1.0 + factor * t_ref[i])
            high, low = split(phi)
            flow_ref[k % 3, i] = dot(two_ref[i], jnp.concatenate([high, low], 0))
        for rows in blocks(slots):
            flow = weights_ref[0, 4, rows] * flow_ref[k % 3, 0, rows]
            flow = flow + weights_ref[0, 5, rows] * flow_ref[k % 3, 1, rows]
            number = num0[k, rows] + factor * flow
            out_ref[k, rows] = number / (1.0 + factor * total_ref[0, rows])


def call(kernel, out_shape, scratch, operands, specs=None, flops=0):
    whole = pl.BlockSpec(memory_space=pltpu.VMEM)
    specs = specs or {}
    moved = sum(o.size * o.dtype.itemsize for o in operands)
    moved += sum(o.size * o.dtype.itemsize for o in out_shape)
    return pl.pallas_call(
        kernel,
        out_shape=out_shape,
        grid=(1,),
        in_specs=[specs.get(i, whole) for i in range(len(operands))],
        out_specs=[whole] * len(out_shape),
        scratch_shapes=scratch,
        compiler_params=pltpu.CompilerParams(vmem_limit_bytes=VMEM_LIMIT),
        cost_estimate=pl.CostEstimate(flops=flops, bytes_accessed=moved, transcendentals=0),
    )(*operands)


def per_device(state, coef, new_group, face_lists, lewis):
    groups = lax.axis_size("group")
    members = lax.axis_size("member")
    up = [(i, i + 1) for i in range(members - 1)]
    down = [(i + 1, i) for i in range(members - 1)]
    slots, species, cells = state.shape[2:]
    capacity = slots // groups
    extra = list_columns(groups)
    start = cells + extra
    smem = pl.BlockSpec(memory_space=pltpu.SMEM)

    def shape(*dims, dtype=F32):
        return jax.ShapeDtypeStruct(dims, dtype)

    (send,) = call(
        functools.partial(pack_kernel, groups, capacity),
        [shape(slots, start + species * cells, dtype=BF16)],
        [],
        (
            new_group[0],
            jnp.transpose(face_lists[0], (1, 0, 2)),
            jnp.transpose(state[0, 0], (1, 0, 2)),
            coef[0, 0],
        ),
    )
    got = lax.all_to_all(send, "group", split_axis=0, concat_axis=0, tiled=True)
    got_lo = lax.ppermute(got, "member", up)
    got_hi = lax.ppermute(got, "member", down)
    got_lo2 = lax.ppermute(got_lo, "member", up)
    got_hi2 = lax.ppermute(got_hi, "member", down)
    head = pl.BlockSpec((slots, start), lambda i: (0, 0))
    sort, x_pick, y_pick, z_pick, weights, total, coef_lo, coef_hi = call(
        functools.partial(prepare_kernel, groups),
        [
            shape(3, slots, slots, dtype=BF16),
            shape(3, slots, 2 * slots, dtype=BF16),
            shape(3, slots, 2 * slots, dtype=BF16),
            shape(6, slots, slots, dtype=BF16),
            shape(3, 6, slots, cells),
            shape(3, slots, cells),
            shape(slots, cells),
            shape(slots, cells),
        ],
        [],
        (got, got_lo, got_hi),
        specs={0: head, 1: head, 2: head},
        flops=100_000_000,
    )
    num0, num_lo, num_hi = call(
        functools.partial(inner_kernel, 0, start),
        [shape(species, slots, cells)] * 3,
        [
            pltpu.VMEM((3, 3, slots, cells), F32),
            pltpu.VMEM((3, 4, slots, cells), F32),
            pltpu.VMEM((3, 4, slots, cells), F32),
            pltpu.VMEM((3, 4, slots, cells), F32),
            pltpu.VMEM((3, slots, cells), F32),
        ],
        (lewis, sort, x_pick, y_pick, z_pick, weights, total, got, got_lo, got_hi),
        specs={0: smem},
        flops=2_000_000_000,
    )
    (out,) = call(
        functools.partial(outer_kernel, 0, start, start),
        [shape(species, slots, cells)],
        [
            pltpu.VMEM((2, slots, slots), BF16),
            pltpu.VMEM((2, slots, cells), F32),
            pltpu.VMEM((2, slots, cells), F32),
            pltpu.VMEM((2, slots, 2 * slots), BF16),
            pltpu.VMEM((3, 2, slots, cells), F32),
        ],
        (
            lewis, z_pick, weights, total, coef_lo, coef_hi, num0, num_lo, num_hi,
            got_lo2, got_hi2, got_lo2, got_hi2,
        ),
        specs={0: smem, 11: head, 12: head},
        flops=1_000_000_000,
    )
    return jnp.transpose(out, (1, 0, 2))[None, None]


def solution(mesh):
    return jax.shard_map(
        per_device,
        mesh=mesh,
        in_specs=(
            P("group", "member", None, None, None),
            P("group", "member", None, None),
            P("group", "member", None),
            P("group", "member", None, None),
            P(),
        ),
        out_specs=P("group", "member", None, None, None),
        check_vma=False,
    )
```

time: 267 us -> 64.8 us (0.24)
  local copies, waits for them, and re-layouts: 173 us -> 3.24 us
  other arithmetic: 44.8 us -> 0 us
  starting transfers between devices: 31.4 us -> 10.6 us
  Pallas kernels: 0 us -> 18.7 us
  waiting for transfers between devices: 3.85 us -> 15.3 us
  blocking collectives: 9.46 us -> 16.5 us
    slice x14 -> x0, local copies, waits for them, and re-layouts: 48.9 us -> none  [the longest x3 15.4 us: beside_all(): field[..., 0::PX]]
    gather x18 -> x0, local copies, waits for them, and re-layouts: 37.4 us -> none  [pick_rows(): taken = jnp.take(field, jnp.clip(index, 0, field.shape[0] - 1), axis=0)]
    scatter x4 -> x0, local copies, waits for them, and re-layouts: 28.7 us -> none  [the longest x1 14.2 us: per_device(): send_state = jnp.zeros((groups * capacity,) + old_state.shape[1:], jnp.bf...]
    pallas_call x0 -> x4, Pallas kernels: none -> 18.7 us  [call(): pl.pallas_call(kernel, out_shape=out_shape, grid=(1,), in_specs=[specs.ge...]
    all_to_all x0 -> x1, blocking collectives: none -> 16.5 us  [per_device(): got = lax.all_to_all(send, 'group', split_axis=0, concat_axis=0, tiled=True)]
    ppermute x6 -> x4, waiting for transfers between devices: 0.02 us -> 15.3 us  [the longest x1 13.1 us: per_device(): got_lo = lax.ppermute(got, 'member', up)]
    select_n x10 -> x0, other arithmetic: 15 us -> none  [the longest x8 14.3 us: pick_rows(): return jnp.where((index >= 0)[:, None, None], taken, 0.0)]
    ppermute x4 -> x0, local copies, waits for them, and re-layouts: 13.4 us -> none  [the longest x2 6.7 us: with_halo(): lax.ppermute(lax.slice_in_dim(block, 0, width, axis=dim), axis, backward)]
  transfers between devices with their start and end apart: 9 -> 4, of which waited for: 1 -> 2; matrix products, arithmetic and copies ran while one was open for 53% -> 0% of each run, Pallas kernels for 0% -> 22%
where the time goes in v1:
time: 64.8 us; the launch traced here: 64.5 us
  Pallas kernels  18.7 us (29%)
  blocking collectives  16.5 us (25%)
  waiting for transfers between devices  15.3 us (24%)
  starting transfers between devices  10.6 us (16%)
  local copies, waits for them, and re-layouts  3.24 us (5%)
    pallas_call x4, Pallas kernels, call(): pl.pallas_call(kernel, out_shape=out_shape, grid=(1,), in_specs=[specs.ge...  18.7 us
    all_to_all x1, blocking collectives, per_device(): got = lax.all_to_all(send, 'group', split_axis=0, concat_axis=0, tiled=True)  16.5 us
    ppermute x1, waiting for transfers between devices, per_device(): got_lo = lax.ppermute(got, 'member', up)  13.1 us
    ppermute x1, starting transfers between devices, per_device(): got_lo2 = lax.ppermute(got_lo, 'member', up)  4.42 us
    ppermute x1, starting transfers between devices, per_device(): got_lo = lax.ppermute(got, 'member', up)  3.64 us
    unnamed x10, local copies, waits for them, and re-layouts  3.24 us
    ppermute x1, waiting for transfers between devices, per_device(): got_hi2 = lax.ppermute(got_hi, 'member', down)  2.18 us
  transfers between devices with their start and end apart: 4, of which 2 were waited for; matrix products, arithmetic and copies ran while one was open for 0% of the time, Pallas kernels for 22%

profile of v1, /device:TPU:0, one launch (start us, length us, event | category | flops | bytes accessed | tf_op | source)
XLA Modules:
  0.0 64.5 jit_solution(18334696469818895239)
XLA Ops:
  0.0 0.0 copy-start
  0.0 1.1 %copy-done = bf16[1,1,128,9,256]{4,2,3,1,0:T(8,128)(2,1)S(1)} copy-done((bf16[1,1,128,9,256]{4,2,3,1,0:T(8,128)(2,1)S(1)}, bf16[1,1,128,9,256]{4,2,3,1,0:T(8,128)(2,1)}, u32[]{:S(2)}) %copy-start) | copy-done | bytes 589848
  1.1 0.0 copy-start.1
  1.1 0.8 %copy-done.1 = bf16[1,1,128,256]{3,2,1,0:T(8,128)(2,1)S(1)} copy-done((bf16[1,1,128,256]{3,2,1,0:T(8,128)(2,1)S(1)}, bf16[1,1,128,256]{3,2,1,0:T(8,128)(2,1)}, u32[]{:S(2)}) %copy-start.1) | copy-done | bytes 65560
  1.9 0.0 copy-start.2
  1.9 0.7 %copy-done.2 = s32[1,1,6,128]{3,1,2,0:T(1,128)S(1)} copy-done((s32[1,1,6,128]{3,1,2,0:T(1,128)S(1)}, s32[1,1,6,128]{3,1,2,0:T(1,128)}, u32[]{:S(2)}) %copy-start.2) | copy-done | bytes 3096
  2.6 0.0 copy-start.3
  2.6 0.7 %copy-done.3 = s32[1,1,128]{2,1,0:T(1,128)S(1)} copy-done((s32[1,1,128]{2,1,0:T(1,128)S(1)}, s32[1,1,128]{2,1,0:T(1,128)}, u32[]{:S(2)}) %copy-start.3) | copy-done | bytes 536
  3.2 0.5 shard_map.55
  3.7 16.5 %all_to_all.11 = bf16[8,16,2688]{2,1,0:T(8,128)(2,1)S(1)} all-to-all(bf16[8,16,2688]{2,1,0:T(8,128)(2,1)S(1)} %bitcast.15), channel_id=1, replica_groups=mesh['group'=8,'member'=4] {'group'}, dimensions={0} | all-to-all | bytes 1376256 | tf_op jit(solution)/shard_map/all_to_all | solution.py:301
  20.2 0.0 copy-start.4
  20.2 3.6 %collective-permute-start = (bf16[128,2688]{1,0:T(8,128)(2,1)S(1)}, bf16[128,2688]{1,0:T(8,128)(2,1)S(1)}, u32[]{:S(2)}, u32[]{:S(2)}) collective-permute-start(bf16[128,2688]{1,0:T(8,128)(2,1)S(1)} %bitcast.11), channel_id=1, source_target_pairs={{0,1},{1,2},{2,3},{4,5},{5,6},{6,7},{8,9},{9,10},{10,11},{12,13},{... | collective-permute-start | bytes 2064392 | tf_op jit(solution)/shard_map/ppermute | solution.py:302
  23.9 1.3 %collective-permute-start.1 = (bf16[128,2688]{1,0:T(8,128)(2,1)S(1)}, bf16[128,2688]{1,0:T(8,128)(2,1)S(1)}, u32[]{:S(2)}, u32[]{:S(2)}) collective-permute-start(bf16[128,2688]{1,0:T(8,128)(2,1)S(1)} %bitcast.12), channel_id=1, source_target_pairs={{1,0},{2,1},{3,2},{5,4},{6,5},{7,6},{9,8},{10,9},{11,10},{13,12},{... | collective-permute-start | bytes 2064392 | tf_op jit(solution)/shard_map/ppermute | solution.py:303
  25.2 13.1 %collective-permute-done.head_lo.got_lo = bf16[128,2688]{1,0:T(8,128)(2,1)S(1)} collective-permute-done((bf16[128,2688]{1,0:T(8,128)(2,1)S(1)}, bf16[128,2688]{1,0:T(8,128)(2,1)S(1)}, u32[]{:S(2)}, u32[]{:S(2)}) %collective-permute-start) | collective-permute-done | bytes 688160 | tf_op jit(solution)/shard_map/ppermute | solution.py:302
  38.3 4.4 %collective-permute-start.2 = (bf16[128,2688]{1,0:T(8,128)(2,1)S(1)}, bf16[128,2688]{1,0:T(8,128)(2,1)S(1)}, u32[]{:S(2)}, u32[]{:S(2)}) collective-permute-start(bf16[128,2688]{1,0:T(8,128)(2,1)S(1)} %collective-permute-done.head_lo.got_lo), channel_id=1, source_target_pairs={{0,1},{1,2},{2,3},{4,5},{5,6},{6,7},{8,9},{9,10},{10,11},{12,13},{... | collective-permute-start | bytes 2064392 | tf_op jit(solution)/shard_map/ppermute | solution.py:304
  42.7 0.0 collective-permute-done.1.head_hi.got_hi
  42.7 1.3 %collective-permute-start.3 = (bf16[128,2688]{1,0:T(8,128)(2,1)S(1)}, bf16[128,2688]{1,0:T(8,128)(2,1)S(1)}, u32[]{:S(2)}, u32[]{:S(2)}) collective-permute-start(bf16[128,2688]{1,0:T(8,128)(2,1)S(1)} %collective-permute-done.1.head_hi.got_hi), channel_id=1, source_target_pairs={{1,0},{2,1},{3,2},{5,4},{6,5},{7,6},{9,8},{10,9},{11,10},{13,12},{... | collective-permute-start | bytes 2064392 | tf_op jit(solution)/shard_map/ppermute | solution.py:305
  44.0 1.5 %shard_map.56 = (bf16[3,128,128]{2,1,0:T(8,128)(2,1)S(1)}, bf16[3,128,256]{2,1,0:T(8,128)(2,1)S(1)}, bf16[3,128,256]{2,1,0:T(8,128)(2,1)S(1)}, bf16[6,128,128]{2...) custom-call(bf16[128,2688]{1,0:T(8,128)(2,1)S(1)} %bitcast.13, ...), custom_call_target="tpu_custom_call" | custom-call | flops 100000000 | bytes 5767168 | tf_op jit(solution)/shard_map/pallas_call | solution.py:264
  45.5 0.0 copy-done.4
  45.5 12.7 %shard_map.57 = (f32[9,128,256]{2,1,0:T(8,128)S(1)}, f32[9,128,256]{2,1,0:T(8,128)S(1)}, f32[9,128,256]{2,1,0:T(8,128)S(1)}) custom-call(f32[9]{0:T(128)S(1)} %copy-done.4, bf16[3,128,128]{2,1,0:T(8,128)(2,1)S(1)} %get-tuple-element.21.sort_ref, bf16[3,128,256]{2,1,0:T(8,128)(2,1)S(1)} %get-tuple-element.22.x_pick, ...), custom_call_target="tpu_custom_call" | custom-call | flops 2000000000 | bytes 9044004 | tf_op jit(solution)/shard_map/pallas_call | solution.py:264
  58.2 0.0 collective-permute-done.2.got_lo2.head_lo2
  58.2 2.2 %collective-permute-done.3.got_hi2.head_hi2 = bf16[128,2688]{1,0:T(8,128)(2,1)S(1)} collective-permute-done((bf16[128,2688]{1,0:T(8,128)(2,1)S(1)}, bf16[128,2688]{1,0:T(8,128)(2,1)S(1)}, u32[]{:S(2)}, u32[]{:S(2)}) %collective-permute-start.3) | collective-permute-done | bytes 688160 | tf_op jit(solution)/shard_map/ppermute | solution.py:305
  60.4 4.0 %shard_map.58 = f32[9,128,256]{2,1,0:T(8,128)} custom-call(f32[9]{0:T(128)S(1)} %copy-done.4, bf16[6,128,128]{2,1,0:T(8,128)(2,1)S(1)} %get-tuple-element.16.z_pick, f32[3,6,128,256]{3,2,1,0:T(8,128)S(1)} %get-tuple-element.17.weights_ref, f32[3,128,256]{2,1,0:T(8,128)S(1)} %get-tuple-element.18.total_ref, f32[128,256]{1,0:T(8,128)S(1)} %get-tuple-element.19.coef_lo, ...), custom_call_target="tpu_custom_call" | custom-call | flops 1000000000 | bytes 10682404 | tf_op jit(solution)/shard_map/pallas_call | solution.py:264
Async XLA Ops:
  0.0 1.1 %copy-start = (bf16[1,1,128,9,256]{4,2,3,1,0:T(8,128)(2,1)S(1)}, bf16[1,1,128,9,256]{4,2,3,1,0:T(8,128)(2,1)}, u32[]{:S(2)}) copy-start(bf16[1,1,128,9,256]{4,2,3,1,0:T(8,128)(2,1)} %param.5) | copy-start | bytes 1769476
  1.1 0.8 %copy-start.1 = (bf16[1,1,128,256]{3,2,1,0:T(8,128)(2,1)S(1)}, bf16[1,1,128,256]{3,2,1,0:T(8,128)(2,1)}, u32[]{:S(2)}) copy-start(bf16[1,1,128,256]{3,2,1,0:T(8,128)(2,1)} %param.6) | copy-start | bytes 196612
  1.9 0.7 %copy-start.2 = (s32[1,1,6,128]{3,1,2,0:T(1,128)S(1)}, s32[1,1,6,128]{3,1,2,0:T(1,128)}, u32[]{:S(2)}) copy-start(s32[1,1,6,128]{3,1,2,0:T(1,128)} %param.8) | copy-start | bytes 9220
  2.6 0.7 %copy-start.3 = (s32[1,1,128]{2,1,0:T(1,128)S(1)}, s32[1,1,128]{2,1,0:T(1,128)}, u32[]{:S(2)}) copy-start(s32[1,1,128]{2,1,0:T(1,128)} %param.7) | copy-start | bytes 1540
  20.2 25.3 %copy-start.4 = (f32[9]{0:T(128)S(1)}, f32[9]{0:T(128)}, u32[]{:S(2)}) copy-start(f32[9]{0:T(128)} %lewis_ref.3) | copy-start | bytes 112
  20.2 18.1 %collective-permute-start = (bf16[128,2688]{1,0:T(8,128)(2,1)S(1)}, bf16[128,2688]{1,0:T(8,128)(2,1)S(1)}, u32[]{:S(2)}, u32[]{:S(2)}) collective-permute-start(bf16[128,2688]{1,0:T(8,128)(2,1)S(1)} %bitcast.11), channel_id=1, source_target_pairs={{0,1},{1,2},{2,3},{4,5},{5,6},{6,7},{8,9},{9,10},{10,11},{12,13},{... | collective-permute-start | bytes 2064392 | tf_op jit(solution)/shard_map/ppermute | solution.py:302
  23.9 18.9 %collective-permute-start.1 = (bf16[128,2688]{1,0:T(8,128)(2,1)S(1)}, bf16[128,2688]{1,0:T(8,128)(2,1)S(1)}, u32[]{:S(2)}, u32[]{:S(2)}) collective-permute-start(bf16[128,2688]{1,0:T(8,128)(2,1)S(1)} %bitcast.12), channel_id=1, source_target_pairs={{1,0},{2,1},{3,2},{5,4},{6,5},{7,6},{9,8},{10,9},{11,10},{13,12},{... | collective-permute-start | bytes 2064392 | tf_op jit(solution)/shard_map/ppermute | solution.py:303
  38.3 19.9 %collective-permute-start.2 = (bf16[128,2688]{1,0:T(8,128)(2,1)S(1)}, bf16[128,2688]{1,0:T(8,128)(2,1)S(1)}, u32[]{:S(2)}, u32[]{:S(2)}) collective-permute-start(bf16[128,2688]{1,0:T(8,128)(2,1)S(1)} %collective-permute-done.head_lo.got_lo), channel_id=1, source_target_pairs={{0,1},{1,2},{2,3},{4,5},{5,6},{6,7},{8,9},{9,10},{10,11},{12,13},{... | collective-permute-start | bytes 2064392 | tf_op jit(solution)/shard_map/ppermute | solution.py:304
  42.7 17.7 %collective-permute-start.3 = (bf16[128,2688]{1,0:T(8,128)(2,1)S(1)}, bf16[128,2688]{1,0:T(8,128)(2,1)S(1)}, u32[]{:S(2)}, u32[]{:S(2)}) collective-permute-start(bf16[128,2688]{1,0:T(8,128)(2,1)S(1)} %collective-permute-done.1.head_hi.got_hi), channel_id=1, source_target_pairs={{1,0},{2,1},{3,2},{5,4},{6,5},{7,6},{9,8},{10,9},{11,10},{13,12},{... | collective-permute-start | bytes 2064392 | tf_op jit(solution)/shard_map/ppermute | solution.py:305

commit v2 on v1

v2 whole, which is shorter than its diff:
```python
import functools

import jax
import jax.numpy as jnp
from jax import lax
from jax.experimental import pallas as pl
from jax.experimental.pallas import tpu as pltpu
from jax.sharding import PartitionSpec as P

PX = 16
PY = 16
FACES = 6
LANES = 128
F32 = jnp.float32
BF16 = jnp.bfloat16
VMEM_LIMIT = 28 * 1024 * 1024


def dot(a, b):
    return jnp.dot(a, b, preferred_element_type=F32)


def dot_first(a, b):
    return lax.dot_general(a, b, (((0,), (0,)), ((), ())), preferred_element_type=F32)


def iota(shape, dim):
    return lax.broadcasted_iota(jnp.int32, shape, dim)


def ones_where(mask):
    return jnp.where(mask, 1.0, 0.0).astype(BF16)


def list_blocks(capacity):
    return -(-FACES // capacity)


def pack_kernel(
    groups, capacity, cuts, dest_ref, lists_ref, state_hbm, coef_hbm, *rest
):
    sends = rest[: len(cuts)]
    state_ref, coef_ref, sems = rest[len(cuts) :]
    species, slots, cells = state_ref.shape
    coef_copy = pltpu.make_async_copy(coef_hbm, coef_ref, sems.at[species])
    coef_copy.start()
    copies = [
        pltpu.make_async_copy(state_hbm.at[k], state_ref.at[k], sems.at[k]) for k in range(species)
    ]
    for copy in copies:
        copy.start()
    dest = dest_ref[...]
    onehot = iota((groups, slots), 0) == dest
    earlier = dot(
        ones_where(onehot), ones_where(iota((slots, slots), 0) < iota((slots, slots), 1))
    )
    running = jnp.sum(jnp.where(onehot, earlier, 0.0), axis=0, keepdims=True).astype(jnp.int32)
    position = jnp.where(dest >= 0, dest * capacity + running, -1)
    place = ones_where(iota((slots, slots), 0) == position)
    first = lax.axis_index("group") * capacity
    row = iota((slots, slots), 0) - first
    for b in range(list_blocks(capacity)):
        block = jnp.zeros((slots, slots), F32)
        for i in range(min(capacity, FACES - b * capacity)):
            entry = (lists_ref[b * capacity + i] + 1).astype(F32)
            block = jnp.where(row == i, entry, block)
        at = slice(cells + b * slots, cells + (b + 1) * slots)
        sends[0][:, at] = block.astype(BF16)
    coef_copy.wait()
    sends[0][:, :cells] = dot(place, coef_ref[...]).astype(BF16)
    k = 0
    for send, count in zip(sends, cuts):
        start = send.shape[1] - count * cells
        for i in range(count):
            copies[k].wait()
            at = slice(start + i * cells, start + (i + 1) * cells)
            send[:, at] = dot(place, state_ref[k]).astype(BF16)
            k += 1


def unpack_lists(capacity, blocks):
    slots = blocks.shape[0]
    select = ones_where(lax.rem(iota((8, slots), 1), capacity) == iota((8, slots), 0))
    lists = []
    for face in range(FACES):
        b, i = divmod(face, capacity)
        if i == 0:
            rows = dot(select, blocks[:, b * slots : (b + 1) * slots]).astype(jnp.int32) - 1
        lists.append(rows[i : i + 1])
    return lists


def sorting(coef_rows):
    slots = coef_rows.shape[0]
    lead = coef_rows[:, :slots].astype(F32)[:, :1]
    valid = jnp.broadcast_to(lead, (slots, slots)) > 0.0
    slot = dot(
        ones_where(iota((slots, slots), 1) < iota((slots, slots), 0)), ones_where(valid)
    ).astype(jnp.int32)
    return ones_where(valid & (slot == iota((slots, slots), 1)))


def picking(entry):
    slots = entry.shape[1]
    return ones_where(iota((slots, slots), 0) == entry)


def twice(matrix):
    return jnp.concatenate([matrix, matrix], 0)


def split(field):
    high = field.astype(BF16)
    low = (field - high.astype(F32)).astype(BF16)
    return jnp.concatenate([high, low], 1)


def weighted_xy(weights, field_ref, edge_ref, y):
    at = PX + y * PX
    first = iota((8, LANES), 0) == 0
    last = iota((8, LANES), 0) == 7
    left = field_ref[at - 1 : at - 1 + PX]
    left = jnp.concatenate([jnp.where(first, edge_ref[0, y : y + 1], left[:8]), left[8:]], 0)
    right = field_ref[at + 1 : at + 1 + PX]
    right = jnp.concatenate([right[:8], jnp.where(last, edge_ref[1, y : y + 1], right[8:])], 0)
    flow = weights[0] * left + weights[1] * right
    flow = flow + weights[2] * field_ref[at - PX : at]
    return flow + weights[3] * field_ref[at + PX : at + 2 * PX]


def fill_edges(picks, fields, edges, exact):
    cells = fields[0].shape[0] - 2 * PX
    for face in range(4):
        if face < 2:
            rows = pl.ds(PX + (PX - 1 if face == 0 else 0), PY, stride=PX)
        else:
            rows = pl.ds(cells if face == 2 else PX, PX)
        taken = jnp.concatenate([field[rows] for field in fields], 0)
        if exact:
            got = dot(taken.astype(BF16), picks[face])
        else:
            got = dot(split(taken), twice(picks[face]))
        for i, (field, edge) in enumerate(zip(fields, edges)):
            part = got[i * PX : (i + 1) * PX]
            if face < 2:
                edge[face] = part
            elif face == 2:
                field[:PX] = part
            else:
                field[PX + cells :] = part


def prepare_kernel(
    capacity, head0, head_lo, head_hi,
    sort_ref, xy_pick, z_pick, weights_ref, total_ref, coef_lo, coef_hi, field_ref, edge_ref,
):
    slots = head0.shape[0]
    cells = coef_lo.shape[0]
    heads = (head0, head_lo, head_hi)
    coefs, lists = [], []
    for d in range(3):
        rows = heads[d][:, :cells]
        sort_ref[d] = sorting(rows)
        coef = dot_first(rows, sort_ref[d])
        coefs.append(coef.astype(BF16))
        field_ref[d, PX : PX + cells] = coef
        lists.append(unpack_lists(capacity, heads[d][:, cells:]))
        for face in range(4):
            xy_pick[d, face] = picking(lists[d][face])
        fill_edges(
            [xy_pick[d, f] for f in range(4)], [field_ref.at[d]], [edge_ref.at[d]], True
        )
    for i, (d, face) in enumerate(((0, 4), (0, 5), (1, 5), (2, 4), (1, 4), (2, 5))):
        z_pick[i] = picking(lists[d][face])
    coef_lo[...] = field_ref[1, PX : PX + cells]
    coef_hi[...] = field_ref[2, PX : PX + cells]
    for d in range(3):
        field = field_ref[d, PX : PX + cells]
        for i, source in (((0, 1), (1, 2)), ((2, 0),), ((3, 0),))[d]:
            near = dot(coefs[source], z_pick[i])
            weights_ref[d, 4 + (i if d == 0 else 0)] = 0.5 * (field + near)
        first = iota((8, LANES), 0) == 0
        last = iota((8, LANES), 0) == 7
        for y in range(PY):
            at = PX + y * PX
            rows = slice(y * PX, (y + 1) * PX)
            own = field_ref[d, at : at + PX]
            left = field_ref[d, at - 1 : at - 1 + PX]
            edge = edge_ref[d, 0, y : y + 1]
            left = jnp.concatenate([jnp.where(first, edge, left[:8]), left[8:]], 0)
            right = field_ref[d, at + 1 : at + 1 + PX]
            edge = edge_ref[d, 1, y : y + 1]
            right = jnp.concatenate([right[:8], jnp.where(last, edge, right[8:])], 0)
            near = (left, right, field_ref[d, at - PX : at], field_ref[d, at + PX : at + 2 * PX])
            total = weights_ref[d, 4, rows]
            if d == 0:
                total = total + weights_ref[d, 5, rows]
            for f in range(4):
                w = 0.5 * (own + near[f])
                weights_ref[d, f, rows] = w
                total = total + w
            total_ref[d, rows] = total


def inner_kernel(
    first, lewis_ref, sort_ref, xy_pick, z_pick, weights_ref, total_ref, got0, got_lo, got_hi,
    num0, num_lo, num_hi, field_ref, edge_ref, z_ref, phi_ref,
):
    species, cells, slots = num0.shape
    start = got0.shape[1] - species * cells
    gots = (got0, got_lo, got_hi)
    numbers = (num0, num_lo, num_hi)
    factor = [lewis_ref[first + k] for k in range(species)]
    for k in range(species):
        at = slice(start + k * cells, start + (k + 1) * cells)
        flat = []
        for d in range(3):
            field = dot_first(gots[d][:, at], sort_ref[d])
            field_ref[d, k, PX : PX + cells] = field
            flat.append(field.astype(BF16))
        for i, source in enumerate((1, 2, 0, 0)):
            z_ref[i, k] = dot(flat[source], z_pick[i])
    for d in range(3):
        fill_edges(
            [xy_pick[d, f] for f in range(4)],
            [field_ref.at[d, k] for k in range(species)],
            [edge_ref.at[d, k] for k in range(species)],
            True,
        )
    for d in range(3):
        for y in range(PY):
            rows = slice(y * PX, (y + 1) * PX)
            weights = [weights_ref[d, f, rows] for f in range(6 if d == 0 else 5)]
            for k in range(species):
                field = field_ref[d, k, PX + y * PX : 2 * PX + y * PX]
                flow = weighted_xy(weights, field_ref.at[d, k], edge_ref.at[d, k], y)
                if d == 0:
                    flow = flow + weights[4] * z_ref[0, k, rows] + weights[5] * z_ref[1, k, rows]
                    number = field + factor[k] * flow
                    phi = number / (1.0 + factor[k] * total_ref[0, rows])
                    phi_ref[k, PX + y * PX : 2 * PX + y * PX] = phi
                else:
                    flow = flow + weights[4] * z_ref[1 + d, k, rows]
                    numbers[d][k, rows] = field + factor[k] * flow
    fill_edges(
        [xy_pick[0, f] for f in range(4)],
        [phi_ref.at[k] for k in range(species)],
        [edge_ref.at[0, k] for k in range(species)],
        False,
    )
    for y in range(PY):
        rows = slice(y * PX, (y + 1) * PX)
        weights = [weights_ref[0, f, rows] for f in range(4)]
        for k in range(species):
            flow = weighted_xy(weights, phi_ref.at[k], edge_ref.at[0, k], y)
            num0[k, rows] = field_ref[0, k, PX + y * PX : 2 * PX + y * PX] + factor[k] * flow


def outer_kernel(
    first, lewis_ref, z_pick, weights_ref, total_ref, coef_lo, coef_hi,
    num0, num_lo, num_hi, got_lo2, got_hi2, head_lo2, head_hi2,
    out_ref, far_ref, w_ref, t_ref, two_ref,
):
    species, cells, slots = num0.shape
    start = got_lo2.shape[1] - species * cells
    gots, numbers = (got_lo2, got_hi2), (num_lo, num_hi)
    for i, (rows, coef) in enumerate(((head_lo2, coef_lo), (head_hi2, coef_hi))):
        far = dot(sorting(rows[:, :cells]), z_pick[4 + i]).astype(BF16)
        far_ref[i] = far
        w = 0.5 * (coef[...] + dot_first(rows[:, :cells], far))
        w_ref[i] = w
        t_ref[i] = total_ref[1 + i] + w
        two_ref[i] = twice(z_pick[i])
    for k in range(species):
        at = slice(start + k * cells, start + (k + 1) * cells)
        factor = lewis_ref[first + k]
        flow = None
        for i in range(2):
            ghost = dot_first(gots[i][:, at], far_ref[i])
            phi = (numbers[i][k] + factor * (w_ref[i] * ghost)) / (1.0 + factor * t_ref[i])
            term = weights_ref[0, 4 + i] * dot(split(phi), two_ref[i])
            flow = term if flow is None else flow + term
        out = (num0[k] + factor * flow) / (1.0 + factor * total_ref[0])
        out_ref[k] = jnp.transpose(out, (1, 0))


def call(kernel, out_shape, scratch, operands, specs=None, flops=0):
    whole = pl.BlockSpec(memory_space=pltpu.VMEM)
    specs = specs or {}
    moved = sum(o.size * o.dtype.itemsize for o in operands)
    moved += sum(o.size * o.dtype.itemsize for o in out_shape)
    return pl.pallas_call(
        kernel,
        out_shape=out_shape,
        grid=(1,),
        in_specs=[specs.get(i, whole) for i in range(len(operands))],
        out_specs=[whole] * len(out_shape),
        scratch_shapes=scratch,
        compiler_params=pltpu.CompilerParams(vmem_limit_bytes=VMEM_LIMIT),
        cost_estimate=pl.CostEstimate(flops=flops, bytes_accessed=moved, transcendentals=0),
    )(*operands)


def per_device(state, coef, new_group, face_lists, lewis):
    groups = lax.axis_size("group")
    members = lax.axis_size("member")
    up = [(i, i + 1) for i in range(members - 1)]
    down = [(i + 1, i) for i in range(members - 1)]
    slots, species, cells = state.shape[2:]
    capacity = slots // groups
    start = cells + list_blocks(capacity) * slots
    cuts = (3, species - 3)
    firsts = (0, 3)
    smem = pl.BlockSpec(memory_space=pltpu.SMEM)
    hbm = pl.BlockSpec(memory_space=pltpu.HBM)
    head = pl.BlockSpec((slots, start), lambda i: (0, 0))

    def shape(*dims, dtype=F32):
        return jax.ShapeDtypeStruct(dims, dtype)

    sends = call(
        functools.partial(pack_kernel, groups, capacity, cuts),
        [
            shape(slots, count * cells + (0 if c else start), dtype=BF16)
            for c, count in enumerate(cuts)
        ],
        [
            pltpu.VMEM((species, slots, cells), BF16),
            pltpu.VMEM((slots, cells), BF16),
            pltpu.SemaphoreType.DMA((species + 1,)),
        ],
        (
            new_group[0],
            jnp.transpose(face_lists[0], (1, 0, 2)),
            jnp.transpose(state[0, 0], (1, 0, 2)),
            coef[0, 0],
        ),
        specs={2: hbm, 3: hbm},
    )
    got = [
        lax.all_to_all(send, "group", split_axis=0, concat_axis=0, tiled=True) for send in sends
    ]
    got_lo = [lax.ppermute(rows, "member", up) for rows in got]
    got_hi = [lax.ppermute(rows, "member", down) for rows in got]
    got_lo2 = [lax.ppermute(rows, "member", up) for rows in got_lo]
    got_hi2 = [lax.ppermute(rows, "member", down) for rows in got_hi]
    padded = cells + 2 * PX
    sort, xy_pick, z_pick, weights, total, coef_lo, coef_hi = call(
        functools.partial(prepare_kernel, capacity),
        [
            shape(3, slots, slots, dtype=BF16),
            shape(3, 4, slots, slots, dtype=BF16),
            shape(6, slots, slots, dtype=BF16),
            shape(3, 6, cells, slots),
            shape(3, cells, slots),
            shape(cells, slots),
            shape(cells, slots),
        ],
        [pltpu.VMEM((3, padded, slots), F32), pltpu.VMEM((3, 2, PY, slots), F32)],
        (got[0], got_lo[0], got_hi[0]),
        specs={0: head, 1: head, 2: head},
        flops=100_000_000,
    )
    inner = [
        call(
            functools.partial(inner_kernel, first),
            [shape(count, cells, slots)] * 3,
            [
                pltpu.VMEM((3, count, padded, slots), F32),
                pltpu.VMEM((3, count, 2, PY, slots), F32),
                pltpu.VMEM((4, count, cells, slots), F32),
                pltpu.VMEM((count, padded, slots), F32),
            ],
            (lewis, sort, xy_pick, z_pick, weights, total, got[c], got_lo[c], got_hi[c]),
            specs={0: smem},
            flops=200_000_000 * count,
        )
        for c, (first, count) in enumerate(zip(firsts, cuts))
    ]
    outs = [
        call(
            functools.partial(outer_kernel, first),
            [shape(count, slots, cells)],
            [
                pltpu.VMEM((2, slots, slots), BF16),
                pltpu.VMEM((2, cells, slots), F32),
                pltpu.VMEM((2, cells, slots), F32),
                pltpu.VMEM((2, 2 * slots, slots), BF16),
            ],
            (
                lewis, z_pick, weights, total, coef_lo, coef_hi, *inner[c],
                got_lo2[c], got_hi2[c], got_lo2[0], got_hi2[0],
            ),
            specs={0: smem, 11: head, 12: head},
            flops=100_000_000 * count,
        )[0]
        for c, (first, count) in enumerate(zip(firsts, cuts))
    ]
    out = jnp.concatenate(outs, 0)
    return jnp.transpose(out, (1, 0, 2))[None, None]


def solution(mesh):
    return jax.shard_map(
        per_device,
        mesh=mesh,
        in_specs=(
            P("group", "member", None, None, None),
            P("group", "member", None, None),
            P("group", "member", None),
            P("group", "member", None, None),
            P(),
        ),
        out_specs=P("group", "member", None, None, None),
        check_vma=False,
    )
```

time: 64.8 us -> 66.9 us (1.032)
  starting transfers between devices: 10.6 us -> 24.4 us
  waiting for transfers between devices: 15.3 us -> 7.69 us
  blocking collectives: 16.5 us -> 13.3 us
  Pallas kernels: 18.7 us -> 16.5 us
  other arithmetic: 0 us -> 1.09 us
    ppermute x4 -> x8, starting transfers between devices: 10.6 us -> 21 us  [the longest x2 8.79 us: per_device(): got_lo2 = [lax.ppermute(rows, 'member', up) for rows in got_lo]]
    ppermute x4 -> x8, waiting for transfers between devices: 15.3 us -> 5.31 us  [the longest x2 3.69 us: per_device(): got_hi2 = [lax.ppermute(rows, 'member', down) for rows in got_hi]]
    all_to_all x0 -> x1, starting transfers between devices: none -> 3.42 us  [per_device(): lax.all_to_all(send, 'group', split_axis=0, concat_axis=0, tiled=True)]
    all_to_all x1, blocking collectives: 16.5 us -> 13.3 us  [per_device(): lax.all_to_all(send, 'group', split_axis=0, concat_axis=0, tiled=True)]
    all_to_all x0 -> x1, waiting for transfers between devices: none -> 2.37 us  [per_device(): lax.all_to_all(send, 'group', split_axis=0, concat_axis=0, tiled=True)]
    pallas_call x4 -> x6, Pallas kernels: 18.7 us -> 16.5 us  [call(): pl.pallas_call(kernel, out_shape=out_shape, grid=(1,), in_specs=[specs.ge...]
    broadcast_in_dim x0 -> x1, other arithmetic: none -> 1.09 us  [per_device(): return jnp.transpose(out, (1, 0, 2))[None, None]]
  transfers between devices with their start and end apart: 4 -> 9, of which waited for: 2 -> 5; matrix products, arithmetic and copies ran while one was open for 0% -> 0% of each run, Pallas kernels for 22% -> 16%
where the time goes in v2:
time: 66.9 us; the launch traced here: 66.3 us
  starting transfers between devices  24.4 us (36%)
  Pallas kernels  16.5 us (25%)
  blocking collectives  13.3 us (20%)
  waiting for transfers between devices  7.69 us (11%)
  local copies, waits for them, and re-layouts  3.25 us (5%)
  other arithmetic  1.09 us (2%)
    pallas_call x6, Pallas kernels, call(): pl.pallas_call(kernel, out_shape=out_shape, grid=(1,), in_specs=[specs.ge...  16.5 us
    all_to_all x1, blocking collectives, per_device(): lax.all_to_all(send, 'group', split_axis=0, concat_axis=0, tiled=True)  13.3 us
    ppermute x2, starting transfers between devices, per_device(): got_lo2 = [lax.ppermute(rows, 'member', up) for rows in got_lo]  8.79 us
    ppermute x2, starting transfers between devices, per_device(): got_lo = [lax.ppermute(rows, 'member', up) for rows in got]  7.02 us
    ppermute x2, waiting for transfers between devices, per_device(): got_hi2 = [lax.ppermute(rows, 'member', down) for rows in got_hi]  3.69 us
    all_to_all x1, starting transfers between devices, per_device(): lax.all_to_all(send, 'group', split_axis=0, concat_axis=0, tiled=True)  3.42 us
    unnamed x10, local copies, waits for them, and re-layouts  3.25 us
    ppermute x2, starting transfers between devices, per_device(): got_hi = [lax.ppermute(rows, 'member', down) for rows in got]  2.58 us
  transfers between devices with their start and end apart: 9, of which 5 were waited for; matrix products, arithmetic and copies ran while one was open for 0% of the time, Pallas kernels for 16%

profile of v2, /device:TPU:0, one launch (start us, length us, event | category | flops | bytes accessed | tf_op | source)
XLA Modules:
  0.0 66.3 jit_solution(16228156942192373321)
XLA Ops:
  0.0 0.0 copy-start
  0.0 1.1 %copy-done = bf16[1,1,128,9,256]{4,2,3,1,0:T(8,128)(2,1)S(1)} copy-done((bf16[1,1,128,9,256]{4,2,3,1,0:T(8,128)(2,1)S(1)}, bf16[1,1,128,9,256]{4,2,3,1,0:T(8,128)(2,1)}, u32[]{:S(2)}) %copy-start) | copy-done | bytes 589848
  1.1 0.0 copy-start.1
  1.1 0.8 %copy-done.1 = bf16[1,1,128,256]{3,2,1,0:T(8,128)(2,1)S(1)} copy-done((bf16[1,1,128,256]{3,2,1,0:T(8,128)(2,1)S(1)}, bf16[1,1,128,256]{3,2,1,0:T(8,128)(2,1)}, u32[]{:S(2)}) %copy-start.1) | copy-done | bytes 65560
  1.9 0.0 copy-start.3
  1.9 0.7 %copy-done.3 = s32[1,1,6,128]{3,1,2,0:T(1,128)S(1)} copy-done((s32[1,1,6,128]{3,1,2,0:T(1,128)S(1)}, s32[1,1,6,128]{3,1,2,0:T(1,128)}, u32[]{:S(2)}) %copy-start.3) | copy-done | bytes 3096
  2.6 0.0 copy-start.4
  2.6 0.7 copy-done.4
  3.2 3.3 %shard_map.55 = (bf16[128,1152]{1,0:T(8,128)(2,1)}, bf16[128,1536]{1,0:T(8,128)(2,1)S(1)}) custom-call(s32[1,128]{1,0:T(1,128)S(1)} %bitcast.25, s32[6,1,128]{2,1,0:T(1,128)S(1)} %bitcast.24, bf16[9,128,256]{2,1,0:T(8,128)(2,1)S(1)} %bitcast.21, bf16[128,256]{1,0:T(8,128)(2,1)S(1)} %bitcast.23), custom_call_target="tpu_custom_call" | custom-call | bytes 1347072 | tf_op jit(solution)/shard_map/pallas_call | solution.py:292
  6.5 0.0 copy-start.2
  6.5 13.3 %all_to_all.22 = bf16[8,16,1536]{2,1,0:T(8,128)(2,1)S(1)} all-to-all(bf16[8,16,1536]{2,1,0:T(8,128)(2,1)S(1)} %bitcast.22), channel_id=1, replica_groups=mesh['group'=8,'member'=4] {'group'}, dimensions={0} | all-to-all | bytes 786432 | tf_op jit(solution)/shard_map/all_to_all | solution.py:341
  19.8 3.4 %all-to-all-start = ((bf16[8,16,1152]{2,1,0:T(8,128)(2,1)}), bf16[8,16,1152]{2,1,0:T(8,128)(2,1)S(1)}, u32[]{:S(2)}, u32[]{:S(2)}) async-start(bf16[8,16,1152]{2,1,0:T(8,128)(2,1)} %bitcast.5), calls=%async_computation | async-start | bytes 589824 | tf_op jit(solution)/shard_map/all_to_all | solution.py:341
  23.3 3.5 %collective-permute-start.4 = (bf16[128,1536]{1,0:T(8,128)(2,1)S(1)}, bf16[128,1536]{1,0:T(8,128)(2,1)S(1)}, u32[]{:S(2)}, u32[]{:S(2)}) collective-permute-start(bf16[128,1536]{1,0:T(8,128)(2,1)S(1)} %bitcast.18), channel_id=1, source_target_pairs={{0,1},{1,2},{2,3},{4,5},{5,6},{6,7},{8,9},{9,10},{10,11},{12,13},{... | collective-permute-start | bytes 1179656 | tf_op jit(solution)/shard_map/ppermute | solution.py:343
  26.8 1.3 %collective-permute-start.5 = (bf16[128,1536]{1,0:T(8,128)(2,1)S(1)}, bf16[128,1536]{1,0:T(8,128)(2,1)S(1)}, u32[]{:S(2)}, u32[]{:S(2)}) collective-permute-start(bf16[128,1536]{1,0:T(8,128)(2,1)S(1)} %bitcast.19), channel_id=1, source_target_pairs={{1,0},{2,1},{3,2},{5,4},{6,5},{7,6},{9,8},{10,9},{11,10},{13,12},{... | collective-permute-start | bytes 1179656 | tf_op jit(solution)/shard_map/ppermute | solution.py:344
  28.1 2.4 %all-to-all-done = bf16[8,16,1152]{2,1,0:T(8,128)(2,1)S(1)} async-done(((bf16[8,16,1152]{2,1,0:T(8,128)(2,1)}), bf16[8,16,1152]{2,1,0:T(8,128)(2,1)S(1)}, u32[]{:S(2)}, u32[]{:S(2)}) %all-to-all-start) | async-done | bytes 294944 | tf_op jit(solution)/shard_map/all_to_all | solution.py:341
  30.5 3.5 %collective-permute-start = (bf16[128,1152]{1,0:T(8,128)(2,1)S(1)}, bf16[128,1152]{1,0:T(8,128)(2,1)S(1)}, u32[]{:S(2)}, u32[]{:S(2)}) collective-permute-start(bf16[128,1152]{1,0:T(8,128)(2,1)S(1)} %bitcast.14), channel_id=1, source_target_pairs={{0,1},{1,2},{2,3},{4,5},{5,6},{6,7},{8,9},{9,10},{10,11},{12,13},{... | collective-permute-start | bytes 884744 | tf_op jit(solution)/shard_map/ppermute | solution.py:343
  34.0 1.3 %collective-permute-start.1 = (bf16[128,1152]{1,0:T(8,128)(2,1)S(1)}, bf16[128,1152]{1,0:T(8,128)(2,1)S(1)}, u32[]{:S(2)}, u32[]{:S(2)}) collective-permute-start(bf16[128,1152]{1,0:T(8,128)(2,1)S(1)} %bitcast.15), channel_id=1, source_target_pairs={{1,0},{2,1},{3,2},{5,4},{6,5},{7,6},{9,8},{10,9},{11,10},{13,12},{... | collective-permute-start | bytes 884744 | tf_op jit(solution)/shard_map/ppermute | solution.py:344
  35.3 0.9 %collective-permute-done.4.got_lo = bf16[128,1536]{1,0:T(8,128)(2,1)S(1)} collective-permute-done((bf16[128,1536]{1,0:T(8,128)(2,1)S(1)}, bf16[128,1536]{1,0:T(8,128)(2,1)S(1)}, u32[]{:S(2)}, u32[]{:S(2)}) %collective-permute-start.4) | collective-permute-done | bytes 393248 | tf_op jit(solution)/shard_map/ppermute | solution.py:343
  36.2 4.4 %collective-permute-start.6 = (bf16[128,1536]{1,0:T(8,128)(2,1)S(1)}, bf16[128,1536]{1,0:T(8,128)(2,1)S(1)}, u32[]{:S(2)}, u32[]{:S(2)}) collective-permute-start(bf16[128,1536]{1,0:T(8,128)(2,1)S(1)} %collective-permute-done.4.got_lo), channel_id=1, source_target_pairs={{0,1},{1,2},{2,3},{4,5},{5,6},{6,7},{8,9},{9,10},{10,11},{12,13},{... | collective-permute-start | bytes 1179656 | tf_op jit(solution)/shard_map/ppermute | solution.py:345
  40.6 0.0 collective-permute-done.5.got_hi
  40.7 1.3 %collective-permute-start.7 = (bf16[128,1536]{1,0:T(8,128)(2,1)S(1)}, bf16[128,1536]{1,0:T(8,128)(2,1)S(1)}, u32[]{:S(2)}, u32[]{:S(2)}) collective-permute-start(bf16[128,1536]{1,0:T(8,128)(2,1)S(1)} %collective-permute-done.5.got_hi), channel_id=1, source_target_pairs={{1,0},{2,1},{3,2},{5,4},{6,5},{7,6},{9,8},{10,9},{11,10},{13,12},{... | collective-permute-start | bytes 1179656 | tf_op jit(solution)/shard_map/ppermute | solution.py:346
  42.0 0.6 collective-permute-done.head_lo.got_lo
  42.5 4.4 %collective-permute-start.2 = (bf16[128,1152]{1,0:T(8,128)(2,1)S(1)}, bf16[128,1152]{1,0:T(8,128)(2,1)S(1)}, u32[]{:S(2)}, u32[]{:S(2)}) collective-permute-start(bf16[128,1152]{1,0:T(8,128)(2,1)S(1)} %collective-permute-done.head_lo.got_lo), channel_id=1, source_target_pairs={{0,1},{1,2},{2,3},{4,5},{5,6},{6,7},{8,9},{9,10},{10,11},{12,13},{... | collective-permute-start | bytes 884744 | tf_op jit(solution)/shard_map/ppermute | solution.py:345
  46.9 0.1 collective-permute-done.1.head_hi.got_hi
  47.0 1.3 %collective-permute-start.3 = (bf16[128,1152]{1,0:T(8,128)(2,1)S(1)}, bf16[128,1152]{1,0:T(8,128)(2,1)S(1)}, u32[]{:S(2)}, u32[]{:S(2)}) collective-permute-start(bf16[128,1152]{1,0:T(8,128)(2,1)S(1)} %collective-permute-done.1.head_hi.got_hi), channel_id=1, source_target_pairs={{1,0},{2,1},{3,2},{5,4},{6,5},{7,6},{9,8},{10,9},{11,10},{13,12},{... | collective-permute-start | bytes 884744 | tf_op jit(solution)/shard_map/ppermute | solution.py:346
  48.3 1.4 %shard_map.56 = (bf16[3,128,128]{2,1,0:T(8,128)(2,1)S(1)}, bf16[3,4,128,128]{3,2,1,0:T(8,128)(2,1)S(1)}, bf16[6,128,128]{2,1,0:T(8,128)(2,1)S(1)}, f32[3,6,256,1...) custom-call(bf16[128,1152]{1,0:T(8,128)(2,1)S(1)} %bitcast.16, ...), custom_call_target="tpu_custom_call" | custom-call | flops 100000000 | bytes 4587520 | tf_op jit(solution)/shard_map/pallas_call | solution.py:292
  49.7 0.0 copy-done.2
  49.7 2.7 %shard_map.57 = (f32[3,256,128]{2,1,0:T(8,128)S(1)}, f32[3,256,128]{2,1,0:T(8,128)S(1)}, f32[3,256,128]{2,1,0:T(8,128)S(1)}) custom-call(f32[9]{0:T(128)S(1)} %copy-done.2, bf16[3,128,128]{2,1,0:T(8,128)(2,1)S(1)} %get-tuple-element.26.sort_ref, bf16[3,4,128,128]{3,2,1,0:T(8,128)(2,1)S(1)} %get-tuple-element.27.xy_pick, ...), custom_call_target="tpu_custom_call" | custom-call | flops 600000000 | bytes 5505060 | tf_op jit(solution)/shard_map/pallas_call | solution.py:292
  52.5 4.7 %shard_map.59 = (f32[6,256,128]{2,1,0:T(8,128)S(1)}, f32[6,256,128]{2,1,0:T(8,128)S(1)}, f32[6,256,128]{2,1,0:T(8,128)S(1)}) custom-call(f32[9]{0:T(128)S(1)} %copy-done.2, bf16[3,128,128]{2,1,0:T(8,128)(2,1)S(1)} %get-tuple-element.26.sort_ref, bf16[3,4,128,128]{3,2,1,0:T(8,128)(2,1)S(1)} %get-tuple-element.27.xy_pick, ...), custom_call_target="tpu_custom_call" | custom-call | flops 1200000000 | bytes 6979620 | tf_op jit(solution)/shard_map/pallas_call | solution.py:292
  57.2 0.0 collective-permute-done.2.got_lo2.head_lo2
  57.2 3.7 %collective-permute-done.3.got_hi2.head_hi2 = bf16[128,1152]{1,0:T(8,128)(2,1)S(1)} collective-permute-done((bf16[128,1152]{1,0:T(8,128)(2,1)S(1)}, bf16[128,1152]{1,0:T(8,128)(2,1)S(1)}, u32[]{:S(2)}, u32[]{:S(2)}) %collective-permute-start.3) | collective-permute-done | bytes 294944 | tf_op jit(solution)/shard_map/ppermute | solution.py:346
  60.9 1.9 %shard_map.58 = f32[3,128,256]{2,1,0:T(8,128)S(1)} custom-call(f32[9]{0:T(128)S(1)} %copy-done.2, bf16[6,128,128]{2,1,0:T(8,128)(2,1)S(1)} %get-tuple-element.21.z_pick, f32[3,6,256,128]{3,2,1,0:T(8,128)S(1)} %get-tuple-element.22.weights_ref, f32[3,256,128]{2,1,0:T(8,128)S(1)} %get-tuple-element.23.total_ref, f32[256,128]{1,0:T(8,128)S(1)} %get-tuple-element.24.coef_lo, ...), custom_call_target="tpu_custom_call" | custom-call | flops 300000000 | bytes 5963812 | tf_op jit(solution)/shard_map/pallas_call | solution.py:292
  62.7 0.0 collective-permute-done.6.got_lo2
  62.7 0.0 collective-permute-done.7.got_hi2
  62.8 2.5 %shard_map.60 = f32[6,128,256]{2,1,0:T(8,128)S(1)} custom-call(f32[9]{0:T(128)S(1)} %copy-done.2, bf16[6,128,128]{2,1,0:T(8,128)(2,1)S(1)} %get-tuple-element.21.z_pick, f32[3,6,256,128]{3,2,1,0:T(8,128)S(1)} %get-tuple-element.22.weights_ref, f32[3,256,128]{2,1,0:T(8,128)S(1)} %get-tuple-element.23.total_ref, f32[256,128]{1,0:T(8,128)S(1)} %get-tuple-element.24.coef_lo, ...), custom_call_target="tpu_custom_call" | custom-call | flops 600000000 | bytes 7733284 | tf_op jit(solution)/shard_map/pallas_call | solution.py:292
  65.2 1.1 %maximum_bitcast_fusion = f32[1,1,128,9,256]{4,2,3,1,0:T(8,128)} fusion(f32[6,128,256]{2,1,0:T(8,128)S(1)} %shard_map.60, f32[3,128,256]{2,1,0:T(8,128)S(1)} %shard_map.58), kind=kLoop, calls=%fused_computation | loop fusion | flops 294912 | bytes 2359296 | tf_op jit(solution)/shard_map/broadcast_in_dim | solution.py:400
Async XLA Ops:
  0.0 1.1 %copy-start = (bf16[1,1,128,9,256]{4,2,3,1,0:T(8,128)(2,1)S(1)}, bf16[1,1,128,9,256]{4,2,3,1,0:T(8,128)(2,1)}, u32[]{:S(2)}) copy-start(bf16[1,1,128,9,256]{4,2,3,1,0:T(8,128)(2,1)} %param.5) | copy-start | bytes 1769476
  1.1 0.8 %copy-start.1 = (bf16[1,1,128,256]{3,2,1,0:T(8,128)(2,1)S(1)}, bf16[1,1,128,256]{3,2,1,0:T(8,128)(2,1)}, u32[]{:S(2)}) copy-start(bf16[1,1,128,256]{3,2,1,0:T(8,128)(2,1)} %param.6) | copy-start | bytes 196612
  1.9 0.7 %copy-start.3 = (s32[1,1,6,128]{3,1,2,0:T(1,128)S(1)}, s32[1,1,6,128]{3,1,2,0:T(1,128)}, u32[]{:S(2)}) copy-start(s32[1,1,6,128]{3,1,2,0:T(1,128)} %param.8) | copy-start | bytes 9220
  2.6 0.7 copy-start.4
  6.5 43.2 %copy-start.2 = (f32[9]{0:T(128)S(1)}, f32[9]{0:T(128)}, u32[]{:S(2)}) copy-start(f32[9]{0:T(128)} %lewis_ref.7) | copy-start | bytes 112
  19.8 10.6 %all-to-all-start = ((bf16[8,16,1152]{2,1,0:T(8,128)(2,1)}), bf16[8,16,1152]{2,1,0:T(8,128)(2,1)S(1)}, u32[]{:S(2)}, u32[]{:S(2)}) async-start(bf16[8,16,1152]{2,1,0:T(8,128)(2,1)} %bitcast.5), calls=%async_computation | async-start | bytes 589824 | tf_op jit(solution)/shard_map/all_to_all | solution.py:341
  23.3 13.0 %collective-permute-start.4 = (bf16[128,1536]{1,0:T(8,128)(2,1)S(1)}, bf16[128,1536]{1,0:T(8,128)(2,1)S(1)}, u32[]{:S(2)}, u32[]{:S(2)}) collective-permute-start(bf16[128,1536]{1,0:T(8,128)(2,1)S(1)} %bitcast.18), channel_id=1, source_target_pairs={{0,1},{1,2},{2,3},{4,5},{5,6},{6,7},{8,9},{9,10},{10,11},{12,13},{... | collective-permute-start | bytes 1179656 | tf_op jit(solution)/shard_map/ppermute | solution.py:343
  26.8 13.9 %collective-permute-start.5 = (bf16[128,1536]{1,0:T(8,128)(2,1)S(1)}, bf16[128,1536]{1,0:T(8,128)(2,1)S(1)}, u32[]{:S(2)}, u32[]{:S(2)}) collective-permute-start(bf16[128,1536]{1,0:T(8,128)(2,1)S(1)} %bitcast.19), channel_id=1, source_target_pairs={{1,0},{2,1},{3,2},{5,4},{6,5},{7,6},{9,8},{10,9},{11,10},{13,12},{... | collective-permute-start | bytes 1179656 | tf_op jit(solution)/shard_map/ppermute | solution.py:344
  30.5 12.1 %collective-permute-start = (bf16[128,1152]{1,0:T(8,128)(2,1)S(1)}, bf16[128,1152]{1,0:T(8,128)(2,1)S(1)}, u32[]{:S(2)}, u32[]{:S(2)}) collective-permute-start(bf16[128,1152]{1,0:T(8,128)(2,1)S(1)} %bitcast.14), channel_id=1, source_target_pairs={{0,1},{1,2},{2,3},{4,5},{5,6},{6,7},{8,9},{9,10},{10,11},{12,13},{... | collective-permute-start | bytes 884744 | tf_op jit(solution)/shard_map/ppermute | solution.py:343
  34.0 13.0 %collective-permute-start.1 = (bf16[128,1152]{1,0:T(8,128)(2,1)S(1)}, bf16[128,1152]{1,0:T(8,128)(2,1)S(1)}, u32[]{:S(2)}, u32[]{:S(2)}) collective-permute-start(bf16[128,1152]{1,0:T(8,128)(2,1)S(1)} %bitcast.15), channel_id=1, source_target_pairs={{1,0},{2,1},{3,2},{5,4},{6,5},{7,6},{9,8},{10,9},{11,10},{13,12},{... | collective-permute-start | bytes 884744 | tf_op jit(solution)/shard_map/ppermute | solution.py:344
  36.2 26.5 %collective-permute-start.6 = (bf16[128,1536]{1,0:T(8,128)(2,1)S(1)}, bf16[128,1536]{1,0:T(8,128)(2,1)S(1)}, u32[]{:S(2)}, u32[]{:S(2)}) collective-permute-start(bf16[128,1536]{1,0:T(8,128)(2,1)S(1)} %collective-permute-done.4.got_lo), channel_id=1, source_target_pairs={{0,1},{1,2},{2,3},{4,5},{5,6},{6,7},{8,9},{9,10},{10,11},{12,13},{... | collective-permute-start | bytes 1179656 | tf_op jit(solution)/shard_map/ppermute | solution.py:345
  40.7 22.1 %collective-permute-start.7 = (bf16[128,1536]{1,0:T(8,128)(2,1)S(1)}, bf16[128,1536]{1,0:T(8,128)(2,1)S(1)}, u32[]{:S(2)}, u32[]{:S(2)}) collective-permute-start(bf16[128,1536]{1,0:T(8,128)(2,1)S(1)} %collective-permute-done.5.got_hi), channel_id=1, source_target_pairs={{1,0},{2,1},{3,2},{5,4},{6,5},{7,6},{9,8},{10,9},{11,10},{13,12},{... | collective-permute-start | bytes 1179656 | tf_op jit(solution)/shard_map/ppermute | solution.py:346
  42.5 14.6 %collective-permute-start.2 = (bf16[128,1152]{1,0:T(8,128)(2,1)S(1)}, bf16[128,1152]{1,0:T(8,128)(2,1)S(1)}, u32[]{:S(2)}, u32[]{:S(2)}) collective-permute-start(bf16[128,1152]{1,0:T(8,128)(2,1)S(1)} %collective-permute-done.head_lo.got_lo), channel_id=1, source_target_pairs={{0,1},{1,2},{2,3},{4,5},{5,6},{6,7},{8,9},{9,10},{10,11},{12,13},{... | collective-permute-start | bytes 884744 | tf_op jit(solution)/shard_map/ppermute | solution.py:345
  47.0 13.9 %collective-permute-start.3 = (bf16[128,1152]{1,0:T(8,128)(2,1)S(1)}, bf16[128,1152]{1,0:T(8,128)(2,1)S(1)}, u32[]{:S(2)}, u32[]{:S(2)}) collective-permute-start(bf16[128,1152]{1,0:T(8,128)(2,1)S(1)} %collective-permute-done.1.head_hi.got_hi), channel_id=1, source_target_pairs={{1,0},{2,1},{3,2},{5,4},{6,5},{7,6},{9,8},{10,9},{11,10},{13,12},{... | collective-permute-start | bytes 884744 | tf_op jit(solution)/shard_map/ppermute | solution.py:346

commit v3 on v0

v3 whole, which is shorter than its diff:
```python
import functools

import jax
import jax.numpy as jnp
from jax import lax
from jax.experimental import pallas as pl
from jax.experimental.pallas import tpu as pltpu
from jax.sharding import PartitionSpec as P

PX = 16
PY = 16
FACES = 6
LANES = 128
HALF = PX // 2
PITCH = PX + 8
F32 = jnp.float32
BF16 = jnp.bfloat16
VMEM_LIMIT = 28 * 1024 * 1024
PACK_LIMIT = 60 * 1024 * 1024


def dot(a, b):
    return jnp.dot(a, b, preferred_element_type=F32)


def dot_first(a, b):
    return lax.dot_general(a, b, (((0,), (0,)), ((), ())), preferred_element_type=F32)


def iota(shape, dim):
    return lax.broadcasted_iota(jnp.int32, shape, dim)


def ones_where(mask):
    return jnp.where(mask, 1.0, 0.0).astype(BF16)


def pack_kernel(
    groups, capacity, dest_hbm, lists_hbm, state_hbm, coef_hbm, send_hbm, lists_out,
    dest_ref, lists_ref, state_ref, coef_ref, send, in_sems, out_sems,
):
    species, slots, cells = state_ref.shape
    copies = [
        pltpu.make_async_copy(source, target, in_sems.at[i])
        for i, (source, target) in enumerate(
            (
                (dest_hbm, dest_ref),
                (coef_hbm, coef_ref),
                (state_hbm, state_ref),
                (lists_hbm, lists_ref),
            )
        )
    ]
    for copy in copies:
        copy.start()
    copies[0].wait()
    dest = dest_ref[...]
    onehot = iota((groups, slots), 0) == dest
    earlier = dot(
        ones_where(onehot), ones_where(iota((slots, slots), 0) < iota((slots, slots), 1))
    )
    running = jnp.sum(jnp.where(onehot, earlier, 0.0), axis=0, keepdims=True).astype(jnp.int32)
    position = jnp.where(dest >= 0, dest * capacity + running, -1)
    place = ones_where(iota((slots, slots), 0) == position)
    copies[1].wait()
    send[:, :cells] = dot(place, coef_ref[...]).astype(BF16)
    copies[2].wait()
    out_copies = []
    middle = cells + species // 2 * cells
    for k in range(species):
        at = slice((k + 1) * cells, (k + 2) * cells)
        send[:, at] = dot(place, state_ref[k]).astype(BF16)
        if at.stop in (middle, send.shape[1]):
            at = slice(0 if at.stop == middle else middle, at.stop)
            i = len(out_copies)
            out_copies.append(
                pltpu.make_async_copy(send.at[:, at], send_hbm.at[:, at], out_sems.at[i])
            )
            out_copies[-1].start()
    copies[3].wait()
    none = jnp.zeros((1, slots), jnp.int32)
    rows = [lists_ref[f] + 1 for f in range(FACES)] + [none] * (8 - FACES)
    lists_out[...] = jnp.concatenate(rows, 0)
    for copy in out_copies:
        copy.wait()


def sorting(coef_rows):
    slots = coef_rows.shape[0]
    lead = coef_rows[:, :slots].astype(F32)[:, :1]
    valid = jnp.broadcast_to(lead, (slots, slots)) > 0.0
    slot = dot(
        ones_where(iota((slots, slots), 1) < iota((slots, slots), 0)), ones_where(valid)
    ).astype(jnp.int32)
    return ones_where(valid & (slot == iota((slots, slots), 1)))


def picking(entry):
    slots = entry.shape[1]
    return ones_where(iota((slots, slots), 0) == entry)


def twice(matrix):
    return jnp.concatenate([matrix, matrix], 0)


def split(field):
    high = field.astype(BF16)
    low = (field - high.astype(F32)).astype(BF16)
    return jnp.concatenate([high, low], 1)


PADDED = (PY + 2) * PITCH


def row(y):
    return (y + 1) * PITCH + PITCH - PX


def step(start):
    return pl.ds(start, HALF, stride=2)


def natural(y, odd):
    return step(y * PX + odd)


def halves(y, odd):
    return slice(y * PX + odd * HALF, y * PX + (odd + 1) * HALF)


def put(padded, field):
    for y in range(PY):
        padded[row(y) : row(y) + PX] = field[y * PX : (y + 1) * PX]


def beside_xy(padded, y, odd):
    at = row(y) + odd
    return [padded[step(at + shift)] for shift in (-1, 1, -PITCH, PITCH)]


def weighted(weights, values):
    flow = weights[0] * values[0]
    for w, v in zip(weights[1:], values[1:]):
        flow = flow + w * v
    return flow


def fill_edges(picks, fields, exact):
    x_first, x_last = row(0), row(0) + PX - 1
    places = (
        (pl.ds(x_last, PY, stride=PITCH), pl.ds(x_first - 1, PY, stride=PITCH)),
        (pl.ds(x_first, PY, stride=PITCH), pl.ds(x_last + 1, PY, stride=PITCH)),
        (pl.ds(row(PY - 1), PX), pl.ds(row(-1), PX)),
        (pl.ds(row(0), PX), pl.ds(row(PY), PX)),
    )
    for pick, (source, target) in zip(picks, places):
        taken = jnp.concatenate([field[source] for field in fields], 0)
        got = dot(taken.astype(BF16), pick) if exact else dot(split(taken), twice(pick))
        for i, field in enumerate(fields):
            field[target] = got[i * PX : (i + 1) * PX]


def pick_kernel(members, lists0, all_lists, pick_ref, xy_pick, z_pick):
    slots = lists0.shape[1]
    member = lax.axis_index("member")
    lists_lo = jnp.where(member > 0, all_lists[jnp.maximum(member - 1, 0)], 0)
    lists_hi = jnp.where(member < members - 1, all_lists[jnp.minimum(member + 1, members - 1)], 0)

    def picking(lists, face):
        return ones_where(iota((slots, slots), 0) == lists[face : face + 1] - 1)

    for face in range(FACES):
        pick_ref[face] = picking(lists0, face)
    for d, lists in enumerate((lists_lo, lists_hi)):
        for face in range(4):
            xy_pick[d, face] = picking(lists, face)
    z_pick[0] = jnp.concatenate([picking(lists_lo, 5), picking(lists_hi, 4)], 1)
    z_pick[1] = jnp.concatenate([picking(lists_lo, 4), picking(lists_hi, 5)], 1)


def own_kernel(
    lewis_ref, got, pick_ref,
    later_ref, coef_ref, weights_ref, flat_ref, base_ref, rhs_ref, coef_pad, field_ref,
):
    species, cells, slots = base_ref.shape
    later_ref[...] = got[:, got.shape[1] - later_ref.shape[1] :]
    sort = sorting(got[:, :cells])
    coef = dot_first(got[:, :cells], sort)
    coef_ref[...] = coef
    put(coef_pad, coef)
    picks = [pick_ref[face] for face in range(4)]
    fill_edges(picks, [coef_pad], True)
    for k in range(species):
        field = dot_first(got[:, (k + 1) * cells : (k + 2) * cells], sort)
        put(field_ref.at[k], field)
        flat_ref[k] = field.astype(BF16)
    fill_edges(picks, [field_ref.at[k] for k in range(species)], True)
    factor = [lewis_ref[k] for k in range(species)]
    for y in range(PY):
        for odd in range(2):
            at = halves(y, odd)
            own = coef_pad[step(row(y) + odd)]
            weights = [0.5 * (own + near) for near in beside_xy(coef_pad, y, odd)]
            for f in range(4):
                weights_ref[f, at] = weights[f]
            for k in range(species):
                field = field_ref[k, step(row(y) + odd)]
                flow = weighted(weights, beside_xy(field_ref.at[k], y, odd))
                base_ref[k, at] = field + factor[k] * flow
                rhs_ref[k, at] = field


def prepare_kernel(
    head_lo, head_hi, coef0, pick0, weights0, xy_pick, z_pick,
    sort_ref, z_natural, z_halves, total0, beside_ref, total_ref, coef_ref, padded, z_ref,
):
    cells, slots = coef0.shape
    for d, head in enumerate((head_lo, head_hi)):
        rows = head[...]
        sort = sorting(rows)
        both = jnp.concatenate([sort, dot(sort, pick0[4 + d]).astype(BF16)], 1)
        sort_ref[d] = both
        coef = dot_first(rows, both)
        coef_ref[d] = coef[:, :slots]
        put(padded.at[d], coef[:, :slots])
        z_natural[d] = 0.5 * (coef0[...] + coef[:, slots:])
        fill_edges([xy_pick[d, f] for f in range(4)], [padded.at[d]], True)
    near = dot(coef0[...].astype(BF16), z_pick[0])
    z_ref[0] = near[:, :slots]
    z_ref[1] = near[:, slots:]
    for y in range(PY):
        for odd in range(2):
            at = halves(y, odd)
            total = None
            for i in range(2):
                w = z_natural[i, natural(y, odd)]
                z_halves[i, at] = w
                total = w if total is None else total + w
            for f in range(4):
                total = total + weights0[f, at]
            total0[at] = total
            for d in range(2):
                own = padded[d, step(row(y) + odd)]
                near = [*beside_xy(padded.at[d], y, odd), z_ref[d, natural(y, odd)]]
                total = None
                for f in range(5):
                    w = 0.5 * (own + near[f])
                    beside_ref[d, f, at] = w
                    total = w if total is None else total + w
                total_ref[d, natural(y, odd)] = total


def inner_kernel(
    first, lewis_ref, sort_ref, xy_pick, z_pick, z_halves, total0, beside_ref,
    pick0, weights0, flat_ref, base_ref, rhs_ref, got_lo, got_hi,
    num0, scale0, num_lo, num_hi, field_ref, z_ref, phi_ref,
):
    species, cells, slots = num0.shape
    start = got_lo.shape[1] - species * cells
    gots, numbers = (got_lo, got_hi), (num_lo, num_hi)
    factor = [lewis_ref[first + k] for k in range(species)]
    for k in range(species):
        at = slice(start + k * cells, start + (k + 1) * cells)
        near = dot(flat_ref[first + k], z_pick[0])
        for d in range(2):
            both = dot_first(gots[d][:, at], sort_ref[d])
            put(field_ref.at[d, k], both[:, :slots])
            z_ref[d, k] = both[:, slots:]
            z_ref[2 + d, k] = near[:, d * slots : (d + 1) * slots]
    for y in range(PY):
        for odd in range(2):
            at = halves(y, odd)
            weights = [z_halves[i, at] for i in range(2)]
            total = total0[at]
            for k in range(species):
                near = [z_ref[i, k, natural(y, odd)] for i in range(2)]
                number = base_ref[first + k, at] + factor[k] * weighted(weights, near)
                inverse = 1.0 / (1.0 + factor[k] * total)
                phi_ref[k, step(row(y) + odd)] = number * inverse
                scale0[k, natural(y, odd)] = inverse
    fill_edges([pick0[f] for f in range(4)], [phi_ref.at[k] for k in range(species)], False)
    for d in range(2):
        fill_edges(
            [xy_pick[d, f] for f in range(4)], [field_ref.at[d, k] for k in range(species)], True
        )
    for d in range(2):
        for y in range(PY):
            for odd in range(2):
                at = halves(y, odd)
                weights = [beside_ref[d, f, at] for f in range(5)]
                for k in range(species):
                    near = beside_xy(field_ref.at[d, k], y, odd)
                    near.append(z_ref[2 + d, k, natural(y, odd)])
                    numbers[d][k, natural(y, odd)] = (
                        field_ref[d, k, step(row(y) + odd)] + factor[k] * weighted(weights, near)
                    )
    for y in range(PY):
        for odd in range(2):
            at = halves(y, odd)
            weights = [weights0[f, at] for f in range(4)]
            for k in range(species):
                near = beside_xy(phi_ref.at[k], y, odd)
                inverse = scale0[k, natural(y, odd)]
                number = rhs_ref[first + k, at] + factor[k] * weighted(weights, near)
                num0[k, natural(y, odd)] = number * inverse
                scale0[k, natural(y, odd)] = factor[k] * inverse


def far_kernel(pick0, z_pick, total_ref, coef_ref, head_lo2, head_hi2, far_ref, w_ref, t_ref, two_ref):
    cells = coef_ref.shape[1]
    slots = coef_ref.shape[2]
    none = jnp.zeros((slots, slots), BF16)
    rows = [head_lo2[...], head_hi2[...]]
    fars = []
    for i in range(2):
        fars.append(dot(sorting(rows[i]), z_pick[1, :, i * slots : (i + 1) * slots]).astype(BF16))
        two_ref[i] = twice(pick0[4 + i])
    far = jnp.concatenate(
        [jnp.concatenate([fars[0], none], 1), jnp.concatenate([none, fars[1]], 1)], 0
    )
    far_ref[...] = far
    near = dot_first(jnp.concatenate(rows, 0), far)
    for i in range(2):
        w = 0.5 * (coef_ref[i] + near[:, i * slots : (i + 1) * slots])
        w_ref[i] = w
        t_ref[i] = total_ref[i] + w


def outer_kernel(
    first, lewis_ref, far_ref, w_ref, t_ref, two_ref, z_natural,
    num0, scale0, num_lo, num_hi, got_lo2, got_hi2, *rest,
):
    species, cells, slots = num0.shape
    start = got_lo2.shape[1] - species * cells
    numbers = (num_lo, num_hi)
    copies = []
    if first:
        early, out_hbm, out_ref, sems = rest
        copies.append(
            pltpu.make_async_copy(early, out_hbm.at[:first], sems.at[species])
        )
        copies[-1].start()
    else:
        (out_ref,) = rest
    for k in range(species):
        at = slice(start + k * cells, start + (k + 1) * cells)
        factor = lewis_ref[first + k]
        ghosts = dot_first(jnp.concatenate([got_lo2[:, at], got_hi2[:, at]], 0), far_ref[...])
        flow = None
        for i in range(2):
            ghost = ghosts[:, i * slots : (i + 1) * slots]
            phi = (numbers[i][k] + factor * (w_ref[i] * ghost)) * (1.0 / (1.0 + factor * t_ref[i]))
            term = z_natural[i] * dot(split(phi), two_ref[i])
            flow = term if flow is None else flow + term
        out_ref[k] = jnp.transpose(num0[k] + scale0[k] * flow, (1, 0))
        if first:
            copies.append(pltpu.make_async_copy(out_ref.at[k], out_hbm.at[first + k], sems.at[k]))
            copies[-1].start()
    for copy in copies:
        copy.wait()


def call(
    kernel, out_shape, scratch, operands, specs=None, outs=None, flops=0, limit=0,
    grid=(1,),
):
    whole = pl.BlockSpec(memory_space=pltpu.VMEM)
    specs = specs or {}
    moved = sum(o.size * o.dtype.itemsize for o in operands)
    moved += sum(o.size * o.dtype.itemsize for o in out_shape)
    return pl.pallas_call(
        kernel,
        out_shape=out_shape,
        grid=grid,
        in_specs=[specs.get(i, whole) for i in range(len(operands))],
        out_specs=outs or [whole] * len(out_shape),
        scratch_shapes=scratch,
        compiler_params=pltpu.CompilerParams(vmem_limit_bytes=limit or VMEM_LIMIT),
        cost_estimate=pl.CostEstimate(flops=flops, bytes_accessed=moved, transcendentals=0),
    )(*operands)


def per_device(state, coef, new_group, face_lists, lewis):
    groups = lax.axis_size("group")
    members = lax.axis_size("member")
    up = [(i, i + 1) for i in range(members - 1)]
    down = [(i + 1, i) for i in range(members - 1)]
    slots, species, cells = state.shape[2:]
    capacity = slots // groups
    cuts = (species - species // 2, species // 2)
    firsts = (0, cuts[0])
    width = (1 + species) * cells
    middle = (1 + cuts[0]) * cells
    smem = pl.BlockSpec(memory_space=pltpu.SMEM)
    anywhere = pl.BlockSpec(memory_space=pl.ANY)
    head = pl.BlockSpec((slots, cells), lambda i: (0, 0))

    def shape(*dims, dtype=F32):
        return jax.ShapeDtypeStruct(dims, dtype)

    send, lists = call(
        functools.partial(pack_kernel, groups, capacity),
        [shape(slots, width, dtype=BF16), shape(8, slots, dtype=jnp.int32)],
        [
            pltpu.VMEM((1, slots), jnp.int32),
            pltpu.VMEM((FACES, 1, slots), jnp.int32),
            pltpu.VMEM((species, slots, cells), BF16),
            pltpu.VMEM((slots, cells), BF16),
            pltpu.VMEM((slots, width), BF16),
            pltpu.SemaphoreType.DMA((4,)),
            pltpu.SemaphoreType.DMA((2,)),
        ],
        (
            new_group[0],
            jnp.transpose(face_lists[0], (1, 0, 2)),
            jnp.transpose(state[0, 0], (1, 0, 2)),
            coef[0, 0],
        ),
        specs={i: anywhere for i in range(4)},
        outs=[anywhere, pl.BlockSpec(memory_space=pltpu.VMEM)],
        limit=PACK_LIMIT,
        grid=(),
    )
    rows = lax.all_to_all(send, "group", split_axis=0, concat_axis=0, tiled=True)
    all_lists = lax.all_gather(lists, "member")
    rows, all_lists = lax.optimization_barrier((rows, all_lists))
    pick0, xy_pick, z_pick = call(
        functools.partial(pick_kernel, members),
        [
            shape(FACES, slots, slots, dtype=BF16),
            shape(2, 4, slots, slots, dtype=BF16),
            shape(2, slots, 2 * slots, dtype=BF16),
        ],
        [],
        (lists, all_lists),
    )
    later, coef0, weights0, flat, base, rhs = call(
        own_kernel,
        [
            shape(slots, width - middle, dtype=BF16),
            shape(cells, slots),
            shape(4, cells, slots),
            shape(species, cells, slots, dtype=BF16),
            shape(species, cells, slots),
            shape(species, cells, slots),
        ],
        [pltpu.VMEM((PADDED, slots), F32), pltpu.VMEM((species, PADDED, slots), F32)],
        (lewis, rows, pick0),
        specs={0: smem},
        flops=500_000_000,
    )
    got = [rows[:, :middle], later]
    got_lo = [lax.ppermute(part, "member", up) for part in got]
    got_hi = [lax.ppermute(part, "member", down) for part in got]
    got_lo2 = [lax.ppermute(part, "member", up) for part in got_lo]
    got_hi2 = [lax.ppermute(part, "member", down) for part in got_hi]
    sort, z_natural, z_halves, total0, beside, total, coefs = call(
        prepare_kernel,
        [
            shape(2, slots, 2 * slots, dtype=BF16),
            shape(2, cells, slots),
            shape(2, cells, slots),
            shape(cells, slots),
            shape(2, 5, cells, slots),
            shape(2, cells, slots),
            shape(2, cells, slots),
        ],
        [pltpu.VMEM((2, PADDED, slots), F32), pltpu.VMEM((2, cells, slots), F32)],
        (got_lo[0], got_hi[0], coef0, pick0, weights0, xy_pick, z_pick),
        specs={0: head, 1: head},
        flops=100_000_000,
    )
    inner = [
        call(
            functools.partial(inner_kernel, first),
            [shape(count, cells, slots)] * 4,
            [
                pltpu.VMEM((2, count, PADDED, slots), F32),
                pltpu.VMEM((4, count, cells, slots), F32),
                pltpu.VMEM((count, PADDED, slots), F32),
            ],
            (
                lewis, sort, xy_pick, z_pick, z_halves, total0, beside,
                pick0, weights0, flat, base, rhs, got_lo[c], got_hi[c],
            ),
            specs={0: smem},
            flops=200_000_000 * count,
        )
        for c, (first, count) in enumerate(zip(firsts, cuts))
    ]
    far = call(
        far_kernel,
        [
            shape(2 * slots, 2 * slots, dtype=BF16),
            shape(2, cells, slots),
            shape(2, cells, slots),
            shape(2, 2 * slots, slots, dtype=BF16),
        ],
        [],
        (pick0, z_pick, total, coefs, got_lo2[0], got_hi2[0]),
        specs={4: head, 5: head},
        flops=50_000_000,
    )
    (early,) = call(
        functools.partial(outer_kernel, 0),
        [shape(cuts[0], slots, cells)],
        [],
        (lewis, *far, z_natural, *inner[0], got_lo2[0], got_hi2[0]),
        specs={0: smem},
        flops=100_000_000 * cuts[0],
    )
    (out,) = call(
        functools.partial(outer_kernel, firsts[1]),
        [shape(species, slots, cells)],
        [pltpu.VMEM((cuts[1], slots, cells), F32), pltpu.SemaphoreType.DMA((cuts[1] + 1,))],
        (lewis, *far, z_natural, *inner[1], got_lo2[1], got_hi2[1], early),
        specs={0: smem},
        outs=[anywhere],
        flops=100_000_000 * cuts[1],
    )
    return jnp.transpose(out, (1, 0, 2))[None, None]


def solution(mesh):
    return jax.shard_map(
        per_device,
        mesh=mesh,
        in_specs=(
            P("group", "member", None, None, None),
            P("group", "member", None, None),
            P("group", "member", None),
            P("group", "member", None, None),
            P(),
        ),
        out_specs=P("group", "member", None, None, None),
        check_vma=False,
    )
```

time: 267 us -> 57.9 us (0.22)
  local copies, waits for them, and re-layouts: 173 us -> 0.04 us
  other arithmetic: 44.8 us -> 0 us
  Pallas kernels: 0 us -> 15.2 us
  blocking collectives: 9.46 us -> 13.4 us
  starting transfers between devices: 31.4 us -> 27.6 us
  waiting for transfers between devices: 3.85 us -> 1.06 us
    slice x14 -> x1, local copies, waits for them, and re-layouts: 48.9 us -> 0.03 us  [per_device(): got = [rows[:, :middle], later]]
    gather x18 -> x0, local copies, waits for them, and re-layouts: 37.4 us -> none  [pick_rows(): taken = jnp.take(field, jnp.clip(index, 0, field.shape[0] - 1), axis=0)]
    scatter x4 -> x0, local copies, waits for them, and re-layouts: 28.7 us -> none  [the longest x1 14.2 us: per_device(): send_state = jnp.zeros((groups * capacity,) + old_state.shape[1:], jnp.bf...]
    pallas_call x0 -> x9, Pallas kernels: none -> 15.2 us  [call(): pl.pallas_call(kernel, out_shape=out_shape, grid=grid, in_specs=[specs.ge...]
    select_n x10 -> x0, other arithmetic: 15 us -> none  [the longest x8 14.3 us: pick_rows(): return jnp.where((index >= 0)[:, None, None], taken, 0.0)]
    ppermute x4 -> x0, local copies, waits for them, and re-layouts: 13.4 us -> none  [the longest x2 6.7 us: with_halo(): lax.ppermute(lax.slice_in_dim(block, 0, width, axis=dim), axis, backward)]
    all_gather x0 -> x1, blocking collectives: none -> 13.4 us  [per_device(): all_lists = lax.all_gather(lists, 'member')]
    reshape x6 -> x0, local copies, waits for them, and re-layouts: 12.8 us -> none  [the longest x2 3.96 us: beside_all(): jnp.repeat(pick_rows(field[..., 0::PX], lists[1]), PX, axis=-1)]
  transfers between devices with their start and end apart: 9 -> 9, of which waited for: 1 -> 2; matrix products, arithmetic and copies ran while one was open for 53% -> 0% of each run, Pallas kernels for 0% -> 18%
where the time goes in v3:
time: 57.9 us; the launch traced here: 57.4 us
  starting transfers between devices  27.6 us (48%)
  Pallas kernels  15.2 us (26%)
  blocking collectives  13.4 us (23%)
  waiting for transfers between devices  1.06 us (2%)
    pallas_call x9, Pallas kernels, call(): pl.pallas_call(kernel, out_shape=out_shape, grid=grid, in_specs=[specs.ge...  15.2 us
    all_gather x1, blocking collectives, per_device(): all_lists = lax.all_gather(lists, 'member')  13.4 us
    ppermute x2, starting transfers between devices, per_device(): got_lo2 = [lax.ppermute(part, 'member', up) for part in got_lo]  9.13 us
    ppermute x2, starting transfers between devices, per_device(): got_lo = [lax.ppermute(part, 'member', up) for part in got]  8.07 us
    all_to_all x1, starting transfers between devices, per_device(): lax.all_to_all(send, 'group', split_axis=0, concat_axis=0, tiled=True)  5.18 us
    ppermute x2, starting transfers between devices, per_device(): got_hi = [lax.ppermute(part, 'member', down) for part in got]  2.58 us
    ppermute x2, starting transfers between devices, per_device(): got_hi2 = [lax.ppermute(part, 'member', down) for part in got_hi]  2.58 us
  transfers between devices with their start and end apart: 9, of which 2 were waited for; matrix products, arithmetic and copies ran while one was open for 0% of the time, Pallas kernels for 18%

profile of v3, /device:TPU:0, one launch (start us, length us, event | category | flops | bytes accessed | tf_op | source)
XLA Modules:
  0.0 57.4 jit_solution(4457229235643330854)
XLA Ops:
  0.0 2.8 %shard_map.55 = (bf16[128,2560]{1,0:T(8,128)(2,1)}, s32[8,128]{1,0:T(8,128)}) custom-call(s32[1,128]{1,0:T(1,128)} %bitcast.19, s32[6,1,128]{2,1,0:T(1,128)} %bitcast.18, bf16[9,128,256]{2,1,0:T(8,128)(2,1)} %bitcast.16, bf16[128,256]{1,0:T(8,128)(2,1)} %bitcast.17), custom_call_target="tpu_custom_call" | custom-call | bytes 1318400 | tf_op jit(solution)/shard_map/pallas_call | solution.py:372
  2.8 0.0 copy-start
  2.8 0.0 copy-start.1
  2.8 5.2 %all-to-all-start = ((bf16[8,16,2560]{2,1,0:T(8,128)(2,1)}), bf16[8,16,2560]{2,1,0:T(8,128)(2,1)S(1)}, u32[]{:S(2)}, u32[]{:S(2)}) async-start(bf16[8,16,2560]{2,1,0:T(8,128)(2,1)} %bitcast.15), calls=%async_computation | async-start | bytes 1310720 | tf_op jit(solution)/shard_map/all_to_all | solution.py:425
  8.0 0.0 copy-done
  8.0 13.4 %all-gather = s32[32,128]{1,0:T(8,128)S(1)} all-gather(s32[8,128]{1,0:T(8,128)S(1)} %copy-done), channel_id=2, replica_groups=mesh['group'=8,'member'=4] {'member'}, dimensions={0}, use_global_device_ids=true | all-gather | bytes 20480 | tf_op jit(solution)/shard_map/all_gather | solution.py:426
  21.4 0.0 all-to-all-done
  21.4 3.5 %collective-permute-start = (bf16[128,1536]{1,0:T(8,128)(2,1)S(1)}, bf16[128,1536]{1,0:T(8,128)(2,1)S(1)}, u32[]{:S(2)}, u32[]{:S(2)}) collective-permute-start(bf16[128,1536]{1,0:T(8,128)(2,1)S(1)} %slice.3), channel_id=1, source_target_pairs={{0,1},{1,2},{2,3},{4,5},{5,6},{6,7},{8,9},{9,10},{10,11},{12,13},{... | collective-permute-start | bytes 1179656 | tf_op jit(solution)/shard_map/ppermute | solution.py:454
  24.9 1.3 %collective-permute-start.1 = (bf16[128,1536]{1,0:T(8,128)(2,1)S(1)}, bf16[128,1536]{1,0:T(8,128)(2,1)S(1)}, u32[]{:S(2)}, u32[]{:S(2)}) collective-permute-start(bf16[128,1536]{1,0:T(8,128)(2,1)S(1)} %slice.3), channel_id=1, source_target_pairs={{1,0},{2,1},{3,2},{5,4},{6,5},{7,6},{9,8},{10,9},{11,10},{13,12},{... | collective-permute-start | bytes 1179656 | tf_op jit(solution)/shard_map/ppermute | solution.py:455
  26.2 0.1 shard_map.56
  26.3 0.0 copy-done.1
  26.4 1.9 %shard_map.57 = (bf16[128,1024]{1,0:T(8,128)(2,1)S(1)}, f32[256,128]{1,0:T(8,128)S(1)}, f32[4,256,128]{2,1,0:T(8,128)S(1)}, bf16[9,256,128]{2,1,0:T(8,128)(2,1)S...) custom-call(f32[9]{0:T(128)S(1)} %copy-done.1, bf16[128,2560]{1,0:T(8,128)(2,1)S(1)} %bitcast.13, ...), custom_call_target="tpu_custom_call" | custom-call | flops 500000000 | bytes 4718628 | tf_op jit(solution)/shard_map/pallas_call | solution.py:372
  28.3 4.6 %collective-permute-start.4 = (bf16[128,1024]{1,0:T(8,128)(2,1)S(1)}, bf16[128,1024]{1,0:T(8,128)(2,1)S(1)}, u32[]{:S(2)}, u32[]{:S(2)}) collective-permute-start(bf16[128,1024]{1,0:T(8,128)(2,1)S(1)} %get-tuple-element.60), channel_id=1, source_target_pairs={{0,1},{1,2},{2,3},{4,5},{5,6},{6,7},{8,9},{9,10},{10,11},{12,13},{... | collective-permute-start | bytes 786440 | tf_op jit(solution)/shard_map/ppermute | solution.py:454
  32.9 1.3 %collective-permute-start.5 = (bf16[128,1024]{1,0:T(8,128)(2,1)S(1)}, bf16[128,1024]{1,0:T(8,128)(2,1)S(1)}, u32[]{:S(2)}, u32[]{:S(2)}) collective-permute-start(bf16[128,1024]{1,0:T(8,128)(2,1)S(1)} %get-tuple-element.60), channel_id=1, source_target_pairs={{1,0},{2,1},{3,2},{5,4},{6,5},{7,6},{9,8},{10,9},{11,10},{13,12},{... | collective-permute-start | bytes 786440 | tf_op jit(solution)/shard_map/ppermute | solution.py:455
  34.2 0.0 collective-permute-done.head_lo.got_lo
  34.2 4.6 %collective-permute-start.2 = (bf16[128,1536]{1,0:T(8,128)(2,1)S(1)}, bf16[128,1536]{1,0:T(8,128)(2,1)S(1)}, u32[]{:S(2)}, u32[]{:S(2)}) collective-permute-start(bf16[128,1536]{1,0:T(8,128)(2,1)S(1)} %collective-permute-done.head_lo.got_lo), channel_id=1, source_target_pairs={{0,1},{1,2},{2,3},{4,5},{5,6},{6,7},{8,9},{9,10},{10,11},{12,13},{... | collective-permute-start | bytes 1179656 | tf_op jit(solution)/shard_map/ppermute | solution.py:456
  38.8 0.0 collective-permute-done.1.head_hi.got_hi
  38.8 1.3 %collective-permute-start.3 = (bf16[128,1536]{1,0:T(8,128)(2,1)S(1)}, bf16[128,1536]{1,0:T(8,128)(2,1)S(1)}, u32[]{:S(2)}, u32[]{:S(2)}) collective-permute-start(bf16[128,1536]{1,0:T(8,128)(2,1)S(1)} %collective-permute-done.1.head_hi.got_hi), channel_id=1, source_target_pairs={{1,0},{2,1},{3,2},{5,4},{6,5},{7,6},{9,8},{10,9},{11,10},{13,12},{... | collective-permute-start | bytes 1179656 | tf_op jit(solution)/shard_map/ppermute | solution.py:457
  40.1 0.0 collective-permute-done.4.got_lo
  40.1 4.6 %collective-permute-start.6 = (bf16[128,1024]{1,0:T(8,128)(2,1)S(1)}, bf16[128,1024]{1,0:T(8,128)(2,1)S(1)}, u32[]{:S(2)}, u32[]{:S(2)}) collective-permute-start(bf16[128,1024]{1,0:T(8,128)(2,1)S(1)} %collective-permute-done.4.got_lo), channel_id=1, source_target_pairs={{0,1},{1,2},{2,3},{4,5},{5,6},{6,7},{8,9},{9,10},{10,11},{12,13},{... | collective-permute-start | bytes 786440 | tf_op jit(solution)/shard_map/ppermute | solution.py:456
  44.7 0.0 collective-permute-done.5.got_hi
  44.7 1.3 %collective-permute-start.7 = (bf16[128,1024]{1,0:T(8,128)(2,1)S(1)}, bf16[128,1024]{1,0:T(8,128)(2,1)S(1)}, u32[]{:S(2)}, u32[]{:S(2)}) collective-permute-start(bf16[128,1024]{1,0:T(8,128)(2,1)S(1)} %collective-permute-done.5.got_hi), channel_id=1, source_target_pairs={{1,0},{2,1},{3,2},{5,4},{6,5},{7,6},{9,8},{10,9},{11,10},{13,12},{... | collective-permute-start | bytes 786440 | tf_op jit(solution)/shard_map/ppermute | solution.py:457
  46.0 1.2 %shard_map.58 = (bf16[2,128,256]{2,1,0:T(8,128)(2,1)S(1)}, f32[2,256,128]{2,1,0:T(8,128)S(1)}, f32[2,256,128]{2,1,0:T(8,128)S(1)}, f32[256,128]{1,0:T(8,128)S(1)...) custom-call(bf16[128,1536]{1,0:T(8,128)(2,1)S(1)} %collective-permute-done.head_lo.got_lo, ...), custom_call_target="tpu_custom_call" | custom-call | flops 100000000 | bytes 4653056 | tf_op jit(solution)/shard_map/pallas_call | solution.py:372
  47.1 2.2 %shard_map.60 = (f32[4,256,128]{2,1,0:T(8,128)S(1)}, f32[4,256,128]{2,1,0:T(8,128)S(1)}, f32[4,256,128]{2,1,0:T(8,128)S(1)}, f32[4,256,128]{2,1,0:T(8,128)S(1)}) custom-call(f32[9]{0:T(128)S(1)} %copy-done.1, bf16[2,128,256]{2,1,0:T(8,128)(2,1)S(1)} %get-tuple-element.53.sort_ref, bf16[2,4,128,128]{3,2,1,0:T(8,128)(2,1)S(1)} %get-tuple-element.45.xy_pick, ...), custom_call_target="tpu_custom_call" | custom-call | flops 800000000 | bytes 8519716 | tf_op jit(solution)/shard_map/pallas_call | solution.py:372
  49.4 2.5 %shard_map.61 = (f32[5,256,128]{2,1,0:T(8,128)S(1)}, f32[5,256,128]{2,1,0:T(8,128)S(1)}, f32[5,256,128]{2,1,0:T(8,128)S(1)}, f32[5,256,128]{2,1,0:T(8,128)S(1)}) custom-call(f32[9]{0:T(128)S(1)} %copy-done.1, bf16[2,128,256]{2,1,0:T(8,128)(2,1)S(1)} %get-tuple-element.53.sort_ref, bf16[2,4,128,128]{3,2,1,0:T(8,128)(2,1)S(1)} %get-tuple-element.45.xy_pick, ...), custom_call_target="tpu_custom_call" | custom-call | flops 1000000000 | bytes 9306148 | tf_op jit(solution)/shard_map/pallas_call | solution.py:372
  51.9 0.0 collective-permute-done.2.head_lo2.got_lo2
  51.9 0.5 collective-permute-done.3.head_hi2.got_hi2
  52.4 0.5 shard_map.59
  52.9 1.7 %shard_map.62.rest_0_ = f32[5,128,256]{2,1,0:T(8,128)S(1)} custom-call(f32[9]{0:T(128)S(1)} %copy-done.1, bf16[256,256]{1,0:T(8,128)(2,1)S(1)} %get-tuple-element.48.far_ref, f32[2,256,128]{2,1,0:T(8,128)S(1)} %get-tuple-element.49.w_ref, f32[2,256,128]{2,1,0:T(8,128)S(1)} %get-tuple-element.50.t_ref, bf16[2,256,128]{2,1,0:T(8,128)(2,1)S(1)} %get-tuple-element.51.two_ref, ...), custom_call_target="tpu_custom_call" | custom-call | flops 500000000 | bytes 5111844 | tf_op jit(solution)/shard_map/pallas_call | solution.py:372
  54.6 0.0 collective-permute-done.6.got_lo2
  54.7 0.5 collective-permute-done.7.got_hi2
  55.2 2.3 %shard_map.63 = f32[9,128,256]{2,1,0:T(8,128)} custom-call(f32[9]{0:T(128)S(1)} %copy-done.1, bf16[256,256]{1,0:T(8,128)(2,1)S(1)} %get-tuple-element.48.far_ref, f32[2,256,128]{2,1,0:T(8,128)S(1)} %get-tuple-element.49.w_ref, f32[2,256,128]{2,1,0:T(8,128)S(1)} %get-tuple-element.50.t_ref, bf16[2,256,128]{2,1,0:T(8,128)(2,1)S(1)} %get-tuple-element.51.two_ref, ...), custom_call_target="tpu_custom_call" | custom-call | flops 400000000 | bytes 5505060 | tf_op jit(solution)/shard_map/pallas_call | solution.py:372
  (1 shorter events, 0.0 us)
Async XLA Ops:
  2.8 5.2 %copy-start = (s32[8,128]{1,0:T(8,128)S(1)}, s32[8,128]{1,0:T(8,128)}, u32[]{:S(2)}) copy-start(s32[8,128]{1,0:T(8,128)} %get-tuple-element.37.lists0) | copy-start | bytes 12292
  2.8 23.5 %copy-start.1 = (f32[9]{0:T(128)S(1)}, f32[9]{0:T(128)}, u32[]{:S(2)}) copy-start(f32[9]{0:T(128)} %lewis_ref.9) | copy-start | bytes 112
  2.8 18.5 %all-to-all-start = ((bf16[8,16,2560]{2,1,0:T(8,128)(2,1)}), bf16[8,16,2560]{2,1,0:T(8,128)(2,1)S(1)}, u32[]{:S(2)}, u32[]{:S(2)}) async-start(bf16[8,16,2560]{2,1,0:T(8,128)(2,1)} %bitcast.15), calls=%async_computation | async-start | bytes 1310720 | tf_op jit(solution)/shard_map/all_to_all | solution.py:425
  21.4 12.8 %collective-permute-start = (bf16[128,1536]{1,0:T(8,128)(2,1)S(1)}, bf16[128,1536]{1,0:T(8,128)(2,1)S(1)}, u32[]{:S(2)}, u32[]{:S(2)}) collective-permute-start(bf16[128,1536]{1,0:T(8,128)(2,1)S(1)} %slice.3), channel_id=1, source_target_pairs={{0,1},{1,2},{2,3},{4,5},{5,6},{6,7},{8,9},{9,10},{10,11},{12,13},{... | collective-permute-start | bytes 1179656 | tf_op jit(solution)/shard_map/ppermute | solution.py:454
  24.9 13.8 %collective-permute-start.1 = (bf16[128,1536]{1,0:T(8,128)(2,1)S(1)}, bf16[128,1536]{1,0:T(8,128)(2,1)S(1)}, u32[]{:S(2)}, u32[]{:S(2)}) collective-permute-start(bf16[128,1536]{1,0:T(8,128)(2,1)S(1)} %slice.3), channel_id=1, source_target_pairs={{1,0},{2,1},{3,2},{5,4},{6,5},{7,6},{9,8},{10,9},{11,10},{13,12},{... | collective-permute-start | bytes 1179656 | tf_op jit(solution)/shard_map/ppermute | solution.py:455
  28.3 11.8 %collective-permute-start.4 = (bf16[128,1024]{1,0:T(8,128)(2,1)S(1)}, bf16[128,1024]{1,0:T(8,128)(2,1)S(1)}, u32[]{:S(2)}, u32[]{:S(2)}) collective-permute-start(bf16[128,1024]{1,0:T(8,128)(2,1)S(1)} %get-tuple-element.60), channel_id=1, source_target_pairs={{0,1},{1,2},{2,3},{4,5},{5,6},{6,7},{8,9},{9,10},{10,11},{12,13},{... | collective-permute-start | bytes 786440 | tf_op jit(solution)/shard_map/ppermute | solution.py:454
  32.9 11.8 %collective-permute-start.5 = (bf16[128,1024]{1,0:T(8,128)(2,1)S(1)}, bf16[128,1024]{1,0:T(8,128)(2,1)S(1)}, u32[]{:S(2)}, u32[]{:S(2)}) collective-permute-start(bf16[128,1024]{1,0:T(8,128)(2,1)S(1)} %get-tuple-element.60), channel_id=1, source_target_pairs={{1,0},{2,1},{3,2},{5,4},{6,5},{7,6},{9,8},{10,9},{11,10},{13,12},{... | collective-permute-start | bytes 786440 | tf_op jit(solution)/shard_map/ppermute | solution.py:455
  34.2 17.7 %collective-permute-start.2 = (bf16[128,1536]{1,0:T(8,128)(2,1)S(1)}, bf16[128,1536]{1,0:T(8,128)(2,1)S(1)}, u32[]{:S(2)}, u32[]{:S(2)}) collective-permute-start(bf16[128,1536]{1,0:T(8,128)(2,1)S(1)} %collective-permute-done.head_lo.got_lo), channel_id=1, source_target_pairs={{0,1},{1,2},{2,3},{4,5},{5,6},{6,7},{8,9},{9,10},{10,11},{12,13},{... | collective-permute-start | bytes 1179656 | tf_op jit(solution)/shard_map/ppermute | solution.py:456
  38.8 13.6 %collective-permute-start.3 = (bf16[128,1536]{1,0:T(8,128)(2,1)S(1)}, bf16[128,1536]{1,0:T(8,128)(2,1)S(1)}, u32[]{:S(2)}, u32[]{:S(2)}) collective-permute-start(bf16[128,1536]{1,0:T(8,128)(2,1)S(1)} %collective-permute-done.1.head_hi.got_hi), channel_id=1, source_target_pairs={{1,0},{2,1},{3,2},{5,4},{6,5},{7,6},{9,8},{10,9},{11,10},{13,12},{... | collective-permute-start | bytes 1179656 | tf_op jit(solution)/shard_map/ppermute | solution.py:457
  40.1 14.6 %collective-permute-start.6 = (bf16[128,1024]{1,0:T(8,128)(2,1)S(1)}, bf16[128,1024]{1,0:T(8,128)(2,1)S(1)}, u32[]{:S(2)}, u32[]{:S(2)}) collective-permute-start(bf16[128,1024]{1,0:T(8,128)(2,1)S(1)} %collective-permute-done.4.got_lo), channel_id=1, source_target_pairs={{0,1},{1,2},{2,3},{4,5},{5,6},{6,7},{8,9},{9,10},{10,11},{12,13},{... | collective-permute-start | bytes 786440 | tf_op jit(solution)/shard_map/ppermute | solution.py:456
  44.7 10.5 %collective-permute-start.7 = (bf16[128,1024]{1,0:T(8,128)(2,1)S(1)}, bf16[128,1024]{1,0:T(8,128)(2,1)S(1)}, u32[]{:S(2)}, u32[]{:S(2)}) collective-permute-start(bf16[128,1024]{1,0:T(8,128)(2,1)S(1)} %collective-permute-done.5.got_hi), channel_id=1, source_target_pairs={{1,0},{2,1},{3,2},{5,4},{6,5},{7,6},{9,8},{10,9},{11,10},{13,12},{... | collective-permute-start | bytes 786440 | tf_op jit(solution)/shard_map/ppermute | solution.py:457

commit v4 on v3

--- a/solution.py
+++ b/solution.py
@@ -161,11 +161,8 @@
             field[target] = got[i * PX : (i + 1) * PX]
 
 
-def pick_kernel(members, lists0, all_lists, pick_ref, xy_pick, z_pick):
+def pick_kernel(lists0, lists_lo, lists_hi, pick_ref, xy_pick, z_pick):
     slots = lists0.shape[1]
-    member = lax.axis_index("member")
-    lists_lo = jnp.where(member > 0, all_lists[jnp.maximum(member - 1, 0)], 0)
-    lists_hi = jnp.where(member < members - 1, all_lists[jnp.minimum(member + 1, members - 1)], 0)
 
     def picking(lists, face):
         return ones_where(iota((slots, slots), 0) == lists[face : face + 1] - 1)
@@ -181,10 +178,9 @@
 
 def own_kernel(
     lewis_ref, got, pick_ref,
-    later_ref, coef_ref, weights_ref, flat_ref, base_ref, rhs_ref, coef_pad, field_ref,
+    coef_ref, weights_ref, flat_ref, base_ref, rhs_ref, coef_pad, field_ref,
 ):
     species, cells, slots = base_ref.shape
-    later_ref[...] = got[:, got.shape[1] - later_ref.shape[1] :]
     sort = sorting(got[:, :cells])
     coef = dot_first(got[:, :cells], sort)
     coef_ref[...] = coef
@@ -423,22 +419,25 @@
         grid=(),
     )
     rows = lax.all_to_all(send, "group", split_axis=0, concat_axis=0, tiled=True)
-    all_lists = lax.all_gather(lists, "member")
-    rows, all_lists = lax.optimization_barrier((rows, all_lists))
+    lists_lo = lax.ppermute(lists, "member", up)
+    lists_hi = lax.ppermute(lists, "member", down)
     pick0, xy_pick, z_pick = call(
-        functools.partial(pick_kernel, members),
+        pick_kernel,
         [
             shape(FACES, slots, slots, dtype=BF16),
             shape(2, 4, slots, slots, dtype=BF16),
             shape(2, slots, 2 * slots, dtype=BF16),
         ],
         [],
-        (lists, all_lists),
-    )
-    later, coef0, weights0, flat, base, rhs = call(
+        (lists, lists_lo, lists_hi),
+    )
+    rows, pick0, xy_pick, z_pick = lax.optimization_barrier((rows, pick0, xy_pick, z_pick))
+    got = [rows[:, :middle], rows[:, middle:]]
+    got_lo = [lax.ppermute(part, "member", up) for part in got]
+    got_hi = [lax.ppermute(part, "member", down) for part in got]
+    coef0, weights0, flat, base, rhs = call(
         own_kernel,
         [
-            shape(slots, width - middle, dtype=BF16),
             shape(cells, slots),
             shape(4, cells, slots),
             shape(species, cells, slots, dtype=BF16),
@@ -450,9 +449,9 @@
         specs={0: smem},
         flops=500_000_000,
     )
-    got = [rows[:, :middle], later]
-    got_lo = [lax.ppermute(part, "member", up) for part in got]
-    got_hi = [lax.ppermute(part, "member", down) for part in got]
+    got_lo[0], got_hi[0], coef0, weights0, flat, base, rhs = lax.optimization_barrier(
+        (got_lo[0], got_hi[0], coef0, weights0, flat, base, rhs)
+    )
     got_lo2 = [lax.ppermute(part, "member", up) for part in got_lo]
     got_hi2 = [lax.ppermute(part, "member", down) for part in got_hi]
     sort, z_natural, z_halves, total0, beside, total, coefs = call(

time: 57.9 us -> 57.7 us (level)
  blocking collectives: 13.4 us -> 0 us
  waiting for transfers between devices: 1.06 us -> 9.73 us
  starting transfers between devices: 27.6 us -> 31.2 us
  Pallas kernels: 15.2 us -> 16 us
    all_gather x1 -> x0, blocking collectives: 13.4 us -> none  [per_device(): all_lists = lax.all_gather(lists, 'member')]
    ppermute x0 -> x2, starting transfers between devices: none -> 4.77 us  [the longest x1 3.48 us: per_device(): lists_lo = lax.ppermute(lists, 'member', up)]
    ppermute x0 -> x2, waiting for transfers between devices: none -> 4.2 us  [the longest x1 4.19 us: per_device(): lists_hi = lax.ppermute(lists, 'member', down)]
    ppermute x2, waiting for transfers between devices: 0.01 us -> 3.47 us  [per_device(): got_hi = [lax.ppermute(part, 'member', down) for part in got]]
    all_to_all x1, waiting for transfers between devices: 0.01 us -> 2.04 us  [per_device(): lax.all_to_all(send, 'group', split_axis=0, concat_axis=0, tiled=True)]
    ppermute x2, starting transfers between devices: 9.13 us -> 8.04 us  [per_device(): got_lo2 = [lax.ppermute(part, 'member', up) for part in got_lo]]
    ppermute x2, waiting for transfers between devices: 1.04 us -> 0.01 us  [per_device(): got_hi2 = [lax.ppermute(part, 'member', down) for part in got_hi]]
    pallas_call x9, Pallas kernels: 15.2 us -> 16 us  [call(): pl.pallas_call(kernel, out_shape=out_shape, grid=grid, in_specs=[specs.ge...]
  transfers between devices with their start and end apart: 9 -> 11, of which waited for: 2 -> 3; matrix products, arithmetic and copies ran while one was open for 0% -> 0% of each run, Pallas kernels for 18% -> 19%
where the time goes in v4:
time: 57.7 us; the launch traced here: 57.2 us
  starting transfers between devices  31.2 us (54%)
  Pallas kernels  16 us (28%)
  waiting for transfers between devices  9.73 us (17%)
    pallas_call x9, Pallas kernels, call(): pl.pallas_call(kernel, out_shape=out_shape, grid=grid, in_specs=[specs.ge...  16 us
    ppermute x2, starting transfers between devices, per_device(): got_lo = [lax.ppermute(part, 'member', up) for part in got]  8.07 us
    ppermute x2, starting transfers between devices, per_device(): got_lo2 = [lax.ppermute(part, 'member', up) for part in got_lo]  8.04 us
    all_to_all x1, starting transfers between devices, per_device(): lax.all_to_all(send, 'group', split_axis=0, concat_axis=0, tiled=True)  5.18 us
    ppermute x1, waiting for transfers between devices, per_device(): lists_hi = lax.ppermute(lists, 'member', down)  4.19 us
    ppermute x1, starting transfers between devices, per_device(): lists_lo = lax.ppermute(lists, 'member', up)  3.48 us
    ppermute x2, waiting for transfers between devices, per_device(): got_hi = [lax.ppermute(part, 'member', down) for part in got]  3.47 us
    ppermute x2, starting transfers between devices, per_device(): got_hi2 = [lax.ppermute(part, 'member', down) for part in got_hi]  2.58 us
  transfers between devices with their start and end apart: 11, of which 3 were waited for; matrix products, arithmetic and copies ran while one was open for 0% of the time, Pallas kernels for 19%

profile of v4, /device:TPU:0, one launch (start us, length us, event | category | flops | bytes accessed | tf_op | source)
XLA Modules:
  0.0 57.2 jit_solution(13863453372272821765)
XLA Ops:
  0.0 2.8 %shard_map.55 = (bf16[128,2560]{1,0:T(8,128)(2,1)}, s32[8,128]{1,0:T(8,128)}) custom-call(s32[1,128]{1,0:T(1,128)} %bitcast.18, s32[6,1,128]{2,1,0:T(1,128)} %bitcast.17, bf16[9,128,256]{2,1,0:T(8,128)(2,1)} %bitcast.15, bf16[128,256]{1,0:T(8,128)(2,1)} %bitcast.16), custom_call_target="tpu_custom_call" | custom-call | bytes 1318400 | tf_op jit(solution)/shard_map/pallas_call | solution.py:368
  2.8 0.0 copy-start.1
  2.8 0.0 copy-start
  2.8 5.2 %all-to-all-start = ((bf16[8,16,2560]{2,1,0:T(8,128)(2,1)}), bf16[8,16,2560]{2,1,0:T(8,128)(2,1)S(1)}, u32[]{:S(2)}, u32[]{:S(2)}) async-start(bf16[8,16,2560]{2,1,0:T(8,128)(2,1)} %bitcast.14), calls=%async_computation | async-start | bytes 1310720 | tf_op jit(solution)/shard_map/all_to_all | solution.py:421
  8.0 0.0 copy-done.1
  8.0 3.5 %collective-permute-start = (s32[8,128]{1,0:T(8,128)S(1)}, s32[8,128]{1,0:T(8,128)S(1)}, u32[]{:S(2)}, u32[]{:S(2)}) collective-permute-start(s32[8,128]{1,0:T(8,128)S(1)} %copy-done.1), channel_id=1, source_target_pairs={{0,1},{1,2},{2,3},{4,5},{5,6},{6,7},{8,9},{9,10},{10,11},{12,13},{... | collective-permute-start | bytes 12296 | tf_op jit(solution)/shard_map/ppermute | solution.py:422
  11.5 1.3 %collective-permute-start.1 = (s32[8,128]{1,0:T(8,128)S(1)}, s32[8,128]{1,0:T(8,128)S(1)}, u32[]{:S(2)}, u32[]{:S(2)}) collective-permute-start(s32[8,128]{1,0:T(8,128)S(1)} %copy-done.1), channel_id=1, source_target_pairs={{1,0},{2,1},{3,2},{5,4},{6,5},{7,6},{9,8},{10,9},{11,10},{13,12},{... | collective-permute-start | bytes 12296 | tf_op jit(solution)/shard_map/ppermute | solution.py:423
  12.8 0.0 collective-permute-done.lists_lo
  12.8 4.2 %collective-permute-done.1.lists_hi = s32[8,128]{1,0:T(8,128)S(1)} collective-permute-done((s32[8,128]{1,0:T(8,128)S(1)}, s32[8,128]{1,0:T(8,128)S(1)}, u32[]{:S(2)}, u32[]{:S(2)}) %collective-permute-start.1) | collective-permute-done | bytes 4128 | tf_op jit(solution)/shard_map/ppermute | solution.py:423
  17.0 0.1 shard_map.56
  17.1 2.0 %all-to-all-done = bf16[8,16,2560]{2,1,0:T(8,128)(2,1)S(1)} async-done(((bf16[8,16,2560]{2,1,0:T(8,128)(2,1)}), bf16[8,16,2560]{2,1,0:T(8,128)(2,1)S(1)}, u32[]{:S(2)}, u32[]{:S(2)}) %all-to-all-start) | async-done | bytes 655392 | tf_op jit(solution)/shard_map/all_to_all | solution.py:421
  19.2 3.5 %collective-permute-start.2 = (bf16[128,1536]{1,0:T(8,128)(2,1)S(1)}, bf16[128,1536]{1,0:T(8,128)(2,1)S(1)}, u32[]{:S(2)}, u32[]{:S(2)}) collective-permute-start(bf16[128,1536]{1,0:T(8,128)(2,1)S(1)} %slice.6), channel_id=1, source_target_pairs={{0,1},{1,2},{2,3},{4,5},{5,6},{6,7},{8,9},{9,10},{10,11},{12,13},{... | collective-permute-start | bytes 1179656 | tf_op jit(solution)/shard_map/ppermute | solution.py:436
  22.7 1.3 %collective-permute-start.3 = (bf16[128,1536]{1,0:T(8,128)(2,1)S(1)}, bf16[128,1536]{1,0:T(8,128)(2,1)S(1)}, u32[]{:S(2)}, u32[]{:S(2)}) collective-permute-start(bf16[128,1536]{1,0:T(8,128)(2,1)S(1)} %slice.6), channel_id=1, source_target_pairs={{1,0},{2,1},{3,2},{5,4},{6,5},{7,6},{9,8},{10,9},{11,10},{13,12},{... | collective-permute-start | bytes 1179656 | tf_op jit(solution)/shard_map/ppermute | solution.py:437
  24.0 4.6 %collective-permute-start.6 = (bf16[128,1024]{1,0:T(8,128)(2,1)S(1)}, bf16[128,1024]{1,0:T(8,128)(2,1)S(1)}, u32[]{:S(2)}, u32[]{:S(2)}) collective-permute-start(bf16[128,1024]{1,0:T(8,128)(2,1)S(1)} %slice.7), channel_id=1, source_target_pairs={{0,1},{1,2},{2,3},{4,5},{5,6},{6,7},{8,9},{9,10},{10,11},{12,13},{... | collective-permute-start | bytes 786440 | tf_op jit(solution)/shard_map/ppermute | solution.py:436
  28.6 1.3 %collective-permute-start.7 = (bf16[128,1024]{1,0:T(8,128)(2,1)S(1)}, bf16[128,1024]{1,0:T(8,128)(2,1)S(1)}, u32[]{:S(2)}, u32[]{:S(2)}) collective-permute-start(bf16[128,1024]{1,0:T(8,128)(2,1)S(1)} %slice.7), channel_id=1, source_target_pairs={{1,0},{2,1},{3,2},{5,4},{6,5},{7,6},{9,8},{10,9},{11,10},{13,12},{... | collective-permute-start | bytes 786440 | tf_op jit(solution)/shard_map/ppermute | solution.py:437
  29.9 0.0 copy-done
  29.9 2.1 %shard_map.57 = (f32[256,128]{1,0:T(8,128)S(1)}, f32[4,256,128]{2,1,0:T(8,128)S(1)}, bf16[9,256,128]{2,1,0:T(8,128)(2,1)S(1)}, f32[9,256,128]{2,1,0:T(8,128)S(1)}, f32[9,256,128]{2,1,0:T(8,128)S(1)}) custom-call(f32[9]{0:T(128)S(1)} %copy-done, bf16[128,2560]{1,0:T(8,128)(2,1)S(1)} %bitcast.13, bf16[6,128,128]{2,1,0:T(8,128)(2,1)S(1)} %get-tuple-element.50.pick_ref.pick0), custom_call_target="tpu_custom_call" | custom-call | flops 500000000 | bytes 4456484 | tf_op jit(solution)/shard_map/pallas_call | solution.py:368
  32.0 0.0 collective-permute-done.2.head_lo.got_lo
  32.0 3.5 %collective-permute-done.3.head_hi.got_hi = bf16[128,1536]{1,0:T(8,128)(2,1)S(1)} collective-permute-done((bf16[128,1536]{1,0:T(8,128)(2,1)S(1)}, bf16[128,1536]{1,0:T(8,128)(2,1)S(1)}, u32[]{:S(2)}, u32[]{:S(2)}) %collective-permute-start.3) | collective-permute-done | bytes 393248 | tf_op jit(solution)/shard_map/ppermute | solution.py:437
  35.5 3.5 %collective-permute-start.4 = (bf16[128,1536]{1,0:T(8,128)(2,1)S(1)}, bf16[128,1536]{1,0:T(8,128)(2,1)S(1)}, u32[]{:S(2)}, u32[]{:S(2)}) collective-permute-start(bf16[128,1536]{1,0:T(8,128)(2,1)S(1)} %collective-permute-done.2.head_lo.got_lo), channel_id=1, source_target_pairs={{0,1},{1,2},{2,3},{4,5},{5,6},{6,7},{8,9},{9,10},{10,11},{12,13},{... | collective-permute-start | bytes 1179656 | tf_op jit(solution)/shard_map/ppermute | solution.py:455
  39.0 1.3 %collective-permute-start.5 = (bf16[128,1536]{1,0:T(8,128)(2,1)S(1)}, bf16[128,1536]{1,0:T(8,128)(2,1)S(1)}, u32[]{:S(2)}, u32[]{:S(2)}) collective-permute-start(bf16[128,1536]{1,0:T(8,128)(2,1)S(1)} %collective-permute-done.3.head_hi.got_hi), channel_id=1, source_target_pairs={{1,0},{2,1},{3,2},{5,4},{6,5},{7,6},{9,8},{10,9},{11,10},{13,12},{... | collective-permute-start | bytes 1179656 | tf_op jit(solution)/shard_map/ppermute | solution.py:456
  40.3 0.0 collective-permute-done.6.got_lo
  40.3 4.6 %collective-permute-start.8 = (bf16[128,1024]{1,0:T(8,128)(2,1)S(1)}, bf16[128,1024]{1,0:T(8,128)(2,1)S(1)}, u32[]{:S(2)}, u32[]{:S(2)}) collective-permute-start(bf16[128,1024]{1,0:T(8,128)(2,1)S(1)} %collective-permute-done.6.got_lo), channel_id=1, source_target_pairs={{0,1},{1,2},{2,3},{4,5},{5,6},{6,7},{8,9},{9,10},{10,11},{12,13},{... | collective-permute-start | bytes 786440 | tf_op jit(solution)/shard_map/ppermute | solution.py:455
  44.9 0.0 collective-permute-done.7.got_hi
  44.9 1.3 %collective-permute-start.9 = (bf16[128,1024]{1,0:T(8,128)(2,1)S(1)}, bf16[128,1024]{1,0:T(8,128)(2,1)S(1)}, u32[]{:S(2)}, u32[]{:S(2)}) collective-permute-start(bf16[128,1024]{1,0:T(8,128)(2,1)S(1)} %collective-permute-done.7.got_hi), channel_id=1, source_target_pairs={{1,0},{2,1},{3,2},{5,4},{6,5},{7,6},{9,8},{10,9},{11,10},{13,12},{... | collective-permute-start | bytes 786440 | tf_op jit(solution)/shard_map/ppermute | solution.py:456
  46.2 1.2 %shard_map.58 = (bf16[2,128,256]{2,1,0:T(8,128)(2,1)S(1)}, f32[2,256,128]{2,1,0:T(8,128)S(1)}, f32[2,256,128]{2,1,0:T(8,128)S(1)}, f32[256,128]{1,0:T(8,128)S(1)...) custom-call(bf16[128,1536]{1,0:T(8,128)(2,1)S(1)} %collective-permute-done.2.head_lo.got_lo, ...), custom_call_target="tpu_custom_call" | custom-call | flops 100000000 | bytes 4653056 | tf_op jit(solution)/shard_map/pallas_call | solution.py:368
  47.3 2.5 %shard_map.60 = (f32[4,256,128]{2,1,0:T(8,128)S(1)}, f32[4,256,128]{2,1,0:T(8,128)S(1)}, f32[4,256,128]{2,1,0:T(8,128)S(1)}, f32[4,256,128]{2,1,0:T(8,128)S(1)}) custom-call(f32[9]{0:T(128)S(1)} %copy-done, bf16[2,128,256]{2,1,0:T(8,128)(2,1)S(1)} %get-tuple-element.70.sort_ref, bf16[2,4,128,128]{3,2,1,0:T(8,128)(2,1)S(1)} %get-tuple-element.62.xy_pick, ...), custom_call_target="tpu_custom_call" | custom-call | flops 800000000 | bytes 8519716 | tf_op jit(solution)/shard_map/pallas_call | solution.py:368
  49.8 2.8 %shard_map.61 = (f32[5,256,128]{2,1,0:T(8,128)S(1)}, f32[5,256,128]{2,1,0:T(8,128)S(1)}, f32[5,256,128]{2,1,0:T(8,128)S(1)}, f32[5,256,128]{2,1,0:T(8,128)S(1)}) custom-call(f32[9]{0:T(128)S(1)} %copy-done, bf16[2,128,256]{2,1,0:T(8,128)(2,1)S(1)} %get-tuple-element.70.sort_ref, bf16[2,4,128,128]{3,2,1,0:T(8,128)(2,1)S(1)} %get-tuple-element.62.xy_pick, ...), custom_call_target="tpu_custom_call" | custom-call | flops 1000000000 | bytes 9306148 | tf_op jit(solution)/shard_map/pallas_call | solution.py:368
  52.6 0.0 collective-permute-done.4.head_lo2.got_lo2
  52.6 0.0 collective-permute-done.5.head_hi2.got_hi2
  52.6 0.5 shard_map.59
  53.1 1.8 %shard_map.62.rest_0_ = f32[5,128,256]{2,1,0:T(8,128)S(1)} custom-call(f32[9]{0:T(128)S(1)} %copy-done, bf16[256,256]{1,0:T(8,128)(2,1)S(1)} %get-tuple-element.65.far_ref, f32[2,256,128]{2,1,0:T(8,128)S(1)} %get-tuple-element.66.w_ref, f32[2,256,128]{2,1,0:T(8,128)S(1)} %get-tuple-element.67.t_ref, bf16[2,256,128]{2,1,0:T(8,128)(2,1)S(1)} %get-tuple-element.68.two_ref, ...), custom_call_target="tpu_custom_call" | custom-call | flops 500000000 | bytes 5111844 | tf_op jit(solution)/shard_map/pallas_call | solution.py:368
  54.9 0.0 collective-permute-done.8.got_lo2
  54.9 0.0 collective-permute-done.9.got_hi2
  54.9 2.3 %shard_map.63 = f32[9,128,256]{2,1,0:T(8,128)} custom-call(f32[9]{0:T(128)S(1)} %copy-done, bf16[256,256]{1,0:T(8,128)(2,1)S(1)} %get-tuple-element.65.far_ref, f32[2,256,128]{2,1,0:T(8,128)S(1)} %get-tuple-element.66.w_ref, f32[2,256,128]{2,1,0:T(8,128)S(1)} %get-tuple-element.67.t_ref, bf16[2,256,128]{2,1,0:T(8,128)(2,1)S(1)} %get-tuple-element.68.two_ref, ...), custom_call_target="tpu_custom_call" | custom-call | flops 400000000 | bytes 5505060 | tf_op jit(solution)/shard_map/pallas_call | solution.py:368
  (2 shorter events, 0.0 us)
Async XLA Ops:
  2.8 5.2 %copy-start.1 = (s32[8,128]{1,0:T(8,128)S(1)}, s32[8,128]{1,0:T(8,128)}, u32[]{:S(2)}) copy-start(s32[8,128]{1,0:T(8,128)} %get-tuple-element.46.lists0) | copy-start | bytes 12292
  2.8 27.1 %copy-start = (f32[9]{0:T(128)S(1)}, f32[9]{0:T(128)}, u32[]{:S(2)}) copy-start(f32[9]{0:T(128)} %lewis_ref.9) | copy-start | bytes 112
  2.8 16.3 %all-to-all-start = ((bf16[8,16,2560]{2,1,0:T(8,128)(2,1)}), bf16[8,16,2560]{2,1,0:T(8,128)(2,1)S(1)}, u32[]{:S(2)}, u32[]{:S(2)}) async-start(bf16[8,16,2560]{2,1,0:T(8,128)(2,1)} %bitcast.14), calls=%async_computation | async-start | bytes 1310720 | tf_op jit(solution)/shard_map/all_to_all | solution.py:421
  8.0 4.8 %collective-permute-start = (s32[8,128]{1,0:T(8,128)S(1)}, s32[8,128]{1,0:T(8,128)S(1)}, u32[]{:S(2)}, u32[]{:S(2)}) collective-permute-start(s32[8,128]{1,0:T(8,128)S(1)} %copy-done.1), channel_id=1, source_target_pairs={{0,1},{1,2},{2,3},{4,5},{5,6},{6,7},{8,9},{9,10},{10,11},{12,13},{... | collective-permute-start | bytes 12296 | tf_op jit(solution)/shard_map/ppermute | solution.py:422
  11.5 5.5 %collective-permute-start.1 = (s32[8,128]{1,0:T(8,128)S(1)}, s32[8,128]{1,0:T(8,128)S(1)}, u32[]{:S(2)}, u32[]{:S(2)}) collective-permute-start(s32[8,128]{1,0:T(8,128)S(1)} %copy-done.1), channel_id=1, source_target_pairs={{1,0},{2,1},{3,2},{5,4},{6,5},{7,6},{9,8},{10,9},{11,10},{13,12},{... | collective-permute-start | bytes 12296 | tf_op jit(solution)/shard_map/ppermute | solution.py:423
  19.2 12.8 %collective-permute-start.2 = (bf16[128,1536]{1,0:T(8,128)(2,1)S(1)}, bf16[128,1536]{1,0:T(8,128)(2,1)S(1)}, u32[]{:S(2)}, u32[]{:S(2)}) collective-permute-start(bf16[128,1536]{1,0:T(8,128)(2,1)S(1)} %slice.6), channel_id=1, source_target_pairs={{0,1},{1,2},{2,3},{4,5},{5,6},{6,7},{8,9},{9,10},{10,11},{12,13},{... | collective-permute-start | bytes 1179656 | tf_op jit(solution)/shard_map/ppermute | solution.py:436
  22.7 12.8 %collective-permute-start.3 = (bf16[128,1536]{1,0:T(8,128)(2,1)S(1)}, bf16[128,1536]{1,0:T(8,128)(2,1)S(1)}, u32[]{:S(2)}, u32[]{:S(2)}) collective-permute-start(bf16[128,1536]{1,0:T(8,128)(2,1)S(1)} %slice.6), channel_id=1, source_target_pairs={{1,0},{2,1},{3,2},{5,4},{6,5},{7,6},{9,8},{10,9},{11,10},{13,12},{... | collective-permute-start | bytes 1179656 | tf_op jit(solution)/shard_map/ppermute | solution.py:437
  24.0 16.2 %collective-permute-start.6 = (bf16[128,1024]{1,0:T(8,128)(2,1)S(1)}, bf16[128,1024]{1,0:T(8,128)(2,1)S(1)}, u32[]{:S(2)}, u32[]{:S(2)}) collective-permute-start(bf16[128,1024]{1,0:T(8,128)(2,1)S(1)} %slice.7), channel_id=1, source_target_pairs={{0,1},{1,2},{2,3},{4,5},{5,6},{6,7},{8,9},{9,10},{10,11},{12,13},{... | collective-permute-start | bytes 786440 | tf_op jit(solution)/shard_map/ppermute | solution.py:436
  28.6 16.2 %collective-permute-start.7 = (bf16[128,1024]{1,0:T(8,128)(2,1)S(1)}, bf16[128,1024]{1,0:T(8,128)(2,1)S(1)}, u32[]{:S(2)}, u32[]{:S(2)}) collective-permute-start(bf16[128,1024]{1,0:T(8,128)(2,1)S(1)} %slice.7), channel_id=1, source_target_pairs={{1,0},{2,1},{3,2},{5,4},{6,5},{7,6},{9,8},{10,9},{11,10},{13,12},{... | collective-permute-start | bytes 786440 | tf_op jit(solution)/shard_map/ppermute | solution.py:437
  35.5 17.1 %collective-permute-start.4 = (bf16[128,1536]{1,0:T(8,128)(2,1)S(1)}, bf16[128,1536]{1,0:T(8,128)(2,1)S(1)}, u32[]{:S(2)}, u32[]{:S(2)}) collective-permute-start(bf16[128,1536]{1,0:T(8,128)(2,1)S(1)} %collective-permute-done.2.head_lo.got_lo), channel_id=1, source_target_pairs={{0,1},{1,2},{2,3},{4,5},{5,6},{6,7},{8,9},{9,10},{10,11},{12,13},{... | collective-permute-start | bytes 1179656 | tf_op jit(solution)/shard_map/ppermute | solution.py:455
  39.0 13.6 %collective-permute-start.5 = (bf16[128,1536]{1,0:T(8,128)(2,1)S(1)}, bf16[128,1536]{1,0:T(8,128)(2,1)S(1)}, u32[]{:S(2)}, u32[]{:S(2)}) collective-permute-start(bf16[128,1536]{1,0:T(8,128)(2,1)S(1)} %collective-permute-done.3.head_hi.got_hi), channel_id=1, source_target_pairs={{1,0},{2,1},{3,2},{5,4},{6,5},{7,6},{9,8},{10,9},{11,10},{13,12},{... | collective-permute-start | bytes 1179656 | tf_op jit(solution)/shard_map/ppermute | solution.py:456
  40.3 14.6 %collective-permute-start.8 = (bf16[128,1024]{1,0:T(8,128)(2,1)S(1)}, bf16[128,1024]{1,0:T(8,128)(2,1)S(1)}, u32[]{:S(2)}, u32[]{:S(2)}) collective-permute-start(bf16[128,1024]{1,0:T(8,128)(2,1)S(1)} %collective-permute-done.6.got_lo), channel_id=1, source_target_pairs={{0,1},{1,2},{2,3},{4,5},{5,6},{6,7},{8,9},{9,10},{10,11},{12,13},{... | collective-permute-start | bytes 786440 | tf_op jit(solution)/shard_map/ppermute | solution.py:455
  44.9 10.1 %collective-permute-start.9 = (bf16[128,1024]{1,0:T(8,128)(2,1)S(1)}, bf16[128,1024]{1,0:T(8,128)(2,1)S(1)}, u32[]{:S(2)}, u32[]{:S(2)}) collective-permute-start(bf16[128,1024]{1,0:T(8,128)(2,1)S(1)} %collective-permute-done.7.got_hi), channel_id=1, source_target_pairs={{1,0},{2,1},{3,2},{5,4},{6,5},{7,6},{9,8},{10,9},{11,10},{13,12},{... | collective-permute-start | bytes 786440 | tf_op jit(solution)/shard_map/ppermute | solution.py:456

commit v5 on v4

--- a/solution.py
+++ b/solution.py
@@ -35,25 +35,8 @@
     return jnp.where(mask, 1.0, 0.0).astype(BF16)
 
 
-def pack_kernel(
-    groups, capacity, dest_hbm, lists_hbm, state_hbm, coef_hbm, send_hbm, lists_out,
-    dest_ref, lists_ref, state_ref, coef_ref, send, in_sems, out_sems,
-):
+def pack_kernel(groups, capacity, dest_ref, lists_ref, state_ref, coef_ref, send_ref, lists_out):
     species, slots, cells = state_ref.shape
-    copies = [
-        pltpu.make_async_copy(source, target, in_sems.at[i])
-        for i, (source, target) in enumerate(
-            (
-                (dest_hbm, dest_ref),
-                (coef_hbm, coef_ref),
-                (state_hbm, state_ref),
-                (lists_hbm, lists_ref),
-            )
-        )
-    ]
-    for copy in copies:
-        copy.start()
-    copies[0].wait()
     dest = dest_ref[...]
     onehot = iota((groups, slots), 0) == dest
     earlier = dot(
@@ -62,27 +45,13 @@
     running = jnp.sum(jnp.where(onehot, earlier, 0.0), axis=0, keepdims=True).astype(jnp.int32)
     position = jnp.where(dest >= 0, dest * capacity + running, -1)
     place = ones_where(iota((slots, slots), 0) == position)
-    copies[1].wait()
-    send[:, :cells] = dot(place, coef_ref[...]).astype(BF16)
-    copies[2].wait()
-    out_copies = []
-    middle = cells + species // 2 * cells
+    send_ref[:, :cells] = dot(place, coef_ref[...]).astype(BF16)
     for k in range(species):
         at = slice((k + 1) * cells, (k + 2) * cells)
-        send[:, at] = dot(place, state_ref[k]).astype(BF16)
-        if at.stop in (middle, send.shape[1]):
-            at = slice(0 if at.stop == middle else middle, at.stop)
-            i = len(out_copies)
-            out_copies.append(
-                pltpu.make_async_copy(send.at[:, at], send_hbm.at[:, at], out_sems.at[i])
-            )
-            out_copies[-1].start()
-    copies[3].wait()
+        send_ref[:, at] = dot(place, state_ref[k]).astype(BF16)
     none = jnp.zeros((1, slots), jnp.int32)
     rows = [lists_ref[f] + 1 for f in range(FACES)] + [none] * (8 - FACES)
     lists_out[...] = jnp.concatenate(rows, 0)
-    for copy in out_copies:
-        copy.wait()
 
 
 def sorting(coef_rows):
@@ -100,6 +69,13 @@
     return ones_where(iota((slots, slots), 0) == entry)
 
 
+def diagonal(a, b):
+    none = jnp.zeros_like(a)
+    return jnp.concatenate(
+        [jnp.concatenate([a, none], 1), jnp.concatenate([none, b], 1)], 0
+    )
+
+
 def twice(matrix):
     return jnp.concatenate([matrix, matrix], 0)
 
@@ -181,16 +157,20 @@
     coef_ref, weights_ref, flat_ref, base_ref, rhs_ref, coef_pad, field_ref,
 ):
     species, cells, slots = base_ref.shape
-    sort = sorting(got[:, :cells])
-    coef = dot_first(got[:, :cells], sort)
-    coef_ref[...] = coef
-    put(coef_pad, coef)
+    sort = diagonal(*[sorting(got[:, :cells])] * 2)
+    fields = []
+    for i in range(0, species + 1, 2):
+        j = min(i + 1, species)
+        pair = [got[:, k * cells : (k + 1) * cells] for k in (i, j)]
+        both = dot_first(jnp.concatenate(pair, 0), sort)
+        fields += [both[:, :slots], both[:, slots:]][: j - i + 1]
+    coef_ref[...] = fields[0]
+    put(coef_pad, fields[0])
     picks = [pick_ref[face] for face in range(4)]
     fill_edges(picks, [coef_pad], True)
     for k in range(species):
-        field = dot_first(got[:, (k + 1) * cells : (k + 2) * cells], sort)
-        put(field_ref.at[k], field)
-        flat_ref[k] = field.astype(BF16)
+        put(field_ref.at[k], fields[k + 1])
+        flat_ref[k] = fields[k + 1].astype(BF16)
     fill_edges(picks, [field_ref.at[k] for k in range(species)], True)
     factor = [lewis_ref[k] for k in range(species)]
     for y in range(PY):
@@ -213,7 +193,7 @@
 ):
     cells, slots = coef0.shape
     for d, head in enumerate((head_lo, head_hi)):
-        rows = head[...]
+        rows = head[:, :cells]
         sort = sorting(rows)
         both = jnp.concatenate([sort, dot(sort, pick0[4 + d]).astype(BF16)], 1)
         sort_ref[d] = both
@@ -248,17 +228,17 @@
 
 
 def inner_kernel(
-    first, lewis_ref, sort_ref, xy_pick, z_pick, z_halves, total0, beside_ref,
-    pick0, weights0, flat_ref, base_ref, rhs_ref, got_lo, got_hi,
+    cuts, lewis_ref, sort_ref, xy_pick, z_pick, z_halves, total0, beside_ref,
+    pick0, weights0, flat_ref, base_ref, rhs_ref, parts,
     num0, scale0, num_lo, num_hi, field_ref, z_ref, phi_ref,
 ):
     species, cells, slots = num0.shape
-    start = got_lo.shape[1] - species * cells
-    gots, numbers = (got_lo, got_hi), (num_lo, num_hi)
-    factor = [lewis_ref[first + k] for k in range(species)]
+    numbers = (num_lo, num_hi)
+    factor = [lewis_ref[k] for k in range(species)]
     for k in range(species):
-        at = slice(start + k * cells, start + (k + 1) * cells)
-        near = dot(flat_ref[first + k], z_pick[0])
+        gots, first = (parts[0], -1) if k < cuts[0] else (parts[1], cuts[0])
+        at = slice((k - first) * cells, (k - first + 1) * cells)
+        near = dot(flat_ref[k], z_pick[0])
         for d in range(2):
             both = dot_first(gots[d][:, at], sort_ref[d])
             put(field_ref.at[d, k], both[:, :slots])
@@ -271,7 +251,7 @@
             total = total0[at]
             for k in range(species):
                 near = [z_ref[i, k, natural(y, odd)] for i in range(2)]
-                number = base_ref[first + k, at] + factor[k] * weighted(weights, near)
+                number = base_ref[k, at] + factor[k] * weighted(weights, near)
                 inverse = 1.0 / (1.0 + factor[k] * total)
                 phi_ref[k, step(row(y) + odd)] = number * inverse
                 scale0[k, natural(y, odd)] = inverse
@@ -298,23 +278,37 @@
             for k in range(species):
                 near = beside_xy(phi_ref.at[k], y, odd)
                 inverse = scale0[k, natural(y, odd)]
-                number = rhs_ref[first + k, at] + factor[k] * weighted(weights, near)
+                number = rhs_ref[k, at] + factor[k] * weighted(weights, near)
                 num0[k, natural(y, odd)] = number * inverse
                 scale0[k, natural(y, odd)] = factor[k] * inverse
+
+
+def both_kernel(
+    cuts, lewis_ref, got_lo, got_hi, later_lo, later_hi,
+    coef0, pick0, weights0, xy_pick, z_pick, flat_ref, base_ref, rhs_ref,
+    z_natural, total_ref, coef_ref, num0, scale0, num_lo, num_hi,
+    sort_ref, z_halves, total0, beside_ref, padded, near_ref, field_ref, z_ref, phi_ref,
+):
+    prepare_kernel(
+        got_lo, got_hi, coef0, pick0, weights0, xy_pick, z_pick,
+        sort_ref, z_natural, z_halves, total0, beside_ref, total_ref, coef_ref, padded, near_ref,
+    )
+    inner_kernel(
+        cuts, lewis_ref, sort_ref, xy_pick, z_pick, z_halves, total0, beside_ref,
+        pick0, weights0, flat_ref, base_ref, rhs_ref, ((got_lo, got_hi), (later_lo, later_hi)),
+        num0, scale0, num_lo, num_hi, field_ref, z_ref, phi_ref,
+    )
 
 
 def far_kernel(pick0, z_pick, total_ref, coef_ref, head_lo2, head_hi2, far_ref, w_ref, t_ref, two_ref):
     cells = coef_ref.shape[1]
     slots = coef_ref.shape[2]
-    none = jnp.zeros((slots, slots), BF16)
-    rows = [head_lo2[...], head_hi2[...]]
+    rows = [head_lo2[:, :cells], head_hi2[:, :cells]]
     fars = []
     for i in range(2):
         fars.append(dot(sorting(rows[i]), z_pick[1, :, i * slots : (i + 1) * slots]).astype(BF16))
         two_ref[i] = twice(pick0[4 + i])
-    far = jnp.concatenate(
-        [jnp.concatenate([fars[0], none], 1), jnp.concatenate([none, fars[1]], 1)], 0
-    )
+    far = diagonal(*fars)
     far_ref[...] = far
     near = dot_first(jnp.concatenate(rows, 0), far)
     for i in range(2):
@@ -327,18 +321,19 @@
     first, lewis_ref, far_ref, w_ref, t_ref, two_ref, z_natural,
     num0, scale0, num_lo, num_hi, got_lo2, got_hi2, *rest,
 ):
-    species, cells, slots = num0.shape
+    if first:
+        early, out_hbm, out_ref, sems = rest
+    else:
+        (out_ref,) = rest
+    species, slots, cells = out_ref.shape
     start = got_lo2.shape[1] - species * cells
     numbers = (num_lo, num_hi)
     copies = []
     if first:
-        early, out_hbm, out_ref, sems = rest
         copies.append(
             pltpu.make_async_copy(early, out_hbm.at[:first], sems.at[species])
         )
         copies[-1].start()
-    else:
-        (out_ref,) = rest
     for k in range(species):
         at = slice(start + k * cells, start + (k + 1) * cells)
         factor = lewis_ref[first + k]
@@ -346,15 +341,28 @@
         flow = None
         for i in range(2):
             ghost = ghosts[:, i * slots : (i + 1) * slots]
-            phi = (numbers[i][k] + factor * (w_ref[i] * ghost)) * (1.0 / (1.0 + factor * t_ref[i]))
+            phi = (numbers[i][first + k] + factor * (w_ref[i] * ghost)) * (1.0 / (1.0 + factor * t_ref[i]))
             term = z_natural[i] * dot(split(phi), two_ref[i])
             flow = term if flow is None else flow + term
-        out_ref[k] = jnp.transpose(num0[k] + scale0[k] * flow, (1, 0))
+        out_ref[k] = jnp.transpose(num0[first + k] + scale0[first + k] * flow, (1, 0))
         if first:
             copies.append(pltpu.make_async_copy(out_ref.at[k], out_hbm.at[first + k], sems.at[k]))
             copies[-1].start()
     for copy in copies:
         copy.wait()
+
+
+def first_outer_kernel(
+    lewis_ref, pick0, z_pick, total_ref, coef_ref, z_natural, num0, scale0, num_lo, num_hi,
+    got_lo2, got_hi2, far_ref, w_ref, t_ref, two_ref, out_ref,
+):
+    far_kernel(
+        pick0, z_pick, total_ref, coef_ref, got_lo2, got_hi2, far_ref, w_ref, t_ref, two_ref
+    )
+    outer_kernel(
+        0, lewis_ref, far_ref, w_ref, t_ref, two_ref, z_natural,
+        num0, scale0, num_lo, num_hi, got_lo2, got_hi2, out_ref,
+    )
 
 
 def call(
@@ -385,12 +393,10 @@
     slots, species, cells = state.shape[2:]
     capacity = slots // groups
     cuts = (species - species // 2, species // 2)
-    firsts = (0, cuts[0])
     width = (1 + species) * cells
     middle = (1 + cuts[0]) * cells
     smem = pl.BlockSpec(memory_space=pltpu.SMEM)
     anywhere = pl.BlockSpec(memory_space=pl.ANY)
-    head = pl.BlockSpec((slots, cells), lambda i: (0, 0))
 
     def shape(*dims, dtype=F32):
         return jax.ShapeDtypeStruct(dims, dtype)
@@ -398,23 +404,13 @@
     send, lists = call(
         functools.partial(pack_kernel, groups, capacity),
         [shape(slots, width, dtype=BF16), shape(8, slots, dtype=jnp.int32)],
-        [
-            pltpu.VMEM((1, slots), jnp.int32),
-            pltpu.VMEM((FACES, 1, slots), jnp.int32),
-            pltpu.VMEM((species, slots, cells), BF16),
-            pltpu.VMEM((slots, cells), BF16),
-            pltpu.VMEM((slots, width), BF16),
-            pltpu.SemaphoreType.DMA((4,)),
-            pltpu.SemaphoreType.DMA((2,)),
-        ],
+        [],
         (
             new_group[0],
             jnp.transpose(face_lists[0], (1, 0, 2)),
             jnp.transpose(state[0, 0], (1, 0, 2)),
             coef[0, 0],
         ),
-        specs={i: anywhere for i in range(4)},
-        outs=[anywhere, pl.BlockSpec(memory_space=pltpu.VMEM)],
         limit=PACK_LIMIT,
         grid=(),
     )
@@ -432,9 +428,9 @@
         (lists, lists_lo, lists_hi),
     )
     rows, pick0, xy_pick, z_pick = lax.optimization_barrier((rows, pick0, xy_pick, z_pick))
-    got = [rows[:, :middle], rows[:, middle:]]
-    got_lo = [lax.ppermute(part, "member", up) for part in got]
-    got_hi = [lax.ppermute(part, "member", down) for part in got]
+    soon = rows[:, :middle]
+    got_lo = [lax.ppermute(soon, "member", up)]
+    got_hi = [lax.ppermute(soon, "member", down)]
     coef0, weights0, flat, base, rhs = call(
         own_kernel,
         [
@@ -449,71 +445,54 @@
         specs={0: smem},
         flops=500_000_000,
     )
-    got_lo[0], got_hi[0], coef0, weights0, flat, base, rhs = lax.optimization_barrier(
-        (got_lo[0], got_hi[0], coef0, weights0, flat, base, rhs)
-    )
+    later, coef0, weights0, flat, base, rhs = lax.optimization_barrier(
+        (rows[:, middle:], coef0, weights0, flat, base, rhs)
+    )
+    got_lo.append(lax.ppermute(later, "member", up))
+    got_hi.append(lax.ppermute(later, "member", down))
     got_lo2 = [lax.ppermute(part, "member", up) for part in got_lo]
     got_hi2 = [lax.ppermute(part, "member", down) for part in got_hi]
-    sort, z_natural, z_halves, total0, beside, total, coefs = call(
-        prepare_kernel,
+
+    z_natural, total, coefs, *numbers = call(
+        functools.partial(both_kernel, cuts),
+        [shape(2, cells, slots)] * 3 + [shape(species, cells, slots)] * 4,
         [
-            shape(2, slots, 2 * slots, dtype=BF16),
-            shape(2, cells, slots),
-            shape(2, cells, slots),
-            shape(cells, slots),
-            shape(2, 5, cells, slots),
-            shape(2, cells, slots),
-            shape(2, cells, slots),
+            pltpu.VMEM((2, slots, 2 * slots), BF16),
+            pltpu.VMEM((2, cells, slots), F32),
+            pltpu.VMEM((cells, slots), F32),
+            pltpu.VMEM((2, 5, cells, slots), F32),
+            pltpu.VMEM((2, PADDED, slots), F32),
+            pltpu.VMEM((2, cells, slots), F32),
+            pltpu.VMEM((2, species, PADDED, slots), F32),
+            pltpu.VMEM((4, species, cells, slots), F32),
+            pltpu.VMEM((species, PADDED, slots), F32),
         ],
-        [pltpu.VMEM((2, PADDED, slots), F32), pltpu.VMEM((2, cells, slots), F32)],
-        (got_lo[0], got_hi[0], coef0, pick0, weights0, xy_pick, z_pick),
-        specs={0: head, 1: head},
-        flops=100_000_000,
-    )
-    inner = [
-        call(
-            functools.partial(inner_kernel, first),
-            [shape(count, cells, slots)] * 4,
-            [
-                pltpu.VMEM((2, count, PADDED, slots), F32),
-                pltpu.VMEM((4, count, cells, slots), F32),
-                pltpu.VMEM((count, PADDED, slots), F32),
-            ],
-            (
-                lewis, sort, xy_pick, z_pick, z_halves, total0, beside,
-                pick0, weights0, flat, base, rhs, got_lo[c], got_hi[c],
-            ),
-            specs={0: smem},
-            flops=200_000_000 * count,
-        )
-        for c, (first, count) in enumerate(zip(firsts, cuts))
-    ]
-    far = call(
-        far_kernel,
+        (
+            lewis, got_lo[0], got_hi[0], got_lo[1], got_hi[1],
+            coef0, pick0, weights0, xy_pick, z_pick, flat, base, rhs,
+        ),
+        specs={0: smem},
+        flops=200_000_000 * species,
+    )
+    *far, early = call(
+        first_outer_kernel,
         [
             shape(2 * slots, 2 * slots, dtype=BF16),
             shape(2, cells, slots),
             shape(2, cells, slots),
             shape(2, 2 * slots, slots, dtype=BF16),
+            shape(cuts[0], slots, cells),
         ],
         [],
-        (pick0, z_pick, total, coefs, got_lo2[0], got_hi2[0]),
-        specs={4: head, 5: head},
-        flops=50_000_000,
-    )
-    (early,) = call(
-        functools.partial(outer_kernel, 0),
-        [shape(cuts[0], slots, cells)],
-        [],
-        (lewis, *far, z_natural, *inner[0], got_lo2[0], got_hi2[0]),
+        (lewis, pick0, z_pick, total, coefs, z_natural, *numbers, got_lo2[0], got_hi2[0]),
         specs={0: smem},
         flops=100_000_000 * cuts[0],
     )
     (out,) = call(
-        functools.partial(outer_kernel, firsts[1]),
+        functools.partial(outer_kernel, cuts[0]),
         [shape(species, slots, cells)],
         [pltpu.VMEM((cuts[1], slots, cells), F32), pltpu.SemaphoreType.DMA((cuts[1] + 1,))],
-        (lewis, *far, z_natural, *inner[1], got_lo2[1], got_hi2[1], early),
+        (lewis, *far, z_natural, *numbers, got_lo2[1], got_hi2[1], early),
         specs={0: smem},
         outs=[anywhere],
         flops=100_000_000 * cuts[1],

time: 57.7 us -> 55.3 us (0.958)
  waiting for transfers between devices: 9.73 us -> 7.6 us
  Pallas kernels: 16 us -> 14.6 us
  starting transfers between devices: 31.2 us -> 32.4 us
    ppermute x4, waiting for transfers between devices: 3.47 us -> 0.01 us  [the longest x1 0.01 us: per_device(): got_hi = [lax.ppermute(soon, 'member', down)]]
    pallas_call x9 -> x6, Pallas kernels: 16 us -> 14.6 us  [call(): pl.pallas_call(kernel, out_shape=out_shape, grid=grid, in_specs=[specs.ge...]
    ppermute x2, waiting for transfers between devices: 0.01 us -> 1.34 us  [per_device(): got_hi2 = [lax.ppermute(part, 'member', down) for part in got_hi]]
    ppermute x2, starting transfers between devices: 8.04 us -> 9.13 us  [per_device(): got_lo2 = [lax.ppermute(part, 'member', up) for part in got_lo]]
  transfers between devices with their start and end apart: 11 -> 11, of which waited for: 3 -> 4; matrix products, arithmetic and copies ran while one was open for 0% -> 0% of each run, Pallas kernels for 19% -> 18%
where the time goes in v5:
time: 55.3 us; the launch traced here: 54.9 us
  starting transfers between devices  32.4 us (59%)
  Pallas kernels  14.6 us (26%)
  waiting for transfers between devices  7.6 us (14%)
    pallas_call x6, Pallas kernels, call(): pl.pallas_call(kernel, out_shape=out_shape, grid=grid, in_specs=[specs.ge...  14.6 us
    ppermute x2, starting transfers between devices, per_device(): got_lo2 = [lax.ppermute(part, 'member', up) for part in got_lo]  9.13 us
    all_to_all x1, starting transfers between devices, per_device(): lax.all_to_all(send, 'group', split_axis=0, concat_axis=0, tiled=True)  5.3 us
    ppermute x1, starting transfers between devices, per_device(): got_lo.append(lax.ppermute(later, 'member', up))  4.55 us
    ppermute x1, waiting for transfers between devices, per_device(): lists_hi = lax.ppermute(lists, 'member', down)  4.19 us
    ppermute x1, starting transfers between devices, per_device(): got_lo = [lax.ppermute(soon, 'member', up)]  3.51 us
    ppermute x1, starting transfers between devices, per_device(): lists_lo = lax.ppermute(lists, 'member', up)  3.48 us
    ppermute x2, starting transfers between devices, per_device(): got_hi2 = [lax.ppermute(part, 'member', down) for part in got_hi]  2.58 us
  transfers between devices with their start and end apart: 11, of which 4 were waited for; matrix products, arithmetic and copies ran while one was open for 0% of the time, Pallas kernels for 18%

profile of v5, /device:TPU:0, one launch (start us, length us, event | category | flops | bytes accessed | tf_op | source)
XLA Modules:
  0.0 54.9 jit_solution(11087146194427574541)
XLA Ops:
  0.0 2.4 %shard_map.55 = (bf16[128,2560]{1,0:T(8,128)(2,1)}, s32[8,128]{1,0:T(8,128)}) custom-call(s32[1,128]{1,0:T(1,128)} %bitcast.18, s32[6,1,128]{2,1,0:T(1,128)} %bitcast.17, bf16[9,128,256]{2,1,0:T(8,128)(2,1)} %bitcast.15, bf16[128,256]{1,0:T(8,128)(2,1)} %bitcast.16), custom_call_target="tpu_custom_call" | custom-call | bytes 1318400 | tf_op jit(solution)/shard_map/pallas_call | solution.py:376
  2.4 0.0 copy-start
  2.4 0.0 copy-start.1
  2.4 5.3 %all-to-all-start = ((bf16[8,16,2560]{2,1,0:T(8,128)(2,1)}), bf16[8,16,2560]{2,1,0:T(8,128)(2,1)S(1)}, u32[]{:S(2)}, u32[]{:S(2)}) async-start(bf16[8,16,2560]{2,1,0:T(8,128)(2,1)} %bitcast.14), calls=%async_computation | async-start | bytes 1310720 | tf_op jit(solution)/shard_map/all_to_all | solution.py:417
  7.7 0.0 copy-done
  7.7 3.5 %collective-permute-start = (s32[8,128]{1,0:T(8,128)S(1)}, s32[8,128]{1,0:T(8,128)S(1)}, u32[]{:S(2)}, u32[]{:S(2)}) collective-permute-start(s32[8,128]{1,0:T(8,128)S(1)} %copy-done), channel_id=1, source_target_pairs={{0,1},{1,2},{2,3},{4,5},{5,6},{6,7},{8,9},{9,10},{10,11},{12,13},{... | collective-permute-start | bytes 12296 | tf_op jit(solution)/shard_map/ppermute | solution.py:418
  11.2 1.3 %collective-permute-start.1 = (s32[8,128]{1,0:T(8,128)S(1)}, s32[8,128]{1,0:T(8,128)S(1)}, u32[]{:S(2)}, u32[]{:S(2)}) collective-permute-start(s32[8,128]{1,0:T(8,128)S(1)} %copy-done), channel_id=1, source_target_pairs={{1,0},{2,1},{3,2},{5,4},{6,5},{7,6},{9,8},{10,9},{11,10},{13,12},{... | collective-permute-start | bytes 12296 | tf_op jit(solution)/shard_map/ppermute | solution.py:419
  12.5 0.0 collective-permute-done.lists_lo
  12.5 4.2 %collective-permute-done.1.lists_hi = s32[8,128]{1,0:T(8,128)S(1)} collective-permute-done((s32[8,128]{1,0:T(8,128)S(1)}, s32[8,128]{1,0:T(8,128)S(1)}, u32[]{:S(2)}, u32[]{:S(2)}) %collective-permute-start.1) | collective-permute-done | bytes 4128 | tf_op jit(solution)/shard_map/ppermute | solution.py:419
  16.7 0.1 shard_map.56
  16.8 2.0 %all-to-all-done = bf16[8,16,2560]{2,1,0:T(8,128)(2,1)S(1)} async-done(((bf16[8,16,2560]{2,1,0:T(8,128)(2,1)}), bf16[8,16,2560]{2,1,0:T(8,128)(2,1)S(1)}, u32[]{:S(2)}, u32[]{:S(2)}) %all-to-all-start) | async-done | bytes 655392 | tf_op jit(solution)/shard_map/all_to_all | solution.py:417
  18.9 3.5 %collective-permute-start.2 = (bf16[128,1536]{1,0:T(8,128)(2,1)S(1)}, bf16[128,1536]{1,0:T(8,128)(2,1)S(1)}, u32[]{:S(2)}, u32[]{:S(2)}) collective-permute-start(bf16[128,1536]{1,0:T(8,128)(2,1)S(1)} %slice.6), channel_id=1, source_target_pairs={{0,1},{1,2},{2,3},{4,5},{5,6},{6,7},{8,9},{9,10},{10,11},{12,13},{... | collective-permute-start | bytes 1179656 | tf_op jit(solution)/shard_map/ppermute | solution.py:432
  22.4 1.3 %collective-permute-start.3 = (bf16[128,1536]{1,0:T(8,128)(2,1)S(1)}, bf16[128,1536]{1,0:T(8,128)(2,1)S(1)}, u32[]{:S(2)}, u32[]{:S(2)}) collective-permute-start(bf16[128,1536]{1,0:T(8,128)(2,1)S(1)} %slice.6), channel_id=1, source_target_pairs={{1,0},{2,1},{3,2},{5,4},{6,5},{7,6},{9,8},{10,9},{11,10},{13,12},{... | collective-permute-start | bytes 1179656 | tf_op jit(solution)/shard_map/ppermute | solution.py:433
  23.7 0.0 copy-done.1
  23.7 2.0 %shard_map.57 = (f32[256,128]{1,0:T(8,128)S(1)}, f32[4,256,128]{2,1,0:T(8,128)S(1)}, bf16[9,256,128]{2,1,0:T(8,128)(2,1)S(1)}, f32[9,256,128]{2,1,0:T(8,128)S(1)}, f32[9,256,128]{2,1,0:T(8,128)S(1)}) custom-call(f32[9]{0:T(128)S(1)} %copy-done.1, bf16[128,2560]{1,0:T(8,128)(2,1)S(1)} %bitcast.13, bf16[6,128,128]{2,1,0:T(8,128)(2,1)S(1)} %get-tuple-element.42.pick_ref.pick0), custom_call_target="tpu_custom_call" | custom-call | flops 500000000 | bytes 4456484 | tf_op jit(solution)/shard_map/pallas_call | solution.py:376
  25.7 4.6 %collective-permute-start.4 = (bf16[128,1024]{1,0:T(8,128)(2,1)S(1)}, bf16[128,1024]{1,0:T(8,128)(2,1)S(1)}, u32[]{:S(2)}, u32[]{:S(2)}) collective-permute-start(bf16[128,1024]{1,0:T(8,128)(2,1)S(1)} %slice.7), channel_id=1, source_target_pairs={{0,1},{1,2},{2,3},{4,5},{5,6},{6,7},{8,9},{9,10},{10,11},{12,13},{... | collective-permute-start | bytes 786440 | tf_op jit(solution)/shard_map/ppermute | solution.py:451
  30.3 1.3 %collective-permute-start.5 = (bf16[128,1024]{1,0:T(8,128)(2,1)S(1)}, bf16[128,1024]{1,0:T(8,128)(2,1)S(1)}, u32[]{:S(2)}, u32[]{:S(2)}) collective-permute-start(bf16[128,1024]{1,0:T(8,128)(2,1)S(1)} %slice.7), channel_id=1, source_target_pairs={{1,0},{2,1},{3,2},{5,4},{6,5},{7,6},{9,8},{10,9},{11,10},{13,12},{... | collective-permute-start | bytes 786440 | tf_op jit(solution)/shard_map/ppermute | solution.py:452
  31.6 0.0 collective-permute-done.2.got_lo
  31.6 4.6 %collective-permute-start.6 = (bf16[128,1536]{1,0:T(8,128)(2,1)S(1)}, bf16[128,1536]{1,0:T(8,128)(2,1)S(1)}, u32[]{:S(2)}, u32[]{:S(2)}) collective-permute-start(bf16[128,1536]{1,0:T(8,128)(2,1)S(1)} %collective-permute-done.2.got_lo), channel_id=1, source_target_pairs={{0,1},{1,2},{2,3},{4,5},{5,6},{6,7},{8,9},{9,10},{10,11},{12,13},{... | collective-permute-start | bytes 1179656 | tf_op jit(solution)/shard_map/ppermute | solution.py:453
  36.2 0.0 collective-permute-done.3.got_hi
  36.2 1.3 %collective-permute-start.7 = (bf16[128,1536]{1,0:T(8,128)(2,1)S(1)}, bf16[128,1536]{1,0:T(8,128)(2,1)S(1)}, u32[]{:S(2)}, u32[]{:S(2)}) collective-permute-start(bf16[128,1536]{1,0:T(8,128)(2,1)S(1)} %collective-permute-done.3.got_hi), channel_id=1, source_target_pairs={{1,0},{2,1},{3,2},{5,4},{6,5},{7,6},{9,8},{10,9},{11,10},{13,12},{... | collective-permute-start | bytes 1179656 | tf_op jit(solution)/shard_map/ppermute | solution.py:454
  37.5 0.0 collective-permute-done.4.later_lo
  37.5 4.6 %collective-permute-start.8 = (bf16[128,1024]{1,0:T(8,128)(2,1)S(1)}, bf16[128,1024]{1,0:T(8,128)(2,1)S(1)}, u32[]{:S(2)}, u32[]{:S(2)}) collective-permute-start(bf16[128,1024]{1,0:T(8,128)(2,1)S(1)} %collective-permute-done.4.later_lo), channel_id=1, source_target_pairs={{0,1},{1,2},{2,3},{4,5},{5,6},{6,7},{8,9},{9,10},{10,11},{12,13},{... | collective-permute-start | bytes 786440 | tf_op jit(solution)/shard_map/ppermute | solution.py:453
  42.1 0.0 collective-permute-done.5.later_hi
  42.1 1.3 %collective-permute-start.9 = (bf16[128,1024]{1,0:T(8,128)(2,1)S(1)}, bf16[128,1024]{1,0:T(8,128)(2,1)S(1)}, u32[]{:S(2)}, u32[]{:S(2)}) collective-permute-start(bf16[128,1024]{1,0:T(8,128)(2,1)S(1)} %collective-permute-done.5.later_hi), channel_id=1, source_target_pairs={{1,0},{2,1},{3,2},{5,4},{6,5},{7,6},{9,8},{10,9},{11,10},{13,12},{... | collective-permute-start | bytes 786440 | tf_op jit(solution)/shard_map/ppermute | solution.py:454
  43.4 5.6 %shard_map.58 = (f32[2,256,128]{2,1,0:T(8,128)S(1)}, f32[2,256,128]{2,1,0:T(8,128)S(1)}, f32[2,256,128]{2,1,0:T(8,128)S(1)}, f32[9,256,128]{2,1,0:T(8,128)S(1)},...) custom-call(f32[9]{0:T(128)S(1)} %copy-done.1, ...), custom_call_target="tpu_custom_call" | custom-call | flops 1800000000 | bytes 11010084 | tf_op jit(solution)/shard_map/pallas_call | solution.py:376
  49.0 0.0 collective-permute-done.6.got_lo2
  49.0 0.8 %collective-permute-done.7.got_hi2 = bf16[128,1536]{1,0:T(8,128)(2,1)S(1)} collective-permute-done((bf16[128,1536]{1,0:T(8,128)(2,1)S(1)}, bf16[128,1536]{1,0:T(8,128)(2,1)S(1)}, u32[]{:S(2)}, u32[]{:S(2)}) %collective-permute-start.7) | collective-permute-done | bytes 393248 | tf_op jit(solution)/shard_map/ppermute | solution.py:454
  49.8 2.2 %shard_map.59 = (bf16[256,256]{1,0:T(8,128)(2,1)S(1)}, f32[2,256,128]{2,1,0:T(8,128)S(1)}, f32[2,256,128]{2,1,0:T(8,128)S(1)}, bf16[2,256,128]{2,1,0:T(8,128)(2,1)S(1)}, f32[5,128,256]{2,1,0:T(8,128)S(1)}) custom-call(f32[9]{0:T(128)S(1)} %copy-done.1, bf16[6,128,128]{2,1,0:T(8,128)(2,1)S(1)} %get-tuple-element.42.pick_ref.pick0, ...), custom_call_target="tpu_custom_call" | custom-call | flops 500000000 | bytes 8060964 | tf_op jit(solution)/shard_map/pallas_call | solution.py:376
  52.0 0.0 collective-permute-done.8.got_lo2
  52.0 0.6 %collective-permute-done.9.got_hi2 = bf16[128,1024]{1,0:T(8,128)(2,1)S(1)} collective-permute-done((bf16[128,1024]{1,0:T(8,128)(2,1)S(1)}, bf16[128,1024]{1,0:T(8,128)(2,1)S(1)}, u32[]{:S(2)}, u32[]{:S(2)}) %collective-permute-start.9) | collective-permute-done | bytes 262176 | tf_op jit(solution)/shard_map/ppermute | solution.py:454
  52.6 2.3 %shard_map.60 = f32[9,128,256]{2,1,0:T(8,128)} custom-call(f32[9]{0:T(128)S(1)} %copy-done.1, bf16[256,256]{1,0:T(8,128)(2,1)S(1)} %get-tuple-element.64.far_ref, f32[2,256,128]{2,1,0:T(8,128)S(1)} %get-tuple-element.65.w_ref, f32[2,256,128]{2,1,0:T(8,128)S(1)} %get-tuple-element.66.t_ref, bf16[2,256,128]{2,1,0:T(8,128)(2,1)S(1)} %get-tuple-element.67.two_ref, ...), custom_call_target="tpu_custom_call" | custom-call | flops 400000000 | bytes 8126500 | tf_op jit(solution)/shard_map/pallas_call | solution.py:376
  (2 shorter events, 0.0 us)
Async XLA Ops:
  2.4 5.3 %copy-start = (s32[8,128]{1,0:T(8,128)S(1)}, s32[8,128]{1,0:T(8,128)}, u32[]{:S(2)}) copy-start(s32[8,128]{1,0:T(8,128)} %get-tuple-element.38.lists0) | copy-start | bytes 12292
  2.4 21.3 %copy-start.1 = (f32[9]{0:T(128)S(1)}, f32[9]{0:T(128)}, u32[]{:S(2)}) copy-start(f32[9]{0:T(128)} %lewis_ref.7) | copy-start | bytes 112
  2.4 16.5 %all-to-all-start = ((bf16[8,16,2560]{2,1,0:T(8,128)(2,1)}), bf16[8,16,2560]{2,1,0:T(8,128)(2,1)S(1)}, u32[]{:S(2)}, u32[]{:S(2)}) async-start(bf16[8,16,2560]{2,1,0:T(8,128)(2,1)} %bitcast.14), calls=%async_computation | async-start | bytes 1310720 | tf_op jit(solution)/shard_map/all_to_all | solution.py:417
  7.7 4.8 %collective-permute-start = (s32[8,128]{1,0:T(8,128)S(1)}, s32[8,128]{1,0:T(8,128)S(1)}, u32[]{:S(2)}, u32[]{:S(2)}) collective-permute-start(s32[8,128]{1,0:T(8,128)S(1)} %copy-done), channel_id=1, source_target_pairs={{0,1},{1,2},{2,3},{4,5},{5,6},{6,7},{8,9},{9,10},{10,11},{12,13},{... | collective-permute-start | bytes 12296 | tf_op jit(solution)/shard_map/ppermute | solution.py:418
  11.2 5.5 %collective-permute-start.1 = (s32[8,128]{1,0:T(8,128)S(1)}, s32[8,128]{1,0:T(8,128)S(1)}, u32[]{:S(2)}, u32[]{:S(2)}) collective-permute-start(s32[8,128]{1,0:T(8,128)S(1)} %copy-done), channel_id=1, source_target_pairs={{1,0},{2,1},{3,2},{5,4},{6,5},{7,6},{9,8},{10,9},{11,10},{13,12},{... | collective-permute-start | bytes 12296 | tf_op jit(solution)/shard_map/ppermute | solution.py:419
  18.9 12.7 %collective-permute-start.2 = (bf16[128,1536]{1,0:T(8,128)(2,1)S(1)}, bf16[128,1536]{1,0:T(8,128)(2,1)S(1)}, u32[]{:S(2)}, u32[]{:S(2)}) collective-permute-start(bf16[128,1536]{1,0:T(8,128)(2,1)S(1)} %slice.6), channel_id=1, source_target_pairs={{0,1},{1,2},{2,3},{4,5},{5,6},{6,7},{8,9},{9,10},{10,11},{12,13},{... | collective-permute-start | bytes 1179656 | tf_op jit(solution)/shard_map/ppermute | solution.py:432
  22.4 13.8 %collective-permute-start.3 = (bf16[128,1536]{1,0:T(8,128)(2,1)S(1)}, bf16[128,1536]{1,0:T(8,128)(2,1)S(1)}, u32[]{:S(2)}, u32[]{:S(2)}) collective-permute-start(bf16[128,1536]{1,0:T(8,128)(2,1)S(1)} %slice.6), channel_id=1, source_target_pairs={{1,0},{2,1},{3,2},{5,4},{6,5},{7,6},{9,8},{10,9},{11,10},{13,12},{... | collective-permute-start | bytes 1179656 | tf_op jit(solution)/shard_map/ppermute | solution.py:433
  25.7 11.8 %collective-permute-start.4 = (bf16[128,1024]{1,0:T(8,128)(2,1)S(1)}, bf16[128,1024]{1,0:T(8,128)(2,1)S(1)}, u32[]{:S(2)}, u32[]{:S(2)}) collective-permute-start(bf16[128,1024]{1,0:T(8,128)(2,1)S(1)} %slice.7), channel_id=1, source_target_pairs={{0,1},{1,2},{2,3},{4,5},{5,6},{6,7},{8,9},{9,10},{10,11},{12,13},{... | collective-permute-start | bytes 786440 | tf_op jit(solution)/shard_map/ppermute | solution.py:451
  30.3 11.8 %collective-permute-start.5 = (bf16[128,1024]{1,0:T(8,128)(2,1)S(1)}, bf16[128,1024]{1,0:T(8,128)(2,1)S(1)}, u32[]{:S(2)}, u32[]{:S(2)}) collective-permute-start(bf16[128,1024]{1,0:T(8,128)(2,1)S(1)} %slice.7), channel_id=1, source_target_pairs={{1,0},{2,1},{3,2},{5,4},{6,5},{7,6},{9,8},{10,9},{11,10},{13,12},{... | collective-permute-start | bytes 786440 | tf_op jit(solution)/shard_map/ppermute | solution.py:452
  31.6 17.4 %collective-permute-start.6 = (bf16[128,1536]{1,0:T(8,128)(2,1)S(1)}, bf16[128,1536]{1,0:T(8,128)(2,1)S(1)}, u32[]{:S(2)}, u32[]{:S(2)}) collective-permute-start(bf16[128,1536]{1,0:T(8,128)(2,1)S(1)} %collective-permute-done.2.got_lo), channel_id=1, source_target_pairs={{0,1},{1,2},{2,3},{4,5},{5,6},{6,7},{8,9},{9,10},{10,11},{12,13},{... | collective-permute-start | bytes 1179656 | tf_op jit(solution)/shard_map/ppermute | solution.py:453
  36.2 13.6 %collective-permute-start.7 = (bf16[128,1536]{1,0:T(8,128)(2,1)S(1)}, bf16[128,1536]{1,0:T(8,128)(2,1)S(1)}, u32[]{:S(2)}, u32[]{:S(2)}) collective-permute-start(bf16[128,1536]{1,0:T(8,128)(2,1)S(1)} %collective-permute-done.3.got_hi), channel_id=1, source_target_pairs={{1,0},{2,1},{3,2},{5,4},{6,5},{7,6},{9,8},{10,9},{11,10},{13,12},{... | collective-permute-start | bytes 1179656 | tf_op jit(solution)/shard_map/ppermute | solution.py:454
  37.5 14.5 %collective-permute-start.8 = (bf16[128,1024]{1,0:T(8,128)(2,1)S(1)}, bf16[128,1024]{1,0:T(8,128)(2,1)S(1)}, u32[]{:S(2)}, u32[]{:S(2)}) collective-permute-start(bf16[128,1024]{1,0:T(8,128)(2,1)S(1)} %collective-permute-done.4.later_lo), channel_id=1, source_target_pairs={{0,1},{1,2},{2,3},{4,5},{5,6},{6,7},{8,9},{9,10},{10,11},{12,13},{... | collective-permute-start | bytes 786440 | tf_op jit(solution)/shard_map/ppermute | solution.py:453
  42.1 10.5 %collective-permute-start.9 = (bf16[128,1024]{1,0:T(8,128)(2,1)S(1)}, bf16[128,1024]{1,0:T(8,128)(2,1)S(1)}, u32[]{:S(2)}, u32[]{:S(2)}) collective-permute-start(bf16[128,1024]{1,0:T(8,128)(2,1)S(1)} %collective-permute-done.5.later_hi), channel_id=1, source_target_pairs={{1,0},{2,1},{3,2},{5,4},{6,5},{7,6},{9,8},{10,9},{11,10},{13,12},{... | collective-permute-start | bytes 786440 | tf_op jit(solution)/shard_map/ppermute | solution.py:454

commit v6 on v5

--- a/solution.py
+++ b/solution.py
@@ -51,6 +51,8 @@
         send_ref[:, at] = dot(place, state_ref[k]).astype(BF16)
     none = jnp.zeros((1, slots), jnp.int32)
     rows = [lists_ref[f] + 1 for f in range(FACES)] + [none] * (8 - FACES)
+    odd = lax.rem(lax.axis_index("group"), 2) == 1
+    rows[4], rows[5] = jnp.where(odd, rows[5], rows[4]), jnp.where(odd, rows[4], rows[5])
     lists_out[...] = jnp.concatenate(rows, 0)
 
 
@@ -317,57 +319,73 @@
         t_ref[i] = total_ref[i] + w
 
 
-def outer_kernel(
-    first, lewis_ref, far_ref, w_ref, t_ref, two_ref, z_natural,
-    num0, scale0, num_lo, num_hi, got_lo2, got_hi2, *rest,
-):
-    if first:
-        early, out_hbm, out_ref, sems = rest
-    else:
-        (out_ref,) = rest
-    species, slots, cells = out_ref.shape
-    start = got_lo2.shape[1] - species * cells
+def finish(ghosts, phi_of, two_ref, z_natural, num0, scale0):
+    slots = num0.shape[1]
+    flow = None
+    for i in range(2):
+        phi = phi_of(i, ghosts[:, i * slots : (i + 1) * slots])
+        term = z_natural[i] * dot(split(phi), two_ref[i])
+        flow = term if flow is None else flow + term
+    return jnp.transpose(num0 + scale0 * flow, (1, 0))
+
+
+def first_outer_kernel(
+    lewis_ref, pick0, z_pick, total_ref, coef_ref, z_natural, num0, scale0, num_lo, num_hi,
+    got_lo2, got_hi2, far_ref, two_ref, offset_ref, slope_ref, out_hbm,
+    w_ref, t_ref, out_ref, sems,
+):
+    far_kernel(
+        pick0, z_pick, total_ref, coef_ref, got_lo2, got_hi2, far_ref, w_ref, t_ref, two_ref
+    )
+    cut, slots, cells = out_ref.shape
     numbers = (num_lo, num_hi)
     copies = []
-    if first:
-        copies.append(
-            pltpu.make_async_copy(early, out_hbm.at[:first], sems.at[species])
-        )
+    for k in range(cut):
+        at = slice((1 + k) * cells, (2 + k) * cells)
+        factor = lewis_ref[k]
+        ghosts = dot_first(jnp.concatenate([got_lo2[:, at], got_hi2[:, at]], 0), far_ref[...])
+
+        def phi_of(i, ghost):
+            number = numbers[i][k] + factor * (w_ref[i] * ghost)
+            return number * (1.0 / (1.0 + factor * t_ref[i]))
+
+        out_ref[k] = finish(ghosts, phi_of, two_ref, z_natural, num0[k], scale0[k])
+        copies.append(pltpu.make_async_copy(out_ref.at[k], out_hbm.at[k], sems.at[k]))
         copies[-1].start()
-    for k in range(species):
-        at = slice(start + k * cells, start + (k + 1) * cells)
-        factor = lewis_ref[first + k]
-        ghosts = dot_first(jnp.concatenate([got_lo2[:, at], got_hi2[:, at]], 0), far_ref[...])
-        flow = None
+    for k in range(cut, num0.shape[0]):
+        factor = lewis_ref[k]
         for i in range(2):
-            ghost = ghosts[:, i * slots : (i + 1) * slots]
-            phi = (numbers[i][first + k] + factor * (w_ref[i] * ghost)) * (1.0 / (1.0 + factor * t_ref[i]))
-            term = z_natural[i] * dot(split(phi), two_ref[i])
-            flow = term if flow is None else flow + term
-        out_ref[k] = jnp.transpose(num0[first + k] + scale0[first + k] * flow, (1, 0))
-        if first:
-            copies.append(pltpu.make_async_copy(out_ref.at[k], out_hbm.at[first + k], sems.at[k]))
-            copies[-1].start()
+            inverse = 1.0 / (1.0 + factor * t_ref[i])
+            offset_ref[i, k - cut] = numbers[i][k] * inverse
+            slope_ref[i, k - cut] = factor * (w_ref[i] * inverse)
     for copy in copies:
         copy.wait()
 
 
-def first_outer_kernel(
-    lewis_ref, pick0, z_pick, total_ref, coef_ref, z_natural, num0, scale0, num_lo, num_hi,
-    got_lo2, got_hi2, far_ref, w_ref, t_ref, two_ref, out_ref,
-):
-    far_kernel(
-        pick0, z_pick, total_ref, coef_ref, got_lo2, got_hi2, far_ref, w_ref, t_ref, two_ref
-    )
-    outer_kernel(
-        0, lewis_ref, far_ref, w_ref, t_ref, two_ref, z_natural,
-        num0, scale0, num_lo, num_hi, got_lo2, got_hi2, out_ref,
-    )
+def second_outer_kernel(
+    far_ref, two_ref, offset_ref, slope_ref, z_natural, num0, scale0, later_lo2, later_hi2, early,
+    out_hbm, out_ref, sems,
+):
+    count, slots, cells = out_ref.shape
+    cut = num0.shape[0] - count
+    copies = []
+    for k in range(count):
+        at = slice(k * cells, (k + 1) * cells)
+        ghosts = dot_first(jnp.concatenate([later_lo2[:, at], later_hi2[:, at]], 0), far_ref[...])
+
+        def phi_of(i, ghost):
+            return offset_ref[i, k] + slope_ref[i, k] * ghost
+
+        out_ref[k] = finish(ghosts, phi_of, two_ref, z_natural, num0[cut + k], scale0[cut + k])
+        copies.append(pltpu.make_async_copy(out_ref.at[k], out_hbm.at[cut + k], sems.at[k]))
+        copies[-1].start()
+    for copy in copies:
+        copy.wait()
 
 
 def call(
     kernel, out_shape, scratch, operands, specs=None, outs=None, flops=0, limit=0,
-    grid=(1,),
+    grid=(1,), aliases=None,
 ):
     whole = pl.BlockSpec(memory_space=pltpu.VMEM)
     specs = specs or {}
@@ -380,6 +398,7 @@
         in_specs=[specs.get(i, whole) for i in range(len(operands))],
         out_specs=outs or [whole] * len(out_shape),
         scratch_shapes=scratch,
+        input_output_aliases=aliases or {},
         compiler_params=pltpu.CompilerParams(vmem_limit_bytes=limit or VMEM_LIMIT),
         cost_estimate=pl.CostEstimate(flops=flops, bytes_accessed=moved, transcendentals=0),
     )(*operands)
@@ -388,8 +407,11 @@
 def per_device(state, coef, new_group, face_lists, lewis):
     groups = lax.axis_size("group")
     members = lax.axis_size("member")
-    up = [(i, i + 1) for i in range(members - 1)]
-    down = [(i + 1, i) for i in range(members - 1)]
+    along = ("group", "member")
+    up = [[(g * members + i, g * members + i + 1) for i in range(members - 1)] for g in range(groups)]
+    down = [[(target, source) for source, target in pairs] for pairs in up]
+    one = [pair for g in range(groups) for pair in (down if g % 2 else up)[g]]
+    two = [pair for g in range(groups) for pair in (up if g % 2 else down)[g]]
     slots, species, cells = state.shape[2:]
     capacity = slots // groups
     cuts = (species - species // 2, species // 2)
@@ -415,8 +437,8 @@
         grid=(),
     )
     rows = lax.all_to_all(send, "group", split_axis=0, concat_axis=0, tiled=True)
-    lists_lo = lax.ppermute(lists, "member", up)
-    lists_hi = lax.ppermute(lists, "member", down)
+    lists_lo = lax.ppermute(lists, along, one)
+    lists_hi = lax.ppermute(lists, along, two)
     pick0, xy_pick, z_pick = call(
         pick_kernel,
         [
@@ -429,8 +451,8 @@
     )
     rows, pick0, xy_pick, z_pick = lax.optimization_barrier((rows, pick0, xy_pick, z_pick))
     soon = rows[:, :middle]
-    got_lo = [lax.ppermute(soon, "member", up)]
-    got_hi = [lax.ppermute(soon, "member", down)]
+    got_lo = [lax.ppermute(soon, along, one)]
+    got_hi = [lax.ppermute(soon, along, two)]
     coef0, weights0, flat, base, rhs = call(
         own_kernel,
         [
@@ -448,10 +470,10 @@
     later, coef0, weights0, flat, base, rhs = lax.optimization_barrier(
         (rows[:, middle:], coef0, weights0, flat, base, rhs)
     )
-    got_lo.append(lax.ppermute(later, "member", up))
-    got_hi.append(lax.ppermute(later, "member", down))
-    got_lo2 = [lax.ppermute(part, "member", up) for part in got_lo]
-    got_hi2 = [lax.ppermute(part, "member", down) for part in got_hi]
+    got_lo.append(lax.ppermute(later, along, one))
+    got_hi.append(lax.ppermute(later, along, two))
+    got_lo2 = [lax.ppermute(part, along, one) for part in got_lo]
+    got_hi2 = [lax.ppermute(part, along, two) for part in got_hi]
 
     z_natural, total, coefs, *numbers = call(
         functools.partial(both_kernel, cuts),
@@ -474,27 +496,37 @@
         specs={0: smem},
         flops=200_000_000 * species,
     )
-    *far, early = call(
+    far, twos, offset, slope, early = call(
         first_outer_kernel,
         [
             shape(2 * slots, 2 * slots, dtype=BF16),
-            shape(2, cells, slots),
-            shape(2, cells, slots),
             shape(2, 2 * slots, slots, dtype=BF16),
-            shape(cuts[0], slots, cells),
+            shape(2, cuts[1], cells, slots),
+            shape(2, cuts[1], cells, slots),
+            shape(species, slots, cells),
         ],
-        [],
+        [
+            pltpu.VMEM((2, cells, slots), F32),
+            pltpu.VMEM((2, cells, slots), F32),
+            pltpu.VMEM((cuts[0], slots, cells), F32),
+            pltpu.SemaphoreType.DMA((cuts[0],)),
+        ],
         (lewis, pick0, z_pick, total, coefs, z_natural, *numbers, got_lo2[0], got_hi2[0]),
         specs={0: smem},
+        outs=[pl.BlockSpec(memory_space=pltpu.VMEM)] * 4 + [anywhere],
         flops=100_000_000 * cuts[0],
     )
     (out,) = call(
-        functools.partial(outer_kernel, cuts[0]),
+        second_outer_kernel,
         [shape(species, slots, cells)],
-        [pltpu.VMEM((cuts[1], slots, cells), F32), pltpu.SemaphoreType.DMA((cuts[1] + 1,))],
-        (lewis, *far, z_natural, *numbers, got_lo2[1], got_hi2[1], early),
-        specs={0: smem},
+        [pltpu.VMEM((cuts[1], slots, cells), F32), pltpu.SemaphoreType.DMA((cuts[1],))],
+        (
+            far, twos, offset, slope, z_natural, numbers[0], numbers[1],
+            got_lo2[1], got_hi2[1], early,
+        ),
+        specs={9: anywhere},
         outs=[anywhere],
+        aliases={9: 0},
         flops=100_000_000 * cuts[1],
     )
     return jnp.transpose(out, (1, 0, 2))[None, None]

time: 55.3 us -> 54.2 us (0.980)
  waiting for transfers between devices: 7.6 us -> 6.5 us
    ppermute x10, waiting for transfers between devices: 5.56 us -> 4.46 us  [the longest x1 4.19 us: per_device(): lists_hi = lax.ppermute(lists, along, two)]
  transfers between devices with their start and end apart: 11 -> 11, of which waited for: 4 -> 3; matrix products, arithmetic and copies ran while one was open for 0% -> 0% of each run, Pallas kernels for 18% -> 19%
where the time goes in v6:
time: 54.2 us; the launch traced here: 53.8 us
  starting transfers between devices  32.4 us (60%)
  Pallas kernels  14.6 us (27%)
  waiting for transfers between devices  6.5 us (12%)
    pallas_call x6, Pallas kernels, call(): pl.pallas_call(kernel, out_shape=out_shape, grid=grid, in_specs=[specs.ge...  14.6 us
    ppermute x2, starting transfers between devices, per_device(): got_lo2 = [lax.ppermute(part, along, one) for part in got_lo]  9.13 us
    all_to_all x1, starting transfers between devices, per_device(): lax.all_to_all(send, 'group', split_axis=0, concat_axis=0, tiled=True)  5.3 us
    ppermute x1, starting transfers between devices, per_device(): got_lo.append(lax.ppermute(later, along, one))  4.55 us
    ppermute x1, waiting for transfers between devices, per_device(): lists_hi = lax.ppermute(lists, along, two)  4.19 us
    ppermute x1, starting transfers between devices, per_device(): got_lo = [lax.ppermute(soon, along, one)]  3.51 us
    ppermute x1, starting transfers between devices, per_device(): lists_lo = lax.ppermute(lists, along, one)  3.48 us
    ppermute x2, starting transfers between devices, per_device(): got_hi2 = [lax.ppermute(part, along, two) for part in got_hi]  2.57 us
  transfers between devices with their start and end apart: 11, of which 3 were waited for; matrix products, arithmetic and copies ran while one was open for 0% of the time, Pallas kernels for 19%

profile of v6, /device:TPU:0, one launch (start us, length us, event | category | flops | bytes accessed | tf_op | source)
XLA Modules:
  0.0 53.8 jit_solution(8021823036585750082)
XLA Ops:
  0.0 2.4 %shard_map.55 = (bf16[128,2560]{1,0:T(8,128)(2,1)}, s32[8,128]{1,0:T(8,128)}) custom-call(s32[1,128]{1,0:T(1,128)} %bitcast.18, s32[6,1,128]{2,1,0:T(1,128)} %bitcast.17, bf16[9,128,256]{2,1,0:T(8,128)(2,1)} %bitcast.15, bf16[128,256]{1,0:T(8,128)(2,1)} %bitcast.16), custom_call_target="tpu_custom_call" | custom-call | bytes 1318400 | tf_op jit(solution)/shard_map/pallas_call | solution.py:394
  2.4 0.0 copy-start
  2.4 0.0 copy-start.1
  2.4 5.3 %all-to-all-start = ((bf16[8,16,2560]{2,1,0:T(8,128)(2,1)}), bf16[8,16,2560]{2,1,0:T(8,128)(2,1)S(1)}, u32[]{:S(2)}, u32[]{:S(2)}) async-start(bf16[8,16,2560]{2,1,0:T(8,128)(2,1)} %bitcast.14), calls=%async_computation | async-start | bytes 1310720 | tf_op jit(solution)/shard_map/all_to_all | solution.py:439
  7.7 0.0 copy-done
  7.7 3.5 %collective-permute-start = (s32[8,128]{1,0:T(8,128)S(1)}, s32[8,128]{1,0:T(8,128)S(1)}, u32[]{:S(2)}, u32[]{:S(2)}) collective-permute-start(s32[8,128]{1,0:T(8,128)S(1)} %copy-done), channel_id=1, source_target_pairs={{0,1},{1,2},{2,3},{5,4},{6,5},{7,6},{8,9},{9,10},{10,11},{13,12},{... | collective-permute-start | bytes 12296 | tf_op jit(solution)/shard_map/ppermute | solution.py:440
  11.2 1.3 %collective-permute-start.1 = (s32[8,128]{1,0:T(8,128)S(1)}, s32[8,128]{1,0:T(8,128)S(1)}, u32[]{:S(2)}, u32[]{:S(2)}) collective-permute-start(s32[8,128]{1,0:T(8,128)S(1)} %copy-done), channel_id=1, source_target_pairs={{1,0},{2,1},{3,2},{4,5},{5,6},{6,7},{9,8},{10,9},{11,10},{12,13},{... | collective-permute-start | bytes 12296 | tf_op jit(solution)/shard_map/ppermute | solution.py:441
  12.5 0.0 collective-permute-done.lists_lo
  12.5 4.2 %collective-permute-done.1.lists_hi = s32[8,128]{1,0:T(8,128)S(1)} collective-permute-done((s32[8,128]{1,0:T(8,128)S(1)}, s32[8,128]{1,0:T(8,128)S(1)}, u32[]{:S(2)}, u32[]{:S(2)}) %collective-permute-start.1) | collective-permute-done | bytes 4128 | tf_op jit(solution)/shard_map/ppermute | solution.py:441
  16.7 0.1 shard_map.56
  16.8 2.0 %all-to-all-done = bf16[8,16,2560]{2,1,0:T(8,128)(2,1)S(1)} async-done(((bf16[8,16,2560]{2,1,0:T(8,128)(2,1)}), bf16[8,16,2560]{2,1,0:T(8,128)(2,1)S(1)}, u32[]{:S(2)}, u32[]{:S(2)}) %all-to-all-start) | async-done | bytes 655392 | tf_op jit(solution)/shard_map/all_to_all | solution.py:439
  18.9 3.5 %collective-permute-start.2 = (bf16[128,1536]{1,0:T(8,128)(2,1)S(1)}, bf16[128,1536]{1,0:T(8,128)(2,1)S(1)}, u32[]{:S(2)}, u32[]{:S(2)}) collective-permute-start(bf16[128,1536]{1,0:T(8,128)(2,1)S(1)} %slice.6), channel_id=1, source_target_pairs={{0,1},{1,2},{2,3},{5,4},{6,5},{7,6},{8,9},{9,10},{10,11},{13,12},{... | collective-permute-start | bytes 1179656 | tf_op jit(solution)/shard_map/ppermute | solution.py:454
  22.4 1.3 %collective-permute-start.3 = (bf16[128,1536]{1,0:T(8,128)(2,1)S(1)}, bf16[128,1536]{1,0:T(8,128)(2,1)S(1)}, u32[]{:S(2)}, u32[]{:S(2)}) collective-permute-start(bf16[128,1536]{1,0:T(8,128)(2,1)S(1)} %slice.6), channel_id=1, source_target_pairs={{1,0},{2,1},{3,2},{4,5},{5,6},{6,7},{9,8},{10,9},{11,10},{12,13},{... | collective-permute-start | bytes 1179656 | tf_op jit(solution)/shard_map/ppermute | solution.py:455
  23.7 0.0 copy-done.1
  23.7 1.8 %shard_map.57 = (f32[256,128]{1,0:T(8,128)S(1)}, f32[4,256,128]{2,1,0:T(8,128)S(1)}, bf16[9,256,128]{2,1,0:T(8,128)(2,1)S(1)}, f32[9,256,128]{2,1,0:T(8,128)S(1)}, f32[9,256,128]{2,1,0:T(8,128)S(1)}) custom-call(f32[9]{0:T(128)S(1)} %copy-done.1, bf16[128,2560]{1,0:T(8,128)(2,1)S(1)} %bitcast.13, bf16[6,128,128]{2,1,0:T(8,128)(2,1)S(1)} %get-tuple-element.42.pick_ref.pick0), custom_call_target="tpu_custom_call" | custom-call | flops 500000000 | bytes 4456484 | tf_op jit(solution)/shard_map/pallas_call | solution.py:394
  25.6 4.6 %collective-permute-start.4 = (bf16[128,1024]{1,0:T(8,128)(2,1)S(1)}, bf16[128,1024]{1,0:T(8,128)(2,1)S(1)}, u32[]{:S(2)}, u32[]{:S(2)}) collective-permute-start(bf16[128,1024]{1,0:T(8,128)(2,1)S(1)} %slice.7), channel_id=1, source_target_pairs={{0,1},{1,2},{2,3},{5,4},{6,5},{7,6},{8,9},{9,10},{10,11},{13,12},{... | collective-permute-start | bytes 786440 | tf_op jit(solution)/shard_map/ppermute | solution.py:473
  30.1 1.3 %collective-permute-start.5 = (bf16[128,1024]{1,0:T(8,128)(2,1)S(1)}, bf16[128,1024]{1,0:T(8,128)(2,1)S(1)}, u32[]{:S(2)}, u32[]{:S(2)}) collective-permute-start(bf16[128,1024]{1,0:T(8,128)(2,1)S(1)} %slice.7), channel_id=1, source_target_pairs={{1,0},{2,1},{3,2},{4,5},{5,6},{6,7},{9,8},{10,9},{11,10},{12,13},{... | collective-permute-start | bytes 786440 | tf_op jit(solution)/shard_map/ppermute | solution.py:474
  31.4 0.0 collective-permute-done.2.got_lo
  31.5 4.6 %collective-permute-start.6 = (bf16[128,1536]{1,0:T(8,128)(2,1)S(1)}, bf16[128,1536]{1,0:T(8,128)(2,1)S(1)}, u32[]{:S(2)}, u32[]{:S(2)}) collective-permute-start(bf16[128,1536]{1,0:T(8,128)(2,1)S(1)} %collective-permute-done.2.got_lo), channel_id=1, source_target_pairs={{0,1},{1,2},{2,3},{5,4},{6,5},{7,6},{8,9},{9,10},{10,11},{13,12},{... | collective-permute-start | bytes 1179656 | tf_op jit(solution)/shard_map/ppermute | solution.py:475
  36.0 0.2 collective-permute-done.3.got_hi
  36.3 1.3 %collective-permute-start.7 = (bf16[128,1536]{1,0:T(8,128)(2,1)S(1)}, bf16[128,1536]{1,0:T(8,128)(2,1)S(1)}, u32[]{:S(2)}, u32[]{:S(2)}) collective-permute-start(bf16[128,1536]{1,0:T(8,128)(2,1)S(1)} %collective-permute-done.3.got_hi), channel_id=1, source_target_pairs={{1,0},{2,1},{3,2},{4,5},{5,6},{6,7},{9,8},{10,9},{11,10},{12,13},{... | collective-permute-start | bytes 1179656 | tf_op jit(solution)/shard_map/ppermute | solution.py:476
  37.6 0.0 collective-permute-done.4.later_lo
  37.6 4.6 %collective-permute-start.8 = (bf16[128,1024]{1,0:T(8,128)(2,1)S(1)}, bf16[128,1024]{1,0:T(8,128)(2,1)S(1)}, u32[]{:S(2)}, u32[]{:S(2)}) collective-permute-start(bf16[128,1024]{1,0:T(8,128)(2,1)S(1)} %collective-permute-done.4.later_lo), channel_id=1, source_target_pairs={{0,1},{1,2},{2,3},{5,4},{6,5},{7,6},{8,9},{9,10},{10,11},{13,12},{... | collective-permute-start | bytes 786440 | tf_op jit(solution)/shard_map/ppermute | solution.py:475
  42.1 0.0 collective-permute-done.5.later_hi
  42.2 1.3 %collective-permute-start.9 = (bf16[128,1024]{1,0:T(8,128)(2,1)S(1)}, bf16[128,1024]{1,0:T(8,128)(2,1)S(1)}, u32[]{:S(2)}, u32[]{:S(2)}) collective-permute-start(bf16[128,1024]{1,0:T(8,128)(2,1)S(1)} %collective-permute-done.5.later_hi), channel_id=1, source_target_pairs={{1,0},{2,1},{3,2},{4,5},{5,6},{6,7},{9,8},{10,9},{11,10},{12,13},{... | collective-permute-start | bytes 786440 | tf_op jit(solution)/shard_map/ppermute | solution.py:476
  43.5 5.3 %shard_map.58 = (f32[2,256,128]{2,1,0:T(8,128)S(1)}, f32[2,256,128]{2,1,0:T(8,128)S(1)}, f32[2,256,128]{2,1,0:T(8,128)S(1)}, f32[9,256,128]{2,1,0:T(8,128)S(1)},...) custom-call(f32[9]{0:T(128)S(1)} %copy-done.1, ...), custom_call_target="tpu_custom_call" | custom-call | flops 1800000000 | bytes 11010084 | tf_op jit(solution)/shard_map/pallas_call | solution.py:394
  48.7 0.0 collective-permute-done.6.got_lo2
  48.7 0.0 collective-permute-done.7.got_hi2
  48.8 3.3 %shard_map.59 = (bf16[256,256]{1,0:T(8,128)(2,1)S(1)}, bf16[2,256,128]{2,1,0:T(8,128)(2,1)S(1)}, f32[2,4,256,128]{3,2,1,0:T(8,128)S(1)}, f32[2,4,256,128]{3,2,1,0:T(8,128)S(1)}, f32[9,128,256]{2,1,0:T(8,128)}) custom-call(f32[9]{0:T(128)S(1)} %copy-done.1, bf16[6,128,128]{2,1,0:T(8,128)(2,1)S(1)} %get-tuple-element.42.pick_ref.pick0, ...), custom_call_target="tpu_custom_call" | custom-call | flops 500000000 | bytes 10158116 | tf_op jit(solution)/shard_map/pallas_call | solution.py:394
  52.0 0.0 collective-permute-done.8.later_lo2
  52.0 0.0 collective-permute-done.9.later_hi2
  52.1 1.7 %shard_map.60 = f32[9,128,256]{2,1,0:T(8,128)} custom-call(bf16[256,256]{1,0:T(8,128)(2,1)S(1)} %get-tuple-element.64.far_ref, bf16[2,256,128]{2,1,0:T(8,128)(2,1)S(1)} %get-tuple-element.65.two_ref, f32[2,4,256,128]{3,2,1,0:T(8,128)S(1)} %get-tuple-element.66.offset_ref, ...), custom_call_target="tpu_custom_call", output_to_operand_aliasing={{}: (9, {})} | custom-call | flops 400000000 | bytes 7864320 | tf_op jit(solution)/shard_map/pallas_call | solution.py:394
  (2 shorter events, 0.0 us)
Async XLA Ops:
  2.4 5.3 %copy-start = (s32[8,128]{1,0:T(8,128)S(1)}, s32[8,128]{1,0:T(8,128)}, u32[]{:S(2)}) copy-start(s32[8,128]{1,0:T(8,128)} %get-tuple-element.38.lists0) | copy-start | bytes 12292
  2.4 21.3 %copy-start.1 = (f32[9]{0:T(128)S(1)}, f32[9]{0:T(128)}, u32[]{:S(2)}) copy-start(f32[9]{0:T(128)} %lewis_ref.5) | copy-start | bytes 112
  2.4 16.5 %all-to-all-start = ((bf16[8,16,2560]{2,1,0:T(8,128)(2,1)}), bf16[8,16,2560]{2,1,0:T(8,128)(2,1)S(1)}, u32[]{:S(2)}, u32[]{:S(2)}) async-start(bf16[8,16,2560]{2,1,0:T(8,128)(2,1)} %bitcast.14), calls=%async_computation | async-start | bytes 1310720 | tf_op jit(solution)/shard_map/all_to_all | solution.py:439
  7.7 4.8 %collective-permute-start = (s32[8,128]{1,0:T(8,128)S(1)}, s32[8,128]{1,0:T(8,128)S(1)}, u32[]{:S(2)}, u32[]{:S(2)}) collective-permute-start(s32[8,128]{1,0:T(8,128)S(1)} %copy-done), channel_id=1, source_target_pairs={{0,1},{1,2},{2,3},{5,4},{6,5},{7,6},{8,9},{9,10},{10,11},{13,12},{... | collective-permute-start | bytes 12296 | tf_op jit(solution)/shard_map/ppermute | solution.py:440
  11.2 5.5 %collective-permute-start.1 = (s32[8,128]{1,0:T(8,128)S(1)}, s32[8,128]{1,0:T(8,128)S(1)}, u32[]{:S(2)}, u32[]{:S(2)}) collective-permute-start(s32[8,128]{1,0:T(8,128)S(1)} %copy-done), channel_id=1, source_target_pairs={{1,0},{2,1},{3,2},{4,5},{5,6},{6,7},{9,8},{10,9},{11,10},{12,13},{... | collective-permute-start | bytes 12296 | tf_op jit(solution)/shard_map/ppermute | solution.py:441
  18.9 12.6 %collective-permute-start.2 = (bf16[128,1536]{1,0:T(8,128)(2,1)S(1)}, bf16[128,1536]{1,0:T(8,128)(2,1)S(1)}, u32[]{:S(2)}, u32[]{:S(2)}) collective-permute-start(bf16[128,1536]{1,0:T(8,128)(2,1)S(1)} %slice.6), channel_id=1, source_target_pairs={{0,1},{1,2},{2,3},{5,4},{6,5},{7,6},{8,9},{9,10},{10,11},{13,12},{... | collective-permute-start | bytes 1179656 | tf_op jit(solution)/shard_map/ppermute | solution.py:454
  22.4 13.9 %collective-permute-start.3 = (bf16[128,1536]{1,0:T(8,128)(2,1)S(1)}, bf16[128,1536]{1,0:T(8,128)(2,1)S(1)}, u32[]{:S(2)}, u32[]{:S(2)}) collective-permute-start(bf16[128,1536]{1,0:T(8,128)(2,1)S(1)} %slice.6), channel_id=1, source_target_pairs={{1,0},{2,1},{3,2},{4,5},{5,6},{6,7},{9,8},{10,9},{11,10},{12,13},{... | collective-permute-start | bytes 1179656 | tf_op jit(solution)/shard_map/ppermute | solution.py:455
  25.6 12.0 %collective-permute-start.4 = (bf16[128,1024]{1,0:T(8,128)(2,1)S(1)}, bf16[128,1024]{1,0:T(8,128)(2,1)S(1)}, u32[]{:S(2)}, u32[]{:S(2)}) collective-permute-start(bf16[128,1024]{1,0:T(8,128)(2,1)S(1)} %slice.7), channel_id=1, source_target_pairs={{0,1},{1,2},{2,3},{5,4},{6,5},{7,6},{8,9},{9,10},{10,11},{13,12},{... | collective-permute-start | bytes 786440 | tf_op jit(solution)/shard_map/ppermute | solution.py:473
  30.1 12.0 %collective-permute-start.5 = (bf16[128,1024]{1,0:T(8,128)(2,1)S(1)}, bf16[128,1024]{1,0:T(8,128)(2,1)S(1)}, u32[]{:S(2)}, u32[]{:S(2)}) collective-permute-start(bf16[128,1024]{1,0:T(8,128)(2,1)S(1)} %slice.7), channel_id=1, source_target_pairs={{1,0},{2,1},{3,2},{4,5},{5,6},{6,7},{9,8},{10,9},{11,10},{12,13},{... | collective-permute-start | bytes 786440 | tf_op jit(solution)/shard_map/ppermute | solution.py:474
  31.5 17.3 %collective-permute-start.6 = (bf16[128,1536]{1,0:T(8,128)(2,1)S(1)}, bf16[128,1536]{1,0:T(8,128)(2,1)S(1)}, u32[]{:S(2)}, u32[]{:S(2)}) collective-permute-start(bf16[128,1536]{1,0:T(8,128)(2,1)S(1)} %collective-permute-done.2.got_lo), channel_id=1, source_target_pairs={{0,1},{1,2},{2,3},{5,4},{6,5},{7,6},{8,9},{9,10},{10,11},{13,12},{... | collective-permute-start | bytes 1179656 | tf_op jit(solution)/shard_map/ppermute | solution.py:475
  36.3 12.5 %collective-permute-start.7 = (bf16[128,1536]{1,0:T(8,128)(2,1)S(1)}, bf16[128,1536]{1,0:T(8,128)(2,1)S(1)}, u32[]{:S(2)}, u32[]{:S(2)}) collective-permute-start(bf16[128,1536]{1,0:T(8,128)(2,1)S(1)} %collective-permute-done.3.got_hi), channel_id=1, source_target_pairs={{1,0},{2,1},{3,2},{4,5},{5,6},{6,7},{9,8},{10,9},{11,10},{12,13},{... | collective-permute-start | bytes 1179656 | tf_op jit(solution)/shard_map/ppermute | solution.py:476
  37.6 14.5 %collective-permute-start.8 = (bf16[128,1024]{1,0:T(8,128)(2,1)S(1)}, bf16[128,1024]{1,0:T(8,128)(2,1)S(1)}, u32[]{:S(2)}, u32[]{:S(2)}) collective-permute-start(bf16[128,1024]{1,0:T(8,128)(2,1)S(1)} %collective-permute-done.4.later_lo), channel_id=1, source_target_pairs={{0,1},{1,2},{2,3},{5,4},{6,5},{7,6},{8,9},{9,10},{10,11},{13,12},{... | collective-permute-start | bytes 786440 | tf_op jit(solution)/shard_map/ppermute | solution.py:475
  42.2 9.9 %collective-permute-start.9 = (bf16[128,1024]{1,0:T(8,128)(2,1)S(1)}, bf16[128,1024]{1,0:T(8,128)(2,1)S(1)}, u32[]{:S(2)}, u32[]{:S(2)}) collective-permute-start(bf16[128,1024]{1,0:T(8,128)(2,1)S(1)} %collective-permute-done.5.later_hi), channel_id=1, source_target_pairs={{1,0},{2,1},{3,2},{4,5},{5,6},{6,7},{9,8},{10,9},{11,10},{12,13},{... | collective-permute-start | bytes 786440 | tf_op jit(solution)/shard_map/ppermute | solution.py:476

commit v7 on v6

--- a/solution.py
+++ b/solution.py
@@ -160,12 +160,13 @@
 ):
     species, cells, slots = base_ref.shape
     sort = diagonal(*[sorting(got[:, :cells])] * 2)
-    fields = []
-    for i in range(0, species + 1, 2):
-        j = min(i + 1, species)
-        pair = [got[:, k * cells : (k + 1) * cells] for k in (i, j)]
-        both = dot_first(jnp.concatenate(pair, 0), sort)
-        fields += [both[:, :slots], both[:, slots:]][: j - i + 1]
+    count = (species + 2) // 2
+    pair = [got[:, : count * cells], got[:, (species + 1 - count) * cells :]]
+    both = dot_first(jnp.concatenate(pair, 0), sort)
+    fields = [both[k * cells : (k + 1) * cells, :slots] for k in range(count)]
+    fields += [
+        both[k * cells : (k + 1) * cells, slots:] for k in range(2 * count - species - 1, count)
+    ]
     coef_ref[...] = fields[0]
     put(coef_pad, fields[0])
     picks = [pick_ref[face] for face in range(4)]
@@ -237,15 +238,23 @@
     species, cells, slots = num0.shape
     numbers = (num_lo, num_hi)
     factor = [lewis_ref[k] for k in range(species)]
+    for d in range(2):
+        k = 0
+        for gots, skip, count in zip(parts, (cells, 0), cuts):
+            both = dot_first(gots[d][:, skip:], sort_ref[d])
+            for i in range(count):
+                rows = slice(i * cells, (i + 1) * cells)
+                put(field_ref.at[d, k], both[rows, :slots])
+                z_ref[d, k] = both[rows, slots:]
+                k += 1
+    near = dot(flat_ref[...].reshape(species * cells, slots), z_pick[0])
     for k in range(species):
-        gots, first = (parts[0], -1) if k < cuts[0] else (parts[1], cuts[0])
-        at = slice((k - first) * cells, (k - first + 1) * cells)
-        near = dot(flat_ref[k], z_pick[0])
         for d in range(2):
-            both = dot_first(gots[d][:, at], sort_ref[d])
-            put(field_ref.at[d, k], both[:, :slots])
-            z_ref[d, k] = both[:, slots:]
-            z_ref[2 + d, k] = near[:, d * slots : (d + 1) * slots]
+            z_ref[2 + d, k] = near[k * cells : (k + 1) * cells, d * slots : (d + 1) * slots]
+    for d in range(2):
+        fill_edges(
+            [xy_pick[d, f] for f in range(4)], [field_ref.at[d, k] for k in range(species)], True
+        )
     for y in range(PY):
         for odd in range(2):
             at = halves(y, odd)
@@ -258,10 +267,6 @@
                 phi_ref[k, step(row(y) + odd)] = number * inverse
                 scale0[k, natural(y, odd)] = inverse
     fill_edges([pick0[f] for f in range(4)], [phi_ref.at[k] for k in range(species)], False)
-    for d in range(2):
-        fill_edges(
-            [xy_pick[d, f] for f in range(4)], [field_ref.at[d, k] for k in range(species)], True
-        )
     for d in range(2):
         for y in range(PY):
             for odd in range(2):
@@ -319,47 +324,47 @@
         t_ref[i] = total_ref[i] + w
 
 
-def finish(ghosts, phi_of, two_ref, z_natural, num0, scale0):
-    slots = num0.shape[1]
-    flow = None
+def finish(ghosts, phi_of, two_ref, z_natural, num0, scale0, first, out_ref):
+    count, slots, cells = out_ref.shape
+    terms = []
     for i in range(2):
-        phi = phi_of(i, ghosts[:, i * slots : (i + 1) * slots])
-        term = z_natural[i] * dot(split(phi), two_ref[i])
-        flow = term if flow is None else flow + term
-    return jnp.transpose(num0 + scale0 * flow, (1, 0))
+        phis = [
+            split(phi_of(k, i, ghosts[k * cells : (k + 1) * cells, i * slots : (i + 1) * slots]))
+            for k in range(count)
+        ]
+        terms.append(dot(jnp.concatenate(phis, 0), two_ref[i]))
+    for k in range(count):
+        rows = slice(k * cells, (k + 1) * cells)
+        flow = z_natural[0] * terms[0][rows] + z_natural[1] * terms[1][rows]
+        out_ref[k] = jnp.transpose(num0[first + k] + scale0[first + k] * flow, (1, 0))
+        yield k
 
 
 def first_outer_kernel(
     lewis_ref, pick0, z_pick, total_ref, coef_ref, z_natural, num0, scale0, num_lo, num_hi,
-    got_lo2, got_hi2, far_ref, two_ref, offset_ref, slope_ref, out_hbm,
-    w_ref, t_ref, out_ref, sems,
+    got_lo2, got_hi2, far_ref, two_ref, offset_ref, slope_ref, out_ref, w_ref, t_ref,
 ):
     far_kernel(
         pick0, z_pick, total_ref, coef_ref, got_lo2, got_hi2, far_ref, w_ref, t_ref, two_ref
     )
     cut, slots, cells = out_ref.shape
     numbers = (num_lo, num_hi)
-    copies = []
-    for k in range(cut):
-        at = slice((1 + k) * cells, (2 + k) * cells)
-        factor = lewis_ref[k]
-        ghosts = dot_first(jnp.concatenate([got_lo2[:, at], got_hi2[:, at]], 0), far_ref[...])
-
-        def phi_of(i, ghost):
-            number = numbers[i][k] + factor * (w_ref[i] * ghost)
-            return number * (1.0 / (1.0 + factor * t_ref[i]))
-
-        out_ref[k] = finish(ghosts, phi_of, two_ref, z_natural, num0[k], scale0[k])
-        copies.append(pltpu.make_async_copy(out_ref.at[k], out_hbm.at[k], sems.at[k]))
-        copies[-1].start()
+    factor = [lewis_ref[k] for k in range(num0.shape[0])]
+    ghosts = dot_first(
+        jnp.concatenate([got_lo2[:, cells:], got_hi2[:, cells:]], 0), far_ref[...]
+    )
+
+    def phi_of(k, i, ghost):
+        number = numbers[i][k] + factor[k] * (w_ref[i] * ghost)
+        return number * (1.0 / (1.0 + factor[k] * t_ref[i]))
+
+    for k in finish(ghosts, phi_of, two_ref, z_natural, num0, scale0, 0, out_ref):
+        pass
     for k in range(cut, num0.shape[0]):
-        factor = lewis_ref[k]
         for i in range(2):
-            inverse = 1.0 / (1.0 + factor * t_ref[i])
+            inverse = 1.0 / (1.0 + factor[k] * t_ref[i])
             offset_ref[i, k - cut] = numbers[i][k] * inverse
-            slope_ref[i, k - cut] = factor * (w_ref[i] * inverse)
-    for copy in copies:
-        copy.wait()
+            slope_ref[i, k - cut] = factor[k] * (w_ref[i] * inverse)
 
 
 def second_outer_kernel(
@@ -368,15 +373,14 @@
 ):
     count, slots, cells = out_ref.shape
     cut = num0.shape[0] - count
-    copies = []
-    for k in range(count):
-        at = slice(k * cells, (k + 1) * cells)
-        ghosts = dot_first(jnp.concatenate([later_lo2[:, at], later_hi2[:, at]], 0), far_ref[...])
-
-        def phi_of(i, ghost):
-            return offset_ref[i, k] + slope_ref[i, k] * ghost
-
-        out_ref[k] = finish(ghosts, phi_of, two_ref, z_natural, num0[cut + k], scale0[cut + k])
+    copies = [pltpu.make_async_copy(early, out_hbm.at[:cut], sems.at[count])]
+    copies[-1].start()
+    ghosts = dot_first(jnp.concatenate([later_lo2[...], later_hi2[...]], 0), far_ref[...])
+
+    def phi_of(k, i, ghost):
+        return offset_ref[i, k] + slope_ref[i, k] * ghost
+
+    for k in finish(ghosts, phi_of, two_ref, z_natural, num0, scale0, cut, out_ref):
         copies.append(pltpu.make_async_copy(out_ref.at[k], out_hbm.at[cut + k], sems.at[k]))
         copies[-1].start()
     for copy in copies:
@@ -385,7 +389,7 @@
 
 def call(
     kernel, out_shape, scratch, operands, specs=None, outs=None, flops=0, limit=0,
-    grid=(1,), aliases=None,
+    grid=(1,),
 ):
     whole = pl.BlockSpec(memory_space=pltpu.VMEM)
     specs = specs or {}
@@ -398,7 +402,6 @@
         in_specs=[specs.get(i, whole) for i in range(len(operands))],
         out_specs=outs or [whole] * len(out_shape),
         scratch_shapes=scratch,
-        input_output_aliases=aliases or {},
         compiler_params=pltpu.CompilerParams(vmem_limit_bytes=limit or VMEM_LIMIT),
         cost_estimate=pl.CostEstimate(flops=flops, bytes_accessed=moved, transcendentals=0),
     )(*operands)
@@ -503,30 +506,22 @@
             shape(2, 2 * slots, slots, dtype=BF16),
             shape(2, cuts[1], cells, slots),
             shape(2, cuts[1], cells, slots),
-            shape(species, slots, cells),
+            shape(cuts[0], slots, cells),
         ],
-        [
-            pltpu.VMEM((2, cells, slots), F32),
-            pltpu.VMEM((2, cells, slots), F32),
-            pltpu.VMEM((cuts[0], slots, cells), F32),
-            pltpu.SemaphoreType.DMA((cuts[0],)),
-        ],
+        [pltpu.VMEM((2, cells, slots), F32), pltpu.VMEM((2, cells, slots), F32)],
         (lewis, pick0, z_pick, total, coefs, z_natural, *numbers, got_lo2[0], got_hi2[0]),
         specs={0: smem},
-        outs=[pl.BlockSpec(memory_space=pltpu.VMEM)] * 4 + [anywhere],
         flops=100_000_000 * cuts[0],
     )
     (out,) = call(
         second_outer_kernel,
         [shape(species, slots, cells)],
-        [pltpu.VMEM((cuts[1], slots, cells), F32), pltpu.SemaphoreType.DMA((cuts[1],))],
+        [pltpu.VMEM((cuts[1], slots, cells), F32), pltpu.SemaphoreType.DMA((cuts[1] + 1,))],
         (
             far, twos, offset, slope, z_natural, numbers[0], numbers[1],
             got_lo2[1], got_hi2[1], early,
         ),
-        specs={9: anywhere},
         outs=[anywhere],
-        aliases={9: 0},
         flops=100_000_000 * cuts[1],
     )
     return jnp.transpose(out, (1, 0, 2))[None, None]

time: 54.2 us -> 53.4 us (0.985)
  Pallas kernels: 14.6 us -> 12.9 us
  waiting for transfers between devices: 6.5 us -> 7.44 us
    pallas_call x6, Pallas kernels: 14.6 us -> 12.9 us  [call(): pl.pallas_call(kernel, out_shape=out_shape, grid=grid, in_specs=[specs.ge...]
    ppermute x2, waiting for transfers between devices: 0.01 us -> 0.98 us  [per_device(): got_hi2 = [lax.ppermute(part, along, two) for part in got_hi]]
  transfers between devices with their start and end apart: 11 -> 11, of which waited for: 3 -> 5; matrix products, arithmetic and copies ran while one was open for 0% -> 0% of each run, Pallas kernels for 19% -> 17%
where the time goes in v7:
time: 53.4 us; the launch traced here: 53 us
  starting transfers between devices  32.4 us (61%)
  Pallas kernels  12.9 us (24%)
  waiting for transfers between devices  7.44 us (14%)
    pallas_call x6, Pallas kernels, call(): pl.pallas_call(kernel, out_shape=out_shape, grid=grid, in_specs=[specs.ge...  12.9 us
    ppermute x2, starting transfers between devices, per_device(): got_lo2 = [lax.ppermute(part, along, one) for part in got_lo]  9.13 us
    all_to_all x1, starting transfers between devices, per_device(): lax.all_to_all(send, 'group', split_axis=0, concat_axis=0, tiled=True)  5.3 us
    ppermute x1, starting transfers between devices, per_device(): got_lo.append(lax.ppermute(later, along, one))  4.57 us
    ppermute x1, waiting for transfers between devices, per_device(): lists_hi = lax.ppermute(lists, along, two)  4.19 us
    ppermute x1, starting transfers between devices, per_device(): got_lo = [lax.ppermute(soon, along, one)]  3.51 us
    ppermute x1, starting transfers between devices, per_device(): lists_lo = lax.ppermute(lists, along, one)  3.48 us
    ppermute x2, starting transfers between devices, per_device(): got_hi2 = [lax.ppermute(part, along, two) for part in got_hi]  2.57 us
  transfers between devices with their start and end apart: 11, of which 5 were waited for; matrix products, arithmetic and copies ran while one was open for 0% of the time, Pallas kernels for 17%

profile of v7, /device:TPU:0, one launch (start us, length us, event | category | flops | bytes accessed | tf_op | source)
XLA Modules:
  0.0 53.0 jit_solution(1250043888221131714)
XLA Ops:
  0.0 2.4 %shard_map.55 = (bf16[128,2560]{1,0:T(8,128)(2,1)}, s32[8,128]{1,0:T(8,128)}) custom-call(s32[1,128]{1,0:T(1,128)} %bitcast.18, s32[6,1,128]{2,1,0:T(1,128)} %bitcast.17, bf16[9,128,256]{2,1,0:T(8,128)(2,1)} %bitcast.15, bf16[128,256]{1,0:T(8,128)(2,1)} %bitcast.16), custom_call_target="tpu_custom_call" | custom-call | bytes 1318400 | tf_op jit(solution)/shard_map/pallas_call | solution.py:398
  2.4 0.0 copy-start
  2.4 0.0 copy-start.1
  2.4 5.3 %all-to-all-start = ((bf16[8,16,2560]{2,1,0:T(8,128)(2,1)}), bf16[8,16,2560]{2,1,0:T(8,128)(2,1)S(1)}, u32[]{:S(2)}, u32[]{:S(2)}) async-start(bf16[8,16,2560]{2,1,0:T(8,128)(2,1)} %bitcast.14), calls=%async_computation | async-start | bytes 1310720 | tf_op jit(solution)/shard_map/all_to_all | solution.py:442
  7.7 0.0 copy-done
  7.7 3.5 %collective-permute-start = (s32[8,128]{1,0:T(8,128)S(1)}, s32[8,128]{1,0:T(8,128)S(1)}, u32[]{:S(2)}, u32[]{:S(2)}) collective-permute-start(s32[8,128]{1,0:T(8,128)S(1)} %copy-done), channel_id=1, source_target_pairs={{0,1},{1,2},{2,3},{5,4},{6,5},{7,6},{8,9},{9,10},{10,11},{13,12},{... | collective-permute-start | bytes 12296 | tf_op jit(solution)/shard_map/ppermute | solution.py:443
  11.2 1.3 %collective-permute-start.1 = (s32[8,128]{1,0:T(8,128)S(1)}, s32[8,128]{1,0:T(8,128)S(1)}, u32[]{:S(2)}, u32[]{:S(2)}) collective-permute-start(s32[8,128]{1,0:T(8,128)S(1)} %copy-done), channel_id=1, source_target_pairs={{1,0},{2,1},{3,2},{4,5},{5,6},{6,7},{9,8},{10,9},{11,10},{12,13},{... | collective-permute-start | bytes 12296 | tf_op jit(solution)/shard_map/ppermute | solution.py:444
  12.5 0.0 collective-permute-done.lists_lo
  12.5 4.2 %collective-permute-done.1.lists_hi = s32[8,128]{1,0:T(8,128)S(1)} collective-permute-done((s32[8,128]{1,0:T(8,128)S(1)}, s32[8,128]{1,0:T(8,128)S(1)}, u32[]{:S(2)}, u32[]{:S(2)}) %collective-permute-start.1) | collective-permute-done | bytes 4128 | tf_op jit(solution)/shard_map/ppermute | solution.py:444
  16.7 0.1 shard_map.56
  16.8 2.0 %all-to-all-done = bf16[8,16,2560]{2,1,0:T(8,128)(2,1)S(1)} async-done(((bf16[8,16,2560]{2,1,0:T(8,128)(2,1)}), bf16[8,16,2560]{2,1,0:T(8,128)(2,1)S(1)}, u32[]{:S(2)}, u32[]{:S(2)}) %all-to-all-start) | async-done | bytes 655392 | tf_op jit(solution)/shard_map/all_to_all | solution.py:442
  18.9 3.5 %collective-permute-start.2 = (bf16[128,1536]{1,0:T(8,128)(2,1)S(1)}, bf16[128,1536]{1,0:T(8,128)(2,1)S(1)}, u32[]{:S(2)}, u32[]{:S(2)}) collective-permute-start(bf16[128,1536]{1,0:T(8,128)(2,1)S(1)} %slice.6), channel_id=1, source_target_pairs={{0,1},{1,2},{2,3},{5,4},{6,5},{7,6},{8,9},{9,10},{10,11},{13,12},{... | collective-permute-start | bytes 1179656 | tf_op jit(solution)/shard_map/ppermute | solution.py:457
  22.4 1.3 %collective-permute-start.3 = (bf16[128,1536]{1,0:T(8,128)(2,1)S(1)}, bf16[128,1536]{1,0:T(8,128)(2,1)S(1)}, u32[]{:S(2)}, u32[]{:S(2)}) collective-permute-start(bf16[128,1536]{1,0:T(8,128)(2,1)S(1)} %slice.6), channel_id=1, source_target_pairs={{1,0},{2,1},{3,2},{4,5},{5,6},{6,7},{9,8},{10,9},{11,10},{12,13},{... | collective-permute-start | bytes 1179656 | tf_op jit(solution)/shard_map/ppermute | solution.py:458
  23.7 0.0 copy-done.1
  23.7 1.9 %shard_map.57 = (f32[256,128]{1,0:T(8,128)S(1)}, f32[4,256,128]{2,1,0:T(8,128)S(1)}, bf16[9,256,128]{2,1,0:T(8,128)(2,1)S(1)}, f32[9,256,128]{2,1,0:T(8,128)S(1)}, f32[9,256,128]{2,1,0:T(8,128)S(1)}) custom-call(f32[9]{0:T(128)S(1)} %copy-done.1, bf16[128,2560]{1,0:T(8,128)(2,1)S(1)} %bitcast.13, bf16[6,128,128]{2,1,0:T(8,128)(2,1)S(1)} %get-tuple-element.42.pick_ref.pick0), custom_call_target="tpu_custom_call" | custom-call | flops 500000000 | bytes 4456484 | tf_op jit(solution)/shard_map/pallas_call | solution.py:398
  25.6 4.6 %collective-permute-start.4 = (bf16[128,1024]{1,0:T(8,128)(2,1)S(1)}, bf16[128,1024]{1,0:T(8,128)(2,1)S(1)}, u32[]{:S(2)}, u32[]{:S(2)}) collective-permute-start(bf16[128,1024]{1,0:T(8,128)(2,1)S(1)} %slice.7), channel_id=1, source_target_pairs={{0,1},{1,2},{2,3},{5,4},{6,5},{7,6},{8,9},{9,10},{10,11},{13,12},{... | collective-permute-start | bytes 786440 | tf_op jit(solution)/shard_map/ppermute | solution.py:476
  30.2 1.3 %collective-permute-start.5 = (bf16[128,1024]{1,0:T(8,128)(2,1)S(1)}, bf16[128,1024]{1,0:T(8,128)(2,1)S(1)}, u32[]{:S(2)}, u32[]{:S(2)}) collective-permute-start(bf16[128,1024]{1,0:T(8,128)(2,1)S(1)} %slice.7), channel_id=1, source_target_pairs={{1,0},{2,1},{3,2},{4,5},{5,6},{6,7},{9,8},{10,9},{11,10},{12,13},{... | collective-permute-start | bytes 786440 | tf_op jit(solution)/shard_map/ppermute | solution.py:477
  31.5 0.0 collective-permute-done.2.got_lo
  31.5 4.6 %collective-permute-start.6 = (bf16[128,1536]{1,0:T(8,128)(2,1)S(1)}, bf16[128,1536]{1,0:T(8,128)(2,1)S(1)}, u32[]{:S(2)}, u32[]{:S(2)}) collective-permute-start(bf16[128,1536]{1,0:T(8,128)(2,1)S(1)} %collective-permute-done.2.got_lo), channel_id=1, source_target_pairs={{0,1},{1,2},{2,3},{5,4},{6,5},{7,6},{8,9},{9,10},{10,11},{13,12},{... | collective-permute-start | bytes 1179656 | tf_op jit(solution)/shard_map/ppermute | solution.py:478
  36.1 0.2 collective-permute-done.3.got_hi
  36.3 1.3 %collective-permute-start.7 = (bf16[128,1536]{1,0:T(8,128)(2,1)S(1)}, bf16[128,1536]{1,0:T(8,128)(2,1)S(1)}, u32[]{:S(2)}, u32[]{:S(2)}) collective-permute-start(bf16[128,1536]{1,0:T(8,128)(2,1)S(1)} %collective-permute-done.3.got_hi), channel_id=1, source_target_pairs={{1,0},{2,1},{3,2},{4,5},{5,6},{6,7},{9,8},{10,9},{11,10},{12,13},{... | collective-permute-start | bytes 1179656 | tf_op jit(solution)/shard_map/ppermute | solution.py:479
  37.6 0.0 collective-permute-done.4.later_lo
  37.6 4.6 %collective-permute-start.8 = (bf16[128,1024]{1,0:T(8,128)(2,1)S(1)}, bf16[128,1024]{1,0:T(8,128)(2,1)S(1)}, u32[]{:S(2)}, u32[]{:S(2)}) collective-permute-start(bf16[128,1024]{1,0:T(8,128)(2,1)S(1)} %collective-permute-done.4.later_lo), channel_id=1, source_target_pairs={{0,1},{1,2},{2,3},{5,4},{6,5},{7,6},{8,9},{9,10},{10,11},{13,12},{... | collective-permute-start | bytes 786440 | tf_op jit(solution)/shard_map/ppermute | solution.py:478
  42.1 0.0 collective-permute-done.5.later_hi
  42.2 1.3 %collective-permute-start.9 = (bf16[128,1024]{1,0:T(8,128)(2,1)S(1)}, bf16[128,1024]{1,0:T(8,128)(2,1)S(1)}, u32[]{:S(2)}, u32[]{:S(2)}) collective-permute-start(bf16[128,1024]{1,0:T(8,128)(2,1)S(1)} %collective-permute-done.5.later_hi), channel_id=1, source_target_pairs={{1,0},{2,1},{3,2},{4,5},{5,6},{6,7},{9,8},{10,9},{11,10},{12,13},{... | collective-permute-start | bytes 786440 | tf_op jit(solution)/shard_map/ppermute | solution.py:479
  43.5 4.9 %shard_map.58 = (f32[2,256,128]{2,1,0:T(8,128)S(1)}, f32[2,256,128]{2,1,0:T(8,128)S(1)}, f32[2,256,128]{2,1,0:T(8,128)S(1)}, f32[9,256,128]{2,1,0:T(8,128)S(1)},...) custom-call(f32[9]{0:T(128)S(1)} %copy-done.1, ...), custom_call_target="tpu_custom_call" | custom-call | flops 1800000000 | bytes 11010084 | tf_op jit(solution)/shard_map/pallas_call | solution.py:398
  48.4 0.0 collective-permute-done.6.got_lo2
  48.4 0.3 collective-permute-done.7.got_hi2
  48.7 2.1 %shard_map.59 = (bf16[256,256]{1,0:T(8,128)(2,1)S(1)}, bf16[2,256,128]{2,1,0:T(8,128)(2,1)S(1)}, f32[2,4,256,128]{3,2,1,0:T(8,128)S(1)}, f32[2,4,256,128]{3,2,1,0:T(8,128)S(1)}, f32[5,128,256]{2,1,0:T(8,128)S(1)}) custom-call(f32[9]{0:T(128)S(1)} %copy-done.1, bf16[6,128,128]{2,1,0:T(8,128)(2,1)S(1)} %get-tuple-element.42.pick_ref.pick0, ...), custom_call_target="tpu_custom_call" | custom-call | flops 500000000 | bytes 9633828 | tf_op jit(solution)/shard_map/pallas_call | solution.py:398
  50.9 0.0 collective-permute-done.8.later_lo2
  50.9 0.7 %collective-permute-done.9.later_hi2 = bf16[128,1024]{1,0:T(8,128)(2,1)S(1)} collective-permute-done((bf16[128,1024]{1,0:T(8,128)(2,1)S(1)}, bf16[128,1024]{1,0:T(8,128)(2,1)S(1)}, u32[]{:S(2)}, u32[]{:S(2)}) %collective-permute-start.9) | collective-permute-done | bytes 262176 | tf_op jit(solution)/shard_map/ppermute | solution.py:479
  51.5 1.4 %shard_map.60 = f32[9,128,256]{2,1,0:T(8,128)} custom-call(bf16[256,256]{1,0:T(8,128)(2,1)S(1)} %get-tuple-element.64.far_ref, bf16[2,256,128]{2,1,0:T(8,128)(2,1)S(1)} %get-tuple-element.65.two_ref, f32[2,4,256,128]{3,2,1,0:T(8,128)S(1)} %get-tuple-element.66.offset_ref, f32[2,4,256,128]{3,2,1,0:T(8,128)S(1)} %get-tuple-element.67.slope_ref, ...), custom_call_target="tpu_custom_call" | custom-call | flops 400000000 | bytes 7340032 | tf_op jit(solution)/shard_map/pallas_call | solution.py:398
  (2 shorter events, 0.0 us)
Async XLA Ops:
  2.4 5.3 %copy-start = (s32[8,128]{1,0:T(8,128)S(1)}, s32[8,128]{1,0:T(8,128)}, u32[]{:S(2)}) copy-start(s32[8,128]{1,0:T(8,128)} %get-tuple-element.38.lists0) | copy-start | bytes 12292
  2.4 21.3 %copy-start.1 = (f32[9]{0:T(128)S(1)}, f32[9]{0:T(128)}, u32[]{:S(2)}) copy-start(f32[9]{0:T(128)} %lewis_ref.5) | copy-start | bytes 112
  2.4 16.5 %all-to-all-start = ((bf16[8,16,2560]{2,1,0:T(8,128)(2,1)}), bf16[8,16,2560]{2,1,0:T(8,128)(2,1)S(1)}, u32[]{:S(2)}, u32[]{:S(2)}) async-start(bf16[8,16,2560]{2,1,0:T(8,128)(2,1)} %bitcast.14), calls=%async_computation | async-start | bytes 1310720 | tf_op jit(solution)/shard_map/all_to_all | solution.py:442
  7.7 4.8 %collective-permute-start = (s32[8,128]{1,0:T(8,128)S(1)}, s32[8,128]{1,0:T(8,128)S(1)}, u32[]{:S(2)}, u32[]{:S(2)}) collective-permute-start(s32[8,128]{1,0:T(8,128)S(1)} %copy-done), channel_id=1, source_target_pairs={{0,1},{1,2},{2,3},{5,4},{6,5},{7,6},{8,9},{9,10},{10,11},{13,12},{... | collective-permute-start | bytes 12296 | tf_op jit(solution)/shard_map/ppermute | solution.py:443
  11.2 5.5 %collective-permute-start.1 = (s32[8,128]{1,0:T(8,128)S(1)}, s32[8,128]{1,0:T(8,128)S(1)}, u32[]{:S(2)}, u32[]{:S(2)}) collective-permute-start(s32[8,128]{1,0:T(8,128)S(1)} %copy-done), channel_id=1, source_target_pairs={{1,0},{2,1},{3,2},{4,5},{5,6},{6,7},{9,8},{10,9},{11,10},{12,13},{... | collective-permute-start | bytes 12296 | tf_op jit(solution)/shard_map/ppermute | solution.py:444
  18.9 12.6 %collective-permute-start.2 = (bf16[128,1536]{1,0:T(8,128)(2,1)S(1)}, bf16[128,1536]{1,0:T(8,128)(2,1)S(1)}, u32[]{:S(2)}, u32[]{:S(2)}) collective-permute-start(bf16[128,1536]{1,0:T(8,128)(2,1)S(1)} %slice.6), channel_id=1, source_target_pairs={{0,1},{1,2},{2,3},{5,4},{6,5},{7,6},{8,9},{9,10},{10,11},{13,12},{... | collective-permute-start | bytes 1179656 | tf_op jit(solution)/shard_map/ppermute | solution.py:457
  22.4 13.9 %collective-permute-start.3 = (bf16[128,1536]{1,0:T(8,128)(2,1)S(1)}, bf16[128,1536]{1,0:T(8,128)(2,1)S(1)}, u32[]{:S(2)}, u32[]{:S(2)}) collective-permute-start(bf16[128,1536]{1,0:T(8,128)(2,1)S(1)} %slice.6), channel_id=1, source_target_pairs={{1,0},{2,1},{3,2},{4,5},{5,6},{6,7},{9,8},{10,9},{11,10},{12,13},{... | collective-permute-start | bytes 1179656 | tf_op jit(solution)/shard_map/ppermute | solution.py:458
  25.6 12.0 %collective-permute-start.4 = (bf16[128,1024]{1,0:T(8,128)(2,1)S(1)}, bf16[128,1024]{1,0:T(8,128)(2,1)S(1)}, u32[]{:S(2)}, u32[]{:S(2)}) collective-permute-start(bf16[128,1024]{1,0:T(8,128)(2,1)S(1)} %slice.7), channel_id=1, source_target_pairs={{0,1},{1,2},{2,3},{5,4},{6,5},{7,6},{8,9},{9,10},{10,11},{13,12},{... | collective-permute-start | bytes 786440 | tf_op jit(solution)/shard_map/ppermute | solution.py:476
  30.2 12.0 %collective-permute-start.5 = (bf16[128,1024]{1,0:T(8,128)(2,1)S(1)}, bf16[128,1024]{1,0:T(8,128)(2,1)S(1)}, u32[]{:S(2)}, u32[]{:S(2)}) collective-permute-start(bf16[128,1024]{1,0:T(8,128)(2,1)S(1)} %slice.7), channel_id=1, source_target_pairs={{1,0},{2,1},{3,2},{4,5},{5,6},{6,7},{9,8},{10,9},{11,10},{12,13},{... | collective-permute-start | bytes 786440 | tf_op jit(solution)/shard_map/ppermute | solution.py:477
  31.5 16.9 %collective-permute-start.6 = (bf16[128,1536]{1,0:T(8,128)(2,1)S(1)}, bf16[128,1536]{1,0:T(8,128)(2,1)S(1)}, u32[]{:S(2)}, u32[]{:S(2)}) collective-permute-start(bf16[128,1536]{1,0:T(8,128)(2,1)S(1)} %collective-permute-done.2.got_lo), channel_id=1, source_target_pairs={{0,1},{1,2},{2,3},{5,4},{6,5},{7,6},{8,9},{9,10},{10,11},{13,12},{... | collective-permute-start | bytes 1179656 | tf_op jit(solution)/shard_map/ppermute | solution.py:478
  36.3 12.5 %collective-permute-start.7 = (bf16[128,1536]{1,0:T(8,128)(2,1)S(1)}, bf16[128,1536]{1,0:T(8,128)(2,1)S(1)}, u32[]{:S(2)}, u32[]{:S(2)}) collective-permute-start(bf16[128,1536]{1,0:T(8,128)(2,1)S(1)} %collective-permute-done.3.got_hi), channel_id=1, source_target_pairs={{1,0},{2,1},{3,2},{4,5},{5,6},{6,7},{9,8},{10,9},{11,10},{12,13},{... | collective-permute-start | bytes 1179656 | tf_op jit(solution)/shard_map/ppermute | solution.py:479
  37.6 13.3 %collective-permute-start.8 = (bf16[128,1024]{1,0:T(8,128)(2,1)S(1)}, bf16[128,1024]{1,0:T(8,128)(2,1)S(1)}, u32[]{:S(2)}, u32[]{:S(2)}) collective-permute-start(bf16[128,1024]{1,0:T(8,128)(2,1)S(1)} %collective-permute-done.4.later_lo), channel_id=1, source_target_pairs={{0,1},{1,2},{2,3},{5,4},{6,5},{7,6},{8,9},{9,10},{10,11},{13,12},{... | collective-permute-start | bytes 786440 | tf_op jit(solution)/shard_map/ppermute | solution.py:478
  42.2 9.4 %collective-permute-start.9 = (bf16[128,1024]{1,0:T(8,128)(2,1)S(1)}, bf16[128,1024]{1,0:T(8,128)(2,1)S(1)}, u32[]{:S(2)}, u32[]{:S(2)}) collective-permute-start(bf16[128,1024]{1,0:T(8,128)(2,1)S(1)} %collective-permute-done.5.later_hi), channel_id=1, source_target_pairs={{1,0},{2,1},{3,2},{4,5},{5,6},{6,7},{9,8},{10,9},{11,10},{12,13},{... | collective-permute-start | bytes 786440 | tf_op jit(solution)/shard_map/ppermute | solution.py:479

commit v8 on v7

--- a/solution.py
+++ b/solution.py
@@ -411,10 +411,18 @@
     groups = lax.axis_size("group")
     members = lax.axis_size("member")
     along = ("group", "member")
-    up = [[(g * members + i, g * members + i + 1) for i in range(members - 1)] for g in range(groups)]
-    down = [[(target, source) for source, target in pairs] for pairs in up]
-    one = [pair for g in range(groups) for pair in (down if g % 2 else up)[g]]
-    two = [pair for g in range(groups) for pair in (up if g % 2 else down)[g]]
+
+    def pairs(upward, ends):
+        steps = []
+        for g in range(groups):
+            for i in range(0 if ends else 1, members if ends else members - 1):
+                target = i + 1 if upward == (g % 2 == 0) else i - 1
+                if 0 <= target < members:
+                    steps.append((g * members + i, g * members + target))
+        return steps
+
+    one, two = pairs(True, True), pairs(False, True)
+    one_on, two_on = pairs(True, False), pairs(False, False)
     slots, species, cells = state.shape[2:]
     capacity = slots // groups
     cuts = (species - species // 2, species // 2)
@@ -475,8 +483,8 @@
     )
     got_lo.append(lax.ppermute(later, along, one))
     got_hi.append(lax.ppermute(later, along, two))
-    got_lo2 = [lax.ppermute(part, along, one) for part in got_lo]
-    got_hi2 = [lax.ppermute(part, along, two) for part in got_hi]
+    got_lo2 = [lax.ppermute(part, along, one_on) for part in got_lo]
+    got_hi2 = [lax.ppermute(part, along, two_on) for part in got_hi]
 
     z_natural, total, coefs, *numbers = call(
         functools.partial(both_kernel, cuts),

time: 53.4 us -> 53.4 us (level)
  waiting for transfers between devices: 7.44 us -> 15.2 us
  starting transfers between devices: 32.4 us -> 24.7 us
    ppermute x4, starting transfers between devices: 11.7 us -> 3.92 us  [the longest x2 2.56 us: per_device(): got_hi2 = [lax.ppermute(part, along, two_on) for part in got_hi]]
    ppermute x1, waiting for transfers between devices: 0.2 us -> 4.08 us  [per_device(): got_hi = [lax.ppermute(soon, along, two)]]
    ppermute x1, waiting for transfers between devices: 0.01 us -> 3.63 us  [per_device(): got_hi.append(lax.ppermute(later, along, two))]
  transfers between devices with their start and end apart: 11 -> 11, of which waited for: 5 -> 6; matrix products, arithmetic and copies ran while one was open for 0% -> 0% of each run, Pallas kernels for 17% -> 17%
where the time goes in v8:
time: 53.4 us; the launch traced here: 53 us
  starting transfers between devices  24.7 us (46%)
  waiting for transfers between devices  15.2 us (28%)
  Pallas kernels  12.9 us (24%)
    pallas_call x6, Pallas kernels, call(): pl.pallas_call(kernel, out_shape=out_shape, grid=grid, in_specs=[specs.ge...  12.9 us
    all_to_all x1, starting transfers between devices, per_device(): lax.all_to_all(send, 'group', split_axis=0, concat_axis=0, tiled=True)  5.3 us
    ppermute x1, starting transfers between devices, per_device(): got_lo.append(lax.ppermute(later, along, one))  4.57 us
    ppermute x1, waiting for transfers between devices, per_device(): lists_hi = lax.ppermute(lists, along, two)  4.19 us
    ppermute x1, waiting for transfers between devices, per_device(): got_hi = [lax.ppermute(soon, along, two)]  4.08 us
    ppermute x1, waiting for transfers between devices, per_device(): got_hi.append(lax.ppermute(later, along, two))  3.63 us
    ppermute x1, starting transfers between devices, per_device(): got_lo = [lax.ppermute(soon, along, one)]  3.51 us
    ppermute x1, starting transfers between devices, per_device(): lists_lo = lax.ppermute(lists, along, one)  3.48 us
  transfers between devices with their start and end apart: 11, of which 6 were waited for; matrix products, arithmetic and copies ran while one was open for 0% of the time, Pallas kernels for 17%

profile of v8, /device:TPU:0, one launch (start us, length us, event | category | flops | bytes accessed | tf_op | source)
XLA Modules:
  0.0 53.0 jit_solution(5420083013108960859)
XLA Ops:
  0.0 2.4 %shard_map.55 = (bf16[128,2560]{1,0:T(8,128)(2,1)}, s32[8,128]{1,0:T(8,128)}) custom-call(s32[1,128]{1,0:T(1,128)} %bitcast.18, s32[6,1,128]{2,1,0:T(1,128)} %bitcast.17, bf16[9,128,256]{2,1,0:T(8,128)(2,1)} %bitcast.15, bf16[128,256]{1,0:T(8,128)(2,1)} %bitcast.16), custom_call_target="tpu_custom_call" | custom-call | bytes 1318400 | tf_op jit(solution)/shard_map/pallas_call | solution.py:398
  2.4 0.0 copy-start
  2.4 0.0 copy-start.1
  2.4 5.3 %all-to-all-start = ((bf16[8,16,2560]{2,1,0:T(8,128)(2,1)}), bf16[8,16,2560]{2,1,0:T(8,128)(2,1)S(1)}, u32[]{:S(2)}, u32[]{:S(2)}) async-start(bf16[8,16,2560]{2,1,0:T(8,128)(2,1)} %bitcast.14), calls=%async_computation | async-start | bytes 1310720 | tf_op jit(solution)/shard_map/all_to_all | solution.py:450
  7.7 0.0 copy-done
  7.7 3.5 %collective-permute-start = (s32[8,128]{1,0:T(8,128)S(1)}, s32[8,128]{1,0:T(8,128)S(1)}, u32[]{:S(2)}, u32[]{:S(2)}) collective-permute-start(s32[8,128]{1,0:T(8,128)S(1)} %copy-done), channel_id=1, source_target_pairs={{0,1},{1,2},{2,3},{5,4},{6,5},{7,6},{8,9},{9,10},{10,11},{13,12},{... | collective-permute-start | bytes 12296 | tf_op jit(solution)/shard_map/ppermute | solution.py:451
  11.2 1.3 %collective-permute-start.1 = (s32[8,128]{1,0:T(8,128)S(1)}, s32[8,128]{1,0:T(8,128)S(1)}, u32[]{:S(2)}, u32[]{:S(2)}) collective-permute-start(s32[8,128]{1,0:T(8,128)S(1)} %copy-done), channel_id=1, source_target_pairs={{1,0},{2,1},{3,2},{4,5},{5,6},{6,7},{9,8},{10,9},{11,10},{12,13},{... | collective-permute-start | bytes 12296 | tf_op jit(solution)/shard_map/ppermute | solution.py:452
  12.5 0.0 collective-permute-done.lists_lo
  12.5 4.2 %collective-permute-done.1.lists_hi = s32[8,128]{1,0:T(8,128)S(1)} collective-permute-done((s32[8,128]{1,0:T(8,128)S(1)}, s32[8,128]{1,0:T(8,128)S(1)}, u32[]{:S(2)}, u32[]{:S(2)}) %collective-permute-start.1) | collective-permute-done | bytes 4128 | tf_op jit(solution)/shard_map/ppermute | solution.py:452
  16.7 0.1 shard_map.56
  16.8 2.0 %all-to-all-done = bf16[8,16,2560]{2,1,0:T(8,128)(2,1)S(1)} async-done(((bf16[8,16,2560]{2,1,0:T(8,128)(2,1)}), bf16[8,16,2560]{2,1,0:T(8,128)(2,1)S(1)}, u32[]{:S(2)}, u32[]{:S(2)}) %all-to-all-start) | async-done | bytes 655392 | tf_op jit(solution)/shard_map/all_to_all | solution.py:450
  18.9 3.5 %collective-permute-start.2 = (bf16[128,1536]{1,0:T(8,128)(2,1)S(1)}, bf16[128,1536]{1,0:T(8,128)(2,1)S(1)}, u32[]{:S(2)}, u32[]{:S(2)}) collective-permute-start(bf16[128,1536]{1,0:T(8,128)(2,1)S(1)} %slice.6), channel_id=1, source_target_pairs={{0,1},{1,2},{2,3},{5,4},{6,5},{7,6},{8,9},{9,10},{10,11},{13,12},{... | collective-permute-start | bytes 1179656 | tf_op jit(solution)/shard_map/ppermute | solution.py:465
  22.4 1.3 %collective-permute-start.3 = (bf16[128,1536]{1,0:T(8,128)(2,1)S(1)}, bf16[128,1536]{1,0:T(8,128)(2,1)S(1)}, u32[]{:S(2)}, u32[]{:S(2)}) collective-permute-start(bf16[128,1536]{1,0:T(8,128)(2,1)S(1)} %slice.6), channel_id=1, source_target_pairs={{1,0},{2,1},{3,2},{4,5},{5,6},{6,7},{9,8},{10,9},{11,10},{12,13},{... | collective-permute-start | bytes 1179656 | tf_op jit(solution)/shard_map/ppermute | solution.py:466
  23.7 0.0 copy-done.1
  23.7 1.9 %shard_map.57 = (f32[256,128]{1,0:T(8,128)S(1)}, f32[4,256,128]{2,1,0:T(8,128)S(1)}, bf16[9,256,128]{2,1,0:T(8,128)(2,1)S(1)}, f32[9,256,128]{2,1,0:T(8,128)S(1)}, f32[9,256,128]{2,1,0:T(8,128)S(1)}) custom-call(f32[9]{0:T(128)S(1)} %copy-done.1, bf16[128,2560]{1,0:T(8,128)(2,1)S(1)} %bitcast.13, bf16[6,128,128]{2,1,0:T(8,128)(2,1)S(1)} %get-tuple-element.42.pick_ref.pick0), custom_call_target="tpu_custom_call" | custom-call | flops 500000000 | bytes 4456484 | tf_op jit(solution)/shard_map/pallas_call | solution.py:398
  25.6 4.6 %collective-permute-start.4 = (bf16[128,1024]{1,0:T(8,128)(2,1)S(1)}, bf16[128,1024]{1,0:T(8,128)(2,1)S(1)}, u32[]{:S(2)}, u32[]{:S(2)}) collective-permute-start(bf16[128,1024]{1,0:T(8,128)(2,1)S(1)} %slice.7), channel_id=1, source_target_pairs={{0,1},{1,2},{2,3},{5,4},{6,5},{7,6},{8,9},{9,10},{10,11},{13,12},{... | collective-permute-start | bytes 786440 | tf_op jit(solution)/shard_map/ppermute | solution.py:484
  30.2 1.3 %collective-permute-start.5 = (bf16[128,1024]{1,0:T(8,128)(2,1)S(1)}, bf16[128,1024]{1,0:T(8,128)(2,1)S(1)}, u32[]{:S(2)}, u32[]{:S(2)}) collective-permute-start(bf16[128,1024]{1,0:T(8,128)(2,1)S(1)} %slice.7), channel_id=1, source_target_pairs={{1,0},{2,1},{3,2},{4,5},{5,6},{6,7},{9,8},{10,9},{11,10},{12,13},{... | collective-permute-start | bytes 786440 | tf_op jit(solution)/shard_map/ppermute | solution.py:485
  31.5 0.0 collective-permute-done.2.got_lo
  31.5 0.7 %collective-permute-start.6 = (bf16[128,1536]{1,0:T(8,128)(2,1)S(1)}, bf16[128,1536]{1,0:T(8,128)(2,1)S(1)}, u32[]{:S(2)}, u32[]{:S(2)}) collective-permute-start(bf16[128,1536]{1,0:T(8,128)(2,1)S(1)} %collective-permute-done.2.got_lo), channel_id=1, source_target_pairs={{1,2},{2,3},{5,4},{6,5},{9,10},{10,11},{13,12},{14,13},{17,18},{18... | collective-permute-start | bytes 1179656 | tf_op jit(solution)/shard_map/ppermute | solution.py:486
  32.2 4.1 %collective-permute-done.3.got_hi = bf16[128,1536]{1,0:T(8,128)(2,1)S(1)} collective-permute-done((bf16[128,1536]{1,0:T(8,128)(2,1)S(1)}, bf16[128,1536]{1,0:T(8,128)(2,1)S(1)}, u32[]{:S(2)}, u32[]{:S(2)}) %collective-permute-start.3) | collective-permute-done | bytes 393248 | tf_op jit(solution)/shard_map/ppermute | solution.py:466
  36.3 1.3 %collective-permute-start.7 = (bf16[128,1536]{1,0:T(8,128)(2,1)S(1)}, bf16[128,1536]{1,0:T(8,128)(2,1)S(1)}, u32[]{:S(2)}, u32[]{:S(2)}) collective-permute-start(bf16[128,1536]{1,0:T(8,128)(2,1)S(1)} %collective-permute-done.3.got_hi), channel_id=1, source_target_pairs={{1,0},{2,1},{5,6},{6,7},{9,8},{10,9},{13,14},{14,15},{17,16},{18,1... | collective-permute-start | bytes 1179656 | tf_op jit(solution)/shard_map/ppermute | solution.py:487
  37.6 0.0 collective-permute-done.4.later_lo
  37.6 0.7 %collective-permute-start.8 = (bf16[128,1024]{1,0:T(8,128)(2,1)S(1)}, bf16[128,1024]{1,0:T(8,128)(2,1)S(1)}, u32[]{:S(2)}, u32[]{:S(2)}) collective-permute-start(bf16[128,1024]{1,0:T(8,128)(2,1)S(1)} %collective-permute-done.4.later_lo), channel_id=1, source_target_pairs={{1,2},{2,3},{5,4},{6,5},{9,10},{10,11},{13,12},{14,13},{17,18},{18... | collective-permute-start | bytes 786440 | tf_op jit(solution)/shard_map/ppermute | solution.py:486
  38.3 3.6 %collective-permute-done.5.later_hi = bf16[128,1024]{1,0:T(8,128)(2,1)S(1)} collective-permute-done((bf16[128,1024]{1,0:T(8,128)(2,1)S(1)}, bf16[128,1024]{1,0:T(8,128)(2,1)S(1)}, u32[]{:S(2)}, u32[]{:S(2)}) %collective-permute-start.5) | collective-permute-done | bytes 262176 | tf_op jit(solution)/shard_map/ppermute | solution.py:485
  41.9 1.3 %collective-permute-start.9 = (bf16[128,1024]{1,0:T(8,128)(2,1)S(1)}, bf16[128,1024]{1,0:T(8,128)(2,1)S(1)}, u32[]{:S(2)}, u32[]{:S(2)}) collective-permute-start(bf16[128,1024]{1,0:T(8,128)(2,1)S(1)} %collective-permute-done.5.later_hi), channel_id=1, source_target_pairs={{1,0},{2,1},{5,6},{6,7},{9,8},{10,9},{13,14},{14,15},{17,16},{18,1... | collective-permute-start | bytes 786440 | tf_op jit(solution)/shard_map/ppermute | solution.py:487
  43.2 5.0 %shard_map.58 = (f32[2,256,128]{2,1,0:T(8,128)S(1)}, f32[2,256,128]{2,1,0:T(8,128)S(1)}, f32[2,256,128]{2,1,0:T(8,128)S(1)}, f32[9,256,128]{2,1,0:T(8,128)S(1)},...) custom-call(f32[9]{0:T(128)S(1)} %copy-done.1, ...), custom_call_target="tpu_custom_call" | custom-call | flops 1800000000 | bytes 11010084 | tf_op jit(solution)/shard_map/pallas_call | solution.py:398
  48.1 0.0 collective-permute-done.6.got_lo2
  48.2 0.6 %collective-permute-done.7.got_hi2 = bf16[128,1536]{1,0:T(8,128)(2,1)S(1)} collective-permute-done((bf16[128,1536]{1,0:T(8,128)(2,1)S(1)}, bf16[128,1536]{1,0:T(8,128)(2,1)S(1)}, u32[]{:S(2)}, u32[]{:S(2)}) %collective-permute-start.7) | collective-permute-done | bytes 393248 | tf_op jit(solution)/shard_map/ppermute | solution.py:487
  48.7 2.1 %shard_map.59 = (bf16[256,256]{1,0:T(8,128)(2,1)S(1)}, bf16[2,256,128]{2,1,0:T(8,128)(2,1)S(1)}, f32[2,4,256,128]{3,2,1,0:T(8,128)S(1)}, f32[2,4,256,128]{3,2,1,0:T(8,128)S(1)}, f32[5,128,256]{2,1,0:T(8,128)S(1)}) custom-call(f32[9]{0:T(128)S(1)} %copy-done.1, bf16[6,128,128]{2,1,0:T(8,128)(2,1)S(1)} %get-tuple-element.42.pick_ref.pick0, ...), custom_call_target="tpu_custom_call" | custom-call | flops 500000000 | bytes 9633828 | tf_op jit(solution)/shard_map/pallas_call | solution.py:398
  50.9 0.0 collective-permute-done.8.later_lo2
  50.9 0.7 %collective-permute-done.9.later_hi2 = bf16[128,1024]{1,0:T(8,128)(2,1)S(1)} collective-permute-done((bf16[128,1024]{1,0:T(8,128)(2,1)S(1)}, bf16[128,1024]{1,0:T(8,128)(2,1)S(1)}, u32[]{:S(2)}, u32[]{:S(2)}) %collective-permute-start.9) | collective-permute-done | bytes 262176 | tf_op jit(solution)/shard_map/ppermute | solution.py:487
  51.5 1.4 %shard_map.60 = f32[9,128,256]{2,1,0:T(8,128)} custom-call(bf16[256,256]{1,0:T(8,128)(2,1)S(1)} %get-tuple-element.64.far_ref, bf16[2,256,128]{2,1,0:T(8,128)(2,1)S(1)} %get-tuple-element.65.two_ref, f32[2,4,256,128]{3,2,1,0:T(8,128)S(1)} %get-tuple-element.66.offset_ref, f32[2,4,256,128]{3,2,1,0:T(8,128)S(1)} %get-tuple-element.67.slope_ref, ...), custom_call_target="tpu_custom_call" | custom-call | flops 400000000 | bytes 7340032 | tf_op jit(solution)/shard_map/pallas_call | solution.py:398
  (2 shorter events, 0.0 us)
Async XLA Ops:
  2.4 5.3 %copy-start = (s32[8,128]{1,0:T(8,128)S(1)}, s32[8,128]{1,0:T(8,128)}, u32[]{:S(2)}) copy-start(s32[8,128]{1,0:T(8,128)} %get-tuple-element.38.lists0) | copy-start | bytes 12292
  2.4 21.3 %copy-start.1 = (f32[9]{0:T(128)S(1)}, f32[9]{0:T(128)}, u32[]{:S(2)}) copy-start(f32[9]{0:T(128)} %lewis_ref.5) | copy-start | bytes 112
  2.4 16.5 %all-to-all-start = ((bf16[8,16,2560]{2,1,0:T(8,128)(2,1)}), bf16[8,16,2560]{2,1,0:T(8,128)(2,1)S(1)}, u32[]{:S(2)}, u32[]{:S(2)}) async-start(bf16[8,16,2560]{2,1,0:T(8,128)(2,1)} %bitcast.14), calls=%async_computation | async-start | bytes 1310720 | tf_op jit(solution)/shard_map/all_to_all | solution.py:450
  7.7 4.8 %collective-permute-start = (s32[8,128]{1,0:T(8,128)S(1)}, s32[8,128]{1,0:T(8,128)S(1)}, u32[]{:S(2)}, u32[]{:S(2)}) collective-permute-start(s32[8,128]{1,0:T(8,128)S(1)} %copy-done), channel_id=1, source_target_pairs={{0,1},{1,2},{2,3},{5,4},{6,5},{7,6},{8,9},{9,10},{10,11},{13,12},{... | collective-permute-start | bytes 12296 | tf_op jit(solution)/shard_map/ppermute | solution.py:451
  11.2 5.5 %collective-permute-start.1 = (s32[8,128]{1,0:T(8,128)S(1)}, s32[8,128]{1,0:T(8,128)S(1)}, u32[]{:S(2)}, u32[]{:S(2)}) collective-permute-start(s32[8,128]{1,0:T(8,128)S(1)} %copy-done), channel_id=1, source_target_pairs={{1,0},{2,1},{3,2},{4,5},{5,6},{6,7},{9,8},{10,9},{11,10},{12,13},{... | collective-permute-start | bytes 12296 | tf_op jit(solution)/shard_map/ppermute | solution.py:452
  18.9 12.6 %collective-permute-start.2 = (bf16[128,1536]{1,0:T(8,128)(2,1)S(1)}, bf16[128,1536]{1,0:T(8,128)(2,1)S(1)}, u32[]{:S(2)}, u32[]{:S(2)}) collective-permute-start(bf16[128,1536]{1,0:T(8,128)(2,1)S(1)} %slice.6), channel_id=1, source_target_pairs={{0,1},{1,2},{2,3},{5,4},{6,5},{7,6},{8,9},{9,10},{10,11},{13,12},{... | collective-permute-start | bytes 1179656 | tf_op jit(solution)/shard_map/ppermute | solution.py:465
  22.4 13.9 %collective-permute-start.3 = (bf16[128,1536]{1,0:T(8,128)(2,1)S(1)}, bf16[128,1536]{1,0:T(8,128)(2,1)S(1)}, u32[]{:S(2)}, u32[]{:S(2)}) collective-permute-start(bf16[128,1536]{1,0:T(8,128)(2,1)S(1)} %slice.6), channel_id=1, source_target_pairs={{1,0},{2,1},{3,2},{4,5},{5,6},{6,7},{9,8},{10,9},{11,10},{12,13},{... | collective-permute-start | bytes 1179656 | tf_op jit(solution)/shard_map/ppermute | solution.py:466
  25.6 12.0 %collective-permute-start.4 = (bf16[128,1024]{1,0:T(8,128)(2,1)S(1)}, bf16[128,1024]{1,0:T(8,128)(2,1)S(1)}, u32[]{:S(2)}, u32[]{:S(2)}) collective-permute-start(bf16[128,1024]{1,0:T(8,128)(2,1)S(1)} %slice.7), channel_id=1, source_target_pairs={{0,1},{1,2},{2,3},{5,4},{6,5},{7,6},{8,9},{9,10},{10,11},{13,12},{... | collective-permute-start | bytes 786440 | tf_op jit(solution)/shard_map/ppermute | solution.py:484
  30.2 11.7 %collective-permute-start.5 = (bf16[128,1024]{1,0:T(8,128)(2,1)S(1)}, bf16[128,1024]{1,0:T(8,128)(2,1)S(1)}, u32[]{:S(2)}, u32[]{:S(2)}) collective-permute-start(bf16[128,1024]{1,0:T(8,128)(2,1)S(1)} %slice.7), channel_id=1, source_target_pairs={{1,0},{2,1},{3,2},{4,5},{5,6},{6,7},{9,8},{10,9},{11,10},{12,13},{... | collective-permute-start | bytes 786440 | tf_op jit(solution)/shard_map/ppermute | solution.py:485
  31.5 16.6 %collective-permute-start.6 = (bf16[128,1536]{1,0:T(8,128)(2,1)S(1)}, bf16[128,1536]{1,0:T(8,128)(2,1)S(1)}, u32[]{:S(2)}, u32[]{:S(2)}) collective-permute-start(bf16[128,1536]{1,0:T(8,128)(2,1)S(1)} %collective-permute-done.2.got_lo), channel_id=1, source_target_pairs={{1,2},{2,3},{5,4},{6,5},{9,10},{10,11},{13,12},{14,13},{17,18},{18... | collective-permute-start | bytes 1179656 | tf_op jit(solution)/shard_map/ppermute | solution.py:486
  36.3 12.5 %collective-permute-start.7 = (bf16[128,1536]{1,0:T(8,128)(2,1)S(1)}, bf16[128,1536]{1,0:T(8,128)(2,1)S(1)}, u32[]{:S(2)}, u32[]{:S(2)}) collective-permute-start(bf16[128,1536]{1,0:T(8,128)(2,1)S(1)} %collective-permute-done.3.got_hi), channel_id=1, source_target_pairs={{1,0},{2,1},{5,6},{6,7},{9,8},{10,9},{13,14},{14,15},{17,16},{18,1... | collective-permute-start | bytes 1179656 | tf_op jit(solution)/shard_map/ppermute | solution.py:487
  37.6 13.3 %collective-permute-start.8 = (bf16[128,1024]{1,0:T(8,128)(2,1)S(1)}, bf16[128,1024]{1,0:T(8,128)(2,1)S(1)}, u32[]{:S(2)}, u32[]{:S(2)}) collective-permute-start(bf16[128,1024]{1,0:T(8,128)(2,1)S(1)} %collective-permute-done.4.later_lo), channel_id=1, source_target_pairs={{1,2},{2,3},{5,4},{6,5},{9,10},{10,11},{13,12},{14,13},{17,18},{18... | collective-permute-start | bytes 786440 | tf_op jit(solution)/shard_map/ppermute | solution.py:486
  41.9 9.6 %collective-permute-start.9 = (bf16[128,1024]{1,0:T(8,128)(2,1)S(1)}, bf16[128,1024]{1,0:T(8,128)(2,1)S(1)}, u32[]{:S(2)}, u32[]{:S(2)}) collective-permute-start(bf16[128,1024]{1,0:T(8,128)(2,1)S(1)} %collective-permute-done.5.later_hi), channel_id=1, source_target_pairs={{1,0},{2,1},{5,6},{6,7},{9,8},{10,9},{13,14},{14,15},{17,16},{18,1... | collective-permute-start | bytes 786440 | tf_op jit(solution)/shard_map/ppermute | solution.py:487

commit v9 on v8

--- a/solution.py
+++ b/solution.py
@@ -51,8 +51,8 @@
         send_ref[:, at] = dot(place, state_ref[k]).astype(BF16)
     none = jnp.zeros((1, slots), jnp.int32)
     rows = [lists_ref[f] + 1 for f in range(FACES)] + [none] * (8 - FACES)
-    odd = lax.rem(lax.axis_index("group"), 2) == 1
-    rows[4], rows[5] = jnp.where(odd, rows[5], rows[4]), jnp.where(odd, rows[4], rows[5])
+    even = lax.rem(lax.axis_index("group"), 2) == 0
+    rows[4], rows[5] = jnp.where(even, rows[5], rows[4]), jnp.where(even, rows[4], rows[5])
     lists_out[...] = jnp.concatenate(rows, 0)
 
 
@@ -416,7 +416,7 @@
         steps = []
         for g in range(groups):
             for i in range(0 if ends else 1, members if ends else members - 1):
-                target = i + 1 if upward == (g % 2 == 0) else i - 1
+                target = i + 1 if upward == (g % 2 == 1) else i - 1
                 if 0 <= target < members:
                     steps.append((g * members + i, g * members + target))
         return steps

time: 53.4 us -> 53.9 us (level)
  starting transfers between devices: 24.7 us -> 26.8 us
  waiting for transfers between devices: 15.2 us -> 13.6 us
    ppermute x2, waiting for transfers between devices: 0.01 us -> 4.66 us  [per_device(): got_lo2 = [lax.ppermute(part, along, one_on) for part in got_lo]]
    ppermute x1, waiting for transfers between devices: 4.08 us -> 0.01 us  [per_device(): got_hi = [lax.ppermute(soon, along, two)]]
    ppermute x1, waiting for transfers between devices: 3.63 us -> 0.01 us  [per_device(): got_hi.append(lax.ppermute(later, along, two))]
    ppermute x1, waiting for transfers between devices: 0.01 us -> 3.62 us  [per_device(): got_lo.append(lax.ppermute(later, along, one))]
    ppermute x1, starting transfers between devices: 1.29 us -> 4.57 us  [per_device(): got_hi = [lax.ppermute(soon, along, two)]]
    ppermute x1, starting transfers between devices: 4.57 us -> 1.29 us  [per_device(): got_lo.append(lax.ppermute(later, along, one))]
    ppermute x1, starting transfers between devices: 1.29 us -> 4.56 us  [per_device(): got_hi.append(lax.ppermute(later, along, two))]
    ppermute x1, starting transfers between devices: 1.29 us -> 4.55 us  [per_device(): lists_hi = lax.ppermute(lists, along, two)]
where the time goes in v9:
time: 53.9 us; the launch traced here: 53.4 us
  starting transfers between devices  26.8 us (50%)
  waiting for transfers between devices  13.6 us (25%)
  Pallas kernels  12.9 us (24%)
    pallas_call x6, Pallas kernels, call(): pl.pallas_call(kernel, out_shape=out_shape, grid=grid, in_specs=[specs.ge...  12.9 us
    all_to_all x1, starting transfers between devices, per_device(): lax.all_to_all(send, 'group', split_axis=0, concat_axis=0, tiled=True)  5.3 us
    ppermute x2, waiting for transfers between devices, per_device(): got_lo2 = [lax.ppermute(part, along, one_on) for part in got_lo]  4.66 us
    ppermute x1, starting transfers between devices, per_device(): got_hi = [lax.ppermute(soon, along, two)]  4.57 us
    ppermute x1, starting transfers between devices, per_device(): got_hi.append(lax.ppermute(later, along, two))  4.56 us
    ppermute x1, starting transfers between devices, per_device(): lists_hi = lax.ppermute(lists, along, two)  4.55 us
    all_to_all x1, waiting for transfers between devices, per_device(): lax.all_to_all(send, 'group', split_axis=0, concat_axis=0, tiled=True)  3.87 us
    ppermute x1, waiting for transfers between devices, per_device(): got_lo.append(lax.ppermute(later, along, one))  3.62 us
  transfers between devices with their start and end apart: 11, of which 6 were waited for; matrix products, arithmetic and copies ran while one was open for 0% of the time, Pallas kernels for 17%

profile of v9, /device:TPU:0, one launch (start us, length us, event | category | flops | bytes accessed | tf_op | source)
XLA Modules:
  0.0 53.4 jit_solution(16751096934307364787)
XLA Ops:
  0.0 2.4 %shard_map.55 = (bf16[128,2560]{1,0:T(8,128)(2,1)}, s32[8,128]{1,0:T(8,128)}) custom-call(s32[1,128]{1,0:T(1,128)} %bitcast.18, s32[6,1,128]{2,1,0:T(1,128)} %bitcast.17, bf16[9,128,256]{2,1,0:T(8,128)(2,1)} %bitcast.15, bf16[128,256]{1,0:T(8,128)(2,1)} %bitcast.16), custom_call_target="tpu_custom_call" | custom-call | bytes 1318400 | tf_op jit(solution)/shard_map/pallas_call | solution.py:398
  2.4 0.0 copy-start
  2.4 0.0 copy-start.1
  2.4 5.3 %all-to-all-start = ((bf16[8,16,2560]{2,1,0:T(8,128)(2,1)}), bf16[8,16,2560]{2,1,0:T(8,128)(2,1)S(1)}, u32[]{:S(2)}, u32[]{:S(2)}) async-start(bf16[8,16,2560]{2,1,0:T(8,128)(2,1)} %bitcast.14), calls=%async_computation | async-start | bytes 1310720 | tf_op jit(solution)/shard_map/all_to_all | solution.py:450
  7.7 0.0 copy-done
  7.7 1.3 %collective-permute-start = (s32[8,128]{1,0:T(8,128)S(1)}, s32[8,128]{1,0:T(8,128)S(1)}, u32[]{:S(2)}, u32[]{:S(2)}) collective-permute-start(s32[8,128]{1,0:T(8,128)S(1)} %copy-done), channel_id=1, source_target_pairs={{1,0},{2,1},{3,2},{4,5},{5,6},{6,7},{9,8},{10,9},{11,10},{12,13},{... | collective-permute-start | bytes 12296 | tf_op jit(solution)/shard_map/ppermute | solution.py:451
  9.0 4.5 %collective-permute-start.1 = (s32[8,128]{1,0:T(8,128)S(1)}, s32[8,128]{1,0:T(8,128)S(1)}, u32[]{:S(2)}, u32[]{:S(2)}) collective-permute-start(s32[8,128]{1,0:T(8,128)S(1)} %copy-done), channel_id=1, source_target_pairs={{0,1},{1,2},{2,3},{5,4},{6,5},{7,6},{8,9},{9,10},{10,11},{13,12},{... | collective-permute-start | bytes 12296 | tf_op jit(solution)/shard_map/ppermute | solution.py:452
  13.6 0.0 collective-permute-done.lists_lo
  13.6 1.3 %collective-permute-done.1.lists_hi = s32[8,128]{1,0:T(8,128)S(1)} collective-permute-done((s32[8,128]{1,0:T(8,128)S(1)}, s32[8,128]{1,0:T(8,128)S(1)}, u32[]{:S(2)}, u32[]{:S(2)}) %collective-permute-start.1) | collective-permute-done | bytes 4128 | tf_op jit(solution)/shard_map/ppermute | solution.py:452
  14.9 0.1 shard_map.56
  15.0 3.9 %all-to-all-done = bf16[8,16,2560]{2,1,0:T(8,128)(2,1)S(1)} async-done(((bf16[8,16,2560]{2,1,0:T(8,128)(2,1)}), bf16[8,16,2560]{2,1,0:T(8,128)(2,1)S(1)}, u32[]{:S(2)}, u32[]{:S(2)}) %all-to-all-start) | async-done | bytes 655392 | tf_op jit(solution)/shard_map/all_to_all | solution.py:450
  18.9 1.3 %collective-permute-start.2 = (bf16[128,1536]{1,0:T(8,128)(2,1)S(1)}, bf16[128,1536]{1,0:T(8,128)(2,1)S(1)}, u32[]{:S(2)}, u32[]{:S(2)}) collective-permute-start(bf16[128,1536]{1,0:T(8,128)(2,1)S(1)} %slice.6), channel_id=1, source_target_pairs={{1,0},{2,1},{3,2},{4,5},{5,6},{6,7},{9,8},{10,9},{11,10},{12,13},{... | collective-permute-start | bytes 1179656 | tf_op jit(solution)/shard_map/ppermute | solution.py:465
  20.2 4.6 %collective-permute-start.3 = (bf16[128,1536]{1,0:T(8,128)(2,1)S(1)}, bf16[128,1536]{1,0:T(8,128)(2,1)S(1)}, u32[]{:S(2)}, u32[]{:S(2)}) collective-permute-start(bf16[128,1536]{1,0:T(8,128)(2,1)S(1)} %slice.6), channel_id=1, source_target_pairs={{0,1},{1,2},{2,3},{5,4},{6,5},{7,6},{8,9},{9,10},{10,11},{13,12},{... | collective-permute-start | bytes 1179656 | tf_op jit(solution)/shard_map/ppermute | solution.py:466
  24.8 0.0 copy-done.1
  24.8 1.9 %shard_map.57 = (f32[256,128]{1,0:T(8,128)S(1)}, f32[4,256,128]{2,1,0:T(8,128)S(1)}, bf16[9,256,128]{2,1,0:T(8,128)(2,1)S(1)}, f32[9,256,128]{2,1,0:T(8,128)S(1)}, f32[9,256,128]{2,1,0:T(8,128)S(1)}) custom-call(f32[9]{0:T(128)S(1)} %copy-done.1, bf16[128,2560]{1,0:T(8,128)(2,1)S(1)} %bitcast.13, bf16[6,128,128]{2,1,0:T(8,128)(2,1)S(1)} %get-tuple-element.42.pick_ref.pick0), custom_call_target="tpu_custom_call" | custom-call | flops 500000000 | bytes 4456484 | tf_op jit(solution)/shard_map/pallas_call | solution.py:398
  26.7 1.3 %collective-permute-start.4 = (bf16[128,1024]{1,0:T(8,128)(2,1)S(1)}, bf16[128,1024]{1,0:T(8,128)(2,1)S(1)}, u32[]{:S(2)}, u32[]{:S(2)}) collective-permute-start(bf16[128,1024]{1,0:T(8,128)(2,1)S(1)} %slice.7), channel_id=1, source_target_pairs={{1,0},{2,1},{3,2},{4,5},{5,6},{6,7},{9,8},{10,9},{11,10},{12,13},{... | collective-permute-start | bytes 786440 | tf_op jit(solution)/shard_map/ppermute | solution.py:484
  28.0 4.6 %collective-permute-start.5 = (bf16[128,1024]{1,0:T(8,128)(2,1)S(1)}, bf16[128,1024]{1,0:T(8,128)(2,1)S(1)}, u32[]{:S(2)}, u32[]{:S(2)}) collective-permute-start(bf16[128,1024]{1,0:T(8,128)(2,1)S(1)} %slice.7), channel_id=1, source_target_pairs={{0,1},{1,2},{2,3},{5,4},{6,5},{7,6},{8,9},{9,10},{10,11},{13,12},{... | collective-permute-start | bytes 786440 | tf_op jit(solution)/shard_map/ppermute | solution.py:485
  32.6 0.1 collective-permute-done.2.got_lo
  32.7 1.3 %collective-permute-start.6 = (bf16[128,1536]{1,0:T(8,128)(2,1)S(1)}, bf16[128,1536]{1,0:T(8,128)(2,1)S(1)}, u32[]{:S(2)}, u32[]{:S(2)}) collective-permute-start(bf16[128,1536]{1,0:T(8,128)(2,1)S(1)} %collective-permute-done.2.got_lo), channel_id=1, source_target_pairs={{1,0},{2,1},{5,6},{6,7},{9,8},{10,9},{13,14},{14,15},{17,16},{18,1... | collective-permute-start | bytes 1179656 | tf_op jit(solution)/shard_map/ppermute | solution.py:486
  34.0 0.0 collective-permute-done.3.got_hi
  34.0 0.7 %collective-permute-start.7 = (bf16[128,1536]{1,0:T(8,128)(2,1)S(1)}, bf16[128,1536]{1,0:T(8,128)(2,1)S(1)}, u32[]{:S(2)}, u32[]{:S(2)}) collective-permute-start(bf16[128,1536]{1,0:T(8,128)(2,1)S(1)} %collective-permute-done.3.got_hi), channel_id=1, source_target_pairs={{1,2},{2,3},{5,4},{6,5},{9,10},{10,11},{13,12},{14,13},{17,18},{18... | collective-permute-start | bytes 1179656 | tf_op jit(solution)/shard_map/ppermute | solution.py:487
  34.7 3.6 %collective-permute-done.4.later_lo = bf16[128,1024]{1,0:T(8,128)(2,1)S(1)} collective-permute-done((bf16[128,1024]{1,0:T(8,128)(2,1)S(1)}, bf16[128,1024]{1,0:T(8,128)(2,1)S(1)}, u32[]{:S(2)}, u32[]{:S(2)}) %collective-permute-start.4) | collective-permute-done | bytes 262176 | tf_op jit(solution)/shard_map/ppermute | solution.py:484
  38.3 1.3 %collective-permute-start.8 = (bf16[128,1024]{1,0:T(8,128)(2,1)S(1)}, bf16[128,1024]{1,0:T(8,128)(2,1)S(1)}, u32[]{:S(2)}, u32[]{:S(2)}) collective-permute-start(bf16[128,1024]{1,0:T(8,128)(2,1)S(1)} %collective-permute-done.4.later_lo), channel_id=1, source_target_pairs={{1,0},{2,1},{5,6},{6,7},{9,8},{10,9},{13,14},{14,15},{17,16},{18,1... | collective-permute-start | bytes 786440 | tf_op jit(solution)/shard_map/ppermute | solution.py:486
  39.6 0.0 collective-permute-done.5.later_hi
  39.6 0.7 %collective-permute-start.9 = (bf16[128,1024]{1,0:T(8,128)(2,1)S(1)}, bf16[128,1024]{1,0:T(8,128)(2,1)S(1)}, u32[]{:S(2)}, u32[]{:S(2)}) collective-permute-start(bf16[128,1024]{1,0:T(8,128)(2,1)S(1)} %collective-permute-done.5.later_hi), channel_id=1, source_target_pairs={{1,2},{2,3},{5,4},{6,5},{9,10},{10,11},{13,12},{14,13},{17,18},{18... | collective-permute-start | bytes 786440 | tf_op jit(solution)/shard_map/ppermute | solution.py:487
  40.3 4.9 %shard_map.58 = (f32[2,256,128]{2,1,0:T(8,128)S(1)}, f32[2,256,128]{2,1,0:T(8,128)S(1)}, f32[2,256,128]{2,1,0:T(8,128)S(1)}, f32[9,256,128]{2,1,0:T(8,128)S(1)},...) custom-call(f32[9]{0:T(128)S(1)} %copy-done.1, ...), custom_call_target="tpu_custom_call" | custom-call | flops 1800000000 | bytes 11010084 | tf_op jit(solution)/shard_map/pallas_call | solution.py:398
  45.2 1.5 %collective-permute-done.6.got_lo2 = bf16[128,1536]{1,0:T(8,128)(2,1)S(1)} collective-permute-done((bf16[128,1536]{1,0:T(8,128)(2,1)S(1)}, bf16[128,1536]{1,0:T(8,128)(2,1)S(1)}, u32[]{:S(2)}, u32[]{:S(2)}) %collective-permute-start.6) | collective-permute-done | bytes 393248 | tf_op jit(solution)/shard_map/ppermute | solution.py:486
  46.7 0.0 collective-permute-done.7.got_hi2
  46.7 2.1 %shard_map.59 = (bf16[256,256]{1,0:T(8,128)(2,1)S(1)}, bf16[2,256,128]{2,1,0:T(8,128)(2,1)S(1)}, f32[2,4,256,128]{3,2,1,0:T(8,128)S(1)}, f32[2,4,256,128]{3,2,1,0:T(8,128)S(1)}, f32[5,128,256]{2,1,0:T(8,128)S(1)}) custom-call(f32[9]{0:T(128)S(1)} %copy-done.1, bf16[6,128,128]{2,1,0:T(8,128)(2,1)S(1)} %get-tuple-element.42.pick_ref.pick0, ...), custom_call_target="tpu_custom_call" | custom-call | flops 500000000 | bytes 9633828 | tf_op jit(solution)/shard_map/pallas_call | solution.py:398
  48.8 3.2 %collective-permute-done.8.later_lo2 = bf16[128,1024]{1,0:T(8,128)(2,1)S(1)} collective-permute-done((bf16[128,1024]{1,0:T(8,128)(2,1)S(1)}, bf16[128,1024]{1,0:T(8,128)(2,1)S(1)}, u32[]{:S(2)}, u32[]{:S(2)}) %collective-permute-start.8) | collective-permute-done | bytes 262176 | tf_op jit(solution)/shard_map/ppermute | solution.py:486
  52.0 0.0 collective-permute-done.9.later_hi2
  52.0 1.4 %shard_map.60 = f32[9,128,256]{2,1,0:T(8,128)} custom-call(bf16[256,256]{1,0:T(8,128)(2,1)S(1)} %get-tuple-element.64.far_ref, bf16[2,256,128]{2,1,0:T(8,128)(2,1)S(1)} %get-tuple-element.65.two_ref, f32[2,4,256,128]{3,2,1,0:T(8,128)S(1)} %get-tuple-element.66.offset_ref, f32[2,4,256,128]{3,2,1,0:T(8,128)S(1)} %get-tuple-element.67.slope_ref, ...), custom_call_target="tpu_custom_call" | custom-call | flops 400000000 | bytes 7340032 | tf_op jit(solution)/shard_map/pallas_call | solution.py:398
  (2 shorter events, 0.0 us)
Async XLA Ops:
  2.4 5.3 %copy-start = (s32[8,128]{1,0:T(8,128)S(1)}, s32[8,128]{1,0:T(8,128)}, u32[]{:S(2)}) copy-start(s32[8,128]{1,0:T(8,128)} %get-tuple-element.38.lists0) | copy-start | bytes 12292
  2.4 22.4 %copy-start.1 = (f32[9]{0:T(128)S(1)}, f32[9]{0:T(128)}, u32[]{:S(2)}) copy-start(f32[9]{0:T(128)} %lewis_ref.5) | copy-start | bytes 112
  2.4 16.5 %all-to-all-start = ((bf16[8,16,2560]{2,1,0:T(8,128)(2,1)}), bf16[8,16,2560]{2,1,0:T(8,128)(2,1)S(1)}, u32[]{:S(2)}, u32[]{:S(2)}) async-start(bf16[8,16,2560]{2,1,0:T(8,128)(2,1)} %bitcast.14), calls=%async_computation | async-start | bytes 1310720 | tf_op jit(solution)/shard_map/all_to_all | solution.py:450
  7.7 5.9 %collective-permute-start = (s32[8,128]{1,0:T(8,128)S(1)}, s32[8,128]{1,0:T(8,128)S(1)}, u32[]{:S(2)}, u32[]{:S(2)}) collective-permute-start(s32[8,128]{1,0:T(8,128)S(1)} %copy-done), channel_id=1, source_target_pairs={{1,0},{2,1},{3,2},{4,5},{5,6},{6,7},{9,8},{10,9},{11,10},{12,13},{... | collective-permute-start | bytes 12296 | tf_op jit(solution)/shard_map/ppermute | solution.py:451
  9.0 5.9 %collective-permute-start.1 = (s32[8,128]{1,0:T(8,128)S(1)}, s32[8,128]{1,0:T(8,128)S(1)}, u32[]{:S(2)}, u32[]{:S(2)}) collective-permute-start(s32[8,128]{1,0:T(8,128)S(1)} %copy-done), channel_id=1, source_target_pairs={{0,1},{1,2},{2,3},{5,4},{6,5},{7,6},{8,9},{9,10},{10,11},{13,12},{... | collective-permute-start | bytes 12296 | tf_op jit(solution)/shard_map/ppermute | solution.py:452
  18.9 13.8 %collective-permute-start.2 = (bf16[128,1536]{1,0:T(8,128)(2,1)S(1)}, bf16[128,1536]{1,0:T(8,128)(2,1)S(1)}, u32[]{:S(2)}, u32[]{:S(2)}) collective-permute-start(bf16[128,1536]{1,0:T(8,128)(2,1)S(1)} %slice.6), channel_id=1, source_target_pairs={{1,0},{2,1},{3,2},{4,5},{5,6},{6,7},{9,8},{10,9},{11,10},{12,13},{... | collective-permute-start | bytes 1179656 | tf_op jit(solution)/shard_map/ppermute | solution.py:465
  20.2 13.8 %collective-permute-start.3 = (bf16[128,1536]{1,0:T(8,128)(2,1)S(1)}, bf16[128,1536]{1,0:T(8,128)(2,1)S(1)}, u32[]{:S(2)}, u32[]{:S(2)}) collective-permute-start(bf16[128,1536]{1,0:T(8,128)(2,1)S(1)} %slice.6), channel_id=1, source_target_pairs={{0,1},{1,2},{2,3},{5,4},{6,5},{7,6},{8,9},{9,10},{10,11},{13,12},{... | collective-permute-start | bytes 1179656 | tf_op jit(solution)/shard_map/ppermute | solution.py:466
  26.7 11.6 %collective-permute-start.4 = (bf16[128,1024]{1,0:T(8,128)(2,1)S(1)}, bf16[128,1024]{1,0:T(8,128)(2,1)S(1)}, u32[]{:S(2)}, u32[]{:S(2)}) collective-permute-start(bf16[128,1024]{1,0:T(8,128)(2,1)S(1)} %slice.7), channel_id=1, source_target_pairs={{1,0},{2,1},{3,2},{4,5},{5,6},{6,7},{9,8},{10,9},{11,10},{12,13},{... | collective-permute-start | bytes 786440 | tf_op jit(solution)/shard_map/ppermute | solution.py:484
  28.0 11.6 %collective-permute-start.5 = (bf16[128,1024]{1,0:T(8,128)(2,1)S(1)}, bf16[128,1024]{1,0:T(8,128)(2,1)S(1)}, u32[]{:S(2)}, u32[]{:S(2)}) collective-permute-start(bf16[128,1024]{1,0:T(8,128)(2,1)S(1)} %slice.7), channel_id=1, source_target_pairs={{0,1},{1,2},{2,3},{5,4},{6,5},{7,6},{8,9},{9,10},{10,11},{13,12},{... | collective-permute-start | bytes 786440 | tf_op jit(solution)/shard_map/ppermute | solution.py:485
  32.7 14.0 %collective-permute-start.6 = (bf16[128,1536]{1,0:T(8,128)(2,1)S(1)}, bf16[128,1536]{1,0:T(8,128)(2,1)S(1)}, u32[]{:S(2)}, u32[]{:S(2)}) collective-permute-start(bf16[128,1536]{1,0:T(8,128)(2,1)S(1)} %collective-permute-done.2.got_lo), channel_id=1, source_target_pairs={{1,0},{2,1},{5,6},{6,7},{9,8},{10,9},{13,14},{14,15},{17,16},{18,1... | collective-permute-start | bytes 1179656 | tf_op jit(solution)/shard_map/ppermute | solution.py:486
  34.0 12.7 %collective-permute-start.7 = (bf16[128,1536]{1,0:T(8,128)(2,1)S(1)}, bf16[128,1536]{1,0:T(8,128)(2,1)S(1)}, u32[]{:S(2)}, u32[]{:S(2)}) collective-permute-start(bf16[128,1536]{1,0:T(8,128)(2,1)S(1)} %collective-permute-done.3.got_hi), channel_id=1, source_target_pairs={{1,2},{2,3},{5,4},{6,5},{9,10},{10,11},{13,12},{14,13},{17,18},{18... | collective-permute-start | bytes 1179656 | tf_op jit(solution)/shard_map/ppermute | solution.py:487
  38.3 13.7 %collective-permute-start.8 = (bf16[128,1024]{1,0:T(8,128)(2,1)S(1)}, bf16[128,1024]{1,0:T(8,128)(2,1)S(1)}, u32[]{:S(2)}, u32[]{:S(2)}) collective-permute-start(bf16[128,1024]{1,0:T(8,128)(2,1)S(1)} %collective-permute-done.4.later_lo), channel_id=1, source_target_pairs={{1,0},{2,1},{5,6},{6,7},{9,8},{10,9},{13,14},{14,15},{17,16},{18,1... | collective-permute-start | bytes 786440 | tf_op jit(solution)/shard_map/ppermute | solution.py:486
  39.6 12.4 %collective-permute-start.9 = (bf16[128,1024]{1,0:T(8,128)(2,1)S(1)}, bf16[128,1024]{1,0:T(8,128)(2,1)S(1)}, u32[]{:S(2)}, u32[]{:S(2)}) collective-permute-start(bf16[128,1024]{1,0:T(8,128)(2,1)S(1)} %collective-permute-done.5.later_hi), channel_id=1, source_target_pairs={{1,2},{2,3},{5,4},{6,5},{9,10},{10,11},{13,12},{14,13},{17,18},{18... | collective-permute-start | bytes 786440 | tf_op jit(solution)/shard_map/ppermute | solution.py:487

commit v10 on v7

--- a/solution.py
+++ b/solution.py
@@ -50,9 +50,7 @@
         at = slice((k + 1) * cells, (k + 2) * cells)
         send_ref[:, at] = dot(place, state_ref[k]).astype(BF16)
     none = jnp.zeros((1, slots), jnp.int32)
-    rows = [lists_ref[f] + 1 for f in range(FACES)] + [none] * (8 - FACES)
-    odd = lax.rem(lax.axis_index("group"), 2) == 1
-    rows[4], rows[5] = jnp.where(odd, rows[5], rows[4]), jnp.where(odd, rows[4], rows[5])
+    rows = [lists_ref[f] + 1 for f in (0, 1, 2, 3, 5, 4)] + [none] * (8 - FACES)
     lists_out[...] = jnp.concatenate(rows, 0)
 
 
@@ -411,10 +409,18 @@
     groups = lax.axis_size("group")
     members = lax.axis_size("member")
     along = ("group", "member")
-    up = [[(g * members + i, g * members + i + 1) for i in range(members - 1)] for g in range(groups)]
-    down = [[(target, source) for source, target in pairs] for pairs in up]
-    one = [pair for g in range(groups) for pair in (down if g % 2 else up)[g]]
-    two = [pair for g in range(groups) for pair in (up if g % 2 else down)[g]]
+
+    def pairs(shift, ends):
+        inside = range(members) if ends else range(1, members - 1)
+        return [
+            (g * members + i, g * members + i + shift)
+            for g in range(groups)
+            for i in inside
+            if 0 <= i + shift < members
+        ]
+
+    one, two = pairs(-1, True), pairs(1, True)
+    one_on, two_on = pairs(-1, False), pairs(1, False)
     slots, species, cells = state.shape[2:]
     capacity = slots // groups
     cuts = (species - species // 2, species // 2)
@@ -475,8 +481,8 @@
     )
     got_lo.append(lax.ppermute(later, along, one))
     got_hi.append(lax.ppermute(later, along, two))
-    got_lo2 = [lax.ppermute(part, along, one) for part in got_lo]
-    got_hi2 = [lax.ppermute(part, along, two) for part in got_hi]
+    got_lo2 = [lax.ppermute(part, along, one_on) for part in got_lo]
+    got_hi2 = [lax.ppermute(part, along, two_on) for part in got_hi]
 
     z_natural, total, coefs, *numbers = call(
         functools.partial(both_kernel, cuts),

time: 53.4 us -> 53.1 us (level)
  the two profiles are of different devices: /device:TPU:0 before, /device:TPU:26 now
where the time goes in v10:
time: 53.1 us; the launch traced here: 52.7 us
  starting transfers between devices  21.5 us (40%)
  waiting for transfers between devices  18.1 us (34%)
  Pallas kernels  12.9 us (24%)
    pallas_call x6, Pallas kernels, call(): pl.pallas_call(kernel, out_shape=out_shape, grid=grid, in_specs=[specs.ge...  12.9 us
    ppermute x1, starting transfers between devices, per_device(): got_lo.append(lax.ppermute(later, along, one))  4.56 us
    ppermute x2, waiting for transfers between devices, per_device(): got_hi2 = [lax.ppermute(part, along, two_on) for part in got_hi]  4.52 us
    all_to_all x1, starting transfers between devices, per_device(): lax.all_to_all(send, 'group', split_axis=0, concat_axis=0, tiled=True)  4.39 us
    ppermute x1, waiting for transfers between devices, per_device(): lists_hi = lax.ppermute(lists, along, two)  4.19 us
    ppermute x1, waiting for transfers between devices, per_device(): got_hi = [lax.ppermute(soon, along, two)]  3.7 us
    ppermute x1, waiting for transfers between devices, per_device(): got_hi.append(lax.ppermute(later, along, two))  3.63 us
    ppermute x2, starting transfers between devices, per_device(): got_hi2 = [lax.ppermute(part, along, two_on) for part in got_hi]  2.56 us
  transfers between devices with their start and end apart: 11, of which 7 were waited for; matrix products, arithmetic and copies ran while one was open for 0% of the time, Pallas kernels for 17%

profile of v10, /device:TPU:26, one launch (start us, length us, event | category | flops | bytes accessed | tf_op | source)
XLA Modules:
  0.0 52.7 jit_solution(604428709704985943)
XLA Ops:
  0.0 2.4 %shard_map.55 = (bf16[128,2560]{1,0:T(8,128)(2,1)}, s32[8,128]{1,0:T(8,128)}) custom-call(s32[1,128]{1,0:T(1,128)} %bitcast.18, s32[6,1,128]{2,1,0:T(1,128)} %bitcast.17, bf16[9,128,256]{2,1,0:T(8,128)(2,1)} %bitcast.15, bf16[128,256]{1,0:T(8,128)(2,1)} %bitcast.16), custom_call_target="tpu_custom_call" | custom-call | bytes 1318400 | tf_op jit(solution)/shard_map/pallas_call | solution.py:396
  2.4 0.0 copy-start
  2.4 0.0 copy-start.1
  2.4 4.4 %all-to-all-start = ((bf16[8,16,2560]{2,1,0:T(8,128)(2,1)}), bf16[8,16,2560]{2,1,0:T(8,128)(2,1)S(1)}, u32[]{:S(2)}, u32[]{:S(2)}) async-start(bf16[8,16,2560]{2,1,0:T(8,128)(2,1)} %bitcast.14), calls=%async_computation | async-start | bytes 1310720 | tf_op jit(solution)/shard_map/all_to_all | solution.py:448
  6.8 0.0 copy-done
  6.8 2.3 %collective-permute-start = (s32[8,128]{1,0:T(8,128)S(1)}, s32[8,128]{1,0:T(8,128)S(1)}, u32[]{:S(2)}, u32[]{:S(2)}) collective-permute-start(s32[8,128]{1,0:T(8,128)S(1)} %copy-done), channel_id=1, source_target_pairs={{1,0},{2,1},{3,2},{5,4},{6,5},{7,6},{9,8},{10,9},{11,10},{13,12},{... | collective-permute-start | bytes 12296 | tf_op jit(solution)/shard_map/ppermute | solution.py:449
  9.1 1.3 %collective-permute-start.1 = (s32[8,128]{1,0:T(8,128)S(1)}, s32[8,128]{1,0:T(8,128)S(1)}, u32[]{:S(2)}, u32[]{:S(2)}) collective-permute-start(s32[8,128]{1,0:T(8,128)S(1)} %copy-done), channel_id=1, source_target_pairs={{0,1},{1,2},{2,3},{4,5},{5,6},{6,7},{8,9},{9,10},{10,11},{12,13},{... | collective-permute-start | bytes 12296 | tf_op jit(solution)/shard_map/ppermute | solution.py:450
  10.4 0.0 collective-permute-done.lists_lo
  10.4 4.2 %collective-permute-done.1.lists_hi = s32[8,128]{1,0:T(8,128)S(1)} collective-permute-done((s32[8,128]{1,0:T(8,128)S(1)}, s32[8,128]{1,0:T(8,128)S(1)}, u32[]{:S(2)}, u32[]{:S(2)}) %collective-permute-start.1) | collective-permute-done | bytes 4128 | tf_op jit(solution)/shard_map/ppermute | solution.py:450
  14.6 0.1 shard_map.56
  14.7 1.7 %all-to-all-done = bf16[8,16,2560]{2,1,0:T(8,128)(2,1)S(1)} async-done(((bf16[8,16,2560]{2,1,0:T(8,128)(2,1)}), bf16[8,16,2560]{2,1,0:T(8,128)(2,1)S(1)}, u32[]{:S(2)}, u32[]{:S(2)}) %all-to-all-start) | async-done | bytes 655392 | tf_op jit(solution)/shard_map/all_to_all | solution.py:448
  16.5 2.4 %collective-permute-start.2 = (bf16[128,1536]{1,0:T(8,128)(2,1)S(1)}, bf16[128,1536]{1,0:T(8,128)(2,1)S(1)}, u32[]{:S(2)}, u32[]{:S(2)}) collective-permute-start(bf16[128,1536]{1,0:T(8,128)(2,1)S(1)} %slice.6), channel_id=1, source_target_pairs={{1,0},{2,1},{3,2},{5,4},{6,5},{7,6},{9,8},{10,9},{11,10},{13,12},{... | collective-permute-start | bytes 1179656 | tf_op jit(solution)/shard_map/ppermute | solution.py:463
  18.9 1.3 %collective-permute-start.3 = (bf16[128,1536]{1,0:T(8,128)(2,1)S(1)}, bf16[128,1536]{1,0:T(8,128)(2,1)S(1)}, u32[]{:S(2)}, u32[]{:S(2)}) collective-permute-start(bf16[128,1536]{1,0:T(8,128)(2,1)S(1)} %slice.6), channel_id=1, source_target_pairs={{0,1},{1,2},{2,3},{4,5},{5,6},{6,7},{8,9},{9,10},{10,11},{12,13},{... | collective-permute-start | bytes 1179656 | tf_op jit(solution)/shard_map/ppermute | solution.py:464
  20.2 0.0 copy-done.1
  20.2 1.9 %shard_map.57 = (f32[256,128]{1,0:T(8,128)S(1)}, f32[4,256,128]{2,1,0:T(8,128)S(1)}, bf16[9,256,128]{2,1,0:T(8,128)(2,1)S(1)}, f32[9,256,128]{2,1,0:T(8,128)S(1)}, f32[9,256,128]{2,1,0:T(8,128)S(1)}) custom-call(f32[9]{0:T(128)S(1)} %copy-done.1, bf16[128,2560]{1,0:T(8,128)(2,1)S(1)} %bitcast.13, bf16[6,128,128]{2,1,0:T(8,128)(2,1)S(1)} %get-tuple-element.42.pick_ref.pick0), custom_call_target="tpu_custom_call" | custom-call | flops 500000000 | bytes 4456484 | tf_op jit(solution)/shard_map/pallas_call | solution.py:396
  22.1 4.6 %collective-permute-start.4 = (bf16[128,1024]{1,0:T(8,128)(2,1)S(1)}, bf16[128,1024]{1,0:T(8,128)(2,1)S(1)}, u32[]{:S(2)}, u32[]{:S(2)}) collective-permute-start(bf16[128,1024]{1,0:T(8,128)(2,1)S(1)} %slice.7), channel_id=1, source_target_pairs={{1,0},{2,1},{3,2},{5,4},{6,5},{7,6},{9,8},{10,9},{11,10},{13,12},{... | collective-permute-start | bytes 786440 | tf_op jit(solution)/shard_map/ppermute | solution.py:482
  26.7 1.3 %collective-permute-start.5 = (bf16[128,1024]{1,0:T(8,128)(2,1)S(1)}, bf16[128,1024]{1,0:T(8,128)(2,1)S(1)}, u32[]{:S(2)}, u32[]{:S(2)}) collective-permute-start(bf16[128,1024]{1,0:T(8,128)(2,1)S(1)} %slice.7), channel_id=1, source_target_pairs={{0,1},{1,2},{2,3},{4,5},{5,6},{6,7},{8,9},{9,10},{10,11},{12,13},{... | collective-permute-start | bytes 786440 | tf_op jit(solution)/shard_map/ppermute | solution.py:483
  28.0 0.4 collective-permute-done.2.got_lo
  28.3 0.7 %collective-permute-start.6 = (bf16[128,1536]{1,0:T(8,128)(2,1)S(1)}, bf16[128,1536]{1,0:T(8,128)(2,1)S(1)}, u32[]{:S(2)}, u32[]{:S(2)}) collective-permute-start(bf16[128,1536]{1,0:T(8,128)(2,1)S(1)} %collective-permute-done.2.got_lo), channel_id=1, source_target_pairs={{1,0},{2,1},{5,4},{6,5},{9,8},{10,9},{13,12},{14,13},{17,16},{18,1... | collective-permute-start | bytes 1179656 | tf_op jit(solution)/shard_map/ppermute | solution.py:484
  29.0 3.7 %collective-permute-done.3.got_hi = bf16[128,1536]{1,0:T(8,128)(2,1)S(1)} collective-permute-done((bf16[128,1536]{1,0:T(8,128)(2,1)S(1)}, bf16[128,1536]{1,0:T(8,128)(2,1)S(1)}, u32[]{:S(2)}, u32[]{:S(2)}) %collective-permute-start.3) | collective-permute-done | bytes 393248 | tf_op jit(solution)/shard_map/ppermute | solution.py:464
  32.7 1.3 %collective-permute-start.7 = (bf16[128,1536]{1,0:T(8,128)(2,1)S(1)}, bf16[128,1536]{1,0:T(8,128)(2,1)S(1)}, u32[]{:S(2)}, u32[]{:S(2)}) collective-permute-start(bf16[128,1536]{1,0:T(8,128)(2,1)S(1)} %collective-permute-done.3.got_hi), channel_id=1, source_target_pairs={{1,2},{2,3},{5,6},{6,7},{9,10},{10,11},{13,14},{14,15},{17,18},{18... | collective-permute-start | bytes 1179656 | tf_op jit(solution)/shard_map/ppermute | solution.py:485
  34.0 0.0 collective-permute-done.4.later_lo
  34.0 0.7 %collective-permute-start.8 = (bf16[128,1024]{1,0:T(8,128)(2,1)S(1)}, bf16[128,1024]{1,0:T(8,128)(2,1)S(1)}, u32[]{:S(2)}, u32[]{:S(2)}) collective-permute-start(bf16[128,1024]{1,0:T(8,128)(2,1)S(1)} %collective-permute-done.4.later_lo), channel_id=1, source_target_pairs={{1,0},{2,1},{5,4},{6,5},{9,8},{10,9},{13,12},{14,13},{17,16},{18,1... | collective-permute-start | bytes 786440 | tf_op jit(solution)/shard_map/ppermute | solution.py:484
  34.7 3.6 %collective-permute-done.5.later_hi = bf16[128,1024]{1,0:T(8,128)(2,1)S(1)} collective-permute-done((bf16[128,1024]{1,0:T(8,128)(2,1)S(1)}, bf16[128,1024]{1,0:T(8,128)(2,1)S(1)}, u32[]{:S(2)}, u32[]{:S(2)}) %collective-permute-start.5) | collective-permute-done | bytes 262176 | tf_op jit(solution)/shard_map/ppermute | solution.py:483
  38.3 1.3 %collective-permute-start.9 = (bf16[128,1024]{1,0:T(8,128)(2,1)S(1)}, bf16[128,1024]{1,0:T(8,128)(2,1)S(1)}, u32[]{:S(2)}, u32[]{:S(2)}) collective-permute-start(bf16[128,1024]{1,0:T(8,128)(2,1)S(1)} %collective-permute-done.5.later_hi), channel_id=1, source_target_pairs={{1,2},{2,3},{5,6},{6,7},{9,10},{10,11},{13,14},{14,15},{17,18},{18... | collective-permute-start | bytes 786440 | tf_op jit(solution)/shard_map/ppermute | solution.py:485
  39.6 4.9 %shard_map.58 = (f32[2,256,128]{2,1,0:T(8,128)S(1)}, f32[2,256,128]{2,1,0:T(8,128)S(1)}, f32[2,256,128]{2,1,0:T(8,128)S(1)}, f32[9,256,128]{2,1,0:T(8,128)S(1)},...) custom-call(f32[9]{0:T(128)S(1)} %copy-done.1, ...), custom_call_target="tpu_custom_call" | custom-call | flops 1800000000 | bytes 11010084 | tf_op jit(solution)/shard_map/pallas_call | solution.py:396
  44.6 0.0 collective-permute-done.6.got_lo2
  44.6 2.2 %collective-permute-done.7.got_hi2 = bf16[128,1536]{1,0:T(8,128)(2,1)S(1)} collective-permute-done((bf16[128,1536]{1,0:T(8,128)(2,1)S(1)}, bf16[128,1536]{1,0:T(8,128)(2,1)S(1)}, u32[]{:S(2)}, u32[]{:S(2)}) %collective-permute-start.7) | collective-permute-done | bytes 393248 | tf_op jit(solution)/shard_map/ppermute | solution.py:485
  46.8 2.1 %shard_map.59 = (bf16[256,256]{1,0:T(8,128)(2,1)S(1)}, bf16[2,256,128]{2,1,0:T(8,128)(2,1)S(1)}, f32[2,4,256,128]{3,2,1,0:T(8,128)S(1)}, f32[2,4,256,128]{3,2,1,0:T(8,128)S(1)}, f32[5,128,256]{2,1,0:T(8,128)S(1)}) custom-call(f32[9]{0:T(128)S(1)} %copy-done.1, bf16[6,128,128]{2,1,0:T(8,128)(2,1)S(1)} %get-tuple-element.42.pick_ref.pick0, ...), custom_call_target="tpu_custom_call" | custom-call | flops 500000000 | bytes 9633828 | tf_op jit(solution)/shard_map/pallas_call | solution.py:396
  48.9 0.0 collective-permute-done.8.later_lo2
  48.9 2.4 %collective-permute-done.9.later_hi2 = bf16[128,1024]{1,0:T(8,128)(2,1)S(1)} collective-permute-done((bf16[128,1024]{1,0:T(8,128)(2,1)S(1)}, bf16[128,1024]{1,0:T(8,128)(2,1)S(1)}, u32[]{:S(2)}, u32[]{:S(2)}) %collective-permute-start.9) | collective-permute-done | bytes 262176 | tf_op jit(solution)/shard_map/ppermute | solution.py:485
  51.3 1.4 %shard_map.60 = f32[9,128,256]{2,1,0:T(8,128)} custom-call(bf16[256,256]{1,0:T(8,128)(2,1)S(1)} %get-tuple-element.64.far_ref, bf16[2,256,128]{2,1,0:T(8,128)(2,1)S(1)} %get-tuple-element.65.two_ref, f32[2,4,256,128]{3,2,1,0:T(8,128)S(1)} %get-tuple-element.66.offset_ref, f32[2,4,256,128]{3,2,1,0:T(8,128)S(1)} %get-tuple-element.67.slope_ref, ...), custom_call_target="tpu_custom_call" | custom-call | flops 400000000 | bytes 7340032 | tf_op jit(solution)/shard_map/pallas_call | solution.py:396
  (2 shorter events, 0.0 us)
Async XLA Ops:
  2.4 4.4 %copy-start = (s32[8,128]{1,0:T(8,128)S(1)}, s32[8,128]{1,0:T(8,128)}, u32[]{:S(2)}) copy-start(s32[8,128]{1,0:T(8,128)} %get-tuple-element.38.lists0) | copy-start | bytes 12292
  2.4 17.8 %copy-start.1 = (f32[9]{0:T(128)S(1)}, f32[9]{0:T(128)}, u32[]{:S(2)}) copy-start(f32[9]{0:T(128)} %lewis_ref.5) | copy-start | bytes 112
  2.4 14.1 %all-to-all-start = ((bf16[8,16,2560]{2,1,0:T(8,128)(2,1)}), bf16[8,16,2560]{2,1,0:T(8,128)(2,1)S(1)}, u32[]{:S(2)}, u32[]{:S(2)}) async-start(bf16[8,16,2560]{2,1,0:T(8,128)(2,1)} %bitcast.14), calls=%async_computation | async-start | bytes 1310720 | tf_op jit(solution)/shard_map/all_to_all | solution.py:448
  6.8 3.7 %collective-permute-start = (s32[8,128]{1,0:T(8,128)S(1)}, s32[8,128]{1,0:T(8,128)S(1)}, u32[]{:S(2)}, u32[]{:S(2)}) collective-permute-start(s32[8,128]{1,0:T(8,128)S(1)} %copy-done), channel_id=1, source_target_pairs={{1,0},{2,1},{3,2},{5,4},{6,5},{7,6},{9,8},{10,9},{11,10},{13,12},{... | collective-permute-start | bytes 12296 | tf_op jit(solution)/shard_map/ppermute | solution.py:449
  9.1 5.5 %collective-permute-start.1 = (s32[8,128]{1,0:T(8,128)S(1)}, s32[8,128]{1,0:T(8,128)S(1)}, u32[]{:S(2)}, u32[]{:S(2)}) collective-permute-start(s32[8,128]{1,0:T(8,128)S(1)} %copy-done), channel_id=1, source_target_pairs={{0,1},{1,2},{2,3},{4,5},{5,6},{6,7},{8,9},{9,10},{10,11},{12,13},{... | collective-permute-start | bytes 12296 | tf_op jit(solution)/shard_map/ppermute | solution.py:450
  16.5 11.8 %collective-permute-start.2 = (bf16[128,1536]{1,0:T(8,128)(2,1)S(1)}, bf16[128,1536]{1,0:T(8,128)(2,1)S(1)}, u32[]{:S(2)}, u32[]{:S(2)}) collective-permute-start(bf16[128,1536]{1,0:T(8,128)(2,1)S(1)} %slice.6), channel_id=1, source_target_pairs={{1,0},{2,1},{3,2},{5,4},{6,5},{7,6},{9,8},{10,9},{11,10},{13,12},{... | collective-permute-start | bytes 1179656 | tf_op jit(solution)/shard_map/ppermute | solution.py:463
  18.9 13.8 %collective-permute-start.3 = (bf16[128,1536]{1,0:T(8,128)(2,1)S(1)}, bf16[128,1536]{1,0:T(8,128)(2,1)S(1)}, u32[]{:S(2)}, u32[]{:S(2)}) collective-permute-start(bf16[128,1536]{1,0:T(8,128)(2,1)S(1)} %slice.6), channel_id=1, source_target_pairs={{0,1},{1,2},{2,3},{4,5},{5,6},{6,7},{8,9},{9,10},{10,11},{12,13},{... | collective-permute-start | bytes 1179656 | tf_op jit(solution)/shard_map/ppermute | solution.py:464
  22.1 11.9 %collective-permute-start.4 = (bf16[128,1024]{1,0:T(8,128)(2,1)S(1)}, bf16[128,1024]{1,0:T(8,128)(2,1)S(1)}, u32[]{:S(2)}, u32[]{:S(2)}) collective-permute-start(bf16[128,1024]{1,0:T(8,128)(2,1)S(1)} %slice.7), channel_id=1, source_target_pairs={{1,0},{2,1},{3,2},{5,4},{6,5},{7,6},{9,8},{10,9},{11,10},{13,12},{... | collective-permute-start | bytes 786440 | tf_op jit(solution)/shard_map/ppermute | solution.py:482
  26.7 11.7 %collective-permute-start.5 = (bf16[128,1024]{1,0:T(8,128)(2,1)S(1)}, bf16[128,1024]{1,0:T(8,128)(2,1)S(1)}, u32[]{:S(2)}, u32[]{:S(2)}) collective-permute-start(bf16[128,1024]{1,0:T(8,128)(2,1)S(1)} %slice.7), channel_id=1, source_target_pairs={{0,1},{1,2},{2,3},{4,5},{5,6},{6,7},{8,9},{9,10},{10,11},{12,13},{... | collective-permute-start | bytes 786440 | tf_op jit(solution)/shard_map/ppermute | solution.py:483
  28.3 16.2 %collective-permute-start.6 = (bf16[128,1536]{1,0:T(8,128)(2,1)S(1)}, bf16[128,1536]{1,0:T(8,128)(2,1)S(1)}, u32[]{:S(2)}, u32[]{:S(2)}) collective-permute-start(bf16[128,1536]{1,0:T(8,128)(2,1)S(1)} %collective-permute-done.2.got_lo), channel_id=1, source_target_pairs={{1,0},{2,1},{5,4},{6,5},{9,8},{10,9},{13,12},{14,13},{17,16},{18,1... | collective-permute-start | bytes 1179656 | tf_op jit(solution)/shard_map/ppermute | solution.py:484
  32.7 14.0 %collective-permute-start.7 = (bf16[128,1536]{1,0:T(8,128)(2,1)S(1)}, bf16[128,1536]{1,0:T(8,128)(2,1)S(1)}, u32[]{:S(2)}, u32[]{:S(2)}) collective-permute-start(bf16[128,1536]{1,0:T(8,128)(2,1)S(1)} %collective-permute-done.3.got_hi), channel_id=1, source_target_pairs={{1,2},{2,3},{5,6},{6,7},{9,10},{10,11},{13,14},{14,15},{17,18},{18... | collective-permute-start | bytes 1179656 | tf_op jit(solution)/shard_map/ppermute | solution.py:485
  34.0 14.9 %collective-permute-start.8 = (bf16[128,1024]{1,0:T(8,128)(2,1)S(1)}, bf16[128,1024]{1,0:T(8,128)(2,1)S(1)}, u32[]{:S(2)}, u32[]{:S(2)}) collective-permute-start(bf16[128,1024]{1,0:T(8,128)(2,1)S(1)} %collective-permute-done.4.later_lo), channel_id=1, source_target_pairs={{1,0},{2,1},{5,4},{6,5},{9,8},{10,9},{13,12},{14,13},{17,16},{18,1... | collective-permute-start | bytes 786440 | tf_op jit(solution)/shard_map/ppermute | solution.py:484
  38.3 12.9 %collective-permute-start.9 = (bf16[128,1024]{1,0:T(8,128)(2,1)S(1)}, bf16[128,1024]{1,0:T(8,128)(2,1)S(1)}, u32[]{:S(2)}, u32[]{:S(2)}) collective-permute-start(bf16[128,1024]{1,0:T(8,128)(2,1)S(1)} %collective-permute-done.5.later_hi), channel_id=1, source_target_pairs={{1,2},{2,3},{5,6},{6,7},{9,10},{10,11},{13,14},{14,15},{17,18},{18... | collective-permute-start | bytes 786440 | tf_op jit(solution)/shard_map/ppermute | solution.py:485

commit v11 on v9

--- a/solution.py
+++ b/solution.py
@@ -35,6 +35,10 @@
     return jnp.where(mask, 1.0, 0.0).astype(BF16)
 
 
+def up_first(group):
+    return group % 4 == 2
+
+
 def pack_kernel(groups, capacity, dest_ref, lists_ref, state_ref, coef_ref, send_ref, lists_out):
     species, slots, cells = state_ref.shape
     dest = dest_ref[...]
@@ -51,8 +55,8 @@
         send_ref[:, at] = dot(place, state_ref[k]).astype(BF16)
     none = jnp.zeros((1, slots), jnp.int32)
     rows = [lists_ref[f] + 1 for f in range(FACES)] + [none] * (8 - FACES)
-    even = lax.rem(lax.axis_index("group"), 2) == 0
-    rows[4], rows[5] = jnp.where(even, rows[5], rows[4]), jnp.where(even, rows[4], rows[5])
+    same = up_first(lax.axis_index("group"))
+    rows[4], rows[5] = jnp.where(same, rows[4], rows[5]), jnp.where(same, rows[5], rows[4])
     lists_out[...] = jnp.concatenate(rows, 0)
 
 
@@ -412,17 +416,17 @@
     members = lax.axis_size("member")
     along = ("group", "member")
 
-    def pairs(upward, ends):
+    def pairs(turn, ends):
         steps = []
         for g in range(groups):
-            for i in range(0 if ends else 1, members if ends else members - 1):
-                target = i + 1 if upward == (g % 2 == 1) else i - 1
-                if 0 <= target < members:
-                    steps.append((g * members + i, g * members + target))
+            shift = 1 if up_first(g) == (turn == 0) else -1
+            for i in range(members) if ends else range(1, members - 1):
+                if 0 <= i + shift < members:
+                    steps.append((g * members + i, g * members + i + shift))
         return steps
 
-    one, two = pairs(True, True), pairs(False, True)
-    one_on, two_on = pairs(True, False), pairs(False, False)
+    one, two = pairs(0, True), pairs(1, True)
+    one_on, two_on = pairs(0, False), pairs(1, False)
     slots, species, cells = state.shape[2:]
     capacity = slots // groups
     cuts = (species - species // 2, species // 2)

time: 53.9 us -> 52 us (0.965)
  the two profiles are of different devices: /device:TPU:0 before, /device:TPU:2 now
where the time goes in v11:
time: 52 us; the launch traced here: 51.5 us
  starting transfers between devices  23.7 us (46%)
  waiting for transfers between devices  14.8 us (28%)
  Pallas kernels  12.9 us (25%)
    pallas_call x6, Pallas kernels, call(): pl.pallas_call(kernel, out_shape=out_shape, grid=grid, in_specs=[specs.ge...  12.9 us
    ppermute x1, starting transfers between devices, per_device(): got_lo.append(lax.ppermute(later, along, one))  4.57 us
    all_to_all x1, starting transfers between devices, per_device(): lax.all_to_all(send, 'group', split_axis=0, concat_axis=0, tiled=True)  4.38 us
    ppermute x1, waiting for transfers between devices, per_device(): lists_hi = lax.ppermute(lists, along, two)  4.19 us
    ppermute x1, starting transfers between devices, per_device(): got_lo = [lax.ppermute(soon, along, one)]  3.51 us
    ppermute x1, starting transfers between devices, per_device(): lists_lo = lax.ppermute(lists, along, one)  3.47 us
    ppermute x1, waiting for transfers between devices, per_device(): got_hi.append(lax.ppermute(later, along, two))  3.41 us
    ppermute x2, waiting for transfers between devices, per_device(): got_hi2 = [lax.ppermute(part, along, two_on) for part in got_hi]  3.1 us
  transfers between devices with their start and end apart: 11, of which 7 were waited for; matrix products, arithmetic and copies ran while one was open for 0% of the time, Pallas kernels for 18%

profile of v11, /device:TPU:2, one launch (start us, length us, event | category | flops | bytes accessed | tf_op | source)
XLA Modules:
  0.0 51.5 jit_solution(13533158063169971457)
XLA Ops:
  0.0 2.4 %shard_map.55 = (bf16[128,2560]{1,0:T(8,128)(2,1)}, s32[8,128]{1,0:T(8,128)}) custom-call(s32[1,128]{1,0:T(1,128)} %bitcast.18, s32[6,1,128]{2,1,0:T(1,128)} %bitcast.17, bf16[9,128,256]{2,1,0:T(8,128)(2,1)} %bitcast.15, bf16[128,256]{1,0:T(8,128)(2,1)} %bitcast.16), custom_call_target="tpu_custom_call" | custom-call | bytes 1318400 | tf_op jit(solution)/shard_map/pallas_call | solution.py:402
  2.4 0.0 copy-start
  2.4 0.0 copy-start.1
  2.4 4.4 %all-to-all-start = ((bf16[8,16,2560]{2,1,0:T(8,128)(2,1)}), bf16[8,16,2560]{2,1,0:T(8,128)(2,1)S(1)}, u32[]{:S(2)}, u32[]{:S(2)}) async-start(bf16[8,16,2560]{2,1,0:T(8,128)(2,1)} %bitcast.14), calls=%async_computation | async-start | bytes 1310720 | tf_op jit(solution)/shard_map/all_to_all | solution.py:454
  6.8 0.0 copy-done
  6.8 3.5 %collective-permute-start = (s32[8,128]{1,0:T(8,128)S(1)}, s32[8,128]{1,0:T(8,128)S(1)}, u32[]{:S(2)}, u32[]{:S(2)}) collective-permute-start(s32[8,128]{1,0:T(8,128)S(1)} %copy-done), channel_id=1, source_target_pairs={{1,0},{2,1},{3,2},{5,4},{6,5},{7,6},{8,9},{9,10},{10,11},{13,12},{... | collective-permute-start | bytes 12296 | tf_op jit(solution)/shard_map/ppermute | solution.py:455
  10.3 1.3 %collective-permute-start.1 = (s32[8,128]{1,0:T(8,128)S(1)}, s32[8,128]{1,0:T(8,128)S(1)}, u32[]{:S(2)}, u32[]{:S(2)}) collective-permute-start(s32[8,128]{1,0:T(8,128)S(1)} %copy-done), channel_id=1, source_target_pairs={{0,1},{1,2},{2,3},{4,5},{5,6},{6,7},{9,8},{10,9},{11,10},{12,13},{... | collective-permute-start | bytes 12296 | tf_op jit(solution)/shard_map/ppermute | solution.py:456
  11.6 0.0 collective-permute-done.lists_lo
  11.6 4.2 %collective-permute-done.1.lists_hi = s32[8,128]{1,0:T(8,128)S(1)} collective-permute-done((s32[8,128]{1,0:T(8,128)S(1)}, s32[8,128]{1,0:T(8,128)S(1)}, u32[]{:S(2)}, u32[]{:S(2)}) %collective-permute-start.1) | collective-permute-done | bytes 4128 | tf_op jit(solution)/shard_map/ppermute | solution.py:456
  15.8 0.1 shard_map.56
  15.9 0.6 %all-to-all-done = bf16[8,16,2560]{2,1,0:T(8,128)(2,1)S(1)} async-done(((bf16[8,16,2560]{2,1,0:T(8,128)(2,1)}), bf16[8,16,2560]{2,1,0:T(8,128)(2,1)S(1)}, u32[]{:S(2)}, u32[]{:S(2)}) %all-to-all-start) | async-done | bytes 655392 | tf_op jit(solution)/shard_map/all_to_all | solution.py:454
  16.5 3.5 %collective-permute-start.2 = (bf16[128,1536]{1,0:T(8,128)(2,1)S(1)}, bf16[128,1536]{1,0:T(8,128)(2,1)S(1)}, u32[]{:S(2)}, u32[]{:S(2)}) collective-permute-start(bf16[128,1536]{1,0:T(8,128)(2,1)S(1)} %slice.6), channel_id=1, source_target_pairs={{1,0},{2,1},{3,2},{5,4},{6,5},{7,6},{8,9},{9,10},{10,11},{13,12},{... | collective-permute-start | bytes 1179656 | tf_op jit(solution)/shard_map/ppermute | solution.py:469
  20.0 1.3 %collective-permute-start.3 = (bf16[128,1536]{1,0:T(8,128)(2,1)S(1)}, bf16[128,1536]{1,0:T(8,128)(2,1)S(1)}, u32[]{:S(2)}, u32[]{:S(2)}) collective-permute-start(bf16[128,1536]{1,0:T(8,128)(2,1)S(1)} %slice.6), channel_id=1, source_target_pairs={{0,1},{1,2},{2,3},{4,5},{5,6},{6,7},{9,8},{10,9},{11,10},{12,13},{... | collective-permute-start | bytes 1179656 | tf_op jit(solution)/shard_map/ppermute | solution.py:470
  21.3 0.0 copy-done.1
  21.4 1.9 %shard_map.57 = (f32[256,128]{1,0:T(8,128)S(1)}, f32[4,256,128]{2,1,0:T(8,128)S(1)}, bf16[9,256,128]{2,1,0:T(8,128)(2,1)S(1)}, f32[9,256,128]{2,1,0:T(8,128)S(1)}, f32[9,256,128]{2,1,0:T(8,128)S(1)}) custom-call(f32[9]{0:T(128)S(1)} %copy-done.1, bf16[128,2560]{1,0:T(8,128)(2,1)S(1)} %bitcast.13, bf16[6,128,128]{2,1,0:T(8,128)(2,1)S(1)} %get-tuple-element.42.pick_ref.pick0), custom_call_target="tpu_custom_call" | custom-call | flops 500000000 | bytes 4456484 | tf_op jit(solution)/shard_map/pallas_call | solution.py:402
  23.2 4.6 %collective-permute-start.4 = (bf16[128,1024]{1,0:T(8,128)(2,1)S(1)}, bf16[128,1024]{1,0:T(8,128)(2,1)S(1)}, u32[]{:S(2)}, u32[]{:S(2)}) collective-permute-start(bf16[128,1024]{1,0:T(8,128)(2,1)S(1)} %slice.7), channel_id=1, source_target_pairs={{1,0},{2,1},{3,2},{5,4},{6,5},{7,6},{8,9},{9,10},{10,11},{13,12},{... | collective-permute-start | bytes 786440 | tf_op jit(solution)/shard_map/ppermute | solution.py:488
  27.8 1.3 %collective-permute-start.5 = (bf16[128,1024]{1,0:T(8,128)(2,1)S(1)}, bf16[128,1024]{1,0:T(8,128)(2,1)S(1)}, u32[]{:S(2)}, u32[]{:S(2)}) collective-permute-start(bf16[128,1024]{1,0:T(8,128)(2,1)S(1)} %slice.7), channel_id=1, source_target_pairs={{0,1},{1,2},{2,3},{4,5},{5,6},{6,7},{9,8},{10,9},{11,10},{12,13},{... | collective-permute-start | bytes 786440 | tf_op jit(solution)/shard_map/ppermute | solution.py:489
  29.1 0.0 collective-permute-done.2.got_lo
  29.1 0.7 %collective-permute-start.6 = (bf16[128,1536]{1,0:T(8,128)(2,1)S(1)}, bf16[128,1536]{1,0:T(8,128)(2,1)S(1)}, u32[]{:S(2)}, u32[]{:S(2)}) collective-permute-start(bf16[128,1536]{1,0:T(8,128)(2,1)S(1)} %collective-permute-done.2.got_lo), channel_id=1, source_target_pairs={{1,0},{2,1},{5,4},{6,5},{9,10},{10,11},{13,12},{14,13},{17,16},{18... | collective-permute-start | bytes 1179656 | tf_op jit(solution)/shard_map/ppermute | solution.py:490
  29.8 1.2 %collective-permute-done.3.got_hi = bf16[128,1536]{1,0:T(8,128)(2,1)S(1)} collective-permute-done((bf16[128,1536]{1,0:T(8,128)(2,1)S(1)}, bf16[128,1536]{1,0:T(8,128)(2,1)S(1)}, u32[]{:S(2)}, u32[]{:S(2)}) %collective-permute-start.3) | collective-permute-done | bytes 393248 | tf_op jit(solution)/shard_map/ppermute | solution.py:470
  31.0 1.3 %collective-permute-start.7 = (bf16[128,1536]{1,0:T(8,128)(2,1)S(1)}, bf16[128,1536]{1,0:T(8,128)(2,1)S(1)}, u32[]{:S(2)}, u32[]{:S(2)}) collective-permute-start(bf16[128,1536]{1,0:T(8,128)(2,1)S(1)} %collective-permute-done.3.got_hi), channel_id=1, source_target_pairs={{1,2},{2,3},{5,6},{6,7},{9,8},{10,9},{13,14},{14,15},{17,18},{18,1... | collective-permute-start | bytes 1179656 | tf_op jit(solution)/shard_map/ppermute | solution.py:491
  32.3 2.2 %collective-permute-done.4.later_lo = bf16[128,1024]{1,0:T(8,128)(2,1)S(1)} collective-permute-done((bf16[128,1024]{1,0:T(8,128)(2,1)S(1)}, bf16[128,1024]{1,0:T(8,128)(2,1)S(1)}, u32[]{:S(2)}, u32[]{:S(2)}) %collective-permute-start.4) | collective-permute-done | bytes 262176 | tf_op jit(solution)/shard_map/ppermute | solution.py:488
  34.5 0.7 %collective-permute-start.8 = (bf16[128,1024]{1,0:T(8,128)(2,1)S(1)}, bf16[128,1024]{1,0:T(8,128)(2,1)S(1)}, u32[]{:S(2)}, u32[]{:S(2)}) collective-permute-start(bf16[128,1024]{1,0:T(8,128)(2,1)S(1)} %collective-permute-done.4.later_lo), channel_id=1, source_target_pairs={{1,0},{2,1},{5,4},{6,5},{9,10},{10,11},{13,12},{14,13},{17,16},{18... | collective-permute-start | bytes 786440 | tf_op jit(solution)/shard_map/ppermute | solution.py:490
  35.2 3.4 %collective-permute-done.5.later_hi = bf16[128,1024]{1,0:T(8,128)(2,1)S(1)} collective-permute-done((bf16[128,1024]{1,0:T(8,128)(2,1)S(1)}, bf16[128,1024]{1,0:T(8,128)(2,1)S(1)}, u32[]{:S(2)}, u32[]{:S(2)}) %collective-permute-start.5) | collective-permute-done | bytes 262176 | tf_op jit(solution)/shard_map/ppermute | solution.py:489
  38.6 1.3 %collective-permute-start.9 = (bf16[128,1024]{1,0:T(8,128)(2,1)S(1)}, bf16[128,1024]{1,0:T(8,128)(2,1)S(1)}, u32[]{:S(2)}, u32[]{:S(2)}) collective-permute-start(bf16[128,1024]{1,0:T(8,128)(2,1)S(1)} %collective-permute-done.5.later_hi), channel_id=1, source_target_pairs={{1,2},{2,3},{5,6},{6,7},{9,8},{10,9},{13,14},{14,15},{17,18},{18,1... | collective-permute-start | bytes 786440 | tf_op jit(solution)/shard_map/ppermute | solution.py:491
  39.9 4.9 %shard_map.58 = (f32[2,256,128]{2,1,0:T(8,128)S(1)}, f32[2,256,128]{2,1,0:T(8,128)S(1)}, f32[2,256,128]{2,1,0:T(8,128)S(1)}, f32[9,256,128]{2,1,0:T(8,128)S(1)},...) custom-call(f32[9]{0:T(128)S(1)} %copy-done.1, ...), custom_call_target="tpu_custom_call" | custom-call | flops 1800000000 | bytes 11010084 | tf_op jit(solution)/shard_map/pallas_call | solution.py:402
  44.9 0.0 collective-permute-done.6.got_lo2
  44.9 2.3 %collective-permute-done.7.got_hi2 = bf16[128,1536]{1,0:T(8,128)(2,1)S(1)} collective-permute-done((bf16[128,1536]{1,0:T(8,128)(2,1)S(1)}, bf16[128,1536]{1,0:T(8,128)(2,1)S(1)}, u32[]{:S(2)}, u32[]{:S(2)}) %collective-permute-start.7) | collective-permute-done | bytes 393248 | tf_op jit(solution)/shard_map/ppermute | solution.py:491
  47.2 2.1 %shard_map.59 = (bf16[256,256]{1,0:T(8,128)(2,1)S(1)}, bf16[2,256,128]{2,1,0:T(8,128)(2,1)S(1)}, f32[2,4,256,128]{3,2,1,0:T(8,128)S(1)}, f32[2,4,256,128]{3,2,1,0:T(8,128)S(1)}, f32[5,128,256]{2,1,0:T(8,128)S(1)}) custom-call(f32[9]{0:T(128)S(1)} %copy-done.1, bf16[6,128,128]{2,1,0:T(8,128)(2,1)S(1)} %get-tuple-element.42.pick_ref.pick0, ...), custom_call_target="tpu_custom_call" | custom-call | flops 500000000 | bytes 9633828 | tf_op jit(solution)/shard_map/pallas_call | solution.py:402
  49.3 0.0 collective-permute-done.8.later_lo2
  49.3 0.8 %collective-permute-done.9.later_hi2 = bf16[128,1024]{1,0:T(8,128)(2,1)S(1)} collective-permute-done((bf16[128,1024]{1,0:T(8,128)(2,1)S(1)}, bf16[128,1024]{1,0:T(8,128)(2,1)S(1)}, u32[]{:S(2)}, u32[]{:S(2)}) %collective-permute-start.9) | collective-permute-done | bytes 262176 | tf_op jit(solution)/shard_map/ppermute | solution.py:491
  50.1 1.4 %shard_map.60 = f32[9,128,256]{2,1,0:T(8,128)} custom-call(bf16[256,256]{1,0:T(8,128)(2,1)S(1)} %get-tuple-element.64.far_ref, bf16[2,256,128]{2,1,0:T(8,128)(2,1)S(1)} %get-tuple-element.65.two_ref, f32[2,4,256,128]{3,2,1,0:T(8,128)S(1)} %get-tuple-element.66.offset_ref, f32[2,4,256,128]{3,2,1,0:T(8,128)S(1)} %get-tuple-element.67.slope_ref, ...), custom_call_target="tpu_custom_call" | custom-call | flops 400000000 | bytes 7340032 | tf_op jit(solution)/shard_map/pallas_call | solution.py:402
  (2 shorter events, 0.0 us)
Async XLA Ops:
  2.4 4.4 %copy-start = (s32[8,128]{1,0:T(8,128)S(1)}, s32[8,128]{1,0:T(8,128)}, u32[]{:S(2)}) copy-start(s32[8,128]{1,0:T(8,128)} %get-tuple-element.38.lists0) | copy-start | bytes 12292
  2.4 19.0 %copy-start.1 = (f32[9]{0:T(128)S(1)}, f32[9]{0:T(128)}, u32[]{:S(2)}) copy-start(f32[9]{0:T(128)} %lewis_ref.5) | copy-start | bytes 112
  2.4 14.1 %all-to-all-start = ((bf16[8,16,2560]{2,1,0:T(8,128)(2,1)}), bf16[8,16,2560]{2,1,0:T(8,128)(2,1)S(1)}, u32[]{:S(2)}, u32[]{:S(2)}) async-start(bf16[8,16,2560]{2,1,0:T(8,128)(2,1)} %bitcast.14), calls=%async_computation | async-start | bytes 1310720 | tf_op jit(solution)/shard_map/all_to_all | solution.py:454
  6.8 4.8 %collective-permute-start = (s32[8,128]{1,0:T(8,128)S(1)}, s32[8,128]{1,0:T(8,128)S(1)}, u32[]{:S(2)}, u32[]{:S(2)}) collective-permute-start(s32[8,128]{1,0:T(8,128)S(1)} %copy-done), channel_id=1, source_target_pairs={{1,0},{2,1},{3,2},{5,4},{6,5},{7,6},{8,9},{9,10},{10,11},{13,12},{... | collective-permute-start | bytes 12296 | tf_op jit(solution)/shard_map/ppermute | solution.py:455
  10.3 5.5 %collective-permute-start.1 = (s32[8,128]{1,0:T(8,128)S(1)}, s32[8,128]{1,0:T(8,128)S(1)}, u32[]{:S(2)}, u32[]{:S(2)}) collective-permute-start(s32[8,128]{1,0:T(8,128)S(1)} %copy-done), channel_id=1, source_target_pairs={{0,1},{1,2},{2,3},{4,5},{5,6},{6,7},{9,8},{10,9},{11,10},{12,13},{... | collective-permute-start | bytes 12296 | tf_op jit(solution)/shard_map/ppermute | solution.py:456
  16.5 12.6 %collective-permute-start.2 = (bf16[128,1536]{1,0:T(8,128)(2,1)S(1)}, bf16[128,1536]{1,0:T(8,128)(2,1)S(1)}, u32[]{:S(2)}, u32[]{:S(2)}) collective-permute-start(bf16[128,1536]{1,0:T(8,128)(2,1)S(1)} %slice.6), channel_id=1, source_target_pairs={{1,0},{2,1},{3,2},{5,4},{6,5},{7,6},{8,9},{9,10},{10,11},{13,12},{... | collective-permute-start | bytes 1179656 | tf_op jit(solution)/shard_map/ppermute | solution.py:469
  20.0 11.0 %collective-permute-start.3 = (bf16[128,1536]{1,0:T(8,128)(2,1)S(1)}, bf16[128,1536]{1,0:T(8,128)(2,1)S(1)}, u32[]{:S(2)}, u32[]{:S(2)}) collective-permute-start(bf16[128,1536]{1,0:T(8,128)(2,1)S(1)} %slice.6), channel_id=1, source_target_pairs={{0,1},{1,2},{2,3},{4,5},{5,6},{6,7},{9,8},{10,9},{11,10},{12,13},{... | collective-permute-start | bytes 1179656 | tf_op jit(solution)/shard_map/ppermute | solution.py:470
  23.2 11.3 %collective-permute-start.4 = (bf16[128,1024]{1,0:T(8,128)(2,1)S(1)}, bf16[128,1024]{1,0:T(8,128)(2,1)S(1)}, u32[]{:S(2)}, u32[]{:S(2)}) collective-permute-start(bf16[128,1024]{1,0:T(8,128)(2,1)S(1)} %slice.7), channel_id=1, source_target_pairs={{1,0},{2,1},{3,2},{5,4},{6,5},{7,6},{8,9},{9,10},{10,11},{13,12},{... | collective-permute-start | bytes 786440 | tf_op jit(solution)/shard_map/ppermute | solution.py:488
  27.8 10.8 %collective-permute-start.5 = (bf16[128,1024]{1,0:T(8,128)(2,1)S(1)}, bf16[128,1024]{1,0:T(8,128)(2,1)S(1)}, u32[]{:S(2)}, u32[]{:S(2)}) collective-permute-start(bf16[128,1024]{1,0:T(8,128)(2,1)S(1)} %slice.7), channel_id=1, source_target_pairs={{0,1},{1,2},{2,3},{4,5},{5,6},{6,7},{9,8},{10,9},{11,10},{12,13},{... | collective-permute-start | bytes 786440 | tf_op jit(solution)/shard_map/ppermute | solution.py:489
  29.1 15.8 %collective-permute-start.6 = (bf16[128,1536]{1,0:T(8,128)(2,1)S(1)}, bf16[128,1536]{1,0:T(8,128)(2,1)S(1)}, u32[]{:S(2)}, u32[]{:S(2)}) collective-permute-start(bf16[128,1536]{1,0:T(8,128)(2,1)S(1)} %collective-permute-done.2.got_lo), channel_id=1, source_target_pairs={{1,0},{2,1},{5,4},{6,5},{9,10},{10,11},{13,12},{14,13},{17,16},{18... | collective-permute-start | bytes 1179656 | tf_op jit(solution)/shard_map/ppermute | solution.py:490
  31.0 16.2 %collective-permute-start.7 = (bf16[128,1536]{1,0:T(8,128)(2,1)S(1)}, bf16[128,1536]{1,0:T(8,128)(2,1)S(1)}, u32[]{:S(2)}, u32[]{:S(2)}) collective-permute-start(bf16[128,1536]{1,0:T(8,128)(2,1)S(1)} %collective-permute-done.3.got_hi), channel_id=1, source_target_pairs={{1,2},{2,3},{5,6},{6,7},{9,8},{10,9},{13,14},{14,15},{17,18},{18,1... | collective-permute-start | bytes 1179656 | tf_op jit(solution)/shard_map/ppermute | solution.py:491
  34.5 14.8 %collective-permute-start.8 = (bf16[128,1024]{1,0:T(8,128)(2,1)S(1)}, bf16[128,1024]{1,0:T(8,128)(2,1)S(1)}, u32[]{:S(2)}, u32[]{:S(2)}) collective-permute-start(bf16[128,1024]{1,0:T(8,128)(2,1)S(1)} %collective-permute-done.4.later_lo), channel_id=1, source_target_pairs={{1,0},{2,1},{5,4},{6,5},{9,10},{10,11},{13,12},{14,13},{17,16},{18... | collective-permute-start | bytes 786440 | tf_op jit(solution)/shard_map/ppermute | solution.py:490
  38.6 11.5 %collective-permute-start.9 = (bf16[128,1024]{1,0:T(8,128)(2,1)S(1)}, bf16[128,1024]{1,0:T(8,128)(2,1)S(1)}, u32[]{:S(2)}, u32[]{:S(2)}) collective-permute-start(bf16[128,1024]{1,0:T(8,128)(2,1)S(1)} %collective-permute-done.5.later_hi), channel_id=1, source_target_pairs={{1,2},{2,3},{5,6},{6,7},{9,8},{10,9},{13,14},{14,15},{17,18},{18,1... | collective-permute-start | bytes 786440 | tf_op jit(solution)/shard_map/ppermute | solution.py:491

commit v12 on v11

--- a/solution.py
+++ b/solution.py
@@ -116,9 +116,14 @@
         padded[row(y) : row(y) + PX] = field[y * PX : (y + 1) * PX]
 
 
-def beside_xy(padded, y, odd):
-    at = row(y) + odd
-    return [padded[step(at + shift)] for shift in (-1, 1, -PITCH, PITCH)]
+def beside_xy(padded, y):
+    at = row(y)
+    even, odd = padded[step(at)], padded[step(at + 1)]
+    below, above = at - PITCH, at + PITCH
+    return (even, odd), (
+        [padded[step(at - 1)], odd, padded[step(below)], padded[step(above)]],
+        [even, padded[step(at + 2)], padded[step(below + 1)], padded[step(above + 1)]],
+    )
 
 
 def weighted(weights, values):
@@ -181,17 +186,17 @@
     fill_edges(picks, [field_ref.at[k] for k in range(species)], True)
     factor = [lewis_ref[k] for k in range(species)]
     for y in range(PY):
+        own, near = beside_xy(coef_pad, y)
+        weights = [[0.5 * (own[odd] + n) for n in near[odd]] for odd in range(2)]
         for odd in range(2):
-            at = halves(y, odd)
-            own = coef_pad[step(row(y) + odd)]
-            weights = [0.5 * (own + near) for near in beside_xy(coef_pad, y, odd)]
             for f in range(4):
-                weights_ref[f, at] = weights[f]
-            for k in range(species):
-                field = field_ref[k, step(row(y) + odd)]
-                flow = weighted(weights, beside_xy(field_ref.at[k], y, odd))
-                base_ref[k, at] = field + factor[k] * flow
-                rhs_ref[k, at] = field
+                weights_ref[f, halves(y, odd)] = weights[odd][f]
+        for k in range(species):
+            field, near = beside_xy(field_ref.at[k], y)
+            for odd in range(2):
+                at = halves(y, odd)
+                base_ref[k, at] = field[odd] + factor[k] * weighted(weights[odd], near[odd])
+                rhs_ref[k, at] = field[odd]
 
 
 def prepare_kernel(
@@ -223,12 +228,14 @@
             for f in range(4):
                 total = total + weights0[f, at]
             total0[at] = total
-            for d in range(2):
-                own = padded[d, step(row(y) + odd)]
-                near = [*beside_xy(padded.at[d], y, odd), z_ref[d, natural(y, odd)]]
+        for d in range(2):
+            own, beside = beside_xy(padded.at[d], y)
+            for odd in range(2):
+                at = halves(y, odd)
+                near = [*beside[odd], z_ref[d, natural(y, odd)]]
                 total = None
                 for f in range(5):
-                    w = 0.5 * (own + near[f])
+                    w = 0.5 * (own[odd] + near[f])
                     beside_ref[d, f, at] = w
                     total = w if total is None else total + w
                 total_ref[d, natural(y, odd)] = total
@@ -273,25 +280,23 @@
     fill_edges([pick0[f] for f in range(4)], [phi_ref.at[k] for k in range(species)], False)
     for d in range(2):
         for y in range(PY):
+            weights = [[beside_ref[d, f, halves(y, odd)] for f in range(5)] for odd in range(2)]
+            for k in range(species):
+                field, near = beside_xy(field_ref.at[d, k], y)
+                for odd in range(2):
+                    at = natural(y, odd)
+                    flow = weighted(weights[odd], [*near[odd], z_ref[2 + d, k, at]])
+                    numbers[d][k, at] = field[odd] + factor[k] * flow
+    for y in range(PY):
+        weights = [[weights0[f, halves(y, odd)] for f in range(4)] for odd in range(2)]
+        for k in range(species):
+            _, near = beside_xy(phi_ref.at[k], y)
             for odd in range(2):
-                at = halves(y, odd)
-                weights = [beside_ref[d, f, at] for f in range(5)]
-                for k in range(species):
-                    near = beside_xy(field_ref.at[d, k], y, odd)
-                    near.append(z_ref[2 + d, k, natural(y, odd)])
-                    numbers[d][k, natural(y, odd)] = (
-                        field_ref[d, k, step(row(y) + odd)] + factor[k] * weighted(weights, near)
-                    )
-    for y in range(PY):
-        for odd in range(2):
-            at = halves(y, odd)
-            weights = [weights0[f, at] for f in range(4)]
-            for k in range(species):
-                near = beside_xy(phi_ref.at[k], y, odd)
-                inverse = scale0[k, natural(y, odd)]
-                number = rhs_ref[k, at] + factor[k] * weighted(weights, near)
-                num0[k, natural(y, odd)] = number * inverse
-                scale0[k, natural(y, odd)] = factor[k] * inverse
+                at = natural(y, odd)
+                inverse = scale0[k, at]
+                number = rhs_ref[k, halves(y, odd)] + factor[k] * weighted(weights[odd], near[odd])
+                num0[k, at] = number * inverse
+                scale0[k, at] = factor[k] * inverse
 
 
 def both_kernel(

time: 52 us -> 52 us (level)
  no operation moved by 1% of the time
where the time goes in v12:
time: 52 us; the launch traced here: 51.5 us
  starting transfers between devices  23.7 us (46%)
  waiting for transfers between devices  14.7 us (28%)
  Pallas kernels  12.9 us (25%)
    pallas_call x6, Pallas kernels, call(): pl.pallas_call(kernel, out_shape=out_shape, grid=grid, in_specs=[specs.ge...  12.9 us
    ppermute x1, starting transfers between devices, per_device(): got_lo.append(lax.ppermute(later, along, one))  4.57 us
    all_to_all x1, starting transfers between devices, per_device(): lax.all_to_all(send, 'group', split_axis=0, concat_axis=0, tiled=True)  4.38 us
    ppermute x1, waiting for transfers between devices, per_device(): lists_hi = lax.ppermute(lists, along, two)  4.19 us
    ppermute x1, starting transfers between devices, per_device(): got_lo = [lax.ppermute(soon, along, one)]  3.51 us
    ppermute x1, starting transfers between devices, per_device(): lists_lo = lax.ppermute(lists, along, one)  3.47 us
    ppermute x1, waiting for transfers between devices, per_device(): got_hi.append(lax.ppermute(later, along, two))  3.41 us
    ppermute x2, waiting for transfers between devices, per_device(): got_hi2 = [lax.ppermute(part, along, two_on) for part in got_hi]  3.08 us
  transfers between devices with their start and end apart: 11, of which 7 were waited for; matrix products, arithmetic and copies ran while one was open for 0% of the time, Pallas kernels for 18%

profile of v12, /device:TPU:2, one launch (start us, length us, event | category | flops | bytes accessed | tf_op | source)
XLA Modules:
  0.0 51.5 jit_solution(6254116898129378691)
XLA Ops:
  0.0 2.4 %shard_map.55 = (bf16[128,2560]{1,0:T(8,128)(2,1)}, s32[8,128]{1,0:T(8,128)}) custom-call(s32[1,128]{1,0:T(1,128)} %bitcast.18, s32[6,1,128]{2,1,0:T(1,128)} %bitcast.17, bf16[9,128,256]{2,1,0:T(8,128)(2,1)} %bitcast.15, bf16[128,256]{1,0:T(8,128)(2,1)} %bitcast.16), custom_call_target="tpu_custom_call" | custom-call | bytes 1318400 | tf_op jit(solution)/shard_map/pallas_call | solution.py:407
  2.4 0.0 copy-start
  2.4 0.0 copy-start.1
  2.4 4.4 %all-to-all-start = ((bf16[8,16,2560]{2,1,0:T(8,128)(2,1)}), bf16[8,16,2560]{2,1,0:T(8,128)(2,1)S(1)}, u32[]{:S(2)}, u32[]{:S(2)}) async-start(bf16[8,16,2560]{2,1,0:T(8,128)(2,1)} %bitcast.14), calls=%async_computation | async-start | bytes 1310720 | tf_op jit(solution)/shard_map/all_to_all | solution.py:459
  6.8 0.0 copy-done
  6.8 3.5 %collective-permute-start = (s32[8,128]{1,0:T(8,128)S(1)}, s32[8,128]{1,0:T(8,128)S(1)}, u32[]{:S(2)}, u32[]{:S(2)}) collective-permute-start(s32[8,128]{1,0:T(8,128)S(1)} %copy-done), channel_id=1, source_target_pairs={{1,0},{2,1},{3,2},{5,4},{6,5},{7,6},{8,9},{9,10},{10,11},{13,12},{... | collective-permute-start | bytes 12296 | tf_op jit(solution)/shard_map/ppermute | solution.py:460
  10.3 1.3 %collective-permute-start.1 = (s32[8,128]{1,0:T(8,128)S(1)}, s32[8,128]{1,0:T(8,128)S(1)}, u32[]{:S(2)}, u32[]{:S(2)}) collective-permute-start(s32[8,128]{1,0:T(8,128)S(1)} %copy-done), channel_id=1, source_target_pairs={{0,1},{1,2},{2,3},{4,5},{5,6},{6,7},{9,8},{10,9},{11,10},{12,13},{... | collective-permute-start | bytes 12296 | tf_op jit(solution)/shard_map/ppermute | solution.py:461
  11.6 0.0 collective-permute-done.lists_lo
  11.6 4.2 %collective-permute-done.1.lists_hi = s32[8,128]{1,0:T(8,128)S(1)} collective-permute-done((s32[8,128]{1,0:T(8,128)S(1)}, s32[8,128]{1,0:T(8,128)S(1)}, u32[]{:S(2)}, u32[]{:S(2)}) %collective-permute-start.1) | collective-permute-done | bytes 4128 | tf_op jit(solution)/shard_map/ppermute | solution.py:461
  15.8 0.1 shard_map.56
  15.9 0.6 %all-to-all-done = bf16[8,16,2560]{2,1,0:T(8,128)(2,1)S(1)} async-done(((bf16[8,16,2560]{2,1,0:T(8,128)(2,1)}), bf16[8,16,2560]{2,1,0:T(8,128)(2,1)S(1)}, u32[]{:S(2)}, u32[]{:S(2)}) %all-to-all-start) | async-done | bytes 655392 | tf_op jit(solution)/shard_map/all_to_all | solution.py:459
  16.5 3.5 %collective-permute-start.2 = (bf16[128,1536]{1,0:T(8,128)(2,1)S(1)}, bf16[128,1536]{1,0:T(8,128)(2,1)S(1)}, u32[]{:S(2)}, u32[]{:S(2)}) collective-permute-start(bf16[128,1536]{1,0:T(8,128)(2,1)S(1)} %slice.6), channel_id=1, source_target_pairs={{1,0},{2,1},{3,2},{5,4},{6,5},{7,6},{8,9},{9,10},{10,11},{13,12},{... | collective-permute-start | bytes 1179656 | tf_op jit(solution)/shard_map/ppermute | solution.py:474
  20.0 1.3 %collective-permute-start.3 = (bf16[128,1536]{1,0:T(8,128)(2,1)S(1)}, bf16[128,1536]{1,0:T(8,128)(2,1)S(1)}, u32[]{:S(2)}, u32[]{:S(2)}) collective-permute-start(bf16[128,1536]{1,0:T(8,128)(2,1)S(1)} %slice.6), channel_id=1, source_target_pairs={{0,1},{1,2},{2,3},{4,5},{5,6},{6,7},{9,8},{10,9},{11,10},{12,13},{... | collective-permute-start | bytes 1179656 | tf_op jit(solution)/shard_map/ppermute | solution.py:475
  21.3 0.0 copy-done.1
  21.4 1.9 %shard_map.57 = (f32[256,128]{1,0:T(8,128)S(1)}, f32[4,256,128]{2,1,0:T(8,128)S(1)}, bf16[9,256,128]{2,1,0:T(8,128)(2,1)S(1)}, f32[9,256,128]{2,1,0:T(8,128)S(1)}, f32[9,256,128]{2,1,0:T(8,128)S(1)}) custom-call(f32[9]{0:T(128)S(1)} %copy-done.1, bf16[128,2560]{1,0:T(8,128)(2,1)S(1)} %bitcast.13, bf16[6,128,128]{2,1,0:T(8,128)(2,1)S(1)} %get-tuple-element.42.pick_ref.pick0), custom_call_target="tpu_custom_call" | custom-call | flops 500000000 | bytes 4456484 | tf_op jit(solution)/shard_map/pallas_call | solution.py:407
  23.2 4.6 %collective-permute-start.4 = (bf16[128,1024]{1,0:T(8,128)(2,1)S(1)}, bf16[128,1024]{1,0:T(8,128)(2,1)S(1)}, u32[]{:S(2)}, u32[]{:S(2)}) collective-permute-start(bf16[128,1024]{1,0:T(8,128)(2,1)S(1)} %slice.7), channel_id=1, source_target_pairs={{1,0},{2,1},{3,2},{5,4},{6,5},{7,6},{8,9},{9,10},{10,11},{13,12},{... | collective-permute-start | bytes 786440 | tf_op jit(solution)/shard_map/ppermute | solution.py:493
  27.8 1.3 %collective-permute-start.5 = (bf16[128,1024]{1,0:T(8,128)(2,1)S(1)}, bf16[128,1024]{1,0:T(8,128)(2,1)S(1)}, u32[]{:S(2)}, u32[]{:S(2)}) collective-permute-start(bf16[128,1024]{1,0:T(8,128)(2,1)S(1)} %slice.7), channel_id=1, source_target_pairs={{0,1},{1,2},{2,3},{4,5},{5,6},{6,7},{9,8},{10,9},{11,10},{12,13},{... | collective-permute-start | bytes 786440 | tf_op jit(solution)/shard_map/ppermute | solution.py:494
  29.1 0.0 collective-permute-done.2.got_lo
  29.1 0.7 %collective-permute-start.6 = (bf16[128,1536]{1,0:T(8,128)(2,1)S(1)}, bf16[128,1536]{1,0:T(8,128)(2,1)S(1)}, u32[]{:S(2)}, u32[]{:S(2)}) collective-permute-start(bf16[128,1536]{1,0:T(8,128)(2,1)S(1)} %collective-permute-done.2.got_lo), channel_id=1, source_target_pairs={{1,0},{2,1},{5,4},{6,5},{9,10},{10,11},{13,12},{14,13},{17,16},{18... | collective-permute-start | bytes 1179656 | tf_op jit(solution)/shard_map/ppermute | solution.py:495
  29.8 1.2 %collective-permute-done.3.got_hi = bf16[128,1536]{1,0:T(8,128)(2,1)S(1)} collective-permute-done((bf16[128,1536]{1,0:T(8,128)(2,1)S(1)}, bf16[128,1536]{1,0:T(8,128)(2,1)S(1)}, u32[]{:S(2)}, u32[]{:S(2)}) %collective-permute-start.3) | collective-permute-done | bytes 393248 | tf_op jit(solution)/shard_map/ppermute | solution.py:475
  31.0 1.3 %collective-permute-start.7 = (bf16[128,1536]{1,0:T(8,128)(2,1)S(1)}, bf16[128,1536]{1,0:T(8,128)(2,1)S(1)}, u32[]{:S(2)}, u32[]{:S(2)}) collective-permute-start(bf16[128,1536]{1,0:T(8,128)(2,1)S(1)} %collective-permute-done.3.got_hi), channel_id=1, source_target_pairs={{1,2},{2,3},{5,6},{6,7},{9,8},{10,9},{13,14},{14,15},{17,18},{18,1... | collective-permute-start | bytes 1179656 | tf_op jit(solution)/shard_map/ppermute | solution.py:496
  32.3 2.2 %collective-permute-done.4.later_lo = bf16[128,1024]{1,0:T(8,128)(2,1)S(1)} collective-permute-done((bf16[128,1024]{1,0:T(8,128)(2,1)S(1)}, bf16[128,1024]{1,0:T(8,128)(2,1)S(1)}, u32[]{:S(2)}, u32[]{:S(2)}) %collective-permute-start.4) | collective-permute-done | bytes 262176 | tf_op jit(solution)/shard_map/ppermute | solution.py:493
  34.5 0.7 %collective-permute-start.8 = (bf16[128,1024]{1,0:T(8,128)(2,1)S(1)}, bf16[128,1024]{1,0:T(8,128)(2,1)S(1)}, u32[]{:S(2)}, u32[]{:S(2)}) collective-permute-start(bf16[128,1024]{1,0:T(8,128)(2,1)S(1)} %collective-permute-done.4.later_lo), channel_id=1, source_target_pairs={{1,0},{2,1},{5,4},{6,5},{9,10},{10,11},{13,12},{14,13},{17,16},{18... | collective-permute-start | bytes 786440 | tf_op jit(solution)/shard_map/ppermute | solution.py:495
  35.2 3.4 %collective-permute-done.5.later_hi = bf16[128,1024]{1,0:T(8,128)(2,1)S(1)} collective-permute-done((bf16[128,1024]{1,0:T(8,128)(2,1)S(1)}, bf16[128,1024]{1,0:T(8,128)(2,1)S(1)}, u32[]{:S(2)}, u32[]{:S(2)}) %collective-permute-start.5) | collective-permute-done | bytes 262176 | tf_op jit(solution)/shard_map/ppermute | solution.py:494
  38.6 1.3 %collective-permute-start.9 = (bf16[128,1024]{1,0:T(8,128)(2,1)S(1)}, bf16[128,1024]{1,0:T(8,128)(2,1)S(1)}, u32[]{:S(2)}, u32[]{:S(2)}) collective-permute-start(bf16[128,1024]{1,0:T(8,128)(2,1)S(1)} %collective-permute-done.5.later_hi), channel_id=1, source_target_pairs={{1,2},{2,3},{5,6},{6,7},{9,8},{10,9},{13,14},{14,15},{17,18},{18,1... | collective-permute-start | bytes 786440 | tf_op jit(solution)/shard_map/ppermute | solution.py:496
  39.9 5.0 %shard_map.58 = (f32[2,256,128]{2,1,0:T(8,128)S(1)}, f32[2,256,128]{2,1,0:T(8,128)S(1)}, f32[2,256,128]{2,1,0:T(8,128)S(1)}, f32[9,256,128]{2,1,0:T(8,128)S(1)},...) custom-call(f32[9]{0:T(128)S(1)} %copy-done.1, ...), custom_call_target="tpu_custom_call" | custom-call | flops 1800000000 | bytes 11010084 | tf_op jit(solution)/shard_map/pallas_call | solution.py:407
  44.9 0.0 collective-permute-done.6.got_lo2
  44.9 2.3 %collective-permute-done.7.got_hi2 = bf16[128,1536]{1,0:T(8,128)(2,1)S(1)} collective-permute-done((bf16[128,1536]{1,0:T(8,128)(2,1)S(1)}, bf16[128,1536]{1,0:T(8,128)(2,1)S(1)}, u32[]{:S(2)}, u32[]{:S(2)}) %collective-permute-start.7) | collective-permute-done | bytes 393248 | tf_op jit(solution)/shard_map/ppermute | solution.py:496
  47.2 2.1 %shard_map.59 = (bf16[256,256]{1,0:T(8,128)(2,1)S(1)}, bf16[2,256,128]{2,1,0:T(8,128)(2,1)S(1)}, f32[2,4,256,128]{3,2,1,0:T(8,128)S(1)}, f32[2,4,256,128]{3,2,1,0:T(8,128)S(1)}, f32[5,128,256]{2,1,0:T(8,128)S(1)}) custom-call(f32[9]{0:T(128)S(1)} %copy-done.1, bf16[6,128,128]{2,1,0:T(8,128)(2,1)S(1)} %get-tuple-element.42.pick_ref.pick0, ...), custom_call_target="tpu_custom_call" | custom-call | flops 500000000 | bytes 9633828 | tf_op jit(solution)/shard_map/pallas_call | solution.py:407
  49.3 0.0 collective-permute-done.8.later_lo2
  49.3 0.8 %collective-permute-done.9.later_hi2 = bf16[128,1024]{1,0:T(8,128)(2,1)S(1)} collective-permute-done((bf16[128,1024]{1,0:T(8,128)(2,1)S(1)}, bf16[128,1024]{1,0:T(8,128)(2,1)S(1)}, u32[]{:S(2)}, u32[]{:S(2)}) %collective-permute-start.9) | collective-permute-done | bytes 262176 | tf_op jit(solution)/shard_map/ppermute | solution.py:496
  50.1 1.4 %shard_map.60 = f32[9,128,256]{2,1,0:T(8,128)} custom-call(bf16[256,256]{1,0:T(8,128)(2,1)S(1)} %get-tuple-element.64.far_ref, bf16[2,256,128]{2,1,0:T(8,128)(2,1)S(1)} %get-tuple-element.65.two_ref, f32[2,4,256,128]{3,2,1,0:T(8,128)S(1)} %get-tuple-element.66.offset_ref, f32[2,4,256,128]{3,2,1,0:T(8,128)S(1)} %get-tuple-element.67.slope_ref, ...), custom_call_target="tpu_custom_call" | custom-call | flops 400000000 | bytes 7340032 | tf_op jit(solution)/shard_map/pallas_call | solution.py:407
  (2 shorter events, 0.0 us)
Async XLA Ops:
  2.4 4.4 %copy-start = (s32[8,128]{1,0:T(8,128)S(1)}, s32[8,128]{1,0:T(8,128)}, u32[]{:S(2)}) copy-start(s32[8,128]{1,0:T(8,128)} %get-tuple-element.38.lists0) | copy-start | bytes 12292
  2.4 19.0 %copy-start.1 = (f32[9]{0:T(128)S(1)}, f32[9]{0:T(128)}, u32[]{:S(2)}) copy-start(f32[9]{0:T(128)} %lewis_ref.5) | copy-start | bytes 112
  2.4 14.1 %all-to-all-start = ((bf16[8,16,2560]{2,1,0:T(8,128)(2,1)}), bf16[8,16,2560]{2,1,0:T(8,128)(2,1)S(1)}, u32[]{:S(2)}, u32[]{:S(2)}) async-start(bf16[8,16,2560]{2,1,0:T(8,128)(2,1)} %bitcast.14), calls=%async_computation | async-start | bytes 1310720 | tf_op jit(solution)/shard_map/all_to_all | solution.py:459
  6.8 4.8 %collective-permute-start = (s32[8,128]{1,0:T(8,128)S(1)}, s32[8,128]{1,0:T(8,128)S(1)}, u32[]{:S(2)}, u32[]{:S(2)}) collective-permute-start(s32[8,128]{1,0:T(8,128)S(1)} %copy-done), channel_id=1, source_target_pairs={{1,0},{2,1},{3,2},{5,4},{6,5},{7,6},{8,9},{9,10},{10,11},{13,12},{... | collective-permute-start | bytes 12296 | tf_op jit(solution)/shard_map/ppermute | solution.py:460
  10.3 5.5 %collective-permute-start.1 = (s32[8,128]{1,0:T(8,128)S(1)}, s32[8,128]{1,0:T(8,128)S(1)}, u32[]{:S(2)}, u32[]{:S(2)}) collective-permute-start(s32[8,128]{1,0:T(8,128)S(1)} %copy-done), channel_id=1, source_target_pairs={{0,1},{1,2},{2,3},{4,5},{5,6},{6,7},{9,8},{10,9},{11,10},{12,13},{... | collective-permute-start | bytes 12296 | tf_op jit(solution)/shard_map/ppermute | solution.py:461
  16.5 12.6 %collective-permute-start.2 = (bf16[128,1536]{1,0:T(8,128)(2,1)S(1)}, bf16[128,1536]{1,0:T(8,128)(2,1)S(1)}, u32[]{:S(2)}, u32[]{:S(2)}) collective-permute-start(bf16[128,1536]{1,0:T(8,128)(2,1)S(1)} %slice.6), channel_id=1, source_target_pairs={{1,0},{2,1},{3,2},{5,4},{6,5},{7,6},{8,9},{9,10},{10,11},{13,12},{... | collective-permute-start | bytes 1179656 | tf_op jit(solution)/shard_map/ppermute | solution.py:474
  20.0 11.0 %collective-permute-start.3 = (bf16[128,1536]{1,0:T(8,128)(2,1)S(1)}, bf16[128,1536]{1,0:T(8,128)(2,1)S(1)}, u32[]{:S(2)}, u32[]{:S(2)}) collective-permute-start(bf16[128,1536]{1,0:T(8,128)(2,1)S(1)} %slice.6), channel_id=1, source_target_pairs={{0,1},{1,2},{2,3},{4,5},{5,6},{6,7},{9,8},{10,9},{11,10},{12,13},{... | collective-permute-start | bytes 1179656 | tf_op jit(solution)/shard_map/ppermute | solution.py:475
  23.2 11.3 %collective-permute-start.4 = (bf16[128,1024]{1,0:T(8,128)(2,1)S(1)}, bf16[128,1024]{1,0:T(8,128)(2,1)S(1)}, u32[]{:S(2)}, u32[]{:S(2)}) collective-permute-start(bf16[128,1024]{1,0:T(8,128)(2,1)S(1)} %slice.7), channel_id=1, source_target_pairs={{1,0},{2,1},{3,2},{5,4},{6,5},{7,6},{8,9},{9,10},{10,11},{13,12},{... | collective-permute-start | bytes 786440 | tf_op jit(solution)/shard_map/ppermute | solution.py:493
  27.8 10.8 %collective-permute-start.5 = (bf16[128,1024]{1,0:T(8,128)(2,1)S(1)}, bf16[128,1024]{1,0:T(8,128)(2,1)S(1)}, u32[]{:S(2)}, u32[]{:S(2)}) collective-permute-start(bf16[128,1024]{1,0:T(8,128)(2,1)S(1)} %slice.7), channel_id=1, source_target_pairs={{0,1},{1,2},{2,3},{4,5},{5,6},{6,7},{9,8},{10,9},{11,10},{12,13},{... | collective-permute-start | bytes 786440 | tf_op jit(solution)/shard_map/ppermute | solution.py:494
  29.1 15.8 %collective-permute-start.6 = (bf16[128,1536]{1,0:T(8,128)(2,1)S(1)}, bf16[128,1536]{1,0:T(8,128)(2,1)S(1)}, u32[]{:S(2)}, u32[]{:S(2)}) collective-permute-start(bf16[128,1536]{1,0:T(8,128)(2,1)S(1)} %collective-permute-done.2.got_lo), channel_id=1, source_target_pairs={{1,0},{2,1},{5,4},{6,5},{9,10},{10,11},{13,12},{14,13},{17,16},{18... | collective-permute-start | bytes 1179656 | tf_op jit(solution)/shard_map/ppermute | solution.py:495
  31.0 16.2 %collective-permute-start.7 = (bf16[128,1536]{1,0:T(8,128)(2,1)S(1)}, bf16[128,1536]{1,0:T(8,128)(2,1)S(1)}, u32[]{:S(2)}, u32[]{:S(2)}) collective-permute-start(bf16[128,1536]{1,0:T(8,128)(2,1)S(1)} %collective-permute-done.3.got_hi), channel_id=1, source_target_pairs={{1,2},{2,3},{5,6},{6,7},{9,8},{10,9},{13,14},{14,15},{17,18},{18,1... | collective-permute-start | bytes 1179656 | tf_op jit(solution)/shard_map/ppermute | solution.py:496
  34.5 14.8 %collective-permute-start.8 = (bf16[128,1024]{1,0:T(8,128)(2,1)S(1)}, bf16[128,1024]{1,0:T(8,128)(2,1)S(1)}, u32[]{:S(2)}, u32[]{:S(2)}) collective-permute-start(bf16[128,1024]{1,0:T(8,128)(2,1)S(1)} %collective-permute-done.4.later_lo), channel_id=1, source_target_pairs={{1,0},{2,1},{5,4},{6,5},{9,10},{10,11},{13,12},{14,13},{17,16},{18... | collective-permute-start | bytes 786440 | tf_op jit(solution)/shard_map/ppermute | solution.py:495
  38.6 11.5 %collective-permute-start.9 = (bf16[128,1024]{1,0:T(8,128)(2,1)S(1)}, bf16[128,1024]{1,0:T(8,128)(2,1)S(1)}, u32[]{:S(2)}, u32[]{:S(2)}) collective-permute-start(bf16[128,1024]{1,0:T(8,128)(2,1)S(1)} %collective-permute-done.5.later_hi), channel_id=1, source_target_pairs={{1,2},{2,3},{5,6},{6,7},{9,8},{10,9},{13,14},{14,15},{17,18},{18,1... | collective-permute-start | bytes 786440 | tf_op jit(solution)/shard_map/ppermute | solution.py:496

commit v13 on v11

--- a/solution.py
+++ b/solution.py
@@ -13,6 +13,7 @@
 LANES = 128
 HALF = PX // 2
 PITCH = PX + 8
+SPARE = 8
 F32 = jnp.float32
 BF16 = jnp.bfloat16
 VMEM_LIMIT = 28 * 1024 * 1024
@@ -92,7 +93,7 @@
     return jnp.concatenate([high, low], 1)
 
 
-PADDED = (PY + 2) * PITCH
+PADDED = (PY + 2) * PITCH + SPARE
 
 
 def row(y):
@@ -207,11 +208,11 @@
         coef = dot_first(rows, both)
         coef_ref[d] = coef[:, :slots]
         put(padded.at[d], coef[:, :slots])
-        z_natural[d] = 0.5 * (coef0[...] + coef[:, slots:])
+        z_natural[d, :cells] = 0.5 * (coef0[...] + coef[:, slots:])
         fill_edges([xy_pick[d, f] for f in range(4)], [padded.at[d]], True)
     near = dot(coef0[...].astype(BF16), z_pick[0])
-    z_ref[0] = near[:, :slots]
-    z_ref[1] = near[:, slots:]
+    z_ref[0, :cells] = near[:, :slots]
+    z_ref[1, :cells] = near[:, slots:]
     for y in range(PY):
         for odd in range(2):
             at = halves(y, odd)
@@ -239,7 +240,8 @@
     pick0, weights0, flat_ref, base_ref, rhs_ref, parts,
     num0, scale0, num_lo, num_hi, field_ref, z_ref, phi_ref,
 ):
-    species, cells, slots = num0.shape
+    species, rows, slots = num0.shape
+    cells = rows - SPARE
     numbers = (num_lo, num_hi)
     factor = [lewis_ref[k] for k in range(species)]
     for d in range(2):
@@ -249,12 +251,12 @@
             for i in range(count):
                 rows = slice(i * cells, (i + 1) * cells)
                 put(field_ref.at[d, k], both[rows, :slots])
-                z_ref[d, k] = both[rows, slots:]
+                z_ref[d, k, :cells] = both[rows, slots:]
                 k += 1
     near = dot(flat_ref[...].reshape(species * cells, slots), z_pick[0])
     for k in range(species):
         for d in range(2):
-            z_ref[2 + d, k] = near[k * cells : (k + 1) * cells, d * slots : (d + 1) * slots]
+            z_ref[2 + d, k, :cells] = near[k * cells : (k + 1) * cells, d * slots : (d + 1) * slots]
     for d in range(2):
         fill_edges(
             [xy_pick[d, f] for f in range(4)], [field_ref.at[d, k] for k in range(species)], True
@@ -325,7 +327,7 @@
     for i in range(2):
         w = 0.5 * (coef_ref[i] + near[:, i * slots : (i + 1) * slots])
         w_ref[i] = w
-        t_ref[i] = total_ref[i] + w
+        t_ref[i] = total_ref[i, :cells] + w
 
 
 def finish(ghosts, phi_of, two_ref, z_natural, num0, scale0, first, out_ref):
@@ -339,8 +341,9 @@
         terms.append(dot(jnp.concatenate(phis, 0), two_ref[i]))
     for k in range(count):
         rows = slice(k * cells, (k + 1) * cells)
-        flow = z_natural[0] * terms[0][rows] + z_natural[1] * terms[1][rows]
-        out_ref[k] = jnp.transpose(num0[first + k] + scale0[first + k] * flow, (1, 0))
+        flow = z_natural[0, :cells] * terms[0][rows] + z_natural[1, :cells] * terms[1][rows]
+        number, scale = num0[first + k, :cells], scale0[first + k, :cells]
+        out_ref[k] = jnp.transpose(number + scale * flow, (1, 0))
         yield k
 
 
@@ -359,7 +362,7 @@
     )
 
     def phi_of(k, i, ghost):
-        number = numbers[i][k] + factor[k] * (w_ref[i] * ghost)
+        number = numbers[i][k, :cells] + factor[k] * (w_ref[i] * ghost)
         return number * (1.0 / (1.0 + factor[k] * t_ref[i]))
 
     for k in finish(ghosts, phi_of, two_ref, z_natural, num0, scale0, 0, out_ref):
@@ -367,7 +370,7 @@
     for k in range(cut, num0.shape[0]):
         for i in range(2):
             inverse = 1.0 / (1.0 + factor[k] * t_ref[i])
-            offset_ref[i, k - cut] = numbers[i][k] * inverse
+            offset_ref[i, k - cut] = numbers[i][k, :cells] * inverse
             slope_ref[i, k - cut] = factor[k] * (w_ref[i] * inverse)
 
 
@@ -432,6 +435,7 @@
     cuts = (species - species // 2, species // 2)
     width = (1 + species) * cells
     middle = (1 + cuts[0]) * cells
+    long = cells + SPARE
     smem = pl.BlockSpec(memory_space=pltpu.SMEM)
     anywhere = pl.BlockSpec(memory_space=pl.ANY)
 
@@ -492,16 +496,16 @@
 
     z_natural, total, coefs, *numbers = call(
         functools.partial(both_kernel, cuts),
-        [shape(2, cells, slots)] * 3 + [shape(species, cells, slots)] * 4,
+        [shape(2, long, slots)] * 2 + [shape(2, cells, slots)] + [shape(species, long, slots)] * 4,
         [
             pltpu.VMEM((2, slots, 2 * slots), BF16),
             pltpu.VMEM((2, cells, slots), F32),
             pltpu.VMEM((cells, slots), F32),
             pltpu.VMEM((2, 5, cells, slots), F32),
             pltpu.VMEM((2, PADDED, slots), F32),
-            pltpu.VMEM((2, cells, slots), F32),
+            pltpu.VMEM((2, long, slots), F32),
             pltpu.VMEM((2, species, PADDED, slots), F32),
-            pltpu.VMEM((4, species, cells, slots), F32),
+            pltpu.VMEM((4, species, long, slots), F32),
             pltpu.VMEM((species, PADDED, slots), F32),
         ],
         (

time: 52 us -> 52.1 us (level)
  the two profiles are of different devices: /device:TPU:2 before, /device:TPU:8 now
where the time goes in v13:
time: 52.1 us; the launch traced here: 51.7 us
  starting transfers between devices  33.1 us (64%)
  Pallas kernels  13.1 us (25%)
  waiting for transfers between devices  5.19 us (10%)
    pallas_call x6, Pallas kernels, call(): pl.pallas_call(kernel, out_shape=out_shape, grid=grid, in_specs=[specs.ge...  13.1 us
    ppermute x2, starting transfers between devices, per_device(): got_hi2 = [lax.ppermute(part, along, two_on) for part in got_hi]  7.44 us
    ppermute x2, starting transfers between devices, per_device(): got_lo2 = [lax.ppermute(part, along, one_on) for part in got_lo]  4.31 us
    all_to_all x1, starting transfers between devices, per_device(): lax.all_to_all(send, 'group', split_axis=0, concat_axis=0, tiled=True)  3.86 us
    ppermute x1, starting transfers between devices, per_device(): lists_hi = lax.ppermute(lists, along, two)  3.49 us
    ppermute x1, starting transfers between devices, per_device(): got_hi = [lax.ppermute(soon, along, two)]  3.49 us
    ppermute x1, starting transfers between devices, per_device(): got_hi.append(lax.ppermute(later, along, two))  3.47 us
    all_to_all x1, waiting for transfers between devices, per_device(): lax.all_to_all(send, 'group', split_axis=0, concat_axis=0, tiled=True)  3.17 us
  transfers between devices with their start and end apart: 11, of which 2 were waited for; matrix products, arithmetic and copies ran while one was open for 0% of the time, Pallas kernels for 18%

profile of v13, /device:TPU:8, one launch (start us, length us, event | category | flops | bytes accessed | tf_op | source)
XLA Modules:
  0.0 51.7 jit_solution(11188576813047450818)
XLA Ops:
  0.0 2.4 %shard_map.55 = (bf16[128,2560]{1,0:T(8,128)(2,1)}, s32[8,128]{1,0:T(8,128)}) custom-call(s32[1,128]{1,0:T(1,128)} %bitcast.18, s32[6,1,128]{2,1,0:T(1,128)} %bitcast.17, bf16[9,128,256]{2,1,0:T(8,128)(2,1)} %bitcast.15, bf16[128,256]{1,0:T(8,128)(2,1)} %bitcast.16), custom_call_target="tpu_custom_call" | custom-call | bytes 1318400 | tf_op jit(solution)/shard_map/pallas_call | solution.py:405
  2.4 0.0 copy-start
  2.4 0.0 copy-start.1
  2.4 3.9 %all-to-all-start = ((bf16[8,16,2560]{2,1,0:T(8,128)(2,1)}), bf16[8,16,2560]{2,1,0:T(8,128)(2,1)S(1)}, u32[]{:S(2)}, u32[]{:S(2)}) async-start(bf16[8,16,2560]{2,1,0:T(8,128)(2,1)} %bitcast.14), calls=%async_computation | async-start | bytes 1310720 | tf_op jit(solution)/shard_map/all_to_all | solution.py:458
  6.3 0.0 copy-done
  6.3 2.4 %collective-permute-start = (s32[8,128]{1,0:T(8,128)S(1)}, s32[8,128]{1,0:T(8,128)S(1)}, u32[]{:S(2)}, u32[]{:S(2)}) collective-permute-start(s32[8,128]{1,0:T(8,128)S(1)} %copy-done), channel_id=1, source_target_pairs={{1,0},{2,1},{3,2},{5,4},{6,5},{7,6},{8,9},{9,10},{10,11},{13,12},{... | collective-permute-start | bytes 12296 | tf_op jit(solution)/shard_map/ppermute | solution.py:459
  8.6 3.5 %collective-permute-start.1 = (s32[8,128]{1,0:T(8,128)S(1)}, s32[8,128]{1,0:T(8,128)S(1)}, u32[]{:S(2)}, u32[]{:S(2)}) collective-permute-start(s32[8,128]{1,0:T(8,128)S(1)} %copy-done), channel_id=1, source_target_pairs={{0,1},{1,2},{2,3},{4,5},{5,6},{6,7},{9,8},{10,9},{11,10},{12,13},{... | collective-permute-start | bytes 12296 | tf_op jit(solution)/shard_map/ppermute | solution.py:460
  12.1 0.0 collective-permute-done.lists_lo
  12.1 2.0 %collective-permute-done.1.lists_hi = s32[8,128]{1,0:T(8,128)S(1)} collective-permute-done((s32[8,128]{1,0:T(8,128)S(1)}, s32[8,128]{1,0:T(8,128)S(1)}, u32[]{:S(2)}, u32[]{:S(2)}) %collective-permute-start.1) | collective-permute-done | bytes 4128 | tf_op jit(solution)/shard_map/ppermute | solution.py:460
  14.1 0.1 shard_map.56
  14.2 3.2 %all-to-all-done = bf16[8,16,2560]{2,1,0:T(8,128)(2,1)S(1)} async-done(((bf16[8,16,2560]{2,1,0:T(8,128)(2,1)}), bf16[8,16,2560]{2,1,0:T(8,128)(2,1)S(1)}, u32[]{:S(2)}, u32[]{:S(2)}) %all-to-all-start) | async-done | bytes 655392 | tf_op jit(solution)/shard_map/all_to_all | solution.py:458
  17.4 2.4 %collective-permute-start.2 = (bf16[128,1536]{1,0:T(8,128)(2,1)S(1)}, bf16[128,1536]{1,0:T(8,128)(2,1)S(1)}, u32[]{:S(2)}, u32[]{:S(2)}) collective-permute-start(bf16[128,1536]{1,0:T(8,128)(2,1)S(1)} %slice.6), channel_id=1, source_target_pairs={{1,0},{2,1},{3,2},{5,4},{6,5},{7,6},{8,9},{9,10},{10,11},{13,12},{... | collective-permute-start | bytes 1179656 | tf_op jit(solution)/shard_map/ppermute | solution.py:473
  19.8 3.5 %collective-permute-start.3 = (bf16[128,1536]{1,0:T(8,128)(2,1)S(1)}, bf16[128,1536]{1,0:T(8,128)(2,1)S(1)}, u32[]{:S(2)}, u32[]{:S(2)}) collective-permute-start(bf16[128,1536]{1,0:T(8,128)(2,1)S(1)} %slice.6), channel_id=1, source_target_pairs={{0,1},{1,2},{2,3},{4,5},{5,6},{6,7},{9,8},{10,9},{11,10},{12,13},{... | collective-permute-start | bytes 1179656 | tf_op jit(solution)/shard_map/ppermute | solution.py:474
  23.3 0.0 copy-done.1
  23.3 1.9 %shard_map.57 = (f32[256,128]{1,0:T(8,128)S(1)}, f32[4,256,128]{2,1,0:T(8,128)S(1)}, bf16[9,256,128]{2,1,0:T(8,128)(2,1)S(1)}, f32[9,256,128]{2,1,0:T(8,128)S(1)}, f32[9,256,128]{2,1,0:T(8,128)S(1)}) custom-call(f32[9]{0:T(128)S(1)} %copy-done.1, bf16[128,2560]{1,0:T(8,128)(2,1)S(1)} %bitcast.13, bf16[6,128,128]{2,1,0:T(8,128)(2,1)S(1)} %get-tuple-element.42.pick_ref.pick0), custom_call_target="tpu_custom_call" | custom-call | flops 500000000 | bytes 4456484 | tf_op jit(solution)/shard_map/pallas_call | solution.py:405
  25.2 2.4 %collective-permute-start.4 = (bf16[128,1024]{1,0:T(8,128)(2,1)S(1)}, bf16[128,1024]{1,0:T(8,128)(2,1)S(1)}, u32[]{:S(2)}, u32[]{:S(2)}) collective-permute-start(bf16[128,1024]{1,0:T(8,128)(2,1)S(1)} %slice.7), channel_id=1, source_target_pairs={{1,0},{2,1},{3,2},{5,4},{6,5},{7,6},{8,9},{9,10},{10,11},{13,12},{... | collective-permute-start | bytes 786440 | tf_op jit(solution)/shard_map/ppermute | solution.py:492
  27.6 3.5 %collective-permute-start.5 = (bf16[128,1024]{1,0:T(8,128)(2,1)S(1)}, bf16[128,1024]{1,0:T(8,128)(2,1)S(1)}, u32[]{:S(2)}, u32[]{:S(2)}) collective-permute-start(bf16[128,1024]{1,0:T(8,128)(2,1)S(1)} %slice.7), channel_id=1, source_target_pairs={{0,1},{1,2},{2,3},{4,5},{5,6},{6,7},{9,8},{10,9},{11,10},{12,13},{... | collective-permute-start | bytes 786440 | tf_op jit(solution)/shard_map/ppermute | solution.py:493
  31.1 0.0 collective-permute-done.2.got_lo
  31.1 2.4 %collective-permute-start.6 = (bf16[128,1536]{1,0:T(8,128)(2,1)S(1)}, bf16[128,1536]{1,0:T(8,128)(2,1)S(1)}, u32[]{:S(2)}, u32[]{:S(2)}) collective-permute-start(bf16[128,1536]{1,0:T(8,128)(2,1)S(1)} %collective-permute-done.2.got_lo), channel_id=1, source_target_pairs={{1,0},{2,1},{5,4},{6,5},{9,10},{10,11},{13,12},{14,13},{17,16},{18... | collective-permute-start | bytes 1179656 | tf_op jit(solution)/shard_map/ppermute | solution.py:494
  33.5 0.0 collective-permute-done.3.got_hi
  33.5 3.5 %collective-permute-start.7 = (bf16[128,1536]{1,0:T(8,128)(2,1)S(1)}, bf16[128,1536]{1,0:T(8,128)(2,1)S(1)}, u32[]{:S(2)}, u32[]{:S(2)}) collective-permute-start(bf16[128,1536]{1,0:T(8,128)(2,1)S(1)} %collective-permute-done.3.got_hi), channel_id=1, source_target_pairs={{1,2},{2,3},{5,6},{6,7},{9,8},{10,9},{13,14},{14,15},{17,18},{18,1... | collective-permute-start | bytes 1179656 | tf_op jit(solution)/shard_map/ppermute | solution.py:495
  37.0 0.0 collective-permute-done.4.later_lo
  37.0 1.9 %collective-permute-start.8 = (bf16[128,1024]{1,0:T(8,128)(2,1)S(1)}, bf16[128,1024]{1,0:T(8,128)(2,1)S(1)}, u32[]{:S(2)}, u32[]{:S(2)}) collective-permute-start(bf16[128,1024]{1,0:T(8,128)(2,1)S(1)} %collective-permute-done.4.later_lo), channel_id=1, source_target_pairs={{1,0},{2,1},{5,4},{6,5},{9,10},{10,11},{13,12},{14,13},{17,16},{18... | collective-permute-start | bytes 786440 | tf_op jit(solution)/shard_map/ppermute | solution.py:494
  38.9 0.0 collective-permute-done.5.later_hi
  38.9 3.9 %collective-permute-start.9 = (bf16[128,1024]{1,0:T(8,128)(2,1)S(1)}, bf16[128,1024]{1,0:T(8,128)(2,1)S(1)}, u32[]{:S(2)}, u32[]{:S(2)}) collective-permute-start(bf16[128,1024]{1,0:T(8,128)(2,1)S(1)} %collective-permute-done.5.later_hi), channel_id=1, source_target_pairs={{1,2},{2,3},{5,6},{6,7},{9,8},{10,9},{13,14},{14,15},{17,18},{18,1... | collective-permute-start | bytes 786440 | tf_op jit(solution)/shard_map/ppermute | solution.py:495
  42.9 5.1 %shard_map.58 = (f32[2,264,128]{2,1,0:T(8,128)S(1)}, f32[2,264,128]{2,1,0:T(8,128)S(1)}, f32[2,256,128]{2,1,0:T(8,128)S(1)}, f32[9,264,128]{2,1,0:T(8,128)S(1)},...) custom-call(f32[9]{0:T(128)S(1)} %copy-done.1, ...), custom_call_target="tpu_custom_call" | custom-call | flops 1800000000 | bytes 11173924 | tf_op jit(solution)/shard_map/pallas_call | solution.py:405
  48.0 0.0 collective-permute-done.6.got_lo2
  48.0 0.0 collective-permute-done.7.got_hi2
  48.0 2.2 %shard_map.59 = (bf16[256,256]{1,0:T(8,128)(2,1)S(1)}, bf16[2,256,128]{2,1,0:T(8,128)(2,1)S(1)}, f32[2,4,256,128]{3,2,1,0:T(8,128)S(1)}, f32[2,4,256,128]{3,2,1,0:T(8,128)S(1)}, f32[5,128,256]{2,1,0:T(8,128)S(1)}) custom-call(f32[9]{0:T(128)S(1)} %copy-done.1, bf16[6,128,128]{2,1,0:T(8,128)(2,1)S(1)} %get-tuple-element.42.pick_ref.pick0, ...), custom_call_target="tpu_custom_call" | custom-call | flops 500000000 | bytes 9797668 | tf_op jit(solution)/shard_map/pallas_call | solution.py:405
  50.2 0.0 collective-permute-done.8.later_lo2
  50.2 0.0 collective-permute-done.9.later_hi2
  50.2 1.5 %shard_map.60 = f32[9,128,256]{2,1,0:T(8,128)} custom-call(bf16[256,256]{1,0:T(8,128)(2,1)S(1)} %get-tuple-element.64.far_ref, bf16[2,256,128]{2,1,0:T(8,128)(2,1)S(1)} %get-tuple-element.65.two_ref, f32[2,4,256,128]{3,2,1,0:T(8,128)S(1)} %get-tuple-element.66.offset_ref, f32[2,4,256,128]{3,2,1,0:T(8,128)S(1)} %get-tuple-element.67.slope_ref, ...), custom_call_target="tpu_custom_call" | custom-call | flops 400000000 | bytes 7421952 | tf_op jit(solution)/shard_map/pallas_call | solution.py:405
  (2 shorter events, 0.0 us)
Async XLA Ops:
  2.4 3.9 %copy-start = (s32[8,128]{1,0:T(8,128)S(1)}, s32[8,128]{1,0:T(8,128)}, u32[]{:S(2)}) copy-start(s32[8,128]{1,0:T(8,128)} %get-tuple-element.38.lists0) | copy-start | bytes 12292
  2.4 20.9 %copy-start.1 = (f32[9]{0:T(128)S(1)}, f32[9]{0:T(128)}, u32[]{:S(2)}) copy-start(f32[9]{0:T(128)} %lewis_ref.5) | copy-start | bytes 112
  2.4 15.0 %all-to-all-start = ((bf16[8,16,2560]{2,1,0:T(8,128)(2,1)}), bf16[8,16,2560]{2,1,0:T(8,128)(2,1)S(1)}, u32[]{:S(2)}, u32[]{:S(2)}) async-start(bf16[8,16,2560]{2,1,0:T(8,128)(2,1)} %bitcast.14), calls=%async_computation | async-start | bytes 1310720 | tf_op jit(solution)/shard_map/all_to_all | solution.py:458
  6.3 5.9 %collective-permute-start = (s32[8,128]{1,0:T(8,128)S(1)}, s32[8,128]{1,0:T(8,128)S(1)}, u32[]{:S(2)}, u32[]{:S(2)}) collective-permute-start(s32[8,128]{1,0:T(8,128)S(1)} %copy-done), channel_id=1, source_target_pairs={{1,0},{2,1},{3,2},{5,4},{6,5},{7,6},{8,9},{9,10},{10,11},{13,12},{... | collective-permute-start | bytes 12296 | tf_op jit(solution)/shard_map/ppermute | solution.py:459
  8.6 5.5 %collective-permute-start.1 = (s32[8,128]{1,0:T(8,128)S(1)}, s32[8,128]{1,0:T(8,128)S(1)}, u32[]{:S(2)}, u32[]{:S(2)}) collective-permute-start(s32[8,128]{1,0:T(8,128)S(1)} %copy-done), channel_id=1, source_target_pairs={{0,1},{1,2},{2,3},{4,5},{5,6},{6,7},{9,8},{10,9},{11,10},{12,13},{... | collective-permute-start | bytes 12296 | tf_op jit(solution)/shard_map/ppermute | solution.py:460
  17.4 13.6 %collective-permute-start.2 = (bf16[128,1536]{1,0:T(8,128)(2,1)S(1)}, bf16[128,1536]{1,0:T(8,128)(2,1)S(1)}, u32[]{:S(2)}, u32[]{:S(2)}) collective-permute-start(bf16[128,1536]{1,0:T(8,128)(2,1)S(1)} %slice.6), channel_id=1, source_target_pairs={{1,0},{2,1},{3,2},{5,4},{6,5},{7,6},{8,9},{9,10},{10,11},{13,12},{... | collective-permute-start | bytes 1179656 | tf_op jit(solution)/shard_map/ppermute | solution.py:473
  19.8 13.7 %collective-permute-start.3 = (bf16[128,1536]{1,0:T(8,128)(2,1)S(1)}, bf16[128,1536]{1,0:T(8,128)(2,1)S(1)}, u32[]{:S(2)}, u32[]{:S(2)}) collective-permute-start(bf16[128,1536]{1,0:T(8,128)(2,1)S(1)} %slice.6), channel_id=1, source_target_pairs={{0,1},{1,2},{2,3},{4,5},{5,6},{6,7},{9,8},{10,9},{11,10},{12,13},{... | collective-permute-start | bytes 1179656 | tf_op jit(solution)/shard_map/ppermute | solution.py:474
  25.2 11.8 %collective-permute-start.4 = (bf16[128,1024]{1,0:T(8,128)(2,1)S(1)}, bf16[128,1024]{1,0:T(8,128)(2,1)S(1)}, u32[]{:S(2)}, u32[]{:S(2)}) collective-permute-start(bf16[128,1024]{1,0:T(8,128)(2,1)S(1)} %slice.7), channel_id=1, source_target_pairs={{1,0},{2,1},{3,2},{5,4},{6,5},{7,6},{8,9},{9,10},{10,11},{13,12},{... | collective-permute-start | bytes 786440 | tf_op jit(solution)/shard_map/ppermute | solution.py:492
  27.6 11.3 %collective-permute-start.5 = (bf16[128,1024]{1,0:T(8,128)(2,1)S(1)}, bf16[128,1024]{1,0:T(8,128)(2,1)S(1)}, u32[]{:S(2)}, u32[]{:S(2)}) collective-permute-start(bf16[128,1024]{1,0:T(8,128)(2,1)S(1)} %slice.7), channel_id=1, source_target_pairs={{0,1},{1,2},{2,3},{4,5},{5,6},{6,7},{9,8},{10,9},{11,10},{12,13},{... | collective-permute-start | bytes 786440 | tf_op jit(solution)/shard_map/ppermute | solution.py:493
  31.1 16.9 %collective-permute-start.6 = (bf16[128,1536]{1,0:T(8,128)(2,1)S(1)}, bf16[128,1536]{1,0:T(8,128)(2,1)S(1)}, u32[]{:S(2)}, u32[]{:S(2)}) collective-permute-start(bf16[128,1536]{1,0:T(8,128)(2,1)S(1)} %collective-permute-done.2.got_lo), channel_id=1, source_target_pairs={{1,0},{2,1},{5,4},{6,5},{9,10},{10,11},{13,12},{14,13},{17,16},{18... | collective-permute-start | bytes 1179656 | tf_op jit(solution)/shard_map/ppermute | solution.py:494
  33.5 14.5 %collective-permute-start.7 = (bf16[128,1536]{1,0:T(8,128)(2,1)S(1)}, bf16[128,1536]{1,0:T(8,128)(2,1)S(1)}, u32[]{:S(2)}, u32[]{:S(2)}) collective-permute-start(bf16[128,1536]{1,0:T(8,128)(2,1)S(1)} %collective-permute-done.3.got_hi), channel_id=1, source_target_pairs={{1,2},{2,3},{5,6},{6,7},{9,8},{10,9},{13,14},{14,15},{17,18},{18,1... | collective-permute-start | bytes 1179656 | tf_op jit(solution)/shard_map/ppermute | solution.py:495
  37.0 13.2 %collective-permute-start.8 = (bf16[128,1024]{1,0:T(8,128)(2,1)S(1)}, bf16[128,1024]{1,0:T(8,128)(2,1)S(1)}, u32[]{:S(2)}, u32[]{:S(2)}) collective-permute-start(bf16[128,1024]{1,0:T(8,128)(2,1)S(1)} %collective-permute-done.4.later_lo), channel_id=1, source_target_pairs={{1,0},{2,1},{5,4},{6,5},{9,10},{10,11},{13,12},{14,13},{17,16},{18... | collective-permute-start | bytes 786440 | tf_op jit(solution)/shard_map/ppermute | solution.py:494
  38.9 11.3 %collective-permute-start.9 = (bf16[128,1024]{1,0:T(8,128)(2,1)S(1)}, bf16[128,1024]{1,0:T(8,128)(2,1)S(1)}, u32[]{:S(2)}, u32[]{:S(2)}) collective-permute-start(bf16[128,1024]{1,0:T(8,128)(2,1)S(1)} %collective-permute-done.5.later_hi), channel_id=1, source_target_pairs={{1,2},{2,3},{5,6},{6,7},{9,8},{10,9},{13,14},{14,15},{17,18},{18,1... | collective-permute-start | bytes 786440 | tf_op jit(solution)/shard_map/ppermute | solution.py:495

commit v14 on v11

--- a/solution.py
+++ b/solution.py
@@ -429,7 +429,7 @@
     one_on, two_on = pairs(0, False), pairs(1, False)
     slots, species, cells = state.shape[2:]
     capacity = slots // groups
-    cuts = (species - species // 2, species // 2)
+    cuts = (species // 2, species - species // 2)
     width = (1 + species) * cells
     middle = (1 + cuts[0]) * cells
     smem = pl.BlockSpec(memory_space=pltpu.SMEM)

time: 52 us -> 52.8 us (1.015)
  waiting for transfers between devices: 14.8 us -> 15.5 us
    ppermute x1, waiting for transfers between devices: 2.24 us -> 4.19 us  [per_device(): got_lo.append(lax.ppermute(later, along, one))]
    ppermute x1, waiting for transfers between devices: 1.19 us -> 0.01 us  [per_device(): got_hi = [lax.ppermute(soon, along, two)]]
    ppermute x2, waiting for transfers between devices: 3.1 us -> 2.46 us  [per_device(): got_hi2 = [lax.ppermute(part, along, two_on) for part in got_hi]]
    ppermute x1, waiting for transfers between devices: 3.41 us -> 4.04 us  [per_device(): got_hi.append(lax.ppermute(later, along, two))]
  transfers between devices with their start and end apart: 11 -> 11, of which waited for: 7 -> 6; matrix products, arithmetic and copies ran while one was open for 0% -> 0% of each run, Pallas kernels for 18% -> 17%
where the time goes in v14:
time: 52.8 us; the launch traced here: 52.3 us
  starting transfers between devices  23.7 us (45%)
  waiting for transfers between devices  15.5 us (29%)
  Pallas kernels  12.9 us (24%)
    pallas_call x6, Pallas kernels, call(): pl.pallas_call(kernel, out_shape=out_shape, grid=grid, in_specs=[specs.ge...  12.9 us
    ppermute x1, starting transfers between devices, per_device(): got_lo.append(lax.ppermute(later, along, one))  4.57 us
    all_to_all x1, starting transfers between devices, per_device(): lax.all_to_all(send, 'group', split_axis=0, concat_axis=0, tiled=True)  4.38 us
    ppermute x1, waiting for transfers between devices, per_device(): got_lo.append(lax.ppermute(later, along, one))  4.19 us
    ppermute x1, waiting for transfers between devices, per_device(): lists_hi = lax.ppermute(lists, along, two)  4.19 us
    ppermute x1, waiting for transfers between devices, per_device(): got_hi.append(lax.ppermute(later, along, two))  4.04 us
    ppermute x1, starting transfers between devices, per_device(): got_lo = [lax.ppermute(soon, along, one)]  3.5 us
    ppermute x1, starting transfers between devices, per_device(): lists_lo = lax.ppermute(lists, along, one)  3.47 us
  transfers between devices with their start and end apart: 11, of which 6 were waited for; matrix products, arithmetic and copies ran while one was open for 0% of the time, Pallas kernels for 17%

profile of v14, /device:TPU:2, one launch (start us, length us, event | category | flops | bytes accessed | tf_op | source)
XLA Modules:
  0.0 52.3 jit_solution(8293572806668845566)
XLA Ops:
  0.0 2.4 %shard_map.55 = (bf16[128,2560]{1,0:T(8,128)(2,1)}, s32[8,128]{1,0:T(8,128)}) custom-call(s32[1,128]{1,0:T(1,128)} %bitcast.17, s32[6,1,128]{2,1,0:T(1,128)} %bitcast.16, bf16[9,128,256]{2,1,0:T(8,128)(2,1)} %bitcast.14, bf16[128,256]{1,0:T(8,128)(2,1)} %bitcast.15), custom_call_target="tpu_custom_call" | custom-call | bytes 1318400 | tf_op jit(solution)/shard_map/pallas_call | solution.py:402
  2.4 0.0 copy-start
  2.4 0.0 copy-start.1
  2.4 4.4 %all-to-all-start = ((bf16[8,16,2560]{2,1,0:T(8,128)(2,1)}), bf16[8,16,2560]{2,1,0:T(8,128)(2,1)S(1)}, u32[]{:S(2)}, u32[]{:S(2)}) async-start(bf16[8,16,2560]{2,1,0:T(8,128)(2,1)} %bitcast.13), calls=%async_computation | async-start | bytes 1310720 | tf_op jit(solution)/shard_map/all_to_all | solution.py:454
  6.8 0.0 copy-done
  6.8 3.5 %collective-permute-start = (s32[8,128]{1,0:T(8,128)S(1)}, s32[8,128]{1,0:T(8,128)S(1)}, u32[]{:S(2)}, u32[]{:S(2)}) collective-permute-start(s32[8,128]{1,0:T(8,128)S(1)} %copy-done), channel_id=1, source_target_pairs={{1,0},{2,1},{3,2},{5,4},{6,5},{7,6},{8,9},{9,10},{10,11},{13,12},{... | collective-permute-start | bytes 12296 | tf_op jit(solution)/shard_map/ppermute | solution.py:455
  10.3 1.3 %collective-permute-start.1 = (s32[8,128]{1,0:T(8,128)S(1)}, s32[8,128]{1,0:T(8,128)S(1)}, u32[]{:S(2)}, u32[]{:S(2)}) collective-permute-start(s32[8,128]{1,0:T(8,128)S(1)} %copy-done), channel_id=1, source_target_pairs={{0,1},{1,2},{2,3},{4,5},{5,6},{6,7},{9,8},{10,9},{11,10},{12,13},{... | collective-permute-start | bytes 12296 | tf_op jit(solution)/shard_map/ppermute | solution.py:456
  11.6 0.0 collective-permute-done.lists_lo
  11.6 4.2 %collective-permute-done.1.lists_hi = s32[8,128]{1,0:T(8,128)S(1)} collective-permute-done((s32[8,128]{1,0:T(8,128)S(1)}, s32[8,128]{1,0:T(8,128)S(1)}, u32[]{:S(2)}, u32[]{:S(2)}) %collective-permute-start.1) | collective-permute-done | bytes 4128 | tf_op jit(solution)/shard_map/ppermute | solution.py:456
  15.8 0.1 shard_map.56
  15.9 0.6 %all-to-all-done = bf16[8,16,2560]{2,1,0:T(8,128)(2,1)S(1)} async-done(((bf16[8,16,2560]{2,1,0:T(8,128)(2,1)}), bf16[8,16,2560]{2,1,0:T(8,128)(2,1)S(1)}, u32[]{:S(2)}, u32[]{:S(2)}) %all-to-all-start) | async-done | bytes 655392 | tf_op jit(solution)/shard_map/all_to_all | solution.py:454
  16.5 3.5 %collective-permute-start.2 = (bf16[128,1280]{1,0:T(8,128)(2,1)S(1)}, bf16[128,1280]{1,0:T(8,128)(2,1)S(1)}, u32[]{:S(2)}, u32[]{:S(2)}) collective-permute-start(bf16[128,1280]{1,0:T(8,128)(2,1)S(1)} %get-tuple-element.70), channel_id=1, source_target_pairs={{1,0},{2,1},{3,2},{5,4},{6,5},{7,6},{8,9},{9,10},{10,11},{13,12},{... | collective-permute-start | bytes 983048 | tf_op jit(solution)/shard_map/ppermute | solution.py:469
  20.0 1.3 %collective-permute-start.3 = (bf16[128,1280]{1,0:T(8,128)(2,1)S(1)}, bf16[128,1280]{1,0:T(8,128)(2,1)S(1)}, u32[]{:S(2)}, u32[]{:S(2)}) collective-permute-start(bf16[128,1280]{1,0:T(8,128)(2,1)S(1)} %get-tuple-element.70), channel_id=1, source_target_pairs={{0,1},{1,2},{2,3},{4,5},{5,6},{6,7},{9,8},{10,9},{11,10},{12,13},{... | collective-permute-start | bytes 983048 | tf_op jit(solution)/shard_map/ppermute | solution.py:470
  21.3 0.0 copy-done.1
  21.3 1.9 %shard_map.57 = (f32[256,128]{1,0:T(8,128)S(1)}, f32[4,256,128]{2,1,0:T(8,128)S(1)}, bf16[9,256,128]{2,1,0:T(8,128)(2,1)S(1)}, f32[9,256,128]{2,1,0:T(8,128)S(1)}, f32[9,256,128]{2,1,0:T(8,128)S(1)}) custom-call(f32[9]{0:T(128)S(1)} %copy-done.1, bf16[128,2560]{1,0:T(8,128)(2,1)S(1)} %bitcast.12, bf16[6,128,128]{2,1,0:T(8,128)(2,1)S(1)} %get-tuple-element.42.pick_ref.pick0), custom_call_target="tpu_custom_call" | custom-call | flops 500000000 | bytes 4456484 | tf_op jit(solution)/shard_map/pallas_call | solution.py:402
  23.2 4.6 %collective-permute-start.4 = (bf16[128,1280]{1,0:T(8,128)(2,1)S(1)}, bf16[128,1280]{1,0:T(8,128)(2,1)S(1)}, u32[]{:S(2)}, u32[]{:S(2)}) collective-permute-start(bf16[128,1280]{1,0:T(8,128)(2,1)S(1)} %get-tuple-element.50), channel_id=1, source_target_pairs={{1,0},{2,1},{3,2},{5,4},{6,5},{7,6},{8,9},{9,10},{10,11},{13,12},{... | collective-permute-start | bytes 983048 | tf_op jit(solution)/shard_map/ppermute | solution.py:488
  27.8 1.3 %collective-permute-start.5 = (bf16[128,1280]{1,0:T(8,128)(2,1)S(1)}, bf16[128,1280]{1,0:T(8,128)(2,1)S(1)}, u32[]{:S(2)}, u32[]{:S(2)}) collective-permute-start(bf16[128,1280]{1,0:T(8,128)(2,1)S(1)} %get-tuple-element.50), channel_id=1, source_target_pairs={{0,1},{1,2},{2,3},{4,5},{5,6},{6,7},{9,8},{10,9},{11,10},{12,13},{... | collective-permute-start | bytes 983048 | tf_op jit(solution)/shard_map/ppermute | solution.py:489
  29.1 0.0 collective-permute-done.2.got_lo
  29.1 0.7 %collective-permute-start.6 = (bf16[128,1280]{1,0:T(8,128)(2,1)S(1)}, bf16[128,1280]{1,0:T(8,128)(2,1)S(1)}, u32[]{:S(2)}, u32[]{:S(2)}) collective-permute-start(bf16[128,1280]{1,0:T(8,128)(2,1)S(1)} %collective-permute-done.2.got_lo), channel_id=1, source_target_pairs={{1,0},{2,1},{5,4},{6,5},{9,10},{10,11},{13,12},{14,13},{17,16},{18... | collective-permute-start | bytes 983048 | tf_op jit(solution)/shard_map/ppermute | solution.py:490
  29.8 0.0 collective-permute-done.3.got_hi
  29.8 1.3 %collective-permute-start.7 = (bf16[128,1280]{1,0:T(8,128)(2,1)S(1)}, bf16[128,1280]{1,0:T(8,128)(2,1)S(1)}, u32[]{:S(2)}, u32[]{:S(2)}) collective-permute-start(bf16[128,1280]{1,0:T(8,128)(2,1)S(1)} %collective-permute-done.3.got_hi), channel_id=1, source_target_pairs={{1,2},{2,3},{5,6},{6,7},{9,8},{10,9},{13,14},{14,15},{17,18},{18,1... | collective-permute-start | bytes 983048 | tf_op jit(solution)/shard_map/ppermute | solution.py:491
  31.1 4.2 %collective-permute-done.4.later_lo = bf16[128,1280]{1,0:T(8,128)(2,1)S(1)} collective-permute-done((bf16[128,1280]{1,0:T(8,128)(2,1)S(1)}, bf16[128,1280]{1,0:T(8,128)(2,1)S(1)}, u32[]{:S(2)}, u32[]{:S(2)}) %collective-permute-start.4) | collective-permute-done | bytes 327712 | tf_op jit(solution)/shard_map/ppermute | solution.py:488
  35.3 0.7 %collective-permute-start.8 = (bf16[128,1280]{1,0:T(8,128)(2,1)S(1)}, bf16[128,1280]{1,0:T(8,128)(2,1)S(1)}, u32[]{:S(2)}, u32[]{:S(2)}) collective-permute-start(bf16[128,1280]{1,0:T(8,128)(2,1)S(1)} %collective-permute-done.4.later_lo), channel_id=1, source_target_pairs={{1,0},{2,1},{5,4},{6,5},{9,10},{10,11},{13,12},{14,13},{17,16},{18... | collective-permute-start | bytes 983048 | tf_op jit(solution)/shard_map/ppermute | solution.py:490
  36.0 4.0 %collective-permute-done.5.later_hi = bf16[128,1280]{1,0:T(8,128)(2,1)S(1)} collective-permute-done((bf16[128,1280]{1,0:T(8,128)(2,1)S(1)}, bf16[128,1280]{1,0:T(8,128)(2,1)S(1)}, u32[]{:S(2)}, u32[]{:S(2)}) %collective-permute-start.5) | collective-permute-done | bytes 327712 | tf_op jit(solution)/shard_map/ppermute | solution.py:489
  40.0 1.3 %collective-permute-start.9 = (bf16[128,1280]{1,0:T(8,128)(2,1)S(1)}, bf16[128,1280]{1,0:T(8,128)(2,1)S(1)}, u32[]{:S(2)}, u32[]{:S(2)}) collective-permute-start(bf16[128,1280]{1,0:T(8,128)(2,1)S(1)} %collective-permute-done.5.later_hi), channel_id=1, source_target_pairs={{1,2},{2,3},{5,6},{6,7},{9,8},{10,9},{13,14},{14,15},{17,18},{18,1... | collective-permute-start | bytes 983048 | tf_op jit(solution)/shard_map/ppermute | solution.py:491
  41.3 4.9 %shard_map.58 = (f32[2,256,128]{2,1,0:T(8,128)S(1)}, f32[2,256,128]{2,1,0:T(8,128)S(1)}, f32[2,256,128]{2,1,0:T(8,128)S(1)}, f32[9,256,128]{2,1,0:T(8,128)S(1)},...) custom-call(f32[9]{0:T(128)S(1)} %copy-done.1, ...), custom_call_target="tpu_custom_call" | custom-call | flops 1800000000 | bytes 11010084 | tf_op jit(solution)/shard_map/pallas_call | solution.py:402
  46.2 0.0 collective-permute-done.6.got_lo2
  46.3 0.8 %collective-permute-done.7.got_hi2 = bf16[128,1280]{1,0:T(8,128)(2,1)S(1)} collective-permute-done((bf16[128,1280]{1,0:T(8,128)(2,1)S(1)}, bf16[128,1280]{1,0:T(8,128)(2,1)S(1)}, u32[]{:S(2)}, u32[]{:S(2)}) %collective-permute-start.7) | collective-permute-done | bytes 327712 | tf_op jit(solution)/shard_map/ppermute | solution.py:491
  47.0 2.1 %shard_map.59 = (bf16[256,256]{1,0:T(8,128)(2,1)S(1)}, bf16[2,256,128]{2,1,0:T(8,128)(2,1)S(1)}, f32[2,5,256,128]{3,2,1,0:T(8,128)S(1)}, f32[2,5,256,128]{3,2,1,0:T(8,128)S(1)}, f32[4,128,256]{2,1,0:T(8,128)S(1)}) custom-call(f32[9]{0:T(128)S(1)} %copy-done.1, bf16[6,128,128]{2,1,0:T(8,128)(2,1)S(1)} %get-tuple-element.42.pick_ref.pick0, ...), custom_call_target="tpu_custom_call" | custom-call | flops 400000000 | bytes 9895972 | tf_op jit(solution)/shard_map/pallas_call | solution.py:402
  49.1 0.0 collective-permute-done.8.later_lo2
  49.2 1.7 %collective-permute-done.9.later_hi2 = bf16[128,1280]{1,0:T(8,128)(2,1)S(1)} collective-permute-done((bf16[128,1280]{1,0:T(8,128)(2,1)S(1)}, bf16[128,1280]{1,0:T(8,128)(2,1)S(1)}, u32[]{:S(2)}, u32[]{:S(2)}) %collective-permute-start.9) | collective-permute-done | bytes 327712 | tf_op jit(solution)/shard_map/ppermute | solution.py:491
  50.8 1.5 %shard_map.60 = f32[9,128,256]{2,1,0:T(8,128)} custom-call(bf16[256,256]{1,0:T(8,128)(2,1)S(1)} %get-tuple-element.64.far_ref, bf16[2,256,128]{2,1,0:T(8,128)(2,1)S(1)} %get-tuple-element.65.two_ref, f32[2,5,256,128]{3,2,1,0:T(8,128)S(1)} %get-tuple-element.66.offset_ref, f32[2,5,256,128]{3,2,1,0:T(8,128)S(1)} %get-tuple-element.67.slope_ref, ...), custom_call_target="tpu_custom_call" | custom-call | flops 500000000 | bytes 7864320 | tf_op jit(solution)/shard_map/pallas_call | solution.py:402
  (1 shorter events, 0.0 us)
Async XLA Ops:
  2.4 4.4 %copy-start = (s32[8,128]{1,0:T(8,128)S(1)}, s32[8,128]{1,0:T(8,128)}, u32[]{:S(2)}) copy-start(s32[8,128]{1,0:T(8,128)} %get-tuple-element.38.lists0) | copy-start | bytes 12292
  2.4 18.9 %copy-start.1 = (f32[9]{0:T(128)S(1)}, f32[9]{0:T(128)}, u32[]{:S(2)}) copy-start(f32[9]{0:T(128)} %lewis_ref.5) | copy-start | bytes 112
  2.4 14.1 %all-to-all-start = ((bf16[8,16,2560]{2,1,0:T(8,128)(2,1)}), bf16[8,16,2560]{2,1,0:T(8,128)(2,1)S(1)}, u32[]{:S(2)}, u32[]{:S(2)}) async-start(bf16[8,16,2560]{2,1,0:T(8,128)(2,1)} %bitcast.13), calls=%async_computation | async-start | bytes 1310720 | tf_op jit(solution)/shard_map/all_to_all | solution.py:454
  6.8 4.8 %collective-permute-start = (s32[8,128]{1,0:T(8,128)S(1)}, s32[8,128]{1,0:T(8,128)S(1)}, u32[]{:S(2)}, u32[]{:S(2)}) collective-permute-start(s32[8,128]{1,0:T(8,128)S(1)} %copy-done), channel_id=1, source_target_pairs={{1,0},{2,1},{3,2},{5,4},{6,5},{7,6},{8,9},{9,10},{10,11},{13,12},{... | collective-permute-start | bytes 12296 | tf_op jit(solution)/shard_map/ppermute | solution.py:455
  10.3 5.5 %collective-permute-start.1 = (s32[8,128]{1,0:T(8,128)S(1)}, s32[8,128]{1,0:T(8,128)S(1)}, u32[]{:S(2)}, u32[]{:S(2)}) collective-permute-start(s32[8,128]{1,0:T(8,128)S(1)} %copy-done), channel_id=1, source_target_pairs={{0,1},{1,2},{2,3},{4,5},{5,6},{6,7},{9,8},{10,9},{11,10},{12,13},{... | collective-permute-start | bytes 12296 | tf_op jit(solution)/shard_map/ppermute | solution.py:456
  16.5 12.6 %collective-permute-start.2 = (bf16[128,1280]{1,0:T(8,128)(2,1)S(1)}, bf16[128,1280]{1,0:T(8,128)(2,1)S(1)}, u32[]{:S(2)}, u32[]{:S(2)}) collective-permute-start(bf16[128,1280]{1,0:T(8,128)(2,1)S(1)} %get-tuple-element.70), channel_id=1, source_target_pairs={{1,0},{2,1},{3,2},{5,4},{6,5},{7,6},{8,9},{9,10},{10,11},{13,12},{... | collective-permute-start | bytes 983048 | tf_op jit(solution)/shard_map/ppermute | solution.py:469
  20.0 9.8 %collective-permute-start.3 = (bf16[128,1280]{1,0:T(8,128)(2,1)S(1)}, bf16[128,1280]{1,0:T(8,128)(2,1)S(1)}, u32[]{:S(2)}, u32[]{:S(2)}) collective-permute-start(bf16[128,1280]{1,0:T(8,128)(2,1)S(1)} %get-tuple-element.70), channel_id=1, source_target_pairs={{0,1},{1,2},{2,3},{4,5},{5,6},{6,7},{9,8},{10,9},{11,10},{12,13},{... | collective-permute-start | bytes 983048 | tf_op jit(solution)/shard_map/ppermute | solution.py:470
  23.2 12.1 %collective-permute-start.4 = (bf16[128,1280]{1,0:T(8,128)(2,1)S(1)}, bf16[128,1280]{1,0:T(8,128)(2,1)S(1)}, u32[]{:S(2)}, u32[]{:S(2)}) collective-permute-start(bf16[128,1280]{1,0:T(8,128)(2,1)S(1)} %get-tuple-element.50), channel_id=1, source_target_pairs={{1,0},{2,1},{3,2},{5,4},{6,5},{7,6},{8,9},{9,10},{10,11},{13,12},{... | collective-permute-start | bytes 983048 | tf_op jit(solution)/shard_map/ppermute | solution.py:488
  27.8 12.2 %collective-permute-start.5 = (bf16[128,1280]{1,0:T(8,128)(2,1)S(1)}, bf16[128,1280]{1,0:T(8,128)(2,1)S(1)}, u32[]{:S(2)}, u32[]{:S(2)}) collective-permute-start(bf16[128,1280]{1,0:T(8,128)(2,1)S(1)} %get-tuple-element.50), channel_id=1, source_target_pairs={{0,1},{1,2},{2,3},{4,5},{5,6},{6,7},{9,8},{10,9},{11,10},{12,13},{... | collective-permute-start | bytes 983048 | tf_op jit(solution)/shard_map/ppermute | solution.py:489
  29.1 17.1 %collective-permute-start.6 = (bf16[128,1280]{1,0:T(8,128)(2,1)S(1)}, bf16[128,1280]{1,0:T(8,128)(2,1)S(1)}, u32[]{:S(2)}, u32[]{:S(2)}) collective-permute-start(bf16[128,1280]{1,0:T(8,128)(2,1)S(1)} %collective-permute-done.2.got_lo), channel_id=1, source_target_pairs={{1,0},{2,1},{5,4},{6,5},{9,10},{10,11},{13,12},{14,13},{17,16},{18... | collective-permute-start | bytes 983048 | tf_op jit(solution)/shard_map/ppermute | solution.py:490
  29.8 17.2 %collective-permute-start.7 = (bf16[128,1280]{1,0:T(8,128)(2,1)S(1)}, bf16[128,1280]{1,0:T(8,128)(2,1)S(1)}, u32[]{:S(2)}, u32[]{:S(2)}) collective-permute-start(bf16[128,1280]{1,0:T(8,128)(2,1)S(1)} %collective-permute-done.3.got_hi), channel_id=1, source_target_pairs={{1,2},{2,3},{5,6},{6,7},{9,8},{10,9},{13,14},{14,15},{17,18},{18,1... | collective-permute-start | bytes 983048 | tf_op jit(solution)/shard_map/ppermute | solution.py:491
  35.3 13.8 %collective-permute-start.8 = (bf16[128,1280]{1,0:T(8,128)(2,1)S(1)}, bf16[128,1280]{1,0:T(8,128)(2,1)S(1)}, u32[]{:S(2)}, u32[]{:S(2)}) collective-permute-start(bf16[128,1280]{1,0:T(8,128)(2,1)S(1)} %collective-permute-done.4.later_lo), channel_id=1, source_target_pairs={{1,0},{2,1},{5,4},{6,5},{9,10},{10,11},{13,12},{14,13},{17,16},{18... | collective-permute-start | bytes 983048 | tf_op jit(solution)/shard_map/ppermute | solution.py:490
  40.0 10.8 %collective-permute-start.9 = (bf16[128,1280]{1,0:T(8,128)(2,1)S(1)}, bf16[128,1280]{1,0:T(8,128)(2,1)S(1)}, u32[]{:S(2)}, u32[]{:S(2)}) collective-permute-start(bf16[128,1280]{1,0:T(8,128)(2,1)S(1)} %collective-permute-done.5.later_hi), channel_id=1, source_target_pairs={{1,2},{2,3},{5,6},{6,7},{9,8},{10,9},{13,14},{14,15},{17,18},{18,1... | collective-permute-start | bytes 983048 | tf_op jit(solution)/shard_map/ppermute | solution.py:491
